TPU v7x, 32 devices: a whole 2x2x4 slice. The times are simulated.
32 devices in a mesh: wide: 8 (over y, x, core), narrow: 4 (over z).
Axes of the slice: x: 2, y: 2, z: 4, core: 2. Of those that a mesh axis runs over, the one named last changes fastest.
Arguments:
- inputs: bfloat16 [32, 258, 1152], P(('wide', 'narrow')), may hold values from -6 to 6
- skip_tokens: bfloat16 [32, 258, 1152], P(('wide', 'narrow')), may hold values from -6 to 6
- cotangent: bfloat16 [32, 258, 1152], P(('wide', 'narrow')), may hold values from -12 to 12
- merge_weight: float32 [2304, 1152], P('wide', 'narrow'), may hold values from -0.125 to 0.125
- merge_moment: float32 [2304, 1152], P('wide', 'narrow'), may hold values from -1536 to 1536
- merge_square: float32 [2304, 1152], P('wide', 'narrow'), may hold values from 74304 to 297216
- attend_weight: float32 [1152, 3456], P('wide', 'narrow'), may hold values from -0.25 to 0.25
- attend_moment: float32 [1152, 3456], P('wide', 'narrow'), may hold values from -1024 to 1024
- attend_square: float32 [1152, 3456], P('wide', 'narrow'), may hold values from 33024 to 132096
- output_weight: float32 [1152, 1152], P('wide', 'narrow'), may hold values from -2 to 2
- output_moment: float32 [1152, 1152], P('wide', 'narrow'), may hold values from -128 to 128
- output_square: float32 [1152, 1152], P('wide', 'narrow'), may hold values from 516 to 2064
- expand_weight: float32 [1152, 4608], P('wide', 'narrow'), may hold values from -0.1875 to 0.1875
- expand_moment: float32 [1152, 4608], P('wide', 'narrow'), may hold values from -160 to 160
- expand_square: float32 [1152, 4608], P('wide', 'narrow'), may hold values from 743.04 to 2972.16
- shrink_weight: float32 [4608, 1152], P('wide', 'narrow'), may hold values from -0.09375 to 0.09375
- shrink_moment: float32 [4608, 1152], P('wide', 'narrow'), may hold values from -320 to 320
- shrink_square: float32 [4608, 1152], P('wide', 'narrow'), may hold values from 2972.16 to 11888.64
- vectors: float32 [12672], P('narrow'), may hold values from -1.2 to 1.5
- vector_moment: float32 [12672], P('narrow'), may hold values from -1024 to 1024
- vector_square: float32 [12672], P('narrow'), may hold values from 33024 to 132096
Outputs:
- outputs: bfloat16 [32, 258, 1152], P(('wide', 'narrow'))
- input_gradient: bfloat16 [32, 258, 1152], P(('wide', 'narrow'))
- skip_gradient: bfloat16 [32, 258, 1152], P(('wide', 'narrow'))
- renewed_merge: float32 [2304, 1152], P('wide', 'narrow')
- moment_merge: float32 [2304, 1152], P('wide', 'narrow')
- square_merge: float32 [2304, 1152], P('wide', 'narrow')
- renewed_attend: float32 [1152, 3456], P('wide', 'narrow')
- moment_attend: float32 [1152, 3456], P('wide', 'narrow')
- square_attend: float32 [1152, 3456], P('wide', 'narrow')
- renewed_output: float32 [1152, 1152], P('wide', 'narrow')
- moment_output: float32 [1152, 1152], P('wide', 'narrow')
- square_output: float32 [1152, 1152], P('wide', 'narrow')
- renewed_expand: float32 [1152, 4608], P('wide', 'narrow')
- moment_expand: float32 [1152, 4608], P('wide', 'narrow')
- square_expand: float32 [1152, 4608], P('wide', 'narrow')
- renewed_shrink: float32 [4608, 1152], P('wide', 'narrow')
- moment_shrink: float32 [4608, 1152], P('wide', 'narrow')
- square_shrink: float32 [4608, 1152], P('wide', 'narrow')
- renewed_vector: float32 [12672], P('narrow')
- moment_vector: float32 [12672], P('narrow')
- square_vector: float32 [12672], P('narrow')
All inputs are finite; a program needn't handle non-finite values.
Results may differ from a plain program's by a relative error of at most 0.017.
The roundings to bfloat16 on the way count: a program that leaves them out, or rounds other values in their place, can miss the bound.
Values may be sent and summed in bfloat16 or wider, within the bound.
No kernel may reach another device: no remote copies, remote signals or barrier semaphores. Data moves between devices by JAX's collectives and lax.ppermute only.
A program may use at most 256 MiB of HBM per device.

v0:
```python
import jax
import jax.numpy as jnp
from jax import lax
from jax.sharding import PartitionSpec as P

D = 1152
FF = 4608
H = 16
HD = 72
STEP = 5


norm_epsilon = 1e-05
adam_epsilon = 1e-08
beta_moment = 0.5
weight_decay = 0.01
rate_merge = 0.04
rate_attend = 0.08
rate_output = 0.6
rate_expand = 0.06
rate_shrink = 0.03
rate_vector = 0.6


def product(left_side, right_side):
    return jnp.dot(left_side, right_side, preferred_element_type=jnp.float32)


def transposed(gradient, matrix):
    return lax.dot_general(
        gradient,
        matrix,
        (((gradient.ndim - 1,), (1,)), ((), ())),
        preferred_element_type=jnp.float32,
    )


def weight_gradient(activations, gradient):
    flat_left = activations.reshape(-1, activations.shape[-1])
    flat_right = gradient.reshape(-1, gradient.shape[-1])
    return lax.dot_general(
        flat_left, flat_right, (((0,), (0,)), ((), ())), preferred_element_type=jnp.float32
    )


def normalize(values):
    centered = values - jnp.mean(values, axis=-1, keepdims=True)
    spread = jnp.mean(centered * centered, axis=-1, keepdims=True)
    inverse = lax.rsqrt(spread + norm_epsilon)
    return (centered * inverse, inverse)


def norm_back(gradient, normed, inverse):
    return inverse * (
        gradient
        - jnp.mean(gradient, axis=-1, keepdims=True)
        - normed * jnp.mean(gradient * normed, axis=-1, keepdims=True)
    )


def row_sum(values):
    return jnp.sum(values, axis=(0, 1))


def unpack(packed):
    return tuple((packed[position * D : (position + 1) * D] for position in range(7))) + (
        packed[7 * D : 7 * D + FF],
    )


def gaussian_unit(values):
    return jax.nn.gelu(values, approximate=False)


def adamw_update(weight, moment, square, gradient, step_rate):
    moment_new = beta_moment * moment + (1.0 - beta_moment) * gradient
    square_new = beta_moment * square + (1.0 - beta_moment) * gradient * gradient
    correct = 1.0 - beta_moment**STEP
    direction = moment_new / correct / (jnp.sqrt(square_new / correct) + adam_epsilon)
    return (weight - step_rate * (direction + weight_decay * weight), moment_new, square_new)


def on_device(
    inputs,
    skip_tokens,
    cotangent,
    merge_weight,
    merge_moment,
    merge_square,
    attend_weight,
    attend_moment,
    attend_square,
    output_weight,
    output_moment,
    output_square,
    expand_weight,
    expand_moment,
    expand_square,
    shrink_weight,
    shrink_moment,
    shrink_square,
    vectors,
    vector_moment,
    vector_square,
):
    merge_low = merge_weight.astype(jnp.bfloat16)
    attend_low = attend_weight.astype(jnp.bfloat16)
    output_low = output_weight.astype(jnp.bfloat16)
    expand_low = expand_weight.astype(jnp.bfloat16)
    shrink_low = shrink_weight.astype(jnp.bfloat16)
    vector_low = vectors.astype(jnp.bfloat16)
    columns = (
        lax.all_gather(merge_low, "narrow", axis=1, tiled=True),
        lax.all_gather(attend_low, "narrow", axis=1, tiled=True),
        lax.all_gather(output_low, "narrow", axis=1, tiled=True),
        lax.all_gather(expand_low, "narrow", axis=1, tiled=True),
        lax.all_gather(shrink_low, "narrow", axis=1, tiled=True),
        lax.all_gather(vector_low, "narrow", axis=0, tiled=True),
    )
    matrices = (
        lax.all_gather(columns[0], "wide", axis=0, tiled=True),
        lax.all_gather(columns[1], "wide", axis=0, tiled=True),
        lax.all_gather(columns[2], "wide", axis=0, tiled=True),
        lax.all_gather(columns[3], "wide", axis=0, tiled=True),
        lax.all_gather(columns[4], "wide", axis=0, tiled=True),
    )
    skip_bias, gain_one, bias_one, output_bias, gain_two, bias_two, shrink_bias, expand_bias = (
        unpack(columns[5].astype(jnp.float32))
    )
    images = inputs.shape[0]
    length = inputs.shape[1]
    softmax_scale = HD ** (-0.5)
    joined = jnp.concatenate([inputs, skip_tokens], axis=-1)
    stream_zero = product(joined, matrices[0]) + skip_bias
    normed_one, inverse_one = normalize(stream_zero)
    attend_input = (normed_one * gain_one + bias_one).astype(jnp.bfloat16)
    mixed_heads = product(attend_input, matrices[1]).astype(jnp.bfloat16)
    query_heads = mixed_heads[..., 0:D].reshape(images, length, H, HD)
    key_heads = mixed_heads[..., D : 2 * D].reshape(images, length, H, HD)
    value_heads = mixed_heads[..., 2 * D : 3 * D].reshape(images, length, H, HD)
    logits = (
        jnp.einsum("blhe,bmhe->bhlm", query_heads, key_heads, preferred_element_type=jnp.float32)
        * softmax_scale
    )
    maxima = jnp.max(logits, axis=-1, keepdims=True)
    log_total = maxima + jnp.log(jnp.sum(jnp.exp(logits - maxima), axis=-1, keepdims=True))
    softmax_low = jnp.exp(logits - log_total).astype(jnp.bfloat16)
    mixture = jnp.einsum(
        "bhlm,bmhe->blhe", softmax_low, value_heads, preferred_element_type=jnp.float32
    )
    mixture = mixture.astype(jnp.bfloat16).reshape(images, length, D)
    stream_one = stream_zero + product(mixture, matrices[2]) + output_bias
    normed_two, inverse_two = normalize(stream_one)
    expand_input = (normed_two * gain_two + bias_two).astype(jnp.bfloat16)
    hidden = product(expand_input, matrices[3]) + expand_bias
    active, pullback = jax.vjp(gaussian_unit, hidden)
    active_low = active.astype(jnp.bfloat16)
    outputs = (stream_one + product(active_low, matrices[4]) + shrink_bias).astype(jnp.bfloat16)
    columns_back = (
        lax.all_gather(merge_low, "narrow", axis=1, tiled=True),
        lax.all_gather(attend_low, "narrow", axis=1, tiled=True),
        lax.all_gather(output_low, "narrow", axis=1, tiled=True),
        lax.all_gather(expand_low, "narrow", axis=1, tiled=True),
        lax.all_gather(shrink_low, "narrow", axis=1, tiled=True),
        lax.all_gather(vector_low, "narrow", axis=0, tiled=True),
    )
    matrices_back = (
        lax.all_gather(columns_back[0], "wide", axis=0, tiled=True),
        lax.all_gather(columns_back[1], "wide", axis=0, tiled=True),
        lax.all_gather(columns_back[2], "wide", axis=0, tiled=True),
        lax.all_gather(columns_back[3], "wide", axis=0, tiled=True),
        lax.all_gather(columns_back[4], "wide", axis=0, tiled=True),
    )
    packed_back = columns_back[5].astype(jnp.float32)
    unpacked = unpack(packed_back)
    gain_first = unpacked[1]
    gain_second = unpacked[4]
    upstream = cotangent.astype(jnp.float32)
    shrink_gradient = weight_gradient(active_low, cotangent)
    delta_active = transposed(cotangent, matrices_back[4])
    delta_hidden = pullback(delta_active)[0]
    hidden_low = delta_hidden.astype(jnp.bfloat16)
    expand_gradient = weight_gradient(expand_input, hidden_low)
    delta_expand = transposed(hidden_low, matrices_back[3])
    delta_one = upstream + norm_back(delta_expand * gain_second, normed_two, inverse_two)
    stream_low = delta_one.astype(jnp.bfloat16)
    output_gradient = weight_gradient(mixture, stream_low)
    delta_mixture = (
        transposed(stream_low, matrices_back[2]).astype(jnp.bfloat16).reshape(images, length, H, HD)
    )
    logits_again = (
        jnp.einsum("blhe,bmhe->bhlm", query_heads, key_heads, preferred_element_type=jnp.float32)
        * softmax_scale
    )
    softmax_again = jnp.exp(logits_again - log_total)
    delta_softmax = jnp.einsum(
        "blhe,bmhe->bhlm", delta_mixture, value_heads, preferred_element_type=jnp.float32
    )
    delta_values = jnp.einsum(
        "bhlm,blhe->bmhe",
        softmax_again.astype(jnp.bfloat16),
        delta_mixture,
        preferred_element_type=jnp.float32,
    )
    delta_logits = softmax_again * (
        delta_softmax - jnp.sum(softmax_again * delta_softmax, axis=-1, keepdims=True)
    )
    delta_scores = (softmax_scale * delta_logits).astype(jnp.bfloat16)
    delta_queries = jnp.einsum(
        "bhlm,bmhe->blhe", delta_scores, key_heads, preferred_element_type=jnp.float32
    )
    delta_keys = jnp.einsum(
        "bhlm,blhe->bmhe", delta_scores, query_heads, preferred_element_type=jnp.float32
    )
    delta_mixed = jnp.concatenate(
        [
            delta_queries.reshape(images, length, D),
            delta_keys.reshape(images, length, D),
            delta_values.reshape(images, length, D),
        ],
        axis=-1,
    ).astype(jnp.bfloat16)
    attend_gradient = weight_gradient(attend_input, delta_mixed)
    delta_attend = transposed(delta_mixed, matrices_back[1])
    delta_zero = delta_one + norm_back(delta_attend * gain_first, normed_one, inverse_one)
    zero_low = delta_zero.astype(jnp.bfloat16)
    merge_gradient = weight_gradient(joined, zero_low)
    delta_joined = transposed(zero_low, matrices_back[0])
    input_gradient = delta_joined[..., 0:D].astype(jnp.bfloat16)
    skip_gradient = delta_joined[..., D : 2 * D].astype(jnp.bfloat16)
    vector_gradient = jnp.concatenate(
        [
            row_sum(delta_zero),
            row_sum(delta_attend * normed_one),
            row_sum(delta_attend),
            row_sum(delta_one),
            row_sum(delta_expand * normed_two),
            row_sum(delta_expand),
            row_sum(upstream),
            row_sum(delta_hidden),
        ]
    )
    owned_rows = (
        lax.psum_scatter(merge_gradient, "wide", scatter_dimension=0, tiled=True),
        lax.psum_scatter(attend_gradient, "wide", scatter_dimension=0, tiled=True),
        lax.psum_scatter(output_gradient, "wide", scatter_dimension=0, tiled=True),
        lax.psum_scatter(expand_gradient, "wide", scatter_dimension=0, tiled=True),
        lax.psum_scatter(shrink_gradient, "wide", scatter_dimension=0, tiled=True),
    )
    vector_total = lax.psum(vector_gradient, "wide")
    parted = (
        lax.psum_scatter(owned_rows[0], "narrow", scatter_dimension=1, tiled=True),
        lax.psum_scatter(owned_rows[1], "narrow", scatter_dimension=1, tiled=True),
        lax.psum_scatter(owned_rows[2], "narrow", scatter_dimension=1, tiled=True),
        lax.psum_scatter(owned_rows[3], "narrow", scatter_dimension=1, tiled=True),
        lax.psum_scatter(owned_rows[4], "narrow", scatter_dimension=1, tiled=True),
        lax.psum_scatter(vector_total, "narrow", scatter_dimension=0, tiled=True),
    )
    merge_new = adamw_update(merge_weight, merge_moment, merge_square, parted[0], rate_merge)
    attend_new = adamw_update(attend_weight, attend_moment, attend_square, parted[1], rate_attend)
    output_new = adamw_update(output_weight, output_moment, output_square, parted[2], rate_output)
    expand_new = adamw_update(expand_weight, expand_moment, expand_square, parted[3], rate_expand)
    shrink_new = adamw_update(shrink_weight, shrink_moment, shrink_square, parted[4], rate_shrink)
    vector_new = adamw_update(vectors, vector_moment, vector_square, parted[5], rate_vector)
    return (
        outputs,
        input_gradient,
        skip_gradient,
        merge_new[0],
        merge_new[1],
        merge_new[2],
        attend_new[0],
        attend_new[1],
        attend_new[2],
        output_new[0],
        output_new[1],
        output_new[2],
        expand_new[0],
        expand_new[1],
        expand_new[2],
        shrink_new[0],
        shrink_new[1],
        shrink_new[2],
        vector_new[0],
        vector_new[1],
        vector_new[2],
    )


def solution(mesh):
    in_specs = (
        P(("wide", "narrow"), None, None),
        P(("wide", "narrow"), None, None),
        P(("wide", "narrow"), None, None),
        P("wide", "narrow"),
        P("wide", "narrow"),
        P("wide", "narrow"),
        P("wide", "narrow"),
        P("wide", "narrow"),
        P("wide", "narrow"),
        P("wide", "narrow"),
        P("wide", "narrow"),
        P("wide", "narrow"),
        P("wide", "narrow"),
        P("wide", "narrow"),
        P("wide", "narrow"),
        P("wide", "narrow"),
        P("wide", "narrow"),
        P("wide", "narrow"),
        P("narrow"),
        P("narrow"),
        P("narrow"),
    )
    out_specs = (
        P(("wide", "narrow"), None, None),
        P(("wide", "narrow"), None, None),
        P(("wide", "narrow"), None, None),
        P("wide", "narrow"),
        P("wide", "narrow"),
        P("wide", "narrow"),
        P("wide", "narrow"),
        P("wide", "narrow"),
        P("wide", "narrow"),
        P("wide", "narrow"),
        P("wide", "narrow"),
        P("wide", "narrow"),
        P("wide", "narrow"),
        P("wide", "narrow"),
        P("wide", "narrow"),
        P("wide", "narrow"),
        P("wide", "narrow"),
        P("wide", "narrow"),
        P("narrow"),
        P("narrow"),
        P("narrow"),
    )
    return jax.shard_map(
        on_device, mesh=mesh, in_specs=in_specs, out_specs=out_specs, check_vma=False
    )
```

profile of v0, /device:TPU:0, one launch (start us, length us, event | category | flops | bytes accessed | tf_op | source)
XLA Modules:
  0.0 1197.7 jit_solution(13935477650223554407)
XLA Ops:
  7.2 1.9 convert_element_type.101
  9.2 1.9 convert_element_type.103
  12.4 32.1 %all_gather.44 = bf16[288,1152]{0,1:T(8,128)(2,1)S(1)} all-gather(bf16[288,288]{0,1:T(8,128)(2,1)S(1)} %copy.105), channel_id=1, replica_groups=mesh['wide'=8,'narrow'=4] {'narrow'}, dimensions={1}, use_global_device_ids=true | all-gather | bytes 829440 | tf_op jit(solution)/shard_map/all_gather | solution.py:113
  45.8 26.6 %all-gather = bf16[4,864,144]{1,2,0:T(8,128)(2,1)S(1)} all-gather(bf16[1,864,144]{1,2,0:T(8,128)(2,1)S(1)} %convert_bitcast_fusion), channel_id=1, replica_groups=mesh['wide'=8,'narrow'=4] {'narrow'}, dimensions={0}, use_global_device_ids=true | all-gather | bytes 1244160 | tf_op jit(solution)/shard_map/all_gather | solution.py:114
  72.7 1.7 reshape.439
  74.6 19.6 %all-gather.1 = bf16[4,288,144]{1,2,0:T(8,128)(2,1)S(1)} all-gather(bf16[1,288,144]{1,2,0:T(8,128)(2,1)S(1)} %convert_bitcast_fusion.1), channel_id=1, replica_groups=mesh['wide'=8,'narrow'=4] {'narrow'}, dimensions={0}, use_global_device_ids=true | all-gather | bytes 414720 | tf_op jit(solution)/shard_map/all_gather | solution.py:115
  96.1 8.7 all-gather.20.cloned.1.call-done
  104.8 2.6 copy.113
  109.2 17.2 %all-reduce = bf16[12672]{0:T(1024)(128)(2,1)S(1)} all-reduce(bf16[12672]{0:T(1024)(128)(2,1)S(1)} %dynamic-update-slice), channel_id=1, replica_groups=mesh['wide'=8,'narrow'=4] {'narrow'}, use_global_device_ids=true, to_apply=%add | all-reduce | flops 12672 | bytes 50688
  127.0 20.6 %all-gather.10.cloned.1.call-done = bf16[2304,1152]{1,0:T(8,128)(2,1)} async-done(((bf16[288,1152]{1,0:T(8,128)(2,1)}), bf16[2304,1152]{1,0:T(8,128)(2,1)}) %all-gather.10.cloned.1.call-update) | async-done | bytes 5308432 | tf_op jit(solution)/shard_map/all_gather | solution.py:121
  147.6 4.6 fusion.92
  152.5 49.4 %all-gather.12.cloned.1.call-done = bf16[1152,3456]{1,0:T(8,128)(2,1)} async-done(((bf16[144,3456]{1,0:T(8,128)(2,1)}), bf16[1152,3456]{1,0:T(8,128)(2,1)}) %all-gather.12.cloned.1.call-update) | async-done | bytes 7962640 | tf_op jit(solution)/shard_map/all_gather | solution.py:122
  202.0 6.0 fusion.2
  209.2 1.5 copy.142
  211.9 1.5 copy.141
  213.5 2.8 multiply_reduce_fusion.1
  219.0 1.5 convolution_convert_fusion.4
  220.4 14.1 %all-gather.14.cloned.1.call-done = bf16[1152,1152]{1,0:T(8,128)(2,1)} async-done(((bf16[144,1152]{1,0:T(8,128)(2,1)}), bf16[1152,1152]{1,0:T(8,128)(2,1)}) %all-gather.14.cloned.1.call-update) | async-done | bytes 2654224 | tf_op jit(solution)/shard_map/all_gather | solution.py:123
  234.6 3.0 fusion.93
  237.8 62.3 %all-gather.18.cloned.1.call-done = bf16[1152,4608]{1,0:T(8,128)(2,1)} async-done(((bf16[144,4608]{1,0:T(8,128)(2,1)}), bf16[1152,4608]{1,0:T(8,128)(2,1)}) %all-gather.18.cloned.1.call-update) | async-done | bytes 10616848 | tf_op jit(solution)/shard_map/all_gather | solution.py:124
  300.2 18.2 %multiply_convert_fusion.1 = (bf16[258,4608]{1,0:T(8,128)(2,1)}, f32[258,4608]{1,0:T(8,128)}, f32[258,4608]{1,0:T(8,128)}) fusion(f32[4608]{0:T(1024)S(1)} %slice.65, bf16[1152,4608]{1,0:T(8,128)(2,1)} %all-gather.18.cloned.1.call-done, f32[258,1152]{1,0:T(8,128)S(1)} %get-tuple-element.157, f32[1152]{0:T(1024)S(1)} %get-tuple-element.145, ...), kind=kOutput, calls=%fused_computation.13 | convolution fusion | flops 2819093760 | bytes 23724048 | tf_op jit(solution)/shard_map/dot_general | solution.py:26
  318.4 47.5 %all-gather.22.cloned.1.call-done = bf16[4608,1152]{1,0:T(8,128)(2,1)} async-done(((bf16[576,1152]{1,0:T(8,128)(2,1)}), bf16[4608,1152]{1,0:T(8,128)(2,1)}) %all-gather.22.cloned.1.call-update) | async-done | bytes 10616848 | tf_op jit(solution)/shard_map/all_gather | solution.py:125
  365.9 11.2 fusion.94
  377.2 8.5 multiply_reduce_fusion.2
  387.3 4.0 fusion.48
  391.6 4.1 convolution_convert_fusion.2
  395.7 2.4 copy.144
  398.0 5.6 fusion.95
  403.7 13.6 %fusion.31 = bf16[16,72,258]{2,1,0:T(8,128)(2,1)} fusion(bf16[258,16,72]{0,2,1:T(8,128)(2,1)} %bitcast.123, f32[16,258,258]{1,2,0:T(8,128)} %fusion.95, f32[16,258,258]{1,2,0:T(8,128)} %copy-done, f32[16,258]{1,0:T(8,128)S(1)} %log_add_fusion), kind=kOutput, calls=%fused_computation.47 | convolution fusion | flops 163250272 | bytes 9725568 | tf_op jit(solution)/shard_map/bhlm,bmhe->blhe/dot_general | solution.py:209
  417.2 13.2 %fusion.34 = bf16[16,72,258]{2,1,0:T(8,128)(2,1)} fusion(bf16[258,16,72]{0,2,1:T(8,128)(2,1)} %bitcast.121, f32[16,258,258]{1,2,0:T(8,128)} %fusion.95, f32[16,258,258]{1,2,0:T(8,128)} %copy-done, f32[16,258]{1,0:T(8,128)S(1)} %log_add_fusion), kind=kOutput, calls=%fused_computation.48 | convolution fusion | flops 163250272 | bytes 9725568 | tf_op jit(solution)/shard_map/bhlm,blhe->bmhe/dot_general | solution.py:212
  430.4 4.5 convolution_convert_fusion.3
  434.9 8.3 multiply_reduce_fusion.3
  444.6 5.8 fusion.44
  451.5 12.2 %fusion.41 = f32[1152,3456]{1,0:T(8,128)} fusion(bf16[258,1152]{0,1:T(8,128)(2,1)S(1)} %bitcast.125, bf16[258,1152]{0,1:T(8,128)(2,1)} %bitcast.130, bf16[258,1152]{0,1:T(8,128)(2,1)} %bitcast.128, f32[258,1152]{1,0:T(8,128)S(1)} %get-tuple-element.153, f32[1152]{0:T(1024)S(1)} %get-tuple-element.148, f32[1152]{0:T(1024)S(1)} %get-tuple-element.147, ...), kind=kOutput, calls=%fused_computation.69 | convolution fusion | flops 2061192960 | bytes 18908688 | tf_op jit(solution)/shard_map/dot_general | solution.py:41
  464.9 13.0 %fusion.51 = f32[4608,1152]{1,0:T(8,128)} fusion(bf16[258,4608]{1,0:T(8,128)(2,1)} %get-tuple-element.135, bf16[1,258,1152]{2,1,0:T(8,128)(2,1)S(1)} %copy-done.14), kind=kOutput, calls=%fused_computation.89 | convolution fusion | flops 2739142656 | bytes 24205824 | tf_op jit(solution)/shard_map/dot_general | solution.py:41
  477.9 12.3 %fusion.37 = f32[1152,4608]{1,0:T(8,128)} fusion(bf16[258,4608]{1,0:T(8,128)(2,1)} %copy-done.16, f32[258,1152]{1,0:T(8,128)S(1)} %get-tuple-element.157, f32[1152]{0:T(1024)S(1)} %get-tuple-element.145, f32[1152]{0:T(1024)S(1)} %get-tuple-element.144, f32[258]{0:T(512)S(1)} %add_rsqrt_fusion, f32[258]{0:T(512)S(1)} %broadcast_multiply_fusion.4), kind=kOutput, calls=%fused_computation.59 | convolution fusion | flops 2740628736 | bytes 24811536 | tf_op jit(solution)/shard_map/dot_general | solution.py:41
  490.3 2.5 copy.137
  492.9 41.7 %reduce-scatter.19.cloned.1.call-done = f32[288,1152]{1,0:T(8,128)} async-done(((f32[2304,1152]{1,0:T(8,128)}), f32[288,1152]{1,0:T(8,128)}) %reduce-scatter.19.cloned.1.call-update) | async-done | bytes 1327120 | tf_op jit(solution)/shard_map/reduce_scatter | solution.py:244
  534.6 3.1 copy.133
  538.0 113.4 %reduce-scatter.21.cloned.1.call-done = f32[144,3456]{1,0:T(8,128)} async-done(((f32[1152,3456]{1,0:T(8,128)}), f32[144,3456]{1,0:T(8,128)}) %reduce-scatter.21.cloned.1.call-update) | async-done | bytes 1990672 | tf_op jit(solution)/shard_map/reduce_scatter | solution.py:245
  651.4 3.6 copy.135
  655.1 137.1 %reduce-scatter.29.cloned.1.call-done = f32[576,1152]{1,0:T(8,128)} async-done(((f32[4608,1152]{1,0:T(8,128)}), f32[576,1152]{1,0:T(8,128)}) %reduce-scatter.29.cloned.1.call-update) | async-done | bytes 2654224 | tf_op jit(solution)/shard_map/reduce_scatter | solution.py:248
  792.2 3.5 copy.139
  795.8 137.1 %reduce-scatter.25.cloned.1.call-done = f32[144,4608]{1,0:T(8,128)} async-done(((f32[1152,4608]{1,0:T(8,128)}), f32[144,4608]{1,0:T(8,128)}) %reduce-scatter.25.cloned.1.call-update) | async-done | bytes 2654224 | tf_op jit(solution)/shard_map/reduce_scatter | solution.py:247
  934.7 2.4 copy.123
  937.8 22.1 %all-reduce.1 = f32[12672]{0:T(1024)S(1)} all-reduce(f32[12672]{0:T(1024)S(1)} %constant_dynamic-update-slice_fusion), channel_id=12, replica_groups=mesh['wide'=8,'narrow'=4] {'narrow'}, use_global_device_ids=true, to_apply=%region_30.0.clone | all-reduce | flops 12672 | bytes 101376
  960.0 22.4 %psum.8 = f32[3168]{0:T(1024)S(1)} all-reduce(f32[3168]{0:T(1024)S(1)} %dynamic-slice.2), channel_id=1, replica_groups=mesh['wide'=8,'narrow'=4] {'wide'}, use_global_device_ids=true, to_apply=%region_29.0 | all-reduce | flops 3168 | bytes 25344 | tf_op jit(solution)/shard_map/psum | solution.py:250
  983.1 4.7 fusion.18
  988.9 7.0 fusion.30
  997.0 2.1 multiply_subtract_fusion.4
  999.1 6.6 reduce-scatter.31.cloned.1.call-done
  1005.8 2.0 copy.134
  1007.8 2.8 multiply_subtract_fusion.3
  1010.5 63.0 %reduce-scatter.33.cloned.1.call-done = f32[864,144]{1,0:T(8,128)} async-done(((f32[3456,144]{1,0:T(8,128)}), f32[864,144]{1,0:T(8,128)}) %reduce-scatter.33.cloned.1.call-update) | async-done | bytes 497680
  1073.5 2.2 copy.136
  1075.8 2.7 multiply_subtract_fusion.2
  1078.5 54.8 %reduce-scatter.37.cloned.1.call-done = f32[288,576]{1,0:T(8,128)} async-done(((f32[1152,576]{1,0:T(8,128)}), f32[288,576]{1,0:T(8,128)}) %reduce-scatter.37.cloned.1.call-update) | async-done | bytes 663568
  1133.3 2.4 copy.140
  1135.7 3.3 multiply_subtract_fusion
  1139.0 2.5 copy.126
  1141.5 2.4 copy.127
  1143.8 2.3 copy.128
  1146.2 41.8 %reduce-scatter.27.cloned.1.call-done = f32[144,1152]{1,0:T(8,128)} async-done(((f32[144,4608]{1,0:T(8,128)}), f32[144,1152]{1,0:T(8,128)}) %reduce-scatter.27.cloned.1.call-update) | async-done | bytes 663568 | tf_op jit(solution)/shard_map/reduce_scatter | solution.py:255
  1188.0 2.7 multiply_subtract_fusion.1
  (146 shorter events, 23.2 us)
Async XLA Ops:
  7.2 38.5 %copy-start.17 = (f32[144,864]{1,0:T(8,128)S(1)}, f32[144,864]{1,0:T(8,128)}, u32[]{:S(2)}) copy-start(f32[144,864]{1,0:T(8,128)} %param.27) | copy-start | bytes 1492996
  7.2 88.3 %all-gather.16.cloned.1.call-start = ((), (), s32[]{:S(2)}) async-start(), calls=%async_computation.13 | async-start | bytes 1658880 | tf_op jit(solution)/shard_map/all_gather | solution.py:116
  9.2 95.7 %all-gather.20.cloned.1.call-start = ((), (), s32[]{:S(2)}) async-start(), calls=%async_computation.15 | async-start | bytes 1843200 | tf_op jit(solution)/shard_map/all_gather | solution.py:117
  11.1 136.5 %all-gather.10.cloned.1.call-start = ((), (), s32[]{:S(2)}) async-start(), calls=%async_computation.10 | async-start | bytes 5971968 | tf_op jit(solution)/shard_map/all_gather | solution.py:121
  44.5 30.1 %copy-start.19 = (f32[144,288]{1,0:T(8,128)S(1)}, f32[144,288]{1,0:T(8,128)}, u32[]{:S(2)}) copy-start(f32[144,288]{1,0:T(8,128)} %param.30) | copy-start | bytes 497668
  45.7 156.3 %all-gather.12.cloned.1.call-start = ((), (), s32[]{:S(2)}) async-start(), calls=%async_computation.11 | async-start | bytes 8957952 | tf_op jit(solution)/shard_map/all_gather | solution.py:122
  74.5 33.0 %copy-start.27 = (f32[3168]{0:T(1024)S(1)}, f32[3168]{0:T(1024)}, u32[]{:S(2)}) copy-start(f32[3168]{0:T(1024)} %param.39) | copy-start | bytes 38020
  74.5 33.1 %copy-start.32 = (u32[32]{0:T(128)S(1)}, u32[32]{0:T(128)}, u32[]{:S(2)}) copy-start(u32[32]{0:T(128)} %constant.134) | copy-start | bytes 388
  74.5 73.1 %copy-start.24 = (bf16[1,258,1152]{2,1,0:T(8,128)(2,1)S(1)}, bf16[1,258,1152]{2,1,0:T(8,128)(2,1)}, u32[]{:S(2)}) copy-start(bf16[1,258,1152]{2,1,0:T(8,128)(2,1)} %param.22) | copy-start | bytes 1783300
  74.5 160.0 %all-gather.14.cloned.1.call-start = ((), (), s32[]{:S(2)}) async-start(), calls=%async_computation.12 | async-start | bytes 2985984 | tf_op jit(solution)/shard_map/all_gather | solution.py:123
  95.5 204.7 %all-gather.18.cloned.1.call-start = ((), (), s32[]{:S(2)}) async-start(), calls=%async_computation.14 | async-start | bytes 11943936 | tf_op jit(solution)/shard_map/all_gather | solution.py:124
  96.1 269.9 %all-gather.22.cloned.1.call-start = ((), (), s32[]{:S(2)}) async-start(), calls=%async_computation.16 | async-start | bytes 11943936 | tf_op jit(solution)/shard_map/all_gather | solution.py:125
  107.5 382.8 %reduce-scatter.23.cloned.1.call-start = ((), (), s32[]{:S(2)}) async-start(), calls=%async_computation.19 | async-start | bytes 5971968 | tf_op jit(solution)/shard_map/reduce_scatter | solution.py:246
  210.7 5.6 copy-start.7
  213.5 4.1 copy-start.3
  216.3 2.7 copy-start
  377.2 8.5 copy-start.16
  377.2 8.5 copy-start.13
  386.3 1.1 copy-start.1
  391.4 6.7 copy-start.4
  391.4 143.2 %reduce-scatter.19.cloned.1.call-start = ((), (), s32[]{:S(2)}) async-start(), calls=%async_computation.17 | async-start | bytes 11943936 | tf_op jit(solution)/shard_map/reduce_scatter | solution.py:244
  417.2 13.2 %copy-start.5 = (bf16[258,1152]{0,1:T(8,128)(2,1)S(1)}, bf16[258,1152]{0,1:T(8,128)(2,1)}, u32[]{:S(2)}) copy-start(bf16[258,1152]{0,1:T(8,128)(2,1)} %copy.144) | copy-start | bytes 1783300
  430.4 4.5 copy-start.20
  430.4 4.5 copy-start.21
  434.9 8.4 copy-start.9
  434.9 8.4 copy-start.2
  434.9 9.7 copy-start.25
  434.9 9.7 copy-start.26
  443.8 0.8 copy-start.15
  450.4 1.2 copy-start.10
  450.4 201.0 %reduce-scatter.21.cloned.1.call-start = ((), (), s32[]{:S(2)}) async-start(), calls=%async_computation.18 | async-start | bytes 17915904 | tf_op jit(solution)/shard_map/reduce_scatter | solution.py:245
  463.7 1.2 copy-start.14
  463.7 328.5 %reduce-scatter.29.cloned.1.call-start = ((), (), s32[]{:S(2)}) async-start(), calls=%async_computation.22 | async-start | bytes 23887872 | tf_op jit(solution)/shard_map/reduce_scatter | solution.py:248
  477.9 455.0 %reduce-scatter.25.cloned.1.call-start = ((), (), s32[]{:S(2)}) async-start(), calls=%async_computation.20 | async-start | bytes 23887872 | tf_op jit(solution)/shard_map/reduce_scatter | solution.py:247
  490.2 505.7 %reduce-scatter.35.cloned.1.call-start = ((), (), s32[]{:S(2)}) async-start(), calls=%async_computation.25 | async-start | bytes 1474560
  492.8 512.9 %reduce-scatter.31.cloned.1.call-start = ((), (), s32[]{:S(2)}) async-start(), calls=%async_computation.23 | async-start | bytes 2211840
  537.7 535.8 %reduce-scatter.33.cloned.1.call-start = ((), (), s32[]{:S(2)}) async-start(), calls=%async_computation.24 | async-start | bytes 4423680
  655.0 277.9 %copy-start.11 = (f32[576,288]{0,1:T(8,128)S(1)}, f32[576,288]{0,1:T(8,128)}, u32[]{:S(2)}) copy-start(f32[576,288]{0,1:T(8,128)} %param.36) | copy-start | bytes 1990660
  655.0 478.3 %reduce-scatter.37.cloned.1.call-start = ((), (), s32[]{:S(2)}) async-start(), calls=%async_computation.26 | async-start | bytes 3686400
  795.7 186.8 %copy-start.28 = (f32[3168]{0:T(1024)S(1)}, f32[3168]{0:T(1024)}, u32[]{:S(2)}) copy-start(f32[3168]{0:T(1024)} %param.39) | copy-start | bytes 38020
  795.7 186.8 %copy-start.29 = (f32[3168]{0:T(1024)S(1)}, f32[3168]{0:T(1024)}, u32[]{:S(2)}) copy-start(f32[3168]{0:T(1024)} %param.40) | copy-start | bytes 38020
  795.7 186.8 %copy-start.30 = (f32[3168]{0:T(1024)S(1)}, f32[3168]{0:T(1024)}, u32[]{:S(2)}) copy-start(f32[3168]{0:T(1024)} %param.41) | copy-start | bytes 38020
  795.7 392.3 %reduce-scatter.27.cloned.1.call-start = ((), (), s32[]{:S(2)}) async-start(), calls=%async_computation.21 | async-start | bytes 3317760 | tf_op jit(solution)/shard_map/reduce_scatter | solution.py:255
  983.1 5.8 copy-start.6
  983.1 5.8 copy-start.31
  995.9 79.9 %copy-start.18 = (f32[144,864]{1,0:T(8,128)S(1)}, f32[144,864]{1,0:T(8,128)}, u32[]{:S(2)}) copy-start(f32[144,864]{1,0:T(8,128)} %param.27) | copy-start | bytes 1492996
  1007.8 127.9 %copy-start.8 = (f32[576,288]{1,0:T(8,128)S(1)}, f32[576,288]{1,0:T(8,128)}, u32[]{:S(2)}) copy-start(f32[576,288]{1,0:T(8,128)} %copy.123) | copy-start | bytes 1990660
  1139.0 49.0 %copy-start.12 = (f32[144,1152]{1,0:T(8,128)S(1)}, f32[144,1152]{1,0:T(8,128)}, u32[]{:S(2)}) copy-start(f32[144,1152]{1,0:T(8,128)} %param.33) | copy-start | bytes 1990660
  1139.0 49.0 %copy-start.22 = (f32[144,1152]{1,0:T(8,128)S(1)}, f32[144,1152]{1,0:T(8,128)}, u32[]{:S(2)}) copy-start(f32[144,1152]{1,0:T(8,128)} %param.34) | copy-start | bytes 1990660
  1139.0 49.0 %copy-start.23 = (f32[144,1152]{1,0:T(8,128)S(1)}, f32[144,1152]{1,0:T(8,128)}, u32[]{:S(2)}) copy-start(f32[144,1152]{1,0:T(8,128)} %param.35) | copy-start | bytes 1990660
Sparse Core Ops, SparseCore 0:
  10.2 50.0 all-gather.15
  62.4 42.3 all-gather.19
  107.3 40.2 all-gather.9
  149.4 52.5 all-gather.11
  204.3 30.2 all-gather.13
  236.3 63.8 all-gather.17
  302.1 63.8 all-gather.21
  391.5 56.9 reduce-scatter.22
  452.4 82.1 reduce-scatter.18
  538.5 112.8 reduce-scatter.20
  655.0 137.1 reduce-scatter.28
  795.7 137.1 reduce-scatter.24
  935.2 30.5 reduce-scatter.34
  968.0 37.7 reduce-scatter.30
  1008.0 65.4 reduce-scatter.32
  1075.8 57.4 reduce-scatter.36
  1135.5 52.5 reduce-scatter.26
where the time goes:
time: 1200 us
  waiting for transfers between devices  799 us (67%)
  matrix products  164 us (14%)
  blocking collectives  140 us (12%)
  local copies, waits for them, and re-layouts  56.2 us (5%)
  other arithmetic  21 us (2%)
  between operations  16.3 us (1%)
    reduce_scatter x1, waiting for transfers between devices, on_device(): lax.psum_scatter(shrink_gradient, 'wide', scatter_dimension=0, tiled=True)  137 us
    reduce_scatter x1, waiting for transfers between devices, on_device(): lax.psum_scatter(expand_gradient, 'wide', scatter_dimension=0, tiled=True)  137 us
    unnamed x21, waiting for transfers between devices  125 us
    reduce_scatter x1, waiting for transfers between devices, on_device(): lax.psum_scatter(attend_gradient, 'wide', scatter_dimension=0, tiled=True)  113 us
    all_gather x1, waiting for transfers between devices, on_device(): lax.all_gather(columns[3], 'wide', axis=0, tiled=True)  62.3 us
    all_gather x1, waiting for transfers between devices, on_device(): lax.all_gather(columns[1], 'wide', axis=0, tiled=True)  49.4 us
    all_gather x1, waiting for transfers between devices, on_device(): lax.all_gather(columns[4], 'wide', axis=0, tiled=True)  47.5 us
    dot_general x5, matrix products, weight_gradient(): lax.dot_general(flat_left, flat_right, (((0,), (0,)), ((), ())), preferre...  47.2 us
  transfers between devices with their start and end apart: 17, of which 14 were waited for; matrix products, arithmetic and copies ran while one was open for 17% of the time, Pallas kernels for 0%

commit v1 on v0

--- a/solution.py
+++ b/solution.py
@@ -1,6 +1,8 @@
 import jax
 import jax.numpy as jnp
 from jax import lax
+from jax.experimental import pallas as pl
+from jax.experimental.pallas import tpu as pltpu
 from jax.sharding import PartitionSpec as P
 
 D = 1152
@@ -80,7 +82,7 @@
     return (weight - step_rate * (direction + weight_decay * weight), moment_new, square_new)
 
 
-def on_device(
+def general_device(
     inputs,
     skip_tokens,
     cotangent,
@@ -287,6 +289,672 @@
     )
 
 
+CORE = 1
+ACROSS = 2
+ALONG = 4
+VMEM_BYTES = 56 * 1024 * 1024
+
+
+def swap_wide(value, bit):
+    return lax.ppermute(value, "wide", [(i, i ^ bit) for i in range(8)])
+
+
+def swap_narrow(value, bit):
+    return lax.ppermute(value, "narrow", [(i, i ^ bit) for i in range(4)])
+
+
+def together(*values):
+    return lax.optimization_barrier(values)
+
+
+def spot():
+    wide = lax.axis_index("wide")
+    narrow = lax.axis_index("narrow")
+    return (wide & 1, (wide >> 1) & 1, (wide >> 2) & 1, narrow & 1, narrow >> 1)
+
+
+def split_rows(rows):
+    return -(-rows // 32) * 16
+
+
+def column_blocks(kind, quarter):
+    if kind == "expand":
+        width = quarter // 2
+        order = [2 * n + p for p in range(2) for n in range(4)]
+    elif kind == "attend":
+        width = quarter // 6
+        order = [8 * part + 2 * n + p for part in range(3) for p in range(2) for n in range(4)]
+    else:
+        width = quarter // 2
+        order = [2 * n + p for p in range(2) for n in range(4)]
+    per = quarter // width
+    return width, [(block // per, (block % per) * width) for block in order]
+
+
+def arrange(kind, shard, far, near):
+    rows, quarter = shard.shape
+    split = split_rows(rows)
+    width, blocks = column_blocks(kind, quarter)
+
+    def kernel(shard_ref, far_ref, near_ref, top_ref, bottom_ref, held):
+        narrow = lax.axis_index("narrow")
+        held[0] = shard_ref[...]
+        held[2] = far_ref[...]
+        held[1] = near_ref[0]
+        held[3] = near_ref[1]
+        for number in range(4):
+            value = held[narrow ^ number]
+            for position, (owner, offset) in enumerate(blocks):
+                if owner == number:
+                    column = position * width
+                    piece = value[:, offset : offset + width]
+                    top_ref[:, column : column + width] = piece[:split]
+                    bottom_ref[:, column : column + width] = piece[split:]
+
+    return pl.pallas_call(
+        kernel,
+        out_shape=(
+            jax.ShapeDtypeStruct((split, 4 * quarter), jnp.bfloat16),
+            jax.ShapeDtypeStruct((rows - split, 4 * quarter), jnp.bfloat16),
+        ),
+        scratch_shapes=[pltpu.VMEM((4, rows, quarter), jnp.bfloat16)],
+        compiler_params=pltpu.CompilerParams(vmem_limit_bytes=VMEM_BYTES),
+        cost_estimate=pl.CostEstimate(
+            flops=0, bytes_accessed=16 * rows * quarter, transcendentals=0
+        ),
+    )(shard, far, near)
+
+
+def place(pieces):
+    split, columns = pieces[0].shape
+    rows = split + pieces[1].shape[0]
+
+    def kernel(*refs):
+        full = refs[8]
+        chip = lax.axis_index("wide") >> 1
+        for relative in range(4):
+            start = (chip ^ relative) * rows
+            top, bottom = refs[2 * relative], refs[2 * relative + 1]
+            full[pl.ds(pl.multiple_of(start, 16), split)] = top[...]
+            full[pl.ds(pl.multiple_of(start + split, 16), rows - split)] = bottom[...]
+
+    return pl.pallas_call(
+        kernel,
+        out_shape=jax.ShapeDtypeStruct((4 * rows, columns), jnp.bfloat16),
+        compiler_params=pltpu.CompilerParams(vmem_limit_bytes=VMEM_BYTES),
+        cost_estimate=pl.CostEstimate(
+            flops=0, bytes_accessed=16 * rows * columns, transcendentals=0
+        ),
+    )(*pieces)
+
+
+def unarrange(kind, kept_top, got_top, kept_bottom, got_bottom):
+    split, columns = kept_top.shape
+    rows = split + kept_bottom.shape[0]
+    quarter = columns // 4
+    width, blocks = column_blocks(kind, quarter)
+
+    def kernel(kept_top_ref, got_top_ref, kept_bottom_ref, got_bottom_ref, keep_ref, send_ref, held):
+        low_bit = lax.axis_index("narrow") & 1
+        held[:split] = add_low(kept_top_ref[...], got_top_ref[...])
+        held[split:] = add_low(kept_bottom_ref[...], got_bottom_ref[...])
+        for position, (owner, offset) in enumerate(blocks):
+            piece = held[:, position * width : (position + 1) * width]
+            high = owner >> 1
+
+            @pl.when(low_bit == (owner & 1))
+            def _():
+                keep_ref[high, :, offset : offset + width] = piece
+
+            @pl.when(low_bit != (owner & 1))
+            def _():
+                send_ref[high, :, offset : offset + width] = piece
+
+    shape = jax.ShapeDtypeStruct((2, rows, quarter), jnp.bfloat16)
+    return pl.pallas_call(
+        kernel,
+        out_shape=(shape, shape),
+        scratch_shapes=[pltpu.VMEM((rows, columns), jnp.bfloat16)],
+        compiler_params=pltpu.CompilerParams(vmem_limit_bytes=VMEM_BYTES),
+        cost_estimate=pl.CostEstimate(
+            flops=0, bytes_accessed=8 * rows * columns, transcendentals=0
+        ),
+    )(kept_top, got_top, kept_bottom, got_bottom)
+
+
+def add_low(left, right):
+    return (left.astype(jnp.float32) + right.astype(jnp.float32)).astype(jnp.bfloat16)
+
+
+def pick(value, index, dim):
+    return lax.dynamic_index_in_dim(value, index, dim, keepdims=False)
+
+
+def halves_of(value, core):
+    middle = value.shape[-1] // 2
+    first, second = value[..., :middle], value[..., middle:]
+    return jnp.where(core == 0, first, second), jnp.where(core == 0, second, first)
+
+
+def whole_of(mine, other, core):
+    return jnp.concatenate(
+        [jnp.where(core == 0, mine, other), jnp.where(core == 0, other, mine)], axis=-1
+    )
+
+
+def inner(value):
+    width = value.shape[-1] // 8
+    return jnp.concatenate(
+        [
+            value[..., (2 * n + p) * width : (2 * n + p + 1) * width]
+            for p in range(2)
+            for n in range(4)
+        ],
+        axis=-1,
+    )
+
+
+def outer(value):
+    width = value.shape[-1] // 8
+    return jnp.concatenate(
+        [
+            value[..., (4 * p + n) * width : (4 * p + n + 1) * width]
+            for n in range(4)
+            for p in range(2)
+        ],
+        axis=-1,
+    )
+
+
+def across_first(top, bottom):
+    return swap_wide(top, ACROSS), swap_wide(bottom, ALONG)
+
+
+def across_second(top, bottom, top_x, bottom_y):
+    return (
+        swap_wide(top, ALONG),
+        swap_wide(bottom, ACROSS),
+        swap_wide(top_x, ALONG),
+        swap_wide(bottom_y, ACROSS),
+    )
+
+
+def placed(top, bottom, first, second):
+    return place(
+        [top, bottom, first[0], second[1], second[0], first[1], second[2], second[3]]
+    )
+
+
+def pair_gradient(left, left_sibling, right, right_sibling):
+    both_left = jnp.concatenate([left, left_sibling], axis=0)
+    both_right = jnp.concatenate([right, right_sibling], axis=0)
+    total = lax.dot_general(
+        both_left, both_right, (((0,), (0,)), ((), ())), preferred_element_type=jnp.float32
+    )
+    return total.astype(jnp.bfloat16).reshape(2, 2, left.shape[1] // 4, right.shape[1])
+
+
+def scatter_first(blocks):
+    _, across, along = spot()[:3]
+    split = split_rows(blocks.shape[2])
+    top, bottom = blocks[:, :, :split], blocks[:, :, split:]
+    kept = (pick(top, across, 1), pick(bottom, along, 0))
+    got = (
+        swap_wide(pick(top, 1 - across, 1), ACROSS),
+        swap_wide(pick(bottom, 1 - along, 0), ALONG),
+    )
+    return kept, got
+
+
+def scatter_second(state):
+    _, across, along = spot()[:3]
+    kept, got = state
+    top, bottom = add_low(kept[0], got[0]), add_low(kept[1], got[1])
+    return (pick(top, along, 0), pick(bottom, across, 0)), (
+        swap_wide(pick(top, 1 - along, 0), ALONG),
+        swap_wide(pick(bottom, 1 - across, 0), ACROSS),
+    )
+
+
+def scatter_third(kind, state):
+    kept, got = state
+    keep, send = unarrange(kind, kept[0], got[0], kept[1], got[1])
+    return keep, swap_narrow(send, 1)
+
+
+def scatter_fourth(state):
+    high_bit = spot()[4]
+    kept, got = state
+    part = add_low(kept, got)
+    return pick(part, high_bit, 0), swap_narrow(pick(part, 1 - high_bit, 0), 2)
+
+
+def scatter_last(state):
+    return state[0].astype(jnp.float32) + state[1].astype(jnp.float32)
+
+
+def gather_vector(far, near, vector):
+    low_bit, high_bit = spot()[3:]
+    own = jnp.stack([vector, far])
+    own = jnp.where(high_bit == 0, own, own[::-1])
+    near = jnp.where(high_bit == 0, near, near[::-1])
+    even = jnp.where(low_bit == 0, own, near)
+    odd = jnp.where(low_bit == 0, near, own)
+    return jnp.concatenate([even[0], odd[0], even[1], odd[1]])
+
+
+def scatter_vector(vector):
+    low_bit, high_bit = spot()[3:]
+    total = vector + swap_wide(vector, CORE)
+    total = total + swap_wide(total, ACROSS)
+    total = total + swap_wide(total, ALONG)
+    halves = total.reshape(2, -1)
+    total = pick(halves, high_bit, 0) + swap_narrow(pick(halves, 1 - high_bit, 0), 2)
+    halves = total.reshape(2, -1)
+    return pick(halves, low_bit, 0) + swap_narrow(pick(halves, 1 - low_bit, 0), 1)
+
+
+def inner_dot(activations, mine, other, core):
+    left, right = halves_of(activations, core)
+    return product(left, mine) + product(right, other)
+
+
+def inner_back(gradient, mine, other, core):
+    return whole_of(transposed(gradient, mine), transposed(gradient, other), core)
+
+
+def on_device(
+    inputs,
+    skip_tokens,
+    cotangent,
+    merge_weight,
+    merge_moment,
+    merge_square,
+    attend_weight,
+    attend_moment,
+    attend_square,
+    output_weight,
+    output_moment,
+    output_square,
+    expand_weight,
+    expand_moment,
+    expand_square,
+    shrink_weight,
+    shrink_moment,
+    shrink_square,
+    vectors,
+    vector_moment,
+    vector_square,
+):
+    core = spot()[0]
+    low = jnp.bfloat16
+    merge_low = merge_weight.astype(low)
+    attend_low = attend_weight.astype(low)
+    output_low = output_weight.astype(low)
+    expand_low = expand_weight.astype(low)
+    shrink_low = shrink_weight.astype(low)
+    vector_low = vectors.astype(low)
+    length = inputs.shape[1]
+    softmax_scale = HD ** (-0.5)
+
+    merge_far = swap_narrow(merge_low, 2)
+    vector_far = swap_narrow(vector_low, 2)
+    joined = inner(jnp.concatenate([inputs[0], skip_tokens[0]], axis=-1))
+    pulled = inner(cotangent[0])
+    merge_far, vector_far, joined, pulled, attend_low, output_low = together(
+        merge_far, vector_far, joined, pulled, attend_low, output_low
+    )
+    merge_near = swap_narrow(jnp.stack([merge_low, merge_far]), 1)
+    vector_near = swap_narrow(jnp.stack([vector_low, vector_far]), 1)
+    attend_far = swap_narrow(attend_low, 2)
+    output_far = swap_narrow(output_low, 2)
+    joined_mine, joined_other = halves_of(joined, core)
+    joined_sibling = swap_wide(joined_other, CORE)
+    pulled_sibling = swap_wide(pulled, CORE)
+    (
+        merge_near,
+        vector_near,
+        attend_far,
+        output_far,
+        joined_sibling,
+        pulled_sibling,
+        joined_mine,
+        joined_other,
+        expand_low,
+    ) = together(
+        merge_near,
+        vector_near,
+        attend_far,
+        output_far,
+        joined_sibling,
+        pulled_sibling,
+        joined_mine,
+        joined_other,
+        expand_low,
+    )
+    merge_top, merge_bottom = arrange("merge", merge_low, merge_far, merge_near)
+    merge_first = across_first(merge_top, merge_bottom)
+    attend_near = swap_narrow(jnp.stack([attend_low, attend_far]), 1)
+    output_near = swap_narrow(jnp.stack([output_low, output_far]), 1)
+    pieces = unpack(gather_vector(vector_far, vector_near, vector_low).astype(jnp.float32))
+    pieces = tuple(inner(piece) for piece in pieces)
+    merge_first, attend_near, output_near, pieces, expand_low = together(
+        merge_first, attend_near, output_near, pieces, expand_low
+    )
+    skip_bias, gain_one, bias_one, output_bias, gain_two, bias_two, shrink_bias, expand_bias = pieces
+    merge_second = across_second(merge_top, merge_bottom, *merge_first)
+    expand_far = swap_narrow(expand_low, 2)
+    attend_top, attend_bottom = arrange("attend", attend_low, attend_far, attend_near)
+    output_top, output_bottom = arrange("output", output_low, output_far, output_near)
+    merge_second, expand_far, attend_top, attend_bottom, output_top, output_bottom = together(
+        merge_second, expand_far, attend_top, attend_bottom, output_top, output_bottom
+    )
+    attend_first = across_first(attend_top, attend_bottom)
+    output_first = across_first(output_top, output_bottom)
+    expand_near = swap_narrow(jnp.stack([expand_low, expand_far]), 1)
+    merge_mine = placed(merge_top, merge_bottom, merge_first, merge_second)
+    merge_other = swap_wide(merge_mine, CORE)
+    attend_first, output_first, expand_near, merge_mine, merge_other, shrink_low = together(
+        attend_first, output_first, expand_near, merge_mine, merge_other, shrink_low
+    )
+    attend_second = across_second(attend_top, attend_bottom, *attend_first)
+    output_second = across_second(output_top, output_bottom, *output_first)
+    shrink_far = swap_narrow(shrink_low, 2)
+    expand_top, expand_bottom = arrange("expand", expand_low, expand_far, expand_near)
+    stream_zero = product(joined_mine, merge_mine) + product(joined_other, merge_other) + skip_bias
+    normed_one, inverse_one = normalize(stream_zero)
+    attend_input = (normed_one * gain_one + bias_one).astype(low)
+    (
+        attend_second,
+        output_second,
+        shrink_far,
+        expand_top,
+        expand_bottom,
+        stream_zero,
+        normed_one,
+        inverse_one,
+        attend_input,
+    ) = together(
+        attend_second,
+        output_second,
+        shrink_far,
+        expand_top,
+        expand_bottom,
+        stream_zero,
+        normed_one,
+        inverse_one,
+        attend_input,
+    )
+    expand_first = across_first(expand_top, expand_bottom)
+    shrink_near = swap_narrow(jnp.stack([shrink_low, shrink_far]), 1)
+    attend_mine = placed(attend_top, attend_bottom, attend_first, attend_second)
+    attend_other = swap_wide(attend_mine, CORE)
+    output_mine = placed(output_top, output_bottom, output_first, output_second)
+    output_other = swap_wide(output_mine, CORE)
+    attend_input_mine, attend_input_other = halves_of(attend_input, core)
+    attend_input_sibling = swap_wide(attend_input_other, CORE)
+    (
+        expand_first,
+        shrink_near,
+        attend_mine,
+        attend_other,
+        output_mine,
+        output_other,
+        attend_input_mine,
+        attend_input_other,
+        attend_input_sibling,
+    ) = together(
+        expand_first,
+        shrink_near,
+        attend_mine,
+        attend_other,
+        output_mine,
+        output_other,
+        attend_input_mine,
+        attend_input_other,
+        attend_input_sibling,
+    )
+    expand_second = across_second(expand_top, expand_bottom, *expand_first)
+    shrink_top, shrink_bottom = arrange("shrink", shrink_low, shrink_far, shrink_near)
+    mixed_heads = (
+        product(attend_input_mine, attend_mine) + product(attend_input_other, attend_other)
+    ).astype(low)
+    query_heads = mixed_heads[..., 0:D].reshape(1, length, H, HD)
+    key_heads = mixed_heads[..., D : 2 * D].reshape(1, length, H, HD)
+    value_heads = mixed_heads[..., 2 * D : 3 * D].reshape(1, length, H, HD)
+    logits = (
+        jnp.einsum("blhe,bmhe->bhlm", query_heads, key_heads, preferred_element_type=jnp.float32)
+        * softmax_scale
+    )
+    maxima = jnp.max(logits, axis=-1, keepdims=True)
+    log_total = maxima + jnp.log(jnp.sum(jnp.exp(logits - maxima), axis=-1, keepdims=True))
+    softmax_low = jnp.exp(logits - log_total).astype(low)
+    mixture = jnp.einsum(
+        "bhlm,bmhe->blhe", softmax_low, value_heads, preferred_element_type=jnp.float32
+    )
+    mixture = mixture.astype(low).reshape(length, D)
+    mixture_mine, mixture_other = halves_of(mixture, core)
+    stream_one = (
+        stream_zero
+        + (product(mixture_mine, output_mine) + product(mixture_other, output_other))
+        + output_bias
+    )
+    normed_two, inverse_two = normalize(stream_one)
+    expand_input = (normed_two * gain_two + bias_two).astype(low)
+    (
+        expand_second,
+        shrink_top,
+        shrink_bottom,
+        stream_one,
+        normed_two,
+        inverse_two,
+        expand_input,
+        mixture_mine,
+        mixture_other,
+    ) = together(
+        expand_second,
+        shrink_top,
+        shrink_bottom,
+        stream_one,
+        normed_two,
+        inverse_two,
+        expand_input,
+        mixture_mine,
+        mixture_other,
+    )
+    shrink_first = across_first(shrink_top, shrink_bottom)
+    mixture_sibling = swap_wide(mixture_other, CORE)
+    expand_input_mine, expand_input_other = halves_of(expand_input, core)
+    expand_input_sibling = swap_wide(expand_input_other, CORE)
+    expand_mine = placed(expand_top, expand_bottom, expand_first, expand_second)
+    expand_other = swap_wide(expand_mine, CORE)
+    expand_input_mine, expand_input_other, expand_mine, expand_other = together(
+        expand_input_mine, expand_input_other, expand_mine, expand_other
+    )
+    hidden = (
+        product(expand_input_mine, expand_mine) + product(expand_input_other, expand_other)
+    ) + expand_bias
+    active, pullback = jax.vjp(gaussian_unit, hidden)
+    active_low = active.astype(low)
+    slope = pullback(jnp.ones_like(hidden))[0]
+    shrink_first, mixture_sibling, expand_input_sibling, active_low, slope = together(
+        shrink_first, mixture_sibling, expand_input_sibling, active_low, slope
+    )
+    shrink_second = across_second(shrink_top, shrink_bottom, *shrink_first)
+    active_mine, active_other = halves_of(active_low, core)
+    active_sibling = swap_wide(active_other, CORE)
+    active_mine, active_other, active_sibling = together(active_mine, active_other, active_sibling)
+    shrink_gradient = pair_gradient(active_mine, active_sibling, pulled, pulled_sibling)
+    shrink_second, shrink_gradient, active_mine, active_other, slope = together(
+        shrink_second, shrink_gradient, active_mine, active_other, slope
+    )
+    shrink_mine = placed(shrink_top, shrink_bottom, shrink_first, shrink_second)
+    shrink_other = swap_wide(shrink_mine, CORE)
+    shrink_parts = scatter_first(shrink_gradient)
+    delta_hidden = inner_back(pulled, shrink_mine, shrink_other, core) * slope
+    hidden_low = delta_hidden.astype(low)
+    hidden_sum = jnp.sum(delta_hidden, axis=0)
+    hidden_low, hidden_sum = together(hidden_low, hidden_sum)
+    hidden_sibling = swap_wide(hidden_low, CORE)
+    delta_expand = inner_back(hidden_low, expand_mine, expand_other, core)
+    hidden_sibling, delta_expand = together(hidden_sibling, delta_expand)
+    expand_gradient = pair_gradient(
+        expand_input_mine, expand_input_sibling, hidden_low, hidden_sibling
+    )
+    upstream = pulled.astype(jnp.float32)
+    delta_one = upstream + norm_back(delta_expand * gain_two, normed_two, inverse_two)
+    stream_low = delta_one.astype(low)
+    sums_two = (
+        jnp.sum(delta_one, axis=0),
+        jnp.sum(delta_expand * normed_two, axis=0),
+        jnp.sum(delta_expand, axis=0),
+    )
+    shrink_parts, expand_gradient, delta_one, stream_low, sums_two = together(
+        shrink_parts, expand_gradient, delta_one, stream_low, sums_two
+    )
+    shrink_parts = scatter_second(shrink_parts)
+    expand_parts = scatter_first(expand_gradient)
+    stream_sibling = swap_wide(stream_low, CORE)
+    delta_mixture = (
+        inner_back(stream_low, output_mine, output_other, core)
+        .astype(low)
+        .reshape(1, length, H, HD)
+    )
+    logits_again = (
+        jnp.einsum("blhe,bmhe->bhlm", query_heads, key_heads, preferred_element_type=jnp.float32)
+        * softmax_scale
+    )
+    softmax_again = jnp.exp(logits_again - log_total)
+    delta_softmax = jnp.einsum(
+        "blhe,bmhe->bhlm", delta_mixture, value_heads, preferred_element_type=jnp.float32
+    )
+    delta_values = jnp.einsum(
+        "bhlm,blhe->bmhe",
+        softmax_again.astype(low),
+        delta_mixture,
+        preferred_element_type=jnp.float32,
+    )
+    delta_logits = softmax_again * (
+        delta_softmax - jnp.sum(softmax_again * delta_softmax, axis=-1, keepdims=True)
+    )
+    delta_scores = (softmax_scale * delta_logits).astype(low)
+    delta_queries = jnp.einsum(
+        "bhlm,bmhe->blhe", delta_scores, key_heads, preferred_element_type=jnp.float32
+    )
+    delta_keys = jnp.einsum(
+        "bhlm,blhe->bmhe", delta_scores, query_heads, preferred_element_type=jnp.float32
+    )
+    delta_mixed = jnp.concatenate(
+        [
+            delta_queries.reshape(length, D),
+            delta_keys.reshape(length, D),
+            delta_values.reshape(length, D),
+        ],
+        axis=-1,
+    ).astype(low)
+    shrink_parts, expand_parts, stream_sibling, delta_mixed = together(
+        shrink_parts, expand_parts, stream_sibling, delta_mixed
+    )
+    shrink_parts = scatter_third("shrink", shrink_parts)
+    expand_parts = scatter_second(expand_parts)
+    mixed_sibling = swap_wide(delta_mixed, CORE)
+    output_gradient = pair_gradient(mixture_mine, mixture_sibling, stream_low, stream_sibling)
+    delta_attend = inner_back(delta_mixed, attend_mine, attend_other, core)
+    mixed_sibling, delta_attend, output_gradient = together(
+        mixed_sibling, delta_attend, output_gradient
+    )
+    attend_gradient = pair_gradient(
+        attend_input_mine, attend_input_sibling, delta_mixed, mixed_sibling
+    )
+    shrink_parts, expand_parts, attend_gradient, output_gradient, delta_attend = together(
+        shrink_parts, expand_parts, attend_gradient, output_gradient, delta_attend
+    )
+    shrink_parts = scatter_fourth(shrink_parts)
+    expand_parts = scatter_third("expand", expand_parts)
+    attend_parts = scatter_first(attend_gradient)
+    output_parts = scatter_first(output_gradient)
+    delta_zero = delta_one + norm_back(delta_attend * gain_one, normed_one, inverse_one)
+    zero_low = delta_zero.astype(low)
+    zero_sibling = swap_wide(zero_low, CORE)
+    vector_gradient = jnp.concatenate(
+        [
+            outer(jnp.sum(delta_zero, axis=0)),
+            outer(jnp.sum(delta_attend * normed_one, axis=0)),
+            outer(jnp.sum(delta_attend, axis=0)),
+            outer(sums_two[0]),
+            outer(sums_two[1]),
+            outer(sums_two[2]),
+            outer(jnp.sum(upstream, axis=0)),
+            outer(hidden_sum),
+        ]
+    )
+    zero_low, zero_sibling = together(zero_low, zero_sibling)
+    merge_gradient = pair_gradient(joined_mine, joined_sibling, zero_low, zero_sibling)
+    shrink_parts, expand_parts, attend_parts, output_parts, merge_gradient, vector_gradient = (
+        together(
+            shrink_parts, expand_parts, attend_parts, output_parts, merge_gradient, vector_gradient
+        )
+    )
+    merge_parts = scatter_first(merge_gradient)
+    attend_parts = scatter_second(attend_parts)
+    output_parts = scatter_second(output_parts)
+    expand_parts = scatter_fourth(expand_parts)
+    vector_total = scatter_vector(vector_gradient)
+    shrink_new = adamw_update(
+        shrink_weight, shrink_moment, shrink_square, scatter_last(shrink_parts), rate_shrink
+    )
+    outputs = outer(
+        (
+            stream_one
+            + (product(active_mine, shrink_mine) + product(active_other, shrink_other))
+            + shrink_bias
+        ).astype(low)
+    )[None]
+    merge_parts, attend_parts, output_parts, expand_parts, shrink_new, outputs = together(
+        merge_parts, attend_parts, output_parts, expand_parts, shrink_new, outputs
+    )
+    merge_parts = scatter_second(merge_parts)
+    attend_parts = scatter_third("attend", attend_parts)
+    output_parts = scatter_third("output", output_parts)
+    delta_joined = outer(inner_back(zero_low, merge_mine, merge_other, core).astype(low))
+    input_gradient = delta_joined[None, :, 0:D]
+    skip_gradient = delta_joined[None, :, D : 2 * D]
+    merge_parts, attend_parts, output_parts, input_gradient, skip_gradient = together(
+        merge_parts, attend_parts, output_parts, input_gradient, skip_gradient
+    )
+    merge_parts = scatter_third("merge", merge_parts)
+    attend_parts = scatter_fourth(attend_parts)
+    output_parts = scatter_fourth(output_parts)
+    expand_new = adamw_update(
+        expand_weight, expand_moment, expand_square, scatter_last(expand_parts), rate_expand
+    )
+    merge_parts, attend_parts, output_parts, expand_new = together(
+        merge_parts, attend_parts, output_parts, expand_new
+    )
+    merge_parts = scatter_fourth(merge_parts)
+    attend_new = adamw_update(
+        attend_weight, attend_moment, attend_square, scatter_last(attend_parts), rate_attend
+    )
+    output_new = adamw_update(
+        output_weight, output_moment, output_square, scatter_last(output_parts), rate_output
+    )
+    merge_new = adamw_update(
+        merge_weight, merge_moment, merge_square, scatter_last(merge_parts), rate_merge
+    )
+    vector_new = adamw_update(vectors, vector_moment, vector_square, vector_total, rate_vector)
+    return (
+        outputs,
+        input_gradient,
+        skip_gradient,
+        *merge_new,
+        *attend_new,
+        *output_new,
+        *expand_new,
+        *shrink_new,
+        *vector_new,
+    )
+
+
 def solution(mesh):
     in_specs = (
         P(("wide", "narrow"), None, None),
@@ -334,6 +1002,7 @@
         P("narrow"),
         P("narrow"),
     )
+    tuned = mesh.shape["wide"] == 8 and mesh.shape["narrow"] == 4
     return jax.shard_map(
-        on_device, mesh=mesh, in_specs=in_specs, out_specs=out_specs, check_vma=False
-    )
+        on_device if tuned else general_device, mesh=mesh, in_specs=in_specs, out_specs=out_specs, check_vma=False
+    )

time: 1200 us -> 626 us (0.52)
  waiting for transfers between devices: 799 us -> 201 us
  blocking collectives: 140 us -> 0 us
  starting transfers between devices: 1.13 us -> 75.6 us
  Pallas kernels: 0 us -> 54.8 us
  local copies, waits for them, and re-layouts: 56.2 us -> 97 us
  matrix products: 164 us -> 135 us
  other arithmetic: 21 us -> 48.6 us
  between operations: 16.3 us -> 3.18 us
    reduce_scatter x6 -> x0, waiting for transfers between devices: 471 us -> none  [the longest x1 137 us: on_device(): lax.psum_scatter(shrink_gradient, 'wide', scatter_dimension=0, tiled=True)]
    all_gather x7 -> x0, waiting for transfers between devices: 203 us -> none  [the longest x1 62.3 us: on_device(): lax.all_gather(columns[3], 'wide', axis=0, tiled=True)]
    ppermute x0 -> x92, waiting for transfers between devices: none -> 201 us  [the longest x24 103 us: swap_narrow(): return lax.ppermute(value, 'narrow', [(i, i ^ bit) for i in range(4)])]
    unnamed x21 -> x0, waiting for transfers between devices: 125 us -> none
    all_gather x3 -> x0, blocking collectives: 78.3 us -> none  [the longest x1 32.1 us: on_device(): lax.all_gather(merge_low, 'narrow', axis=1, tiled=True)]
    ppermute x0 -> x92, starting transfers between devices: none -> 75.6 us  [the longest x68 56.8 us: swap_wide(): return lax.ppermute(value, 'wide', [(i, i ^ bit) for i in range(8)])]
    pallas_call x0 -> x15, Pallas kernels: none -> 54.8 us  [the longest x5 20.9 us: place(): pl.pallas_call(kernel, out_shape=jax.ShapeDtypeStruct((4 * rows, columns)...]
    unnamed x2 -> x0, blocking collectives: 39.3 us -> none
  transfers between devices with their start and end apart: 17 -> 92, of which waited for: 14 -> 34; matrix products, arithmetic and copies ran while one was open for 17% -> 40% of each run, Pallas kernels for 0% -> 5%
where the time goes in v1:
time: 626 us; the launch traced here: 616 us
  waiting for transfers between devices  201 us (32%)
  matrix products  135 us (22%)
  local copies, waits for them, and re-layouts  97 us (15%)
  starting transfers between devices  75.6 us (12%)
  Pallas kernels  54.8 us (9%)
  other arithmetic  48.6 us (8%)
    ppermute x24, waiting for transfers between devices, swap_narrow(): return lax.ppermute(value, 'narrow', [(i, i ^ bit) for i in range(4)])  103 us
    ppermute x68, waiting for transfers between devices, swap_wide(): return lax.ppermute(value, 'wide', [(i, i ^ bit) for i in range(8)])  98.8 us
    ppermute x68, starting transfers between devices, swap_wide(): return lax.ppermute(value, 'wide', [(i, i ^ bit) for i in range(8)])  56.8 us
    dot_general x10, matrix products, product(): return jnp.dot(left_side, right_side, preferred_element_type=jnp.float32)  35.6 us
    dot_general x10, matrix products, transposed(): lax.dot_general(gradient, matrix, (((gradient.ndim - 1,), (1,)), ((), ())...  32.7 us
    dot_general x5, matrix products, pair_gradient(): lax.dot_general(both_left, both_right, (((0,), (0,)), ((), ())), preferre...  28 us
    squeeze x24, local copies, waits for them, and re-layouts, pick(): return lax.dynamic_index_in_dim(value, index, dim, keepdims=False)  22.4 us
    pallas_call x5, Pallas kernels, place(): pl.pallas_call(kernel, out_shape=jax.ShapeDtypeStruct((4 * rows, columns)...  20.9 us
  transfers between devices with their start and end apart: 92, of which 34 were waited for; matrix products, arithmetic and copies ran while one was open for 40% of the time, Pallas kernels for 5%

profile of v1, /device:TPU:0, one launch (start us, length us, event | category | flops | bytes accessed | tf_op | source)
XLA Modules:
  0.0 616.1 jit_solution(11253905212452813880)
XLA Ops:
  1.5 4.0 collective-permute-start.1
  12.8 2.8 concatenate.103
  15.6 3.6 collective-permute-done.far_ref
  23.2 15.8 %collective-permute-done.3 = bf16[2,3168]{1,0:T(2,128)(2,1)S(1)} collective-permute-done((bf16[2,3168]{1,0:T(2,128)(2,1)S(1)}, bf16[2,3168]{1,0:T(2,128)(2,1)S(1)}, u32[]{:S(2)}, u32[]{:S(2)}) %collective-permute-start.3) | collective-permute-done | bytes 12704 | tf_op jit(solution)/shard_map/ppermute | solution.py:303
  40.3 6.2 %collective-permute-done.5.far_ref = bf16[144,288]{1,0:T(8,128)(2,1)S(1)} collective-permute-done((bf16[144,288]{1,0:T(8,128)(2,1)S(1)}, bf16[144,288]{1,0:T(8,128)(2,1)S(1)}, u32[]{:S(2)}, u32[]{:S(2)}) %collective-permute-start.5) | collective-permute-done | bytes 82976 | tf_op jit(solution)/shard_map/ppermute | solution.py:303
  47.8 2.6 shard_map.364
  59.5 12.3 %collective-permute-done.13.near_ref = bf16[2,144,288]{2,1,0:T(8,128)(2,1)} collective-permute-done((bf16[2,144,288]{2,1,0:T(8,128)(2,1)S(1)}, bf16[2,144,288]{2,1,0:T(8,128)(2,1)}, u32[]{:S(2)}, u32[]{:S(2)}) %collective-permute-start.13) | collective-permute-done | bytes 165920 | tf_op jit(solution)/shard_map/ppermute | solution.py:303
  75.6 3.0 shard_map.365
  82.7 4.3 collective-permute-done.15.refs_7_
  87.0 3.5 collective-permute-done.16.far_ref
  90.6 3.5 shard_map.367
  97.6 13.6 %collective-permute-done.22.refs_5_ = bf16[64,1152]{1,0:T(8,128)(2,1)S(1)} collective-permute-done((bf16[64,1152]{1,0:T(8,128)(2,1)S(1)}, bf16[64,1152]{1,0:T(8,128)(2,1)S(1)}, u32[]{:S(2)}, u32[]{:S(2)}) %collective-permute-start.22) | collective-permute-done | bytes 147488 | tf_op jit(solution)/shard_map/ppermute | solution.py:299
  113.6 4.5 collective-permute-done.21.refs_2_
  123.7 3.0 fusion.127
  129.4 5.2 collective-permute-done.18.refs_3_
  135.7 3.5 collective-permute-done.17.refs_4_
  141.6 2.7 shard_map.368
  144.4 7.6 %collective-permute-done.31.far_ref = bf16[576,288]{1,0:T(8,128)(2,1)S(1)} collective-permute-done((bf16[576,288]{1,0:T(8,128)(2,1)S(1)}, bf16[576,288]{1,0:T(8,128)(2,1)S(1)}, u32[]{:S(2)}, u32[]{:S(2)}) %collective-permute-start.31) | collective-permute-done | bytes 331808 | tf_op jit(solution)/shard_map/ppermute | solution.py:303
  153.1 4.2 shard_map.369
  157.4 2.6 shard_map.370
  167.6 13.9 %collective-permute-done.35.refs_5_ = bf16[64,4608]{1,0:T(8,128)(2,1)} collective-permute-done((bf16[64,4608]{1,0:T(8,128)(2,1)}, bf16[64,4608]{1,0:T(8,128)(2,1)}, u32[]{:S(2)}, u32[]{:S(2)}) %collective-permute-start.35) | collective-permute-done | bytes 589856 | tf_op jit(solution)/shard_map/ppermute | solution.py:299
  186.3 3.8 fusion.128
  196.7 3.1 multiply_reduce_fusion.1
  214.4 3.6 shard_map.371
  218.4 5.3 shard_map.372
  226.8 6.5 %collective-permute-done.48 = bf16[576,4608]{1,0:T(8,128)(2,1)S(1)} collective-permute-done((bf16[576,4608]{1,0:T(8,128)(2,1)}, bf16[576,4608]{1,0:T(8,128)(2,1)S(1)}, u32[]{:S(2)}, u32[]{:S(2)}) %collective-permute-start.48) | collective-permute-done | bytes 5308448 | tf_op jit(solution)/shard_map/ppermute | solution.py:299
  237.6 14.8 %multiply_add_fusion = (f32[258,4608]{1,0:T(8,128)}, f32[258,4608]{1,0:T(8,128)S(1)}, f32[258,4608]{1,0:T(8,128)S(1)}) fusion(f32[4608]{0:T(1024)S(1)} %copy-done.121, f32[258,4608]{1,0:T(8,128)S(1)} %fusion.130, bf16[258,576]{1,0:T(8,128)(2,1)S(1)} %get-tuple-element.314, bf16[576,4608]{1,0:T(8,128)(2,1)S(1)} %bitcast.202), kind=kOutput, calls=%fused_computation.18 | convolution fusion | flops 1452791808 | bytes 24645888 | tf_op jit(solution)/shard_map/dot_general | solution.py:28
  258.6 7.6 %convolution_convert_fusion = bf16[2304,1152]{1,0:T(8,128)(2,1)} fusion(bf16[258,2304]{1,0:T(8,128)(2,1)S(1)} %collective-permute-done.51, bf16[258,2304]{1,0:T(8,128)(2,1)S(1)} %get-tuple-element.398, bf16[258,1152]{1,0:T(8,128)(2,1)} %collective-permute-done.7, bf16[258,1152]{1,0:T(8,128)(2,1)S(1)} %concatenate.104), kind=kOutput, calls=%fused_computation.1 | convolution fusion | flops 2748930048 | bytes 8875008 | tf_op jit(solution)/shard_map/dot_general | solution.py:491
  266.2 6.0 collective-permute-done.42.refs_4_
  274.3 11.6 %collective-permute-done.49.refs_6_ = bf16[288,1152]{1,0:T(8,128)(2,1)S(1)} collective-permute-done((bf16[288,1152]{1,0:T(8,128)(2,1)S(1)}, bf16[288,1152]{1,0:T(8,128)(2,1)S(1)}, u32[]{:S(2)}, u32[]{:S(2)}) %collective-permute-start.49) | collective-permute-done | bytes 663584 | tf_op jit(solution)/shard_map/ppermute | solution.py:299
  288.2 5.3 shard_map.373
  294.2 3.0 fusion.104
  302.6 4.4 fusion.131
  311.3 4.3 fusion.135
  321.2 5.3 fusion.132
  326.5 5.3 broadcast_select_fusion.9
  335.1 9.2 %convolution_convert_fusion.1 = bf16[576,4608]{1,0:T(8,128)(2,1)} fusion(bf16[258,4608]{1,0:T(8,128)(2,1)} %collective-permute-done.55, bf16[258,4608]{1,0:T(8,128)(2,1)} %get-tuple-element.334, bf16[258,576]{1,0:T(8,128)(2,1)S(1)} %copy-done.137, bf16[258,576]{1,0:T(8,128)(2,1)S(1)} %get-tuple-element.314), kind=kOutput, calls=%fused_computation.2 | convolution fusion | flops 2752496640 | bytes 10658304 | tf_op jit(solution)/shard_map/dot_general | solution.py:491
  351.7 3.2 slice.745
  372.4 4.4 fusion.57
  376.8 12.9 %fusion.37 = bf16[16,72,258]{2,1,0:T(8,128)(2,1)} fusion(bf16[258,16,72]{0,2,1:T(8,128)(2,1)S(1)} %bitcast.215, f32[16,258,258]{1,2,0:T(8,128)} %fusion.57, f32[16,258,258]{1,2,0:T(8,128)} %copy-done, f32[16,258]{1,0:T(8,128)S(1)} %log_add_fusion), kind=kOutput, calls=%fused_computation.66 | convolution fusion | flops 163250272 | bytes 9725568 | tf_op jit(solution)/shard_map/bhlm,bmhe->blhe/dot_general | solution.py:841
  391.9 12.9 %fusion.40 = bf16[16,72,258]{2,1,0:T(8,128)(2,1)} fusion(bf16[258,16,72]{0,2,1:T(8,128)(2,1)} %bitcast.213, f32[16,258,258]{1,2,0:T(8,128)} %fusion.57, f32[16,258,258]{1,2,0:T(8,128)} %copy-done, f32[16,258]{1,0:T(8,128)} %copy-done.106), kind=kOutput, calls=%fused_computation.67 | convolution fusion | flops 163250272 | bytes 9725568 | tf_op jit(solution)/shard_map/bhlm,blhe->bmhe/dot_general | solution.py:844
  404.8 4.2 convolution_convert_fusion.5
  414.4 4.1 collective-permute-done.59
  418.5 4.6 shard_map.374
  432.4 3.9 fusion.134
  439.1 2.6 convolution_convert_fusion.4
  441.7 4.7 convolution_convert_fusion.3
  446.5 3.7 collective-permute-done.62.got_top_ref
  464.9 4.4 shard_map.375
  478.2 3.9 select_convert_fusion
  483.4 3.9 convolution_convert_fusion.2
  487.2 14.1 %collective-permute-done.65 = bf16[576,288]{0,1:T(8,128)(2,1)S(1)} collective-permute-done((bf16[576,288]{0,1:T(8,128)(2,1)S(1)}, bf16[576,288]{0,1:T(8,128)(2,1)S(1)}, u32[]{:S(2)}, u32[]{:S(2)}) %collective-permute-start.65) | collective-permute-done | bytes 331808 | tf_op jit(solution)/shard_map/ppermute | solution.py:303
  516.0 12.8 %collective-permute-done.88 = f32[12672]{0:T(1024)S(1)} collective-permute-done((f32[12672]{0:T(1024)S(1)}, f32[12672]{0:T(1024)S(1)}, u32[]{:S(2)}, u32[]{:S(2)}) %collective-permute-start.88) | collective-permute-done | bytes 50720 | tf_op jit(solution)/shard_map/ppermute | solution.py:299
  535.4 2.7 collective-permute-done.90
  540.1 3.4 multiply_subtract_fusion
  543.7 9.5 %collective-permute-done.78 = bf16[144,1152]{1,0:T(8,128)(2,1)S(1)} collective-permute-done((bf16[144,1152]{1,0:T(8,128)(2,1)}, bf16[144,1152]{1,0:T(8,128)(2,1)S(1)}, u32[]{:S(2)}, u32[]{:S(2)}) %collective-permute-start.78) | collective-permute-done | bytes 331808 | tf_op jit(solution)/shard_map/ppermute | solution.py:303
  556.5 5.0 shard_map.376
  571.3 2.7 shard_map.377
  574.7 5.4 collective-permute-done.82
  584.6 3.2 shard_map.378
  590.3 3.4 collective-permute-done.85
  593.7 4.8 collective-permute-done.84
  598.5 6.1 collective-permute-done.83
  607.4 6.9 %collective-permute-done.86 = bf16[288,288]{1,0:T(8,128)(2,1)S(1)} collective-permute-done((bf16[288,288]{1,0:T(8,128)(2,1)S(1)}, bf16[288,288]{1,0:T(8,128)(2,1)S(1)}, u32[]{:S(2)}, u32[]{:S(2)}) %collective-permute-start.86) | collective-permute-done | bytes 165920 | tf_op jit(solution)/shard_map/ppermute | solution.py:303
  (626 shorter events, 238.0 us)
Async XLA Ops:
  19.2 27.3 %collective-permute-start.4 = (bf16[144,864]{1,0:T(8,128)(2,1)S(1)}, bf16[144,864]{1,0:T(8,128)(2,1)S(1)}, u32[]{:S(2)}, u32[]{:S(2)}) collective-permute-start(bf16[144,864]{1,0:T(8,128)(2,1)S(1)} %convert_element_type.260.shard_ref), channel_id=1, source_target_pairs={{0,2},{1,3},{2,0},{3,1},{4,6},{5,7},{6,4},{7,5},{8,10},{9,11},{10,... | collective-permute-start | bytes 746504 | tf_op jit(solution)/shard_map/ppermute | solution.py:303
  19.3 27.3 %collective-permute-start.7 = (bf16[258,1152]{1,0:T(8,128)(2,1)S(1)}, bf16[258,1152]{1,0:T(8,128)(2,1)}, u32[]{:S(2)}, u32[]{:S(2)}) collective-permute-start(bf16[258,1152]{1,0:T(8,128)(2,1)S(1)} %concatenate.104), channel_id=1, source_target_pairs={{0,4},{4,0},{8,12},{12,8},{16,20},{20,16},{24,28},{28,24},{1,5},{5... | collective-permute-start | bytes 1783304 | tf_op jit(solution)/shard_map/ppermute | solution.py:299
  20.5 26.1 %collective-permute-start.6 = (bf16[258,1152]{1,0:T(8,128)(2,1)}, bf16[258,1152]{1,0:T(8,128)(2,1)}, u32[]{:S(2)}, u32[]{:S(2)}) collective-permute-start(bf16[258,1152]{1,0:T(8,128)(2,1)} %get-tuple-element.274), channel_id=1, source_target_pairs={{0,4},{4,0},{8,12},{12,8},{16,20},{20,16},{24,28},{28,24},{1,5},{5... | collective-permute-start | bytes 1783304 | tf_op jit(solution)/shard_map/ppermute | solution.py:299
  21.1 25.5 %collective-permute-start.2 = (bf16[2,288,288]{2,1,0:T(8,128)(2,1)S(1)}, bf16[2,288,288]{2,1,0:T(8,128)(2,1)S(1)}, u32[]{:S(2)}, u32[]{:S(2)}) collective-permute-start(bf16[2,288,288]{2,1,0:T(8,128)(2,1)S(1)} %pad_maximum_fusion.7), channel_id=1, source_target_pairs={{0,1},{1,0},{2,3},{3,2},{4,5},{5,4},{6,7},{7,6},{8,9},{9,8},{10,11... | collective-permute-start | bytes 995336 | tf_op jit(solution)/shard_map/ppermute | solution.py:303
  23.0 16.0 %collective-permute-start.3 = (bf16[2,3168]{1,0:T(2,128)(2,1)S(1)}, bf16[2,3168]{1,0:T(2,128)(2,1)S(1)}, u32[]{:S(2)}, u32[]{:S(2)}) collective-permute-start(bf16[2,3168]{1,0:T(2,128)(2,1)S(1)} %pad_maximum_fusion.9), channel_id=1, source_target_pairs={{0,1},{1,0},{2,3},{3,2},{4,5},{5,4},{6,7},{7,6},{8,9},{9,8},{10,11... | collective-permute-start | bytes 38024 | tf_op jit(solution)/shard_map/ppermute | solution.py:303
  50.4 21.9 %collective-permute-start.10 = (bf16[144,1152]{1,0:T(8,128)(2,1)}, bf16[144,1152]{1,0:T(8,128)(2,1)S(1)}, u32[]{:S(2)}, u32[]{:S(2)}) collective-permute-start(bf16[144,1152]{1,0:T(8,128)(2,1)} %get-tuple-element.240.refs_0_), channel_id=1, source_target_pairs={{0,8},{4,12},{8,0},{12,4},{16,24},{20,28},{24,16},{28,20},{1,9},{5... | collective-permute-start | bytes 995336 | tf_op jit(solution)/shard_map/ppermute | solution.py:299
  51.9 28.8 %collective-permute-start.8 = (bf16[144,1152]{1,0:T(8,128)(2,1)}, bf16[144,1152]{1,0:T(8,128)(2,1)}, u32[]{:S(2)}, u32[]{:S(2)}) collective-permute-start(bf16[144,1152]{1,0:T(8,128)(2,1)} %get-tuple-element.240.refs_0_), channel_id=1, source_target_pairs={{0,16},{4,20},{8,24},{12,28},{16,0},{20,4},{24,8},{28,12},{1,17},{... | collective-permute-start | bytes 995336 | tf_op jit(solution)/shard_map/ppermute | solution.py:299
  53.4 18.8 %collective-permute-start.11 = (bf16[144,1152]{1,0:T(8,128)(2,1)}, bf16[144,1152]{1,0:T(8,128)(2,1)}, u32[]{:S(2)}, u32[]{:S(2)}) collective-permute-start(bf16[144,1152]{1,0:T(8,128)(2,1)} %get-tuple-element.241.refs_1_), channel_id=1, source_target_pairs={{0,16},{4,20},{8,24},{12,28},{16,0},{20,4},{24,8},{28,12},{1,17},{... | collective-permute-start | bytes 995336 | tf_op jit(solution)/shard_map/ppermute | solution.py:299
  54.0 18.3 %collective-permute-start.12 = (bf16[2,144,864]{2,1,0:T(8,128)(2,1)S(1)}, bf16[2,144,864]{2,1,0:T(8,128)(2,1)S(1)}, u32[]{:S(2)}, u32[]{:S(2)}) collective-permute-start(bf16[2,144,864]{2,1,0:T(8,128)(2,1)S(1)} %pad_maximum_fusion.6), channel_id=1, source_target_pairs={{0,1},{1,0},{2,3},{3,2},{4,5},{5,4},{6,7},{7,6},{8,9},{9,8},{10,11... | collective-permute-start | bytes 1493000 | tf_op jit(solution)/shard_map/ppermute | solution.py:303
  54.2 17.5 %collective-permute-start.13 = (bf16[2,144,288]{2,1,0:T(8,128)(2,1)S(1)}, bf16[2,144,288]{2,1,0:T(8,128)(2,1)}, u32[]{:S(2)}, u32[]{:S(2)}) collective-permute-start(bf16[2,144,288]{2,1,0:T(8,128)(2,1)S(1)} %pad_maximum_fusion.8), channel_id=1, source_target_pairs={{0,1},{1,0},{2,3},{3,2},{4,5},{5,4},{6,7},{7,6},{8,9},{9,8},{10,11... | collective-permute-start | bytes 497672 | tf_op jit(solution)/shard_map/ppermute | solution.py:303
  75.4 15.1 %collective-permute-start.16 = (bf16[144,1152]{1,0:T(8,128)(2,1)S(1)}, bf16[144,1152]{1,0:T(8,128)(2,1)S(1)}, u32[]{:S(2)}, u32[]{:S(2)}) collective-permute-start(bf16[144,1152]{1,0:T(8,128)(2,1)S(1)} %convert_element_type.262.shard_ref), channel_id=1, source_target_pairs={{0,2},{1,3},{2,0},{3,1},{4,6},{5,7},{6,4},{7,5},{8,10},{9,11},{10,... | collective-permute-start | bytes 995336 | tf_op jit(solution)/shard_map/ppermute | solution.py:303
  94.1 28.1 %collective-permute-start.24 = (bf16[1152,1152]{1,0:T(8,128)(2,1)}, bf16[1152,1152]{1,0:T(8,128)(2,1)}, u32[]{:S(2)}, u32[]{:S(2)}) collective-permute-start(bf16[1152,1152]{1,0:T(8,128)(2,1)} %shard_map.367), channel_id=1, source_target_pairs={{0,4},{4,0},{8,12},{12,8},{16,20},{20,16},{24,28},{28,24},{1,5},{5... | collective-permute-start | bytes 7962632 | tf_op jit(solution)/shard_map/ppermute | solution.py:299
  95.0 25.6 %collective-permute-start.23 = (bf16[2,144,1152]{2,1,0:T(8,128)(2,1)}, bf16[2,144,1152]{2,1,0:T(8,128)(2,1)S(1)}, u32[]{:S(2)}, u32[]{:S(2)}) collective-permute-start(bf16[2,144,1152]{2,1,0:T(8,128)(2,1)} %pad_maximum_fusion.4), channel_id=1, source_target_pairs={{0,1},{1,0},{2,3},{3,2},{4,5},{5,4},{6,7},{7,6},{8,9},{9,8},{10,11... | collective-permute-start | bytes 1990664 | tf_op jit(solution)/shard_map/ppermute | solution.py:303
  95.0 25.1 %collective-permute-start.19 = (bf16[80,3456]{1,0:T(8,128)(2,1)S(1)}, bf16[80,3456]{1,0:T(8,128)(2,1)}, u32[]{:S(2)}, u32[]{:S(2)}) collective-permute-start(bf16[80,3456]{1,0:T(8,128)(2,1)S(1)} %copy-done.79), channel_id=1, source_target_pairs={{0,8},{4,12},{8,0},{12,4},{16,24},{20,28},{24,16},{28,20},{1,9},{5... | collective-permute-start | bytes 1658888 | tf_op jit(solution)/shard_map/ppermute | solution.py:299
  95.5 24.1 %collective-permute-start.20 = (bf16[64,3456]{1,0:T(8,128)(2,1)}, bf16[64,3456]{1,0:T(8,128)(2,1)S(1)}, u32[]{:S(2)}, u32[]{:S(2)}) collective-permute-start(bf16[64,3456]{1,0:T(8,128)(2,1)} %get-tuple-element.256.refs_1_), channel_id=1, source_target_pairs={{0,16},{4,20},{8,24},{12,28},{16,0},{20,4},{24,8},{28,12},{1,17},{... | collective-permute-start | bytes 1327112 | tf_op jit(solution)/shard_map/ppermute | solution.py:299
  96.0 15.2 %collective-permute-start.22 = (bf16[64,1152]{1,0:T(8,128)(2,1)S(1)}, bf16[64,1152]{1,0:T(8,128)(2,1)S(1)}, u32[]{:S(2)}, u32[]{:S(2)}) collective-permute-start(bf16[64,1152]{1,0:T(8,128)(2,1)S(1)} %copy-done.112), channel_id=1, source_target_pairs={{0,16},{4,20},{8,24},{12,28},{16,0},{20,4},{24,8},{28,12},{1,17},{... | collective-permute-start | bytes 442376 | tf_op jit(solution)/shard_map/ppermute | solution.py:299
  120.6 18.6 %collective-permute-start.17 = (bf16[80,3456]{1,0:T(8,128)(2,1)S(1)}, bf16[80,3456]{1,0:T(8,128)(2,1)S(1)}, u32[]{:S(2)}, u32[]{:S(2)}) collective-permute-start(bf16[80,3456]{1,0:T(8,128)(2,1)S(1)} %copy-done.79), channel_id=1, source_target_pairs={{0,16},{4,20},{8,24},{12,28},{16,0},{20,4},{24,8},{28,12},{1,17},{... | collective-permute-start | bytes 1658888 | tf_op jit(solution)/shard_map/ppermute | solution.py:299
  122.2 22.2 %collective-permute-start.30 = (bf16[64,1152]{1,0:T(8,128)(2,1)}, bf16[64,1152]{1,0:T(8,128)(2,1)S(1)}, u32[]{:S(2)}, u32[]{:S(2)}) collective-permute-start(bf16[64,1152]{1,0:T(8,128)(2,1)} %copy-done.113), channel_id=1, source_target_pairs={{0,8},{4,12},{8,0},{12,4},{16,24},{20,28},{24,16},{28,20},{1,9},{5... | collective-permute-start | bytes 442376 | tf_op jit(solution)/shard_map/ppermute | solution.py:299
  128.3 16.1 %collective-permute-start.29 = (bf16[80,1152]{1,0:T(8,128)(2,1)}, bf16[80,1152]{1,0:T(8,128)(2,1)S(1)}, u32[]{:S(2)}, u32[]{:S(2)}) collective-permute-start(bf16[80,1152]{1,0:T(8,128)(2,1)} %collective-permute-done.21.refs_2_), channel_id=1, source_target_pairs={{0,16},{4,20},{8,24},{12,28},{16,0},{20,4},{24,8},{28,12},{1,17},{... | collective-permute-start | bytes 552968 | tf_op jit(solution)/shard_map/ppermute | solution.py:299
  128.9 23.2 %collective-permute-start.26 = (bf16[64,3456]{1,0:T(8,128)(2,1)S(1)}, bf16[64,3456]{1,0:T(8,128)(2,1)S(1)}, u32[]{:S(2)}, u32[]{:S(2)}) collective-permute-start(bf16[64,3456]{1,0:T(8,128)(2,1)S(1)} %copy-done.92), channel_id=1, source_target_pairs={{0,8},{4,12},{8,0},{12,4},{16,24},{20,28},{24,16},{28,20},{1,9},{5... | collective-permute-start | bytes 1327112 | tf_op jit(solution)/shard_map/ppermute | solution.py:299
  134.6 17.4 %collective-permute-start.31 = (bf16[576,288]{1,0:T(8,128)(2,1)S(1)}, bf16[576,288]{1,0:T(8,128)(2,1)S(1)}, u32[]{:S(2)}, u32[]{:S(2)}) collective-permute-start(bf16[576,288]{1,0:T(8,128)(2,1)S(1)} %copy.74.shard_ref), channel_id=1, source_target_pairs={{0,2},{1,3},{2,0},{3,1},{4,6},{5,7},{6,4},{7,5},{8,10},{9,11},{10,... | collective-permute-start | bytes 995336 | tf_op jit(solution)/shard_map/ppermute | solution.py:303
  157.3 27.1 %collective-permute-start.37 = (bf16[576,3456]{1,0:T(8,128)(2,1)}, bf16[576,3456]{1,0:T(8,128)(2,1)}, u32[]{:S(2)}, u32[]{:S(2)}) collective-permute-start(bf16[576,3456]{1,0:T(8,128)(2,1)} %shard_map.369), channel_id=1, source_target_pairs={{0,4},{4,0},{8,12},{12,8},{16,20},{20,16},{24,28},{28,24},{1,5},{5... | collective-permute-start | bytes 11943944 | tf_op jit(solution)/shard_map/ppermute | solution.py:299
  160.0 24.4 %collective-permute-start.38 = (bf16[576,1152]{1,0:T(8,128)(2,1)}, bf16[576,1152]{1,0:T(8,128)(2,1)}, u32[]{:S(2)}, u32[]{:S(2)}) collective-permute-start(bf16[576,1152]{1,0:T(8,128)(2,1)} %shard_map.370), channel_id=1, source_target_pairs={{0,4},{4,0},{8,12},{12,8},{16,20},{20,16},{24,28},{28,24},{1,5},{5... | collective-permute-start | bytes 3981320 | tf_op jit(solution)/shard_map/ppermute | solution.py:299
  161.4 23.0 %collective-permute-start.34 = (bf16[80,4608]{1,0:T(8,128)(2,1)}, bf16[80,4608]{1,0:T(8,128)(2,1)}, u32[]{:S(2)}, u32[]{:S(2)}) collective-permute-start(bf16[80,4608]{1,0:T(8,128)(2,1)} %get-tuple-element.279.refs_0_), channel_id=1, source_target_pairs={{0,8},{4,12},{8,0},{12,4},{16,24},{20,28},{24,16},{28,20},{1,9},{5... | collective-permute-start | bytes 2211848 | tf_op jit(solution)/shard_map/ppermute | solution.py:299
  164.4 18.9 %collective-permute-start.36 = (bf16[2,576,288]{1,2,0:T(8,128)(2,1)}, bf16[2,576,288]{1,2,0:T(8,128)(2,1)S(1)}, u32[]{:S(2)}, u32[]{:S(2)}) collective-permute-start(bf16[2,576,288]{1,2,0:T(8,128)(2,1)} %copy.75), channel_id=1, source_target_pairs={{0,1},{1,0},{2,3},{3,2},{4,5},{5,4},{6,7},{7,6},{8,9},{9,8},{10,11... | collective-permute-start | bytes 1990664 | tf_op jit(solution)/shard_map/ppermute | solution.py:303
  165.4 16.2 %collective-permute-start.35 = (bf16[64,4608]{1,0:T(8,128)(2,1)}, bf16[64,4608]{1,0:T(8,128)(2,1)}, u32[]{:S(2)}, u32[]{:S(2)}) collective-permute-start(bf16[64,4608]{1,0:T(8,128)(2,1)} %get-tuple-element.280.refs_1_), channel_id=1, source_target_pairs={{0,16},{4,20},{8,24},{12,28},{16,0},{20,4},{24,8},{28,12},{1,17},{... | collective-permute-start | bytes 1769480 | tf_op jit(solution)/shard_map/ppermute | solution.py:299
  181.6 36.7 %collective-permute-start.33 = (bf16[64,4608]{1,0:T(8,128)(2,1)}, bf16[64,4608]{1,0:T(8,128)(2,1)}, u32[]{:S(2)}, u32[]{:S(2)}) collective-permute-start(bf16[64,4608]{1,0:T(8,128)(2,1)} %get-tuple-element.280.refs_1_), channel_id=1, source_target_pairs={{0,8},{4,12},{8,0},{12,4},{16,24},{20,28},{24,16},{28,20},{1,9},{5... | collective-permute-start | bytes 1769480 | tf_op jit(solution)/shard_map/ppermute | solution.py:299
  183.3 35.0 %collective-permute-start.32 = (bf16[80,4608]{1,0:T(8,128)(2,1)}, bf16[80,4608]{1,0:T(8,128)(2,1)}, u32[]{:S(2)}, u32[]{:S(2)}) collective-permute-start(bf16[80,4608]{1,0:T(8,128)(2,1)} %get-tuple-element.279.refs_0_), channel_id=1, source_target_pairs={{0,16},{4,20},{8,24},{12,28},{16,0},{20,4},{24,8},{28,12},{1,17},{... | collective-permute-start | bytes 2211848 | tf_op jit(solution)/shard_map/ppermute | solution.py:299
  184.5 33.8 %collective-permute-start.41 = (bf16[64,4608]{1,0:T(8,128)(2,1)}, bf16[64,4608]{1,0:T(8,128)(2,1)}, u32[]{:S(2)}, u32[]{:S(2)}) collective-permute-start(bf16[64,4608]{1,0:T(8,128)(2,1)} %collective-permute-done.35.refs_5_), channel_id=1, source_target_pairs={{0,8},{4,12},{8,0},{12,4},{16,24},{20,28},{24,16},{28,20},{1,9},{5... | collective-permute-start | bytes 1769480 | tf_op jit(solution)/shard_map/ppermute | solution.py:299
  186.3 32.0 %collective-permute-start.40 = (bf16[80,4608]{1,0:T(8,128)(2,1)}, bf16[80,4608]{1,0:T(8,128)(2,1)}, u32[]{:S(2)}, u32[]{:S(2)}) collective-permute-start(bf16[80,4608]{1,0:T(8,128)(2,1)} %collective-permute-done.34.refs_2_), channel_id=1, source_target_pairs={{0,16},{4,20},{8,24},{12,28},{16,0},{20,4},{24,8},{28,12},{1,17},{... | collective-permute-start | bytes 2211848 | tf_op jit(solution)/shard_map/ppermute | solution.py:299
  223.7 29.5 %collective-permute-start.46 = (bf16[258,576]{1,0:T(8,128)(2,1)S(1)}, bf16[258,576]{1,0:T(8,128)(2,1)S(1)}, u32[]{:S(2)}, u32[]{:S(2)}) collective-permute-start(bf16[258,576]{1,0:T(8,128)(2,1)S(1)} %copy-done.40), channel_id=1, source_target_pairs={{0,4},{4,0},{8,12},{12,8},{16,20},{20,16},{24,28},{28,24},{1,5},{5... | collective-permute-start | bytes 891656 | tf_op jit(solution)/shard_map/ppermute | solution.py:299
  224.2 29.1 %collective-permute-start.44 = (bf16[288,1152]{1,0:T(8,128)(2,1)S(1)}, bf16[288,1152]{1,0:T(8,128)(2,1)S(1)}, u32[]{:S(2)}, u32[]{:S(2)}) collective-permute-start(bf16[288,1152]{1,0:T(8,128)(2,1)S(1)} %copy-done.68), channel_id=1, source_target_pairs={{0,8},{4,12},{8,0},{12,4},{16,24},{20,28},{24,16},{28,20},{1,9},{5... | collective-permute-start | bytes 1990664 | tf_op jit(solution)/shard_map/ppermute | solution.py:299
  225.4 27.9 %collective-permute-start.45 = (bf16[288,1152]{1,0:T(8,128)(2,1)S(1)}, bf16[288,1152]{1,0:T(8,128)(2,1)S(1)}, u32[]{:S(2)}, u32[]{:S(2)}) collective-permute-start(bf16[288,1152]{1,0:T(8,128)(2,1)S(1)} %copy-done.69), channel_id=1, source_target_pairs={{0,16},{4,20},{8,24},{12,28},{16,0},{20,4},{24,8},{28,12},{1,17},{... | collective-permute-start | bytes 1990664 | tf_op jit(solution)/shard_map/ppermute | solution.py:299
  226.7 26.6 %collective-permute-start.47 = (bf16[258,576]{1,0:T(8,128)(2,1)S(1)}, bf16[258,576]{1,0:T(8,128)(2,1)S(1)}, u32[]{:S(2)}, u32[]{:S(2)}) collective-permute-start(bf16[258,576]{1,0:T(8,128)(2,1)S(1)} %get-tuple-element.316), channel_id=1, source_target_pairs={{0,4},{4,0},{8,12},{12,8},{16,20},{20,16},{24,28},{28,24},{1,5},{5... | collective-permute-start | bytes 891656 | tf_op jit(solution)/shard_map/ppermute | solution.py:299
  254.5 17.7 %collective-permute-start.42 = (bf16[288,1152]{1,0:T(8,128)(2,1)S(1)}, bf16[288,1152]{1,0:T(8,128)(2,1)S(1)}, u32[]{:S(2)}, u32[]{:S(2)}) collective-permute-start(bf16[288,1152]{1,0:T(8,128)(2,1)S(1)} %copy-done.68), channel_id=1, source_target_pairs={{0,16},{4,20},{8,24},{12,28},{16,0},{20,4},{24,8},{28,12},{1,17},{... | collective-permute-start | bytes 1990664 | tf_op jit(solution)/shard_map/ppermute | solution.py:299
  256.5 17.8 %collective-permute-start.43 = (bf16[288,1152]{1,0:T(8,128)(2,1)S(1)}, bf16[288,1152]{1,0:T(8,128)(2,1)S(1)}, u32[]{:S(2)}, u32[]{:S(2)}) collective-permute-start(bf16[288,1152]{1,0:T(8,128)(2,1)S(1)} %copy-done.69), channel_id=1, source_target_pairs={{0,8},{4,12},{8,0},{12,4},{16,24},{20,28},{24,16},{28,20},{1,9},{5... | collective-permute-start | bytes 1990664 | tf_op jit(solution)/shard_map/ppermute | solution.py:299
  256.8 29.1 %collective-permute-start.49 = (bf16[288,1152]{1,0:T(8,128)(2,1)S(1)}, bf16[288,1152]{1,0:T(8,128)(2,1)S(1)}, u32[]{:S(2)}, u32[]{:S(2)}) collective-permute-start(bf16[288,1152]{1,0:T(8,128)(2,1)S(1)} %collective-permute-done.44.refs_2_), channel_id=1, source_target_pairs={{0,16},{4,20},{8,24},{12,28},{16,0},{20,4},{24,8},{28,12},{1,17},{... | collective-permute-start | bytes 1990664 | tf_op jit(solution)/shard_map/ppermute | solution.py:299
  257.7 29.7 %collective-permute-start.50 = (bf16[288,1152]{1,0:T(8,128)(2,1)S(1)}, bf16[288,1152]{1,0:T(8,128)(2,1)S(1)}, u32[]{:S(2)}, u32[]{:S(2)}) collective-permute-start(bf16[288,1152]{1,0:T(8,128)(2,1)S(1)} %collective-permute-done.45.refs_5_), channel_id=1, source_target_pairs={{0,8},{4,12},{8,0},{12,4},{16,24},{20,28},{24,16},{28,20},{1,9},{5... | collective-permute-start | bytes 1990664 | tf_op jit(solution)/shard_map/ppermute | solution.py:299
  298.9 45.3 %collective-permute-start.53 = (bf16[2,288,1152]{2,1,0:T(8,128)(2,1)}, bf16[2,288,1152]{2,1,0:T(8,128)(2,1)}, u32[]{:S(2)}, u32[]{:S(2)}) collective-permute-start(bf16[2,288,1152]{2,1,0:T(8,128)(2,1)} %get-tuple-element.501), channel_id=1, source_target_pairs={{0,16},{4,20},{8,24},{12,28},{16,0},{20,4},{24,8},{28,12},{1,17},{... | collective-permute-start | bytes 3981320 | tf_op jit(solution)/shard_map/ppermute | solution.py:299
  301.7 42.5 %collective-permute-start.52 = (bf16[2,288,1152]{2,1,0:T(8,128)(2,1)}, bf16[2,288,1152]{2,1,0:T(8,128)(2,1)}, u32[]{:S(2)}, u32[]{:S(2)}) collective-permute-start(bf16[2,288,1152]{2,1,0:T(8,128)(2,1)} %get-tuple-element.503), channel_id=1, source_target_pairs={{0,8},{4,12},{8,0},{12,4},{16,24},{20,28},{24,16},{28,20},{1,9},{5... | collective-permute-start | bytes 3981320 | tf_op jit(solution)/shard_map/ppermute | solution.py:299
  311.2 20.9 %collective-permute-start.55 = (bf16[258,4608]{1,0:T(8,128)(2,1)}, bf16[258,4608]{1,0:T(8,128)(2,1)}, u32[]{:S(2)}, u32[]{:S(2)}) collective-permute-start(bf16[258,4608]{1,0:T(8,128)(2,1)} %get-tuple-element.334), channel_id=1, source_target_pairs={{0,4},{4,0},{8,12},{12,8},{16,20},{20,16},{24,28},{28,24},{1,5},{5... | collective-permute-start | bytes 7133192 | tf_op jit(solution)/shard_map/ppermute | solution.py:299
  351.3 63.1 %collective-permute-start.60 = (bf16[258,1152]{1,0:T(8,128)(2,1)}, bf16[258,1152]{1,0:T(8,128)(2,1)}, u32[]{:S(2)}, u32[]{:S(2)}) collective-permute-start(bf16[258,1152]{1,0:T(8,128)(2,1)} %convert_element_type.277), channel_id=1, source_target_pairs={{0,4},{4,0},{8,12},{12,8},{16,20},{20,16},{24,28},{28,24},{1,5},{5... | collective-permute-start | bytes 1783304 | tf_op jit(solution)/shard_map/ppermute | solution.py:299
  364.1 50.3 %collective-permute-start.56 = (bf16[288,1152]{1,0:T(8,128)(2,1)}, bf16[288,1152]{1,0:T(8,128)(2,1)}, u32[]{:S(2)}, u32[]{:S(2)}) collective-permute-start(bf16[288,1152]{1,0:T(8,128)(2,1)} %get-tuple-element.528), channel_id=1, source_target_pairs={{0,16},{4,20},{8,24},{12,28},{16,0},{20,4},{24,8},{28,12},{1,17},{... | collective-permute-start | bytes 1990664 | tf_op jit(solution)/shard_map/ppermute | solution.py:299
  368.5 46.0 %collective-permute-start.57 = (bf16[288,1152]{1,0:T(8,128)(2,1)}, bf16[288,1152]{1,0:T(8,128)(2,1)}, u32[]{:S(2)}, u32[]{:S(2)}) collective-permute-start(bf16[288,1152]{1,0:T(8,128)(2,1)} %get-tuple-element.526), channel_id=1, source_target_pairs={{0,8},{4,12},{8,0},{12,4},{16,24},{20,28},{24,16},{28,20},{1,9},{5... | collective-permute-start | bytes 1990664 | tf_op jit(solution)/shard_map/ppermute | solution.py:299
  371.3 47.3 %collective-permute-start.58 = (bf16[2,80,4608]{2,1,0:T(8,128)(2,1)}, bf16[2,80,4608]{2,1,0:T(8,128)(2,1)}, u32[]{:S(2)}, u32[]{:S(2)}) collective-permute-start(bf16[2,80,4608]{2,1,0:T(8,128)(2,1)} %get-tuple-element.497), channel_id=1, source_target_pairs={{0,8},{4,12},{8,0},{12,4},{16,24},{20,28},{24,16},{28,20},{1,9},{5... | collective-permute-start | bytes 4423688 | tf_op jit(solution)/shard_map/ppermute | solution.py:299
  391.0 27.6 %collective-permute-start.59 = (bf16[2,64,4608]{2,1,0:T(8,128)(2,1)}, bf16[2,64,4608]{2,1,0:T(8,128)(2,1)}, u32[]{:S(2)}, u32[]{:S(2)}) collective-permute-start(bf16[2,64,4608]{2,1,0:T(8,128)(2,1)} %get-tuple-element.507), channel_id=1, source_target_pairs={{0,16},{4,20},{8,24},{12,28},{16,0},{20,4},{24,8},{28,12},{1,17},{... | collective-permute-start | bytes 3538952 | tf_op jit(solution)/shard_map/ppermute | solution.py:299
  424.8 21.7 %collective-permute-start.61 = (bf16[2,576,288]{1,2,0:T(8,128)(2,1)S(1)}, bf16[2,576,288]{1,2,0:T(8,128)(2,1)S(1)}, u32[]{:S(2)}, u32[]{:S(2)}) collective-permute-start(bf16[2,576,288]{1,2,0:T(8,128)(2,1)S(1)} %copy.94), channel_id=1, source_target_pairs={{0,1},{1,0},{2,3},{3,2},{4,5},{5,4},{6,7},{7,6},{8,9},{9,8},{10,11... | collective-permute-start | bytes 1990664 | tf_op jit(solution)/shard_map/ppermute | solution.py:303
  427.8 18.7 %collective-permute-start.63 = (bf16[64,4608]{1,0:T(8,128)(2,1)S(1)}, bf16[64,4608]{1,0:T(8,128)(2,1)S(1)}, u32[]{:S(2)}, u32[]{:S(2)}) collective-permute-start(bf16[64,4608]{1,0:T(8,128)(2,1)S(1)} %get-tuple-element.534), channel_id=1, source_target_pairs={{0,8},{4,12},{8,0},{12,4},{16,24},{20,28},{24,16},{28,20},{1,9},{5... | collective-permute-start | bytes 1769480 | tf_op jit(solution)/shard_map/ppermute | solution.py:299
  431.3 18.9 %collective-permute-start.62 = (bf16[80,4608]{1,0:T(8,128)(2,1)S(1)}, bf16[80,4608]{1,0:T(8,128)(2,1)S(1)}, u32[]{:S(2)}, u32[]{:S(2)}) collective-permute-start(bf16[80,4608]{1,0:T(8,128)(2,1)S(1)} %get-tuple-element.516), channel_id=1, source_target_pairs={{0,16},{4,20},{8,24},{12,28},{16,0},{20,4},{24,8},{28,12},{1,17},{... | collective-permute-start | bytes 2211848 | tf_op jit(solution)/shard_map/ppermute | solution.py:299
  458.6 23.5 %collective-permute-start.70 = (bf16[2,64,1152]{2,1,0:T(8,128)(2,1)}, bf16[2,64,1152]{2,1,0:T(8,128)(2,1)}, u32[]{:S(2)}, u32[]{:S(2)}) collective-permute-start(bf16[2,64,1152]{2,1,0:T(8,128)(2,1)} %get-tuple-element.593), channel_id=1, source_target_pairs={{0,16},{4,20},{8,24},{12,28},{16,0},{20,4},{24,8},{28,12},{1,17},{... | collective-permute-start | bytes 884744 | tf_op jit(solution)/shard_map/ppermute | solution.py:299
  459.7 41.7 %collective-permute-start.69 = (bf16[2,80,1152]{2,1,0:T(8,128)(2,1)}, bf16[2,80,1152]{2,1,0:T(8,128)(2,1)}, u32[]{:S(2)}, u32[]{:S(2)}) collective-permute-start(bf16[2,80,1152]{2,1,0:T(8,128)(2,1)} %get-tuple-element.544), channel_id=1, source_target_pairs={{0,8},{4,12},{8,0},{12,4},{16,24},{20,28},{24,16},{28,20},{1,9},{5... | collective-permute-start | bytes 1105928 | tf_op jit(solution)/shard_map/ppermute | solution.py:299
  469.3 32.1 %collective-permute-start.66 = (bf16[2,144,1152]{2,1,0:T(8,128)(2,1)}, bf16[2,144,1152]{2,1,0:T(8,128)(2,1)}, u32[]{:S(2)}, u32[]{:S(2)}) collective-permute-start(bf16[2,144,1152]{2,1,0:T(8,128)(2,1)} %get-tuple-element.370), channel_id=1, source_target_pairs={{0,1},{1,0},{2,3},{3,2},{4,5},{5,4},{6,7},{7,6},{8,9},{9,8},{10,11... | collective-permute-start | bytes 1990664 | tf_op jit(solution)/shard_map/ppermute | solution.py:303
  472.0 29.4 %collective-permute-start.68 = (bf16[2,64,3456]{2,1,0:T(8,128)(2,1)}, bf16[2,64,3456]{2,1,0:T(8,128)(2,1)}, u32[]{:S(2)}, u32[]{:S(2)}) collective-permute-start(bf16[2,64,3456]{2,1,0:T(8,128)(2,1)} %get-tuple-element.514), channel_id=1, source_target_pairs={{0,16},{4,20},{8,24},{12,28},{16,0},{20,4},{24,8},{28,12},{1,17},{... | collective-permute-start | bytes 2654216 | tf_op jit(solution)/shard_map/ppermute | solution.py:299
  474.4 27.0 %collective-permute-start.67 = (bf16[2,80,3456]{2,1,0:T(8,128)(2,1)S(1)}, bf16[2,80,3456]{2,1,0:T(8,128)(2,1)S(1)}, u32[]{:S(2)}, u32[]{:S(2)}) collective-permute-start(bf16[2,80,3456]{2,1,0:T(8,128)(2,1)S(1)} %get-tuple-element.509), channel_id=1, source_target_pairs={{0,8},{4,12},{8,0},{12,4},{16,24},{20,28},{24,16},{28,20},{1,9},{5... | collective-permute-start | bytes 3317768 | tf_op jit(solution)/shard_map/ppermute | solution.py:299
  482.1 19.3 %collective-permute-start.65 = (bf16[576,288]{0,1:T(8,128)(2,1)S(1)}, bf16[576,288]{0,1:T(8,128)(2,1)S(1)}, u32[]{:S(2)}, u32[]{:S(2)}) collective-permute-start(bf16[576,288]{0,1:T(8,128)(2,1)S(1)} %bitcast.240), channel_id=1, source_target_pairs={{0,2},{1,3},{2,0},{3,1},{4,6},{5,7},{6,4},{7,5},{8,10},{9,11},{10,... | collective-permute-start | bytes 995336 | tf_op jit(solution)/shard_map/ppermute | solution.py:303
  505.1 29.1 %collective-permute-start.77 = (bf16[64,1152]{1,0:T(8,128)(2,1)}, bf16[64,1152]{1,0:T(8,128)(2,1)}, u32[]{:S(2)}, u32[]{:S(2)}) collective-permute-start(bf16[64,1152]{1,0:T(8,128)(2,1)} %get-tuple-element.599), channel_id=1, source_target_pairs={{0,8},{4,12},{8,0},{12,4},{16,24},{20,28},{24,16},{28,20},{1,9},{5... | collective-permute-start | bytes 442376 | tf_op jit(solution)/shard_map/ppermute | solution.py:299
  507.8 32.3 %collective-permute-start.76 = (bf16[80,1152]{1,0:T(8,128)(2,1)}, bf16[80,1152]{1,0:T(8,128)(2,1)}, u32[]{:S(2)}, u32[]{:S(2)}) collective-permute-start(bf16[80,1152]{1,0:T(8,128)(2,1)} %get-tuple-element.597), channel_id=1, source_target_pairs={{0,16},{4,20},{8,24},{12,28},{16,0},{20,4},{24,8},{28,12},{1,17},{... | collective-permute-start | bytes 552968 | tf_op jit(solution)/shard_map/ppermute | solution.py:299
  508.9 44.3 %collective-permute-start.73 = (bf16[2,144,1152]{2,1,0:T(8,128)(2,1)}, bf16[2,144,1152]{2,1,0:T(8,128)(2,1)}, u32[]{:S(2)}, u32[]{:S(2)}) collective-permute-start(bf16[2,144,1152]{2,1,0:T(8,128)(2,1)} %get-tuple-element.522), channel_id=1, source_target_pairs={{0,16},{4,20},{8,24},{12,28},{16,0},{20,4},{24,8},{28,12},{1,17},{... | collective-permute-start | bytes 1990664 | tf_op jit(solution)/shard_map/ppermute | solution.py:299
  511.0 42.2 %collective-permute-start.72 = (bf16[2,144,1152]{2,1,0:T(8,128)(2,1)}, bf16[2,144,1152]{2,1,0:T(8,128)(2,1)}, u32[]{:S(2)}, u32[]{:S(2)}) collective-permute-start(bf16[2,144,1152]{2,1,0:T(8,128)(2,1)} %get-tuple-element.524), channel_id=1, source_target_pairs={{0,8},{4,12},{8,0},{12,4},{16,24},{20,28},{24,16},{28,20},{1,9},{5... | collective-permute-start | bytes 1990664 | tf_op jit(solution)/shard_map/ppermute | solution.py:299
  534.2 18.9 %collective-permute-start.75 = (bf16[64,3456]{1,0:T(8,128)(2,1)S(1)}, bf16[64,3456]{1,0:T(8,128)(2,1)}, u32[]{:S(2)}, u32[]{:S(2)}) collective-permute-start(bf16[64,3456]{1,0:T(8,128)(2,1)S(1)} %get-tuple-element.538), channel_id=1, source_target_pairs={{0,8},{4,12},{8,0},{12,4},{16,24},{20,28},{24,16},{28,20},{1,9},{5... | collective-permute-start | bytes 1327112 | tf_op jit(solution)/shard_map/ppermute | solution.py:299
  553.1 20.9 %collective-permute-start.91 = (f32[3168]{0:T(1024)S(1)}, f32[3168]{0:T(1024)S(1)}, u32[]{:S(2)}, u32[]{:S(2)}) collective-permute-start(f32[3168]{0:T(1024)S(1)} %get-tuple-element.455), channel_id=1, source_target_pairs={{0,1},{1,0},{2,3},{3,2},{4,5},{5,4},{6,7},{7,6},{8,9},{9,8},{10,11... | collective-permute-start | bytes 38024 | tf_op jit(solution)/shard_map/ppermute | solution.py:303
  555.4 24.7 %collective-permute-start.79 = (bf16[144,1152]{1,0:T(8,128)(2,1)}, bf16[144,1152]{1,0:T(8,128)(2,1)S(1)}, u32[]{:S(2)}, u32[]{:S(2)}) collective-permute-start(bf16[144,1152]{1,0:T(8,128)(2,1)} %get-tuple-element.552), channel_id=1, source_target_pairs={{0,16},{4,20},{8,24},{12,28},{16,0},{20,4},{24,8},{28,12},{1,17},{... | collective-permute-start | bytes 995336 | tf_op jit(solution)/shard_map/ppermute | solution.py:299
  561.5 18.6 %collective-permute-start.81 = (bf16[2,144,864]{2,1,0:T(8,128)(2,1)}, bf16[2,144,864]{2,1,0:T(8,128)(2,1)S(1)}, u32[]{:S(2)}, u32[]{:S(2)}) collective-permute-start(bf16[2,144,864]{2,1,0:T(8,128)(2,1)} %get-tuple-element.411), channel_id=1, source_target_pairs={{0,1},{1,0},{2,3},{3,2},{4,5},{5,4},{6,7},{7,6},{8,9},{9,8},{10,11... | collective-permute-start | bytes 1493000 | tf_op jit(solution)/shard_map/ppermute | solution.py:303
  587.9 16.7 %collective-permute-start.83 = (bf16[2,288,288]{2,1,0:T(8,128)(2,1)}, bf16[2,288,288]{2,1,0:T(8,128)(2,1)S(1)}, u32[]{:S(2)}, u32[]{:S(2)}) collective-permute-start(bf16[2,288,288]{2,1,0:T(8,128)(2,1)} %get-tuple-element.425), channel_id=1, source_target_pairs={{0,1},{1,0},{2,3},{3,2},{4,5},{5,4},{6,7},{7,6},{8,9},{9,8},{10,11... | collective-permute-start | bytes 995336 | tf_op jit(solution)/shard_map/ppermute | solution.py:303
  (172 other events, 1734.7 us)

commit v2 on v0

--- a/solution.py
+++ b/solution.py
@@ -1,6 +1,8 @@
 import jax
 import jax.numpy as jnp
 from jax import lax
+from jax.experimental import pallas as pl
+from jax.experimental.pallas import tpu as pltpu
 from jax.sharding import PartitionSpec as P
 
 D = 1152
@@ -80,7 +82,7 @@
     return (weight - step_rate * (direction + weight_decay * weight), moment_new, square_new)
 
 
-def on_device(
+def general_device(
     inputs,
     skip_tokens,
     cotangent,
@@ -287,6 +289,1131 @@
     )
 
 
+CORE = 1
+ACROSS = 2
+ALONG = 4
+PAD = 384
+VMEM_BYTES = 56 * 1024 * 1024
+LIGHT = pl.CostEstimate(flops=0, bytes_accessed=1024, transcendentals=0)
+PARAMS = pltpu.CompilerParams(vmem_limit_bytes=VMEM_BYTES)
+
+
+def swap_wide(value, bit):
+    return lax.ppermute(value, "wide", [(i, i ^ bit) for i in range(8)])
+
+
+def swap_narrow(value, bit):
+    return lax.ppermute(value, "narrow", [(i, i ^ bit) for i in range(4)])
+
+
+def together(*values):
+    return lax.optimization_barrier(values)
+
+
+def spot():
+    wide = lax.axis_index("wide")
+    narrow = lax.axis_index("narrow")
+    return (wide & 1, (wide >> 1) & 1, (wide >> 2) & 1, narrow & 1, narrow >> 1)
+
+
+def split_rows(rows):
+    return -(-rows // 32) * 16
+
+
+def column_blocks(kind, quarter):
+    if kind == "attend_output":
+        width = quarter // 8
+        order = [8 * part + 2 * n + p for part in range(3) for p in range(2) for n in range(4)]
+        blocks = [(block // 6, (block % 6) * width) for block in order]
+        return width, blocks + [(n, (6 + p) * width) for p in range(2) for n in range(4)]
+    width = quarter // 2
+    return width, [(n, p * width) for p in range(2) for n in range(4)]
+
+
+def fold(shard):
+    parts = max(1, shard.shape[0] // (D // 8))
+    height = shard.shape[0] // parts
+    return jnp.concatenate(
+        [shard[part * height : (part + 1) * height] for part in range(parts)], axis=1
+    )
+
+
+def unfold(value, rows):
+    parts = rows // value.shape[0]
+    quarter = value.shape[1] // parts
+    return jnp.concatenate(
+        [value[:, part * quarter : (part + 1) * quarter] for part in range(parts)], axis=0
+    )
+
+
+def arrange(kind, parts, shard, far, near, near_far):
+    height = shard.shape[0]
+    rows, quarter = parts * height, shard.shape[1] // parts
+    split = split_rows(rows)
+    width, blocks = column_blocks(kind, quarter)
+
+    def kernel(shard_ref, far_ref, near_ref, near_far_ref, top_ref, bottom_ref, held):
+        narrow = lax.axis_index("narrow")
+        held[0] = shard_ref[...]
+        held[2] = far_ref[...]
+        held[1] = near_ref[...]
+        held[3] = near_far_ref[...]
+        for number in range(4):
+            value = held[narrow ^ number]
+            for position, (owner, offset) in enumerate(blocks):
+                if owner == number:
+                    column = slice(position * width, (position + 1) * width)
+                    if parts == 1:
+                        piece = value[:, offset : offset + width]
+                        top_ref[:, column] = piece[:split]
+                        bottom_ref[:, column] = piece[split:]
+                    for part in range(parts if parts > 1 else 0):
+                        start = part * quarter + offset
+                        piece = value[:, start : start + width]
+                        row = part * height
+                        if row < split:
+                            top_ref[row : row + height, column] = piece
+                        else:
+                            bottom_ref[row - split : row - split + height, column] = piece
+
+    return pl.pallas_call(
+        kernel,
+        out_shape=(
+            jax.ShapeDtypeStruct((split, 4 * quarter), jnp.bfloat16),
+            jax.ShapeDtypeStruct((rows - split, 4 * quarter), jnp.bfloat16),
+        ),
+        scratch_shapes=[pltpu.VMEM((4,) + shard.shape, jnp.bfloat16)],
+        compiler_params=PARAMS,
+        cost_estimate=LIGHT,
+    )(shard, far, near, near_far)
+
+
+def place(parts, first, second, third):
+    split, columns = parts[0].shape
+    rest = parts[1].shape[0]
+    rows = split + rest
+
+    def kernel(top, bottom, top_x, bottom_y, top_y, bottom_x, top_xy, bottom_xy, full):
+        chip = lax.axis_index("wide") >> 1
+        tops = (top, top_x, top_y, top_xy)
+        bottoms = (bottom, bottom_x, bottom_y, bottom_xy)
+        for relative in range(4):
+            start = (chip ^ relative) * rows
+            full[pl.ds(pl.multiple_of(start, 16), split)] = tops[relative][...]
+            full[pl.ds(pl.multiple_of(start + split, 16), rest)] = bottoms[relative][...]
+
+    return pl.pallas_call(
+        kernel,
+        out_shape=jax.ShapeDtypeStruct((4 * rows, columns), jnp.bfloat16),
+        compiler_params=PARAMS,
+        cost_estimate=LIGHT,
+    )(*parts, *first, *second, *third)
+
+
+def pair_gradient(lefts, rights):
+    height = lefts[0][0].shape[0]
+    rows = height // 4
+    split = split_rows(rows)
+    tokens = rights[0][0].shape[0]
+    widths = [right[0].shape[1] for right in rights]
+    tile = 384 if height > 576 else 1152
+    steps = [width // tile for width in widths]
+    starts = [sum(steps[:position]) for position in range(len(steps))]
+    count = len(lefts)
+
+    def kernel(*refs):
+        left_refs = refs[: 2 * count]
+        right_refs = refs[2 * count : 4 * count]
+        outs, (joint, beside) = refs[4 * count : 4 * count + 8], refs[4 * count + 8 :]
+        step = pl.program_id(0)
+        wide = lax.axis_index("wide")
+        across, along = (wide >> 1) & 1, (wide >> 2) & 1
+
+        @pl.when(step == 0)
+        def _():
+            joint[...] = jnp.zeros_like(joint)
+
+        for number in range(count):
+
+            @pl.when(step == starts[number])
+            def _():
+                beside[:, :PAD] = left_refs[2 * number][...]
+                beside[:, PAD:] = left_refs[2 * number + 1][...]
+
+            @pl.when((step >= starts[number]) & (step < starts[number] + steps[number]))
+            def _():
+                joint[:tokens] = right_refs[2 * number][...]
+                joint[PAD : PAD + tokens] = right_refs[2 * number + 1][...]
+                for y in range(2):
+                    for x in range(2):
+                        first_row = (2 * y + x) * rows
+                        total = jnp.dot(
+                            beside[first_row : first_row + rows],
+                            joint[...],
+                            preferred_element_type=jnp.float32,
+                        ).astype(jnp.bfloat16)
+
+                        for kept_x in range(2):
+                            for kept_y in range(2):
+
+                                @pl.when(
+                                    ((across == x) == (kept_x == 1))
+                                    & ((along == y) == (kept_y == 1))
+                                )
+                                def _():
+                                    outs[2 * (1 - kept_x) + (1 - kept_y)][...] = total[:split]
+                                    outs[4 + 2 * (1 - kept_y) + (1 - kept_x)][...] = total[split:]
+
+    def right_spec(number):
+        return pl.BlockSpec(
+            (tokens, tile),
+            lambda i: (0, jnp.clip(i - starts[number], 0, steps[number] - 1)),
+        )
+
+    in_specs = [pl.BlockSpec((height, PAD), lambda i: (0, 0))] * (2 * count)
+    operands = [left for pair in lefts for left in pair]
+    for number in range(count):
+        in_specs += [right_spec(number)] * 2
+        operands += list(rights[number])
+    top_spec = pl.BlockSpec((split, tile), lambda i: (0, i))
+    bottom_spec = pl.BlockSpec((rows - split, tile), lambda i: (0, i))
+    top_shape = jax.ShapeDtypeStruct((split, sum(widths)), jnp.bfloat16)
+    bottom_shape = jax.ShapeDtypeStruct((rows - split, sum(widths)), jnp.bfloat16)
+    outs = pl.pallas_call(
+        kernel,
+        grid=(sum(steps),),
+        in_specs=in_specs,
+        out_specs=(top_spec,) * 4 + (bottom_spec,) * 4,
+        out_shape=(top_shape,) * 4 + (bottom_shape,) * 4,
+        scratch_shapes=[
+            pltpu.VMEM((2 * PAD, tile), jnp.bfloat16),
+            pltpu.VMEM((height, 2 * PAD), jnp.bfloat16),
+        ],
+        compiler_params=PARAMS,
+        cost_estimate=LIGHT,
+    )(*operands)
+    return outs[:4], outs[4:]
+
+
+def unarrange(kind, parts, top, bottom):
+    split, columns = top[0].shape
+    rest = bottom[0].shape[0]
+    rows = split + rest
+    quarter = columns // 4
+    height = rows // parts
+    width, blocks = column_blocks(kind, quarter)
+
+    def kernel(*refs):
+        tops, bottoms = refs[:3], refs[3:6]
+        keep_ref, keep_far_ref, send_ref, send_far_ref, held = refs[6:]
+        narrow = lax.axis_index("narrow")
+        low_bit, high_bit = narrow & 1, narrow >> 1
+        held[:split] = add_low(*[ref[...] for ref in tops])
+        held[split:] = add_low(*[ref[...] for ref in bottoms])
+        for position, (owner, offset) in enumerate(blocks):
+            piece = held[:, position * width : (position + 1) * width]
+            for kept_low in range(2):
+                for kept_high in range(2):
+                    target = (keep_ref, keep_far_ref, send_ref, send_far_ref)[
+                        2 * (1 - kept_low) + (1 - kept_high)
+                    ]
+
+                    @pl.when(
+                        ((low_bit == (owner & 1)) == (kept_low == 1))
+                        & ((high_bit == (owner >> 1)) == (kept_high == 1))
+                    )
+                    def _():
+                        for part in range(parts):
+                            start = part * quarter + offset
+                            target[:, start : start + width] = piece[
+                                part * height : (part + 1) * height
+                            ]
+
+    shape = jax.ShapeDtypeStruct((height, parts * quarter), jnp.bfloat16)
+    return pl.pallas_call(
+        kernel,
+        out_shape=(shape,) * 4,
+        scratch_shapes=[pltpu.VMEM((rows, columns), jnp.bfloat16)],
+        compiler_params=PARAMS,
+        cost_estimate=LIGHT,
+    )(*top, *bottom)
+
+
+def add_low(*terms):
+    return sum(term.astype(jnp.float32) for term in terms).astype(jnp.bfloat16)
+
+
+def pick(value, index, dim=0):
+    return lax.dynamic_index_in_dim(value, index, dim, keepdims=False)
+
+
+def halves_of(value, core):
+    middle = value.shape[-1] // 2
+    first, second = value[..., :middle], value[..., middle:]
+    return jnp.where(core == 0, first, second), jnp.where(core == 0, second, first)
+
+
+def inner(value):
+    width = value.shape[-1] // 8
+    return jnp.concatenate(
+        [
+            value[..., (2 * n + p) * width : (2 * n + p + 1) * width]
+            for p in range(2)
+            for n in range(4)
+        ],
+        axis=-1,
+    )
+
+
+def outer(value):
+    width = value.shape[-1] // 8
+    return jnp.concatenate(
+        [
+            value[..., (4 * p + n) * width : (4 * p + n + 1) * width]
+            for n in range(4)
+            for p in range(2)
+        ],
+        axis=-1,
+    )
+
+
+def upright(value):
+    return jnp.pad(value, ((0, PAD - value.shape[0]), (0, 0))).T
+
+
+def both(parts, order):
+    if order == 0:
+        return swap_wide(parts[0], ACROSS), swap_wide(parts[1], ALONG)
+    return swap_wide(parts[0], ALONG), swap_wide(parts[1], ACROSS)
+
+
+KEEP_NEAR, KEEP_FAR, SEND_NEAR, SEND_FAR = range(4)
+
+
+def send(blocks, which):
+    return both((blocks[0][which], blocks[1][which]), 0)
+
+
+def forward(blocks, got):
+    return both(tuple(add_low(blocks[i][KEEP_FAR], got[i]) for i in range(2)), 1)
+
+
+def settle(kind, parts, blocks, got_near, got_last):
+    return unarrange(
+        kind, parts, *[(blocks[i][KEEP_NEAR], got_near[i], got_last[i]) for i in range(2)]
+    )
+
+
+def narrow_first(quarters):
+    return swap_narrow(quarters[SEND_FAR], 1), swap_narrow(quarters[SEND_NEAR], 1)
+
+
+def narrow_second(quarters, got):
+    return swap_narrow(add_low(quarters[KEEP_FAR], got[0]), 2)
+
+
+def finish(quarters, got, got_last):
+    return (
+        quarters[KEEP_NEAR].astype(jnp.float32)
+        + got[1].astype(jnp.float32)
+        + got_last.astype(jnp.float32)
+    )
+
+
+def gather_vector(far, near, vector):
+    low_bit, high_bit = spot()[3:]
+    own = jnp.stack([vector, far])
+    own = jnp.where(high_bit == 0, own, own[::-1])
+    near = jnp.where(high_bit == 0, near, near[::-1])
+    even = jnp.where(low_bit == 0, own, near)
+    odd = jnp.where(low_bit == 0, near, own)
+    return jnp.concatenate([even[0], odd[0], even[1], odd[1]])
+
+
+def heavy(kernel, outs, scratch, *operands):
+    return pl.pallas_call(
+        kernel,
+        out_shape=tuple(jax.ShapeDtypeStruct(shape, dtype) for shape, dtype in outs),
+        scratch_shapes=[pltpu.VMEM(shape, dtype) for shape, dtype in scratch],
+        compiler_params=PARAMS,
+        cost_estimate=LIGHT,
+    )(*operands)
+
+
+def dot_rows(left, right):
+    return lax.dot_general(left, right, (((1,), (1,)), ((), ())), preferred_element_type=jnp.float32)
+
+
+def dot_depth(left, right):
+    return lax.dot_general(left, right, (((0,), (0,)), ((), ())), preferred_element_type=jnp.float32)
+
+
+def in_order(mine, other, work):
+    core = lax.axis_index("wide") & 1
+
+    @pl.when(core == 0)
+    def _():
+        work(mine, other)
+
+    @pl.when(core == 1)
+    def _():
+        work(other, mine)
+
+
+def store_upright(value, padded, mine, other):
+    features = value.shape[1]
+    padded[: value.shape[0]] = value
+    turned = padded[...].T.astype(jnp.bfloat16)
+
+    def work(even, odd):
+        even[...] = turned[: features // 2]
+        odd[...] = turned[features // 2 :]
+
+    in_order(mine, other, work)
+
+
+def merge_forward(joined_mine, joined_other, merge_mine, merge_other, bias, gain, shift):
+    length = joined_mine.shape[0]
+
+    def kernel(
+        left, right, mine, other, bias_ref, gain_ref, shift_ref, stream, entry, up_mine, up_other, padded
+    ):
+        padded[...] = jnp.zeros_like(padded)
+        stream[...] = product(left[...], mine[...]) + product(right[...], other[...]) + bias_ref[...]
+        normed = normalize(stream[...])[0]
+        value = (normed * gain_ref[...] + shift_ref[...]).astype(jnp.bfloat16)
+        entry[...] = value
+        store_upright(value.astype(jnp.float32), padded, up_mine, up_other)
+
+    return heavy(
+        kernel,
+        [
+            ((length, D), jnp.float32),
+            ((length, D), jnp.bfloat16),
+            ((D // 2, PAD), jnp.bfloat16),
+            ((D // 2, PAD), jnp.bfloat16),
+        ],
+        [((PAD, D), jnp.float32)],
+        joined_mine,
+        joined_other,
+        merge_mine,
+        merge_other,
+        bias,
+        gain,
+        shift,
+    )
+
+
+def attend_head(heads, head, chances_ref, slot):
+    at = head * HD
+    queries = heads[:, at : at + HD]
+    keys = heads[:, D + at : D + at + HD]
+    values = heads[:, 2 * D + at : 2 * D + at + HD]
+    logits = dot_rows(queries, keys) * HD ** (-0.5)
+    powers = jnp.exp(logits - jnp.max(logits, axis=-1, keepdims=True))
+    chances = powers / jnp.sum(powers, axis=-1, keepdims=True)
+    chances_ref[slot] = chances
+    return product(chances.astype(jnp.bfloat16), values).astype(jnp.bfloat16)
+
+
+def attend_first(entry, mixed_mine, mixed_other):
+    length = entry.shape[0]
+    half = D // 2
+
+    def kernel(entry_ref, mine, other, heads, chances_ref, mix_ref):
+        def project(even, odd):
+            for part in range(3):
+                columns = slice(part * D, (part + 1) * D)
+                heads[:, columns] = (
+                    product(entry_ref[:, :half], even[:, columns])
+                    + product(entry_ref[:, half:], odd[:, columns])
+                ).astype(jnp.bfloat16)
+
+        in_order(mine, other, project)
+        for head in range(H // 2):
+            mix_ref[:, head * HD : (head + 1) * HD] = attend_head(heads, head, chances_ref, head)
+
+    return heavy(
+        kernel,
+        [
+            ((length, 3 * D), jnp.bfloat16),
+            ((H // 2, length, length), jnp.float32),
+            ((length, half), jnp.bfloat16),
+        ],
+        [],
+        entry,
+        mixed_mine,
+        mixed_other,
+    )
+
+
+def attend_second(heads, mix_first, mixed_mine, mixed_other, stream_zero, bias, gain, shift):
+    length = heads.shape[0]
+    half = D // 2
+
+    def kernel(
+        heads_ref,
+        first_ref,
+        mine,
+        other,
+        zero_ref,
+        bias_ref,
+        gain_ref,
+        shift_ref,
+        chances_ref,
+        stream,
+        value_ref,
+        mix_mine,
+        mix_other,
+        up_mine,
+        up_other,
+        mixed,
+        padded,
+    ):
+        padded[...] = jnp.zeros_like(padded)
+        mixed[:, :half] = first_ref[...]
+        for head in range(H // 2, H):
+            mixed[:, head * HD : (head + 1) * HD] = attend_head(
+                heads_ref, head, chances_ref, head - H // 2
+            )
+
+        def leave(even, odd):
+            stream[...] = (
+                zero_ref[...]
+                + (product(mixed[:, :half], even[...]) + product(mixed[:, half:], odd[...]))
+                + bias_ref[...]
+            )
+
+        in_order(mine, other, leave)
+        store_upright(mixed[...].astype(jnp.float32), padded, mix_mine, mix_other)
+        normed = normalize(stream[...])[0]
+        value = (normed * gain_ref[...] + shift_ref[...]).astype(jnp.bfloat16)
+        value_ref[...] = value
+        store_upright(value.astype(jnp.float32), padded, up_mine, up_other)
+
+    full = lambda shape: pl.BlockSpec(shape, lambda i: (0,) * len(shape))
+    shapes = (
+        ((H // 2, length, length), jnp.float32),
+        ((length, D), jnp.float32),
+        ((length, D), jnp.bfloat16),
+        ((half, PAD), jnp.bfloat16),
+        ((half, PAD), jnp.bfloat16),
+        ((half, PAD), jnp.bfloat16),
+        ((half, PAD), jnp.bfloat16),
+    )
+    return pl.pallas_call(
+        kernel,
+        grid=(1,),
+        in_specs=[
+            full((length, 3 * D)),
+            full((length, half)),
+            pl.BlockSpec((half, D), lambda i: (0, 3)),
+            pl.BlockSpec((half, D), lambda i: (0, 3)),
+            full((length, D)),
+            full((1, D)),
+            full((1, D)),
+            full((1, D)),
+        ],
+        out_specs=tuple(full(shape) for shape, _ in shapes),
+        out_shape=tuple(jax.ShapeDtypeStruct(shape, dtype) for shape, dtype in shapes),
+        scratch_shapes=[pltpu.VMEM((length, D), jnp.bfloat16), pltpu.VMEM((PAD, D), jnp.float32)],
+        compiler_params=PARAMS,
+        cost_estimate=LIGHT,
+    )(heads, mix_first, mixed_mine, mixed_other, stream_zero, bias, gain, shift)
+
+
+def expand_forward(entry, expand_mine, expand_other, bias):
+    length = entry.shape[0]
+    half = D // 2
+    tile = D
+    per = FF // 2 // tile
+
+    def kernel(
+        entry_ref, mine, other, bias_ref, active_ref, slope_ref, up_mine, up_other, padded, hidden
+    ):
+        step = pl.program_id(0)
+
+        @pl.when(step == 0)
+        def _():
+            padded[...] = jnp.zeros_like(padded)
+
+        def work(even, odd):
+            hidden[...] = (
+                product(entry_ref[:, :half], even[...]) + product(entry_ref[:, half:], odd[...])
+            ) + bias_ref[...]
+
+        in_order(mine, other, work)
+        value = hidden[...]
+        inside = 0.5 * (1.0 + lax.erf(value * (0.5**0.5)))
+        bell = jnp.exp(-0.5 * value * value) * (2.0 * jnp.pi) ** -0.5
+        active = (value * inside).astype(jnp.bfloat16)
+        slope_ref[...] = inside + value * bell
+        active_ref[...] = active
+        padded[:length] = active.astype(jnp.float32)
+        turned = padded[...].T.astype(jnp.bfloat16)
+        rows = pl.ds(pl.multiple_of(lax.rem(step, per) * tile, tile), tile)
+        core = lax.axis_index("wide") & 1
+
+        @pl.when(step // per == core)
+        def _():
+            up_mine[rows] = turned
+
+        @pl.when(step // per != core)
+        def _():
+            up_other[rows] = turned
+
+    whole = lambda i: (0, 0)
+    across = lambda i: (0, i)
+    return pl.pallas_call(
+        kernel,
+        grid=(FF // tile,),
+        in_specs=[
+            pl.BlockSpec((length, D), whole),
+            pl.BlockSpec((half, tile), across),
+            pl.BlockSpec((half, tile), across),
+            pl.BlockSpec((1, tile), across),
+        ],
+        out_specs=(
+            pl.BlockSpec((length, tile), across),
+            pl.BlockSpec((length, tile), across),
+            pl.BlockSpec((FF // 2, PAD), whole),
+            pl.BlockSpec((FF // 2, PAD), whole),
+        ),
+        out_shape=(
+            jax.ShapeDtypeStruct((length, FF), jnp.bfloat16),
+            jax.ShapeDtypeStruct((length, FF), jnp.float32),
+            jax.ShapeDtypeStruct((FF // 2, PAD), jnp.bfloat16),
+            jax.ShapeDtypeStruct((FF // 2, PAD), jnp.bfloat16),
+        ),
+        scratch_shapes=[
+            pltpu.VMEM((PAD, tile), jnp.float32),
+            pltpu.VMEM((length, tile), jnp.float32),
+        ],
+        compiler_params=PARAMS,
+        cost_estimate=LIGHT,
+    )(entry, expand_mine, expand_other, bias)
+
+
+def hidden_backward(pulled, shrink_mine, shrink_other, slope):
+    length = pulled.shape[0]
+    half = FF // 2
+
+    def kernel(pulled_ref, mine, other, slope_ref, low_ref, sum_ref):
+        core = lax.axis_index("wide") & 1
+        for weight, parity in ((mine, core), (other, 1 - core)):
+            for part in range(half // D):
+                columns = pl.ds(pl.multiple_of(parity * half + part * D, 128), D)
+                delta = (
+                    dot_rows(pulled_ref[...], weight[part * D : (part + 1) * D])
+                    * slope_ref[:, columns]
+                )
+                low_ref[:, columns] = delta.astype(jnp.bfloat16)
+                sum_ref[:, columns] = jnp.sum(delta, axis=0, keepdims=True)
+
+    return heavy(
+        kernel,
+        [((length, FF), jnp.bfloat16), ((1, FF), jnp.float32)],
+        [],
+        pulled,
+        shrink_mine,
+        shrink_other,
+        slope,
+    )
+
+
+def expand_backward(
+    hidden_low, expand_mine, expand_other, pulled, stream_one, gain, mixed_mine, mixed_other
+):
+    length = pulled.shape[0]
+    half = D // 2
+
+    def kernel(
+        hidden_ref,
+        mine,
+        other,
+        pulled_ref,
+        stream_ref,
+        gain_ref,
+        out_mine,
+        out_other,
+        one_ref,
+        low_ref,
+        sums,
+        mix_ref,
+        delta,
+    ):
+        def work(even, odd):
+            delta[:, :half] = dot_rows(hidden_ref[...], even[...])
+            delta[:, half:] = dot_rows(hidden_ref[...], odd[...])
+
+        in_order(mine, other, work)
+        normed, inverse = normalize(stream_ref[...])
+        value = delta[...]
+        one = pulled_ref[...].astype(jnp.float32) + norm_back(value * gain_ref[...], normed, inverse)
+        one_ref[...] = one
+        low_value = one.astype(jnp.bfloat16)
+        low_ref[...] = low_value
+        sums[0:1] = jnp.sum(one, axis=0, keepdims=True)
+        sums[1:2] = jnp.sum(value * normed, axis=0, keepdims=True)
+        sums[2:3] = jnp.sum(value, axis=0, keepdims=True)
+        sums[3:4] = jnp.sum(pulled_ref[...].astype(jnp.float32), axis=0, keepdims=True)
+
+        def back(even, odd):
+            mix_ref[:, :half] = dot_rows(low_value, even[...]).astype(jnp.bfloat16)
+            mix_ref[:, half:] = dot_rows(low_value, odd[...]).astype(jnp.bfloat16)
+
+        in_order(out_mine, out_other, back)
+
+    whole = lambda i: (0, 0)
+    last = lambda i: (0, 3)
+    return pl.pallas_call(
+        kernel,
+        grid=(1,),
+        in_specs=[
+            pl.BlockSpec((length, FF), whole),
+            pl.BlockSpec((half, FF), whole),
+            pl.BlockSpec((half, FF), whole),
+            pl.BlockSpec((length, D), whole),
+            pl.BlockSpec((length, D), whole),
+            pl.BlockSpec((1, D), whole),
+            pl.BlockSpec((half, D), last),
+            pl.BlockSpec((half, D), last),
+        ],
+        out_specs=(
+            pl.BlockSpec((length, D), whole),
+            pl.BlockSpec((length, D), whole),
+            pl.BlockSpec((4, D), whole),
+            pl.BlockSpec((length, D), whole),
+        ),
+        out_shape=(
+            jax.ShapeDtypeStruct((length, D), jnp.float32),
+            jax.ShapeDtypeStruct((length, D), jnp.bfloat16),
+            jax.ShapeDtypeStruct((4, D), jnp.float32),
+            jax.ShapeDtypeStruct((length, D), jnp.bfloat16),
+        ),
+        scratch_shapes=[pltpu.VMEM((length, D), jnp.float32)],
+        compiler_params=PARAMS,
+        cost_estimate=LIGHT,
+    )(hidden_low, expand_mine, expand_other, pulled, stream_one, gain, mixed_mine, mixed_other)
+
+
+def attend_backward(heads, chances_first, chances_second, delta_mixture):
+    length = heads.shape[0]
+    scale = HD ** (-0.5)
+
+    def kernel(heads_ref, first_ref, second_ref, delta_ref, mixed):
+        for head in range(H):
+            at = head * HD
+            queries = heads_ref[:, at : at + HD]
+            keys = heads_ref[:, D + at : D + at + HD]
+            values = heads_ref[:, 2 * D + at : 2 * D + at + HD]
+            delta = delta_ref[:, at : at + HD]
+            chances = (first_ref, second_ref)[head // (H // 2)][head % (H // 2)]
+            pull = dot_rows(delta, values)
+            inner_sum = jnp.sum(chances * pull, axis=-1, keepdims=True)
+            scores = (scale * (chances * (pull - inner_sum))).astype(jnp.bfloat16)
+            mixed[:, at : at + HD] = product(scores, keys).astype(jnp.bfloat16)
+            mixed[:, D + at : D + at + HD] = dot_depth(scores, queries).astype(jnp.bfloat16)
+            mixed[:, 2 * D + at : 2 * D + at + HD] = dot_depth(
+                chances.astype(jnp.bfloat16), delta
+            ).astype(jnp.bfloat16)
+
+    return heavy(
+        kernel,
+        [((length, 3 * D), jnp.bfloat16)],
+        [],
+        heads,
+        chances_first,
+        chances_second,
+        delta_mixture,
+    )[0]
+
+
+def entry_backward(delta_mixed, mixed_mine, mixed_other, delta_one, stream_zero, gain):
+    length = delta_mixed.shape[0]
+    half = D // 2
+
+    def kernel(mixed_ref, mine, other, one_ref, stream_ref, gain_ref, low_ref, sums, delta):
+        def work(even, odd):
+            delta[:, :half] = dot_rows(mixed_ref[...], even[...])
+            delta[:, half:] = dot_rows(mixed_ref[...], odd[...])
+
+        in_order(mine, other, work)
+        normed, inverse = normalize(stream_ref[...])
+        value = delta[...]
+        zero = one_ref[...] + norm_back(value * gain_ref[...], normed, inverse)
+        low_ref[...] = zero.astype(jnp.bfloat16)
+        sums[0:1] = jnp.sum(zero, axis=0, keepdims=True)
+        sums[1:2] = jnp.sum(value * normed, axis=0, keepdims=True)
+        sums[2:3] = jnp.sum(value, axis=0, keepdims=True)
+
+    whole = lambda i: (0, 0)
+    return pl.pallas_call(
+        kernel,
+        grid=(1,),
+        in_specs=[
+            pl.BlockSpec((length, 3 * D), whole),
+            pl.BlockSpec((half, 3 * D), whole),
+            pl.BlockSpec((half, 3 * D), whole),
+            pl.BlockSpec((length, D), whole),
+            pl.BlockSpec((length, D), whole),
+            pl.BlockSpec((1, D), whole),
+        ],
+        out_specs=(pl.BlockSpec((length, D), whole), pl.BlockSpec((3, D), whole)),
+        out_shape=(
+            jax.ShapeDtypeStruct((length, D), jnp.bfloat16),
+            jax.ShapeDtypeStruct((3, D), jnp.float32),
+        ),
+        scratch_shapes=[pltpu.VMEM((length, D), jnp.float32)],
+        compiler_params=PARAMS,
+        cost_estimate=LIGHT,
+    )(delta_mixed, mixed_mine, mixed_other, delta_one, stream_zero, gain)
+
+
+def joined_backward(zero_low, merge_mine, merge_other):
+    length = zero_low.shape[0]
+    width = 2 * D // 8
+
+    def kernel(zero_ref, mine, other, first_ref, second_ref):
+        def work(even, odd):
+            for parity, weight in enumerate((even, odd)):
+                delta = dot_rows(zero_ref[...], weight[...]).astype(jnp.bfloat16)
+                for number in range(4):
+                    target = (first_ref, second_ref)[number // 2]
+                    column = (2 * (number % 2) + parity) * width
+                    target[:, column : column + width] = delta[
+                        :, number * width : (number + 1) * width
+                    ]
+
+        in_order(mine, other, work)
+
+    out = ((length, D), jnp.bfloat16)
+    return heavy(kernel, [out, out], [], zero_low, merge_mine, merge_other)
+
+
+def shrink_forward(active, shrink_mine, shrink_other, stream_one, bias):
+    length = active.shape[0]
+    half = FF // 2
+    width = D // 8
+
+    def kernel(active_ref, mine, other, stream_ref, bias_ref, out_ref):
+        def work(even, odd):
+            total = (
+                stream_ref[...]
+                + (product(active_ref[:, :half], even[...]) + product(active_ref[:, half:], odd[...]))
+                + bias_ref[...]
+            ).astype(jnp.bfloat16)
+            for parity in range(2):
+                for number in range(4):
+                    column = (2 * number + parity) * width
+                    source = (4 * parity + number) * width
+                    out_ref[:, column : column + width] = total[:, source : source + width]
+
+        in_order(mine, other, work)
+
+    return heavy(
+        kernel,
+        [((length, D), jnp.bfloat16)],
+        [],
+        active,
+        shrink_mine,
+        shrink_other,
+        stream_one,
+        bias,
+    )[0]
+
+
+def on_device(
+    inputs,
+    skip_tokens,
+    cotangent,
+    merge_weight,
+    merge_moment,
+    merge_square,
+    attend_weight,
+    attend_moment,
+    attend_square,
+    output_weight,
+    output_moment,
+    output_square,
+    expand_weight,
+    expand_moment,
+    expand_square,
+    shrink_weight,
+    shrink_moment,
+    shrink_square,
+    vectors,
+    vector_moment,
+    vector_square,
+):
+    core, across, along, low_bit, high_bit = spot()
+    low = jnp.bfloat16
+    length = inputs.shape[1]
+    columns = attend_weight.shape[1]
+
+    merge_low = fold(merge_weight.astype(low))
+    vector_low = vectors.astype(low)
+    merge_far = swap_narrow(merge_low, 2)
+    vector_far = swap_narrow(vector_low, 2)
+    mixed_low = jnp.concatenate([attend_weight.astype(low), output_weight.astype(low)], axis=1)
+    merge_far, vector_far, mixed_low = together(merge_far, vector_far, mixed_low)
+    merge_near = swap_narrow(merge_low, 1), swap_narrow(merge_far, 1)
+    vector_near = swap_narrow(jnp.stack([vector_low, vector_far]), 1)
+    joined = inner(jnp.concatenate([inputs[0], skip_tokens[0]], axis=-1))
+    joined_mine, joined_other = halves_of(joined, core)
+    merge_near, vector_near, joined_mine, joined_other = together(
+        merge_near, vector_near, joined_mine, joined_other
+    )
+    merge_parts = arrange("merge", 2, merge_low, merge_far, *merge_near)
+    merge_first = both(merge_parts, 0)
+    merge_second = both(merge_parts, 1)
+    mixed_far = swap_narrow(mixed_low, 2)
+    pulled = inner(cotangent[0])
+    joined_up = upright(joined_mine)
+    joined_up_other = upright(joined_other)
+    merge_first, merge_second, mixed_far, joined_up, joined_up_other, pulled = together(
+        merge_first, merge_second, mixed_far, joined_up, joined_up_other, pulled
+    )
+    merge_third = both(merge_first, 1)
+    mixed_near = swap_narrow(mixed_low, 1), swap_narrow(mixed_far, 1)
+    pieces = unpack(gather_vector(vector_far, vector_near, vector_low).astype(jnp.float32))
+    pieces = tuple(inner(piece)[None] for piece in pieces)
+    expand_low = expand_weight.astype(low)
+    shrink_low = fold(shrink_weight.astype(low))
+    merge_third, mixed_near, pieces, expand_low, shrink_low = together(
+        merge_third, mixed_near, pieces, expand_low, shrink_low
+    )
+    skip_bias, gain_one, bias_one, output_bias, gain_two, bias_two, shrink_bias, expand_bias = pieces
+    mixed_parts = arrange("attend_output", 1, mixed_low, mixed_far, *mixed_near)
+    mixed_first = both(mixed_parts, 0)
+    expand_far = swap_narrow(expand_low, 2)
+    merge_mine = place(merge_parts, merge_first, merge_second, merge_third)
+    mixed_first, expand_far, merge_mine = together(mixed_first, expand_far, merge_mine)
+    mixed_second = both(mixed_parts, 1)
+    expand_near = swap_narrow(expand_low, 1), swap_narrow(expand_far, 1)
+    merge_other = swap_wide(merge_mine, CORE)
+    mixed_second, expand_near, merge_other = together(mixed_second, expand_near, merge_other)
+    mixed_third = both(mixed_first, 1)
+    shrink_far = swap_narrow(shrink_low, 2)
+    joined_sibling = swap_wide(joined_up_other, CORE)
+    stream_zero, attend_input, attend_up, attend_up_other = merge_forward(
+        joined_mine, joined_other, merge_mine, merge_other, skip_bias, gain_one, bias_one
+    )
+    expand_parts = arrange("expand", 1, expand_low, expand_far, *expand_near)
+    mixed_third, shrink_far, joined_sibling, stream_zero, attend_input, attend_up_other, expand_parts = (
+        together(
+            mixed_third,
+            shrink_far,
+            joined_sibling,
+            stream_zero,
+            attend_input,
+            attend_up_other,
+            expand_parts,
+        )
+    )
+    expand_first = both(expand_parts, 0)
+    shrink_near = swap_narrow(shrink_low, 1), swap_narrow(shrink_far, 1)
+    mixed_mine = place(mixed_parts, mixed_first, mixed_second, mixed_third)
+    expand_first, mixed_mine, shrink_near = together(expand_first, mixed_mine, shrink_near)
+    expand_second = both(expand_parts, 1)
+    mixed_other = swap_wide(mixed_mine, CORE)
+    attend_up_sibling = swap_wide(attend_up_other, CORE)
+    shrink_parts = arrange("shrink", 4, shrink_low, shrink_far, *shrink_near)
+    expand_second, mixed_other, attend_up_sibling, shrink_parts = together(
+        expand_second, mixed_other, attend_up_sibling, shrink_parts
+    )
+    expand_third = both(expand_first, 1)
+    heads, chances_first, mix_first = attend_first(attend_input, mixed_mine, mixed_other)
+    expand_third, heads, mix_first = together(expand_third, heads, mix_first)
+    shrink_first = both(shrink_parts, 0)
+    expand_mine = place(expand_parts, expand_first, expand_second, expand_third)
+    expand_other = swap_wide(expand_mine, CORE)
+    (
+        chances_second,
+        stream_one,
+        expand_input,
+        mixture_up,
+        mixture_up_other,
+        expand_up,
+        expand_up_other,
+    ) = attend_second(
+        heads, mix_first, mixed_mine, mixed_other, stream_zero, output_bias, gain_two, bias_two
+    )
+    shrink_first, expand_mine, expand_other, expand_input, mixture_up_other, expand_up_other = (
+        together(
+            shrink_first, expand_mine, expand_other, expand_input, mixture_up_other, expand_up_other
+        )
+    )
+    shrink_second = both(shrink_parts, 1)
+    pulled_sibling = swap_wide(pulled, CORE)
+    mixture_up_sibling = swap_wide(mixture_up_other, CORE)
+    active, slope, active_up, active_up_other = expand_forward(
+        expand_input, expand_mine, expand_other, expand_bias
+    )
+    shrink_second, pulled_sibling, mixture_up_sibling, active, slope, active_up, active_up_other = (
+        together(
+            shrink_second,
+            pulled_sibling,
+            mixture_up_sibling,
+            active,
+            slope,
+            active_up,
+            active_up_other,
+        )
+    )
+    shrink_third = both(shrink_first, 1)
+    expand_up_sibling = swap_wide(expand_up_other, CORE)
+    active_up_sibling = swap_wide(active_up_other, CORE)
+    shrink_blocks = pair_gradient([(active_up, active_up_sibling)], [(pulled, pulled_sibling)])
+    shrink_third, expand_up_sibling, shrink_blocks = together(
+        shrink_third, expand_up_sibling, shrink_blocks
+    )
+    shrink_far_got = send(shrink_blocks, SEND_FAR)
+    shrink_near_got = send(shrink_blocks, SEND_NEAR)
+    shrink_mine = place(shrink_parts, shrink_first, shrink_second, shrink_third)
+    shrink_other = swap_wide(shrink_mine, CORE)
+    hidden_low, hidden_sum = hidden_backward(pulled, shrink_mine, shrink_other, slope)
+    shrink_far_got, shrink_near_got, hidden_low, hidden_sum = together(
+        shrink_far_got, shrink_near_got, hidden_low, hidden_sum
+    )
+    shrink_got_last = forward(shrink_blocks, shrink_far_got)
+    hidden_sibling = swap_wide(hidden_low, CORE)
+    expand_blocks = pair_gradient([(expand_up, expand_up_sibling)], [(hidden_low, hidden_sibling)])
+    shrink_got_last, expand_blocks, hidden_low = together(shrink_got_last, expand_blocks, hidden_low)
+    expand_far_got = send(expand_blocks, SEND_FAR)
+    delta_one, stream_low, sums_two, delta_mixture = expand_backward(
+        hidden_low,
+        expand_mine,
+        expand_other,
+        pulled,
+        stream_one,
+        gain_two,
+        mixed_mine,
+        mixed_other,
+    )
+    expand_far_got, stream_low, delta_mixture = together(expand_far_got, stream_low, delta_mixture)
+    expand_near_got = send(expand_blocks, SEND_NEAR)
+    stream_sibling = swap_wide(stream_low, CORE)
+    delta_mixed = attend_backward(heads, chances_first, chances_second, delta_mixture)
+    expand_near_got, stream_sibling, delta_mixed = together(
+        expand_near_got, stream_sibling, delta_mixed
+    )
+    expand_got_last = forward(expand_blocks, expand_far_got)
+    mixed_sibling = swap_wide(delta_mixed, CORE)
+    shrink_quarters = settle("shrink", 4, shrink_blocks, shrink_near_got, shrink_got_last)
+    mixed_blocks = pair_gradient(
+        [(attend_up, attend_up_sibling), (mixture_up, mixture_up_sibling)],
+        [(delta_mixed, mixed_sibling), (stream_low, stream_sibling)],
+    )
+    expand_got_last, shrink_quarters, mixed_blocks, delta_mixed = together(
+        expand_got_last, shrink_quarters, mixed_blocks, delta_mixed
+    )
+    mixed_far_got = send(mixed_blocks, SEND_FAR)
+    shrink_got = narrow_first(shrink_quarters)
+    zero_low, sums_one = entry_backward(
+        delta_mixed, mixed_mine, mixed_other, delta_one, stream_zero, gain_one
+    )
+    mixed_far_got, shrink_got, zero_low, sums_one = together(
+        mixed_far_got, shrink_got, zero_low, sums_one
+    )
+    mixed_near_got = send(mixed_blocks, SEND_NEAR)
+    shrink_end = narrow_second(shrink_quarters, shrink_got)
+    zero_sibling = swap_wide(zero_low, CORE)
+    vector_total = jnp.concatenate(
+        [
+            outer(row)
+            for row in (
+                sums_one[0],
+                sums_one[1],
+                sums_one[2],
+                sums_two[0],
+                sums_two[1],
+                sums_two[2],
+                sums_two[3],
+                hidden_sum[0],
+            )
+        ]
+    )
+    expand_quarters = settle("expand", 1, expand_blocks, expand_near_got, expand_got_last)
+    mixed_near_got, shrink_end, zero_sibling, vector_total, expand_quarters = together(
+        mixed_near_got, shrink_end, zero_sibling, vector_total, expand_quarters
+    )
+    mixed_got_last = forward(mixed_blocks, mixed_far_got)
+    expand_got = narrow_first(expand_quarters)
+    vector_total = vector_total + swap_wide(vector_total, CORE)
+    merge_blocks = pair_gradient([(joined_up, joined_sibling)], [(zero_low, zero_sibling)])
+    mixed_got_last, expand_got, vector_total, merge_blocks = together(
+        mixed_got_last, expand_got, vector_total, merge_blocks
+    )
+    merge_far_got = send(merge_blocks, SEND_FAR)
+    merge_near_got = send(merge_blocks, SEND_NEAR)
+    expand_end = narrow_second(expand_quarters, expand_got)
+    mixed_quarters = settle("attend_output", 1, mixed_blocks, mixed_near_got, mixed_got_last)
+    outputs = shrink_forward(active, shrink_mine, shrink_other, stream_one, shrink_bias)[None]
+    merge_far_got, merge_near_got, expand_end, mixed_quarters, outputs = together(
+        merge_far_got, merge_near_got, expand_end, mixed_quarters, outputs
+    )
+    merge_got_last = forward(merge_blocks, merge_far_got)
+    mixed_got = narrow_first(mixed_quarters)
+    vector_total = vector_total + swap_wide(vector_total, ACROSS)
+    input_gradient, skip_gradient = joined_backward(zero_low, merge_mine, merge_other)
+    shrink_new = adamw_update(
+        shrink_weight,
+        shrink_moment,
+        shrink_square,
+        unfold(finish(shrink_quarters, shrink_got, shrink_end), shrink_weight.shape[0]),
+        rate_shrink,
+    )
+    merge_got_last, mixed_got, vector_total, input_gradient, skip_gradient, shrink_new = together(
+        merge_got_last, mixed_got, vector_total, input_gradient, skip_gradient, shrink_new
+    )
+    merge_quarters = settle("merge", 2, merge_blocks, merge_near_got, merge_got_last)
+    merge_got = narrow_first(merge_quarters)
+    mixed_end = narrow_second(mixed_quarters, mixed_got)
+    vector_total = vector_total + swap_wide(vector_total, ALONG)
+    expand_new = adamw_update(
+        expand_weight,
+        expand_moment,
+        expand_square,
+        finish(expand_quarters, expand_got, expand_end),
+        rate_expand,
+    )
+    merge_got, mixed_end, vector_total, expand_new = together(
+        merge_got, mixed_end, vector_total, expand_new
+    )
+    merge_end = narrow_second(merge_quarters, merge_got)
+    halves = vector_total.reshape(2, -1)
+    vector_total = pick(halves, high_bit) + swap_narrow(pick(halves, 1 - high_bit), 2)
+    halves = vector_total.reshape(2, -1)
+    vector_total = pick(halves, low_bit) + swap_narrow(pick(halves, 1 - low_bit), 1)
+    mixed_total = finish(mixed_quarters, mixed_got, mixed_end)
+    attend_new = adamw_update(
+        attend_weight, attend_moment, attend_square, mixed_total[:, :columns], rate_attend
+    )
+    output_new = adamw_update(
+        output_weight, output_moment, output_square, mixed_total[:, columns:], rate_output
+    )
+    merge_new = adamw_update(
+        merge_weight,
+        merge_moment,
+        merge_square,
+        unfold(finish(merge_quarters, merge_got, merge_end), merge_weight.shape[0]),
+        rate_merge,
+    )
+    vector_new = adamw_update(vectors, vector_moment, vector_square, vector_total, rate_vector)
+    return (
+        outputs,
+        input_gradient[None],
+        skip_gradient[None],
+        *merge_new,
+        *attend_new,
+        *output_new,
+        *expand_new,
+        *shrink_new,
+        *vector_new,
+    )
+
+
 def solution(mesh):
     in_specs = (
         P(("wide", "narrow"), None, None),
@@ -334,6 +1461,7 @@
         P("narrow"),
         P("narrow"),
     )
+    tuned = mesh.shape["wide"] == 8 and mesh.shape["narrow"] == 4
     return jax.shard_map(
-        on_device, mesh=mesh, in_specs=in_specs, out_specs=out_specs, check_vma=False
-    )
+        on_device if tuned else general_device, mesh=mesh, in_specs=in_specs, out_specs=out_specs, check_vma=False
+    )

time: 1200 us -> 519 us (0.43)
  waiting for transfers between devices: 799 us -> 141 us
  Pallas kernels: 0 us -> 213 us
  matrix products: 164 us -> 0 us
  blocking collectives: 140 us -> 0 us
  starting transfers between devices: 1.13 us -> 80.2 us
  between operations: 16.3 us -> 2 us
    reduce_scatter x6 -> x0, waiting for transfers between devices: 471 us -> none  [the longest x1 137 us: on_device(): lax.psum_scatter(shrink_gradient, 'wide', scatter_dimension=0, tiled=True)]
    pallas_call x0 -> x26, Pallas kernels: none -> 213 us  [the longest x6 64.2 us: heavy(): pl.pallas_call(kernel, out_shape=tuple((jax.ShapeDtypeStruct(shape, dtype...]
    all_gather x7 -> x0, waiting for transfers between devices: 203 us -> none  [the longest x1 62.3 us: on_device(): lax.all_gather(columns[3], 'wide', axis=0, tiled=True)]
    dot_general x21 -> x0, matrix products: 164 us -> none  [the longest x5 47.2 us: weight_gradient(): lax.dot_general(flat_left, flat_right, (((0,), (0,)), ((), ())), preferre...]
    ppermute x0 -> x93, waiting for transfers between devices: none -> 141 us  [the longest x65 73.9 us: swap_wide(): return lax.ppermute(value, 'wide', [(i, i ^ bit) for i in range(8)])]
    unnamed x21 -> x0, waiting for transfers between devices: 125 us -> none
    ppermute x0 -> x93, starting transfers between devices: none -> 80.2 us  [the longest x65 53.5 us: swap_wide(): return lax.ppermute(value, 'wide', [(i, i ^ bit) for i in range(8)])]
    all_gather x3 -> x0, blocking collectives: 78.3 us -> none  [the longest x1 32.1 us: on_device(): lax.all_gather(merge_low, 'narrow', axis=1, tiled=True)]
  transfers between devices with their start and end apart: 17 -> 93, of which waited for: 14 -> 35; matrix products, arithmetic and copies ran while one was open for 17% -> 10% of each run, Pallas kernels for 0% -> 39%
where the time goes in v2:
time: 519 us; the launch traced here: 511 us
  Pallas kernels  213 us (41%)
  waiting for transfers between devices  141 us (27%)
  starting transfers between devices  80.2 us (15%)
  local copies, waits for them, and re-layouts  46.8 us (9%)
  other arithmetic  27.6 us (5%)
    ppermute x65, waiting for transfers between devices, swap_wide(): return lax.ppermute(value, 'wide', [(i, i ^ bit) for i in range(8)])  73.9 us
    ppermute x28, waiting for transfers between devices, swap_narrow(): return lax.ppermute(value, 'narrow', [(i, i ^ bit) for i in range(4)])  67.1 us
    pallas_call x6, Pallas kernels, heavy(): pl.pallas_call(kernel, out_shape=tuple((jax.ShapeDtypeStruct(shape, dtype...  64.2 us
    ppermute x65, starting transfers between devices, swap_wide(): return lax.ppermute(value, 'wide', [(i, i ^ bit) for i in range(8)])  53.5 us
    pallas_call x4, Pallas kernels, pair_gradient(): pl.pallas_call(kernel, grid=(sum(steps),), in_specs=in_specs, out_specs=(...  44.3 us
    ppermute x28, starting transfers between devices, swap_narrow(): return lax.ppermute(value, 'narrow', [(i, i ^ bit) for i in range(4)])  26.6 us
    unnamed x218, local copies, waits for them, and re-layouts  25 us
    pallas_call x4, Pallas kernels, unarrange(): pl.pallas_call(kernel, out_shape=(shape,) * 4, scratch_shapes=[pltpu.VMEM...  21.1 us
  transfers between devices with their start and end apart: 93, of which 35 were waited for; matrix products, arithmetic and copies ran while one was open for 10% of the time, Pallas kernels for 39%

profile of v2, /device:TPU:0, one launch (start us, length us, event | category | flops | bytes accessed | tf_op | source)
XLA Modules:
  0.0 510.6 jit_solution(8955608170350586939)
XLA Ops:
  2.6 4.0 collective-permute-start
  22.4 2.0 concatenate.69.shard_ref
  24.4 2.3 concatenate.59.refs_2_.pulled_ref
  27.4 2.7 collective-permute-start.9
  30.1 2.5 shard_map.364
  39.9 3.5 collective-permute-done.9.far_ref
  43.6 5.8 %collective-permute-done.6.bottom_y = bf16[144,1152]{1,0:T(8,128)(2,1)} collective-permute-done((bf16[144,1152]{1,0:T(8,128)(2,1)}, bf16[144,1152]{1,0:T(8,128)(2,1)}, u32[]{:S(2)}, u32[]{:S(2)}) %collective-permute-start.6) | collective-permute-done | bytes 331808 | tf_op jit(solution)/shard_map/ppermute | solution.py:302
  58.3 1.9 collective-permute-done.13.near_far_ref
  61.0 3.3 shard_map.365
  67.7 3.4 shard_map.366.mine
  71.1 12.2 %collective-permute-done.16.far_ref = bf16[144,1152]{1,0:T(8,128)(2,1)S(1)} collective-permute-done((bf16[144,1152]{1,0:T(8,128)(2,1)S(1)}, bf16[144,1152]{1,0:T(8,128)(2,1)S(1)}, u32[]{:S(2)}, u32[]{:S(2)}) %collective-permute-start.16) | collective-permute-done | bytes 331808 | tf_op jit(solution)/shard_map/ppermute | solution.py:306
  85.5 9.4 %collective-permute-done.23.near_ref = bf16[144,1152]{1,0:T(8,128)(2,1)S(1)} collective-permute-done((bf16[144,1152]{1,0:T(8,128)(2,1)S(1)}, bf16[144,1152]{1,0:T(8,128)(2,1)S(1)}, u32[]{:S(2)}, u32[]{:S(2)}) %collective-permute-start.23) | collective-permute-done | bytes 331808 | tf_op jit(solution)/shard_map/ppermute | solution.py:306
  95.7 3.6 collective-permute-done.22.bottom_x
  99.4 3.3 collective-permute-done.21.top_y
  104.2 4.1 collective-permute-done.24.near_far_ref
  109.0 2.3 copy.45.left
  112.4 3.7 shard_map.368
  116.1 7.5 %shard_map.367 = (f32[258,1152]{1,0:T(8,128)}, bf16[258,1152]{1,0:T(8,128)(2,1)}, bf16[576,384]{1,0:T(8,128)(2,1)}, bf16[576,384]{1,0:T(8,128)(2,1)}) custom-call(bf16[258,1152]{1,0:T(8,128)(2,1)} %copy.45.left, bf16[258,1152]{1,0:T(8,128)(2,1)} %copy.46.right, bf16[1152,1152]{1,0:T(8,128)(2,1)} %shard_map.366.mine, bf16[1152,1152]{1,0:T(8,128)(2,1)} %copy-done.3, ...), custom_call_target="tpu_custom_call" | custom-call | bytes 1024 | tf_op jit(solution)/shard_map/pallas_call | solution.py:634
  127.9 2.0 collective-permute-start.31
  129.9 5.1 %shard_map.369.mine.out_mine = bf16[576,4608]{1,0:T(8,128)(2,1)} custom-call(bf16[80,4608]{1,0:T(8,128)(2,1)} %get-tuple-element.304.top, bf16[64,4608]{1,0:T(8,128)(2,1)} %get-tuple-element.305.bottom, bf16[80,4608]{1,0:T(8,128)(2,1)} %collective-permute-done.14.top_x, bf16[64,4608]{1,0:T(8,128)(2,1)} %collective-permute-done.15.bottom_y, ...), custom_call_target="tpu_custom_call" | custom-call | bytes 1024 | tf_op jit(solution)/shard_map/pallas_call | solution.py:405
  135.1 3.8 collective-permute-done.30.near_ref
  138.8 5.5 %collective-permute-done.31.near_far_ref = bf16[144,1152]{1,0:T(8,128)(2,1)S(1)} collective-permute-done((bf16[144,1152]{1,0:T(8,128)(2,1)}, bf16[144,1152]{1,0:T(8,128)(2,1)S(1)}, u32[]{:S(2)}, u32[]{:S(2)}) %collective-permute-start.31) | collective-permute-done | bytes 331808 | tf_op jit(solution)/shard_map/ppermute | solution.py:306
  149.9 3.5 collective-permute-done.33.refs_1_
  154.9 3.3 shard_map.370
  158.1 6.9 %collective-permute-done.27.bottom_x = bf16[64,4608]{1,0:T(8,128)(2,1)} collective-permute-done((bf16[64,4608]{1,0:T(8,128)(2,1)}, bf16[64,4608]{1,0:T(8,128)(2,1)}, u32[]{:S(2)}, u32[]{:S(2)}) %collective-permute-start.27) | collective-permute-done | bytes 589856 | tf_op jit(solution)/shard_map/ppermute | solution.py:302
  165.8 2.4 copy-done
  168.2 14.8 %shard_map.371 = (bf16[258,3456]{1,0:T(8,128)(2,1)}, f32[8,258,258]{2,1,0:T(8,128)}, bf16[258,576]{1,0:T(8,128)(2,1)}) custom-call(bf16[258,1152]{1,0:T(8,128)(2,1)} %get-tuple-element.347.entry_ref, bf16[576,4608]{1,0:T(8,128)(2,1)} %shard_map.369.mine.out_mine, bf16[576,4608]{1,0:T(8,128)(2,1)} %copy-done), custom_call_target="tpu_custom_call" | custom-call | bytes 1024 | tf_op jit(solution)/shard_map/pallas_call | solution.py:634
  184.0 5.3 %shard_map.372.mine = bf16[576,4608]{1,0:T(8,128)(2,1)} custom-call(bf16[80,4608]{1,0:T(8,128)(2,1)} %get-tuple-element.328.top, bf16[64,4608]{1,0:T(8,128)(2,1)} %get-tuple-element.329.bottom, bf16[80,4608]{1,0:T(8,128)(2,1)} %copy-done.35, bf16[64,4608]{1,0:T(8,128)(2,1)} %copy-done.59, bf16[80,4608]{1,0:T(8,128)(2,1)} %copy-done.36, ...), custom_call_target="tpu_custom_call" | custom-call | bytes 1024 | tf_op jit(solution)/shard_map/pallas_call | solution.py:405
  193.4 13.7 %collective-permute-done.34.top_x = bf16[288,1152]{1,0:T(8,128)(2,1)S(1)} collective-permute-done((bf16[288,1152]{1,0:T(8,128)(2,1)S(1)}, bf16[288,1152]{1,0:T(8,128)(2,1)S(1)}, u32[]{:S(2)}, u32[]{:S(2)}) %collective-permute-start.34) | collective-permute-done | bytes 663584 | tf_op jit(solution)/shard_map/ppermute | solution.py:302
  207.1 13.7 %shard_map.373 = (f32[8,258,258]{2,1,0:T(8,128)}, f32[258,1152]{1,0:T(8,128)}, bf16[258,1152]{1,0:T(8,128)(2,1)}, bf16[576,384]{1,0:T(8,128)(2,1)}, bf16[576,384...) custom-call(bf16[258,3456]{1,0:T(8,128)(2,1)} %get-tuple-element.353.heads_ref, ...), custom_call_target="tpu_custom_call" | custom-call | bytes 1024 | tf_op jit(solution)/shard_map/pallas_call | solution.py:804
  221.1 2.0 copy-done.2
  223.1 13.7 %shard_map.374 = (bf16[258,4608]{1,0:T(8,128)(2,1)}, f32[258,4608]{1,0:T(8,128)}, bf16[2304,384]{1,0:T(8,128)(2,1)}, bf16[2304,384]{1,0:T(8,128)(2,1)}) custom-call(bf16[258,1152]{1,0:T(8,128)(2,1)} %get-tuple-element.367.entry_ref, bf16[576,4608]{1,0:T(8,128)(2,1)} %shard_map.372.mine, bf16[576,4608]{1,0:T(8,128)(2,1)} %copy-done.2, ...), custom_call_target="tpu_custom_call" | custom-call | bytes 1024 | tf_op jit(solution)/shard_map/pallas_call | solution.py:867
  242.0 12.2 %shard_map.375 = (bf16[288,1152]{1,0:T(8,128)(2,1)}, bf16[288,1152]{1,0:T(8,128)(2,1)}, bf16[288,1152]{1,0:T(8,128)(2,1)}, bf16[288,1152]{1,0:T(8,128)(2,1)}, bf...) custom-call(bf16[2304,384]{1,0:T(8,128)(2,1)} %get-tuple-element.375, ...), custom_call_target="tpu_custom_call" | custom-call | bytes 1024 | tf_op jit(solution)/shard_map/pallas_call | solution.py:482
  256.2 5.2 %shard_map.376.mine = bf16[2304,1152]{1,0:T(8,128)(2,1)} custom-call(bf16[288,1152]{1,0:T(8,128)(2,1)} %get-tuple-element.341.top, bf16[288,1152]{1,0:T(8,128)(2,1)} %get-tuple-element.342.bottom, bf16[288,1152]{1,0:T(8,128)(2,1)} %copy-done.46, bf16[288,1152]{1,0:T(8,128)(2,1)} %collective-permute-done.35.bottom_y, ...), custom_call_target="tpu_custom_call" | custom-call | bytes 1024 | tf_op jit(solution)/shard_map/pallas_call | solution.py:405
  265.5 4.8 collective-permute-done.51.other
  270.3 2.3 copy-done.1
  272.7 10.9 %shard_map.377 = (bf16[258,4608]{1,0:T(8,128)(2,1)}, f32[1,4608]{1,0:T(1,128)}) custom-call(bf16[258,1152]{1,0:T(8,128)(2,1)} %concatenate.59.refs_2_.pulled_ref, bf16[2304,1152]{1,0:T(8,128)(2,1)} %shard_map.376.mine, bf16[2304,1152]{1,0:T(8,128)(2,1)} %copy-done.1, f32[258,4608]{1,0:T(8,128)} %get-tuple-element.395.slope_ref), custom_call_target="tpu_custom_call" | custom-call | bytes 1024 | tf_op jit(solution)/shard_map/pallas_call | solution.py:634
  283.6 9.5 %collective-permute-done.49.refs_1_ = bf16[288,1152]{1,0:T(8,128)(2,1)S(1)} collective-permute-done((bf16[288,1152]{1,0:T(8,128)(2,1)}, bf16[288,1152]{1,0:T(8,128)(2,1)S(1)}, u32[]{:S(2)}, u32[]{:S(2)}) %collective-permute-start.49) | collective-permute-done | bytes 663584 | tf_op jit(solution)/shard_map/ppermute | solution.py:302
  296.3 2.2 collective-permute-done.54.refs_3_
  299.9 11.6 %shard_map.378 = (bf16[80,4608]{1,0:T(8,128)(2,1)}, bf16[80,4608]{1,0:T(8,128)(2,1)}, bf16[80,4608]{1,0:T(8,128)(2,1)}, bf16[80,4608]{1,0:T(8,128)(2,1)}, bf16[6...) custom-call(bf16[576,384]{1,0:T(8,128)(2,1)} %get-tuple-element.401.refs_0_,, ...), custom_call_target="tpu_custom_call" | custom-call | bytes 1024 | tf_op jit(solution)/shard_map/pallas_call | solution.py:482
  315.4 14.5 %shard_map.379 = (f32[258,1152]{1,0:T(8,128)}, bf16[258,1152]{1,0:T(8,128)(2,1)}, f32[4,1152]{1,0:T(4,128)}, bf16[258,1152]{1,0:T(8,128)(2,1)}) custom-call(bf16[258,4608]{1,0:T(8,128)(2,1)} %get-tuple-element.415.refs_2_.hidden_ref, bf16[576,4608]{1,0:T(8,128)(2,1)} %shard_map.372.mine, bf16[576,4608]{1,0:T(8,128)(2,1)} %copy-done.2, ...), custom_call_target="tpu_custom_call" | custom-call | bytes 1024 | tf_op jit(solution)/shard_map/pallas_call | solution.py:969
  329.9 2.3 collective-permute-done.55
  332.9 15.4 %shard_map.381.refs_4_.mixed_ref = bf16[258,3456]{1,0:T(8,128)(2,1)} custom-call(bf16[258,3456]{1,0:T(8,128)(2,1)} %get-tuple-element.353.heads_ref, f32[8,258,258]{2,1,0:T(8,128)} %get-tuple-element.439.first_ref, f32[8,258,258]{2,1,0:T(8,128)} %get-tuple-element.440.second_ref, bf16[258,1152]{1,0:T(8,128)(2,1)} %get-tuple-element.441.delta_ref), custom_call_target="tpu_custom_call" | custom-call | bytes 1024 | tf_op jit(solution)/shard_map/pallas_call | solution.py:634
  351.7 5.4 %shard_map.380 = (bf16[144,1152]{1,0:T(8,128)(2,1)}, bf16[144,1152]{1,0:T(8,128)(2,1)}, bf16[144,1152]{1,0:T(8,128)(2,1)}, bf16[144,1152]{1,0:T(8,128)(2,1)}) custom-call(bf16[288,1152]{1,0:T(8,128)(2,1)} %get-tuple-element.422.refs_0_, bf16[288,1152]{1,0:T(8,128)(2,1)} %copy-done.42, bf16[288,1152]{1,0:T(8,128)(2,1)} %copy-done.47, ...), custom_call_target="tpu_custom_call" | custom-call | bytes 1024 | tf_op jit(solution)/shard_map/pallas_call | solution.py:533
  358.4 12.4 %shard_map.382 = (bf16[80,4608]{1,0:T(8,128)(2,1)}, bf16[80,4608]{1,0:T(8,128)(2,1)}, bf16[80,4608]{1,0:T(8,128)(2,1)}, bf16[80,4608]{1,0:T(8,128)(2,1)}, bf16[6...) custom-call(bf16[576,384]{1,0:T(8,128)(2,1)} %get-tuple-element.432.refs_0_,, ...), custom_call_target="tpu_custom_call" | custom-call | bytes 1024 | tf_op jit(solution)/shard_map/pallas_call | solution.py:482
  377.1 9.7 %shard_map.383 = (bf16[258,1152]{1,0:T(8,128)(2,1)}, f32[3,1152]{1,0:T(4,128)}) custom-call(bf16[258,3456]{1,0:T(8,128)(2,1)} %shard_map.381.refs_4_.mixed_ref, bf16[576,4608]{1,0:T(8,128)(2,1)} %shard_map.369.mine.out_mine, bf16[576,4608]{1,0:T(8,128)(2,1)} %copy-done, f32[258,1152]{1,0:T(8,128)} %get-tuple-element.458.one_ref, ...), custom_call_target="tpu_custom_call" | custom-call | bytes 1024 | tf_op jit(solution)/shard_map/pallas_call | solution.py:1051
  386.9 4.9 shard_map.384
  396.6 9.0 %collective-permute-done.70.refs_4_ = bf16[64,4608]{1,0:T(8,128)(2,1)} collective-permute-done((bf16[64,4608]{1,0:T(8,128)(2,1)S(1)}, bf16[64,4608]{1,0:T(8,128)(2,1)}, u32[]{:S(2)}, u32[]{:S(2)}) %collective-permute-start.70) | collective-permute-done | bytes 589856 | tf_op jit(solution)/shard_map/ppermute | solution.py:302
  406.4 2.6 collective-permute-done.71
  409.0 2.0 collective-permute-start.74
  411.7 9.4 %shard_map.387 = bf16[258,1152]{1,0:T(8,128)(2,1)} custom-call(bf16[258,4608]{1,0:T(8,128)(2,1)} %get-tuple-element.512.active_ref, bf16[2304,1152]{1,0:T(8,128)(2,1)} %shard_map.376.mine, bf16[2304,1152]{1,0:T(8,128)(2,1)} %copy-done.1, f32[258,1152]{1,0:T(8,128)} %get-tuple-element.416.stream_ref, f32[1,1152]{1,0:T(1,128)} %broadcast_in_dim.39.bias_ref), custom_call_target="tpu_custom_call" | custom-call | bytes 1024 | tf_op jit(solution)/shard_map/pallas_call | solution.py:634
  421.1 6.2 %shard_map.388 = (bf16[258,1152]{1,0:T(8,128)(2,1)}, bf16[258,1152]{1,0:T(8,128)(2,1)}) custom-call(bf16[258,1152]{1,0:T(8,128)(2,1)} %get-tuple-element.468.refs_2_.zero_ref, bf16[1152,1152]{1,0:T(8,128)(2,1)} %shard_map.366.mine, bf16[1152,1152]{1,0:T(8,128)(2,1)} %copy-done.3), custom_call_target="tpu_custom_call" | custom-call | bytes 1024 | tf_op jit(solution)/shard_map/pallas_call | solution.py:634
  427.3 8.1 %shard_map.385 = (bf16[144,1152]{1,0:T(8,128)(2,1)}, bf16[144,1152]{1,0:T(8,128)(2,1)}, bf16[144,1152]{1,0:T(8,128)(2,1)}, bf16[144,1152]{1,0:T(8,128)(2,1)}, bf...) custom-call(bf16[1152,384]{1,0:T(8,128)(2,1)} %pad_bitcast_fusion.1., ...), custom_call_target="tpu_custom_call" | custom-call | bytes 1024 | tf_op jit(solution)/shard_map/pallas_call | solution.py:482
  442.1 6.9 %shard_map.386 = (bf16[144,1152]{1,0:T(8,128)(2,1)}, bf16[144,1152]{1,0:T(8,128)(2,1)}, bf16[144,1152]{1,0:T(8,128)(2,1)}, bf16[144,1152]{1,0:T(8,128)(2,1)}) custom-call(bf16[80,4608]{1,0:T(8,128)(2,1)} %get-tuple-element.502.refs_0_, bf16[80,4608]{1,0:T(8,128)(2,1)} %copy-done.28, bf16[80,4608]{1,0:T(8,128)(2,1)} %collective-permute-done.67.refs_2_, ...), custom_call_target="tpu_custom_call" | custom-call | bytes 1024 | tf_op jit(solution)/shard_map/pallas_call | solution.py:533
  449.0 5.2 %collective-permute-done.80 = bf16[144,1152]{1,0:T(8,128)(2,1)S(1)} collective-permute-done((bf16[144,1152]{1,0:T(8,128)(2,1)S(1)}, bf16[144,1152]{1,0:T(8,128)(2,1)S(1)}, u32[]{:S(2)}, u32[]{:S(2)}) %collective-permute-start.80) | collective-permute-done | bytes 331808 | tf_op jit(solution)/shard_map/ppermute | solution.py:306
  462.6 2.9 collective-permute-done.82.refs_5_
  465.9 3.2 collective-permute-done.83
  469.0 5.3 %collective-permute-done.84 = bf16[144,1152]{1,0:T(8,128)(2,1)S(1)} collective-permute-done((bf16[144,1152]{1,0:T(8,128)(2,1)S(1)}, bf16[144,1152]{1,0:T(8,128)(2,1)S(1)}, u32[]{:S(2)}, u32[]{:S(2)}) %collective-permute-start.84) | collective-permute-done | bytes 331808 | tf_op jit(solution)/shard_map/ppermute | solution.py:306
  477.0 3.8 shard_map.389
  482.8 2.7 multiply_subtract_fusion.1
  490.0 3.7 collective-permute-done.86
  493.7 2.0 collective-permute-done.87
  497.6 2.9 collective-permute-start.90
  504.6 2.6 collective-permute-done.92
  (451 shorter events, 133.2 us)
Async XLA Ops:
  2.6 16.1 %collective-permute-start = (bf16[144,576]{1,0:T(8,128)(2,1)}, bf16[144,576]{1,0:T(8,128)(2,1)}, u32[]{:S(2)}, u32[]{:S(2)}) collective-permute-start(bf16[144,576]{1,0:T(8,128)(2,1)} %pad_maximum_fusion.5.shard_ref), channel_id=1, source_target_pairs={{0,2},{1,3},{2,0},{3,1},{4,6},{5,7},{6,4},{7,5},{8,10},{9,11},{10,... | collective-permute-start | bytes 497672 | tf_op jit(solution)/shard_map/ppermute | solution.py:306
  6.6 23.4 %collective-permute-start.2 = (bf16[144,576]{1,0:T(8,128)(2,1)}, bf16[144,576]{1,0:T(8,128)(2,1)}, u32[]{:S(2)}, u32[]{:S(2)}) collective-permute-start(bf16[144,576]{1,0:T(8,128)(2,1)} %pad_maximum_fusion.5.shard_ref), channel_id=1, source_target_pairs={{0,1},{1,0},{2,3},{3,2},{4,5},{5,4},{6,7},{7,6},{8,9},{9,8},{10,11... | collective-permute-start | bytes 497672 | tf_op jit(solution)/shard_map/ppermute | solution.py:306
  27.4 16.1 %collective-permute-start.9 = (bf16[144,1152]{1,0:T(8,128)(2,1)S(1)}, bf16[144,1152]{1,0:T(8,128)(2,1)S(1)}, u32[]{:S(2)}, u32[]{:S(2)}) collective-permute-start(bf16[144,1152]{1,0:T(8,128)(2,1)S(1)} %copy-done.21), channel_id=1, source_target_pairs={{0,2},{1,3},{2,0},{3,1},{4,6},{5,7},{6,4},{7,5},{8,10},{9,11},{10,... | collective-permute-start | bytes 995336 | tf_op jit(solution)/shard_map/ppermute | solution.py:306
  34.1 15.3 %collective-permute-start.7 = (bf16[144,1152]{1,0:T(8,128)(2,1)}, bf16[144,1152]{1,0:T(8,128)(2,1)}, u32[]{:S(2)}, u32[]{:S(2)}) collective-permute-start(bf16[144,1152]{1,0:T(8,128)(2,1)} %get-tuple-element.294.top), channel_id=1, source_target_pairs={{0,16},{4,20},{8,24},{12,28},{16,0},{20,4},{24,8},{28,12},{1,17},{... | collective-permute-start | bytes 995336 | tf_op jit(solution)/shard_map/ppermute | solution.py:302
  64.3 19.0 %collective-permute-start.14 = (bf16[80,4608]{1,0:T(8,128)(2,1)}, bf16[80,4608]{1,0:T(8,128)(2,1)}, u32[]{:S(2)}, u32[]{:S(2)}) collective-permute-start(bf16[80,4608]{1,0:T(8,128)(2,1)} %get-tuple-element.304.top), channel_id=1, source_target_pairs={{0,8},{4,12},{8,0},{12,4},{16,24},{20,28},{24,16},{28,20},{1,9},{5... | collective-permute-start | bytes 2211848 | tf_op jit(solution)/shard_map/ppermute | solution.py:302
  65.8 17.5 %collective-permute-start.15 = (bf16[64,4608]{1,0:T(8,128)(2,1)}, bf16[64,4608]{1,0:T(8,128)(2,1)}, u32[]{:S(2)}, u32[]{:S(2)}) collective-permute-start(bf16[64,4608]{1,0:T(8,128)(2,1)} %get-tuple-element.305.bottom), channel_id=1, source_target_pairs={{0,16},{4,20},{8,24},{12,28},{16,0},{20,4},{24,8},{28,12},{1,17},{... | collective-permute-start | bytes 1769480 | tf_op jit(solution)/shard_map/ppermute | solution.py:302
  67.3 16.0 %collective-permute-start.16 = (bf16[144,1152]{1,0:T(8,128)(2,1)S(1)}, bf16[144,1152]{1,0:T(8,128)(2,1)S(1)}, u32[]{:S(2)}, u32[]{:S(2)}) collective-permute-start(bf16[144,1152]{1,0:T(8,128)(2,1)S(1)} %copy-done.19), channel_id=1, source_target_pairs={{0,2},{1,3},{2,0},{3,1},{4,6},{5,7},{6,4},{7,5},{8,10},{9,11},{10,... | collective-permute-start | bytes 995336 | tf_op jit(solution)/shard_map/ppermute | solution.py:306
  83.3 29.1 %collective-permute-start.25 = (bf16[1152,1152]{1,0:T(8,128)(2,1)}, bf16[1152,1152]{1,0:T(8,128)(2,1)S(1)}, u32[]{:S(2)}, u32[]{:S(2)}) collective-permute-start(bf16[1152,1152]{1,0:T(8,128)(2,1)} %shard_map.366.mine), channel_id=1, source_target_pairs={{0,4},{4,0},{8,12},{12,8},{16,20},{20,16},{24,28},{28,24},{1,5},{5... | collective-permute-start | bytes 7962632 | tf_op jit(solution)/shard_map/ppermute | solution.py:302
  83.4 19.4 %collective-permute-start.21 = (bf16[80,4608]{1,0:T(8,128)(2,1)S(1)}, bf16[80,4608]{1,0:T(8,128)(2,1)S(1)}, u32[]{:S(2)}, u32[]{:S(2)}) collective-permute-start(bf16[80,4608]{1,0:T(8,128)(2,1)S(1)} %copy-done.31), channel_id=1, source_target_pairs={{0,16},{4,20},{8,24},{12,28},{16,0},{20,4},{24,8},{28,12},{1,17},{... | collective-permute-start | bytes 2211848 | tf_op jit(solution)/shard_map/ppermute | solution.py:302
  83.9 15.4 %collective-permute-start.22 = (bf16[64,4608]{1,0:T(8,128)(2,1)S(1)}, bf16[64,4608]{1,0:T(8,128)(2,1)S(1)}, u32[]{:S(2)}, u32[]{:S(2)}) collective-permute-start(bf16[64,4608]{1,0:T(8,128)(2,1)S(1)} %copy-done.56), channel_id=1, source_target_pairs={{0,8},{4,12},{8,0},{12,4},{16,24},{20,28},{24,16},{28,20},{1,9},{5... | collective-permute-start | bytes 1769480 | tf_op jit(solution)/shard_map/ppermute | solution.py:302
  85.4 39.9 %collective-permute-start.20 = (bf16[1152,384]{1,0:T(8,128)(2,1)}, bf16[1152,384]{1,0:T(8,128)(2,1)}, u32[]{:S(2)}, u32[]{:S(2)}) collective-permute-start(bf16[1152,384]{1,0:T(8,128)(2,1)} %pad_bitcast_fusion), channel_id=1, source_target_pairs={{0,4},{4,0},{8,12},{12,8},{16,20},{20,16},{24,28},{28,24},{1,5},{5... | collective-permute-start | bytes 2654216 | tf_op jit(solution)/shard_map/ppermute | solution.py:302
  94.9 30.5 %collective-permute-start.17 = (bf16[80,4608]{1,0:T(8,128)(2,1)}, bf16[80,4608]{1,0:T(8,128)(2,1)}, u32[]{:S(2)}, u32[]{:S(2)}) collective-permute-start(bf16[80,4608]{1,0:T(8,128)(2,1)} %collective-permute-done.14.top_x), channel_id=1, source_target_pairs={{0,16},{4,20},{8,24},{12,28},{16,0},{20,4},{24,8},{28,12},{1,17},{... | collective-permute-start | bytes 2211848 | tf_op jit(solution)/shard_map/ppermute | solution.py:302
  103.6 21.7 %collective-permute-start.18 = (bf16[64,4608]{1,0:T(8,128)(2,1)}, bf16[64,4608]{1,0:T(8,128)(2,1)}, u32[]{:S(2)}, u32[]{:S(2)}) collective-permute-start(bf16[64,4608]{1,0:T(8,128)(2,1)} %collective-permute-done.15.bottom_y), channel_id=1, source_target_pairs={{0,8},{4,12},{8,0},{12,4},{16,24},{20,28},{24,16},{28,20},{1,9},{5... | collective-permute-start | bytes 1769480 | tf_op jit(solution)/shard_map/ppermute | solution.py:302
  109.0 16.4 %collective-permute-start.19 = (bf16[144,1152]{1,0:T(8,128)(2,1)}, bf16[144,1152]{1,0:T(8,128)(2,1)}, u32[]{:S(2)}, u32[]{:S(2)}) collective-permute-start(bf16[144,1152]{1,0:T(8,128)(2,1)} %concatenate.69.shard_ref), channel_id=1, source_target_pairs={{0,2},{1,3},{2,0},{3,1},{4,6},{5,7},{6,4},{7,5},{8,10},{9,11},{10,... | collective-permute-start | bytes 995336 | tf_op jit(solution)/shard_map/ppermute | solution.py:306
  125.4 20.5 %collective-permute-start.28 = (bf16[80,4608]{1,0:T(8,128)(2,1)S(1)}, bf16[80,4608]{1,0:T(8,128)(2,1)S(1)}, u32[]{:S(2)}, u32[]{:S(2)}) collective-permute-start(bf16[80,4608]{1,0:T(8,128)(2,1)S(1)} %copy-done.32), channel_id=1, source_target_pairs={{0,8},{4,12},{8,0},{12,4},{16,24},{20,28},{24,16},{28,20},{1,9},{5... | collective-permute-start | bytes 2211848 | tf_op jit(solution)/shard_map/ppermute | solution.py:302
  127.0 17.3 %collective-permute-start.29 = (bf16[64,4608]{1,0:T(8,128)(2,1)S(1)}, bf16[64,4608]{1,0:T(8,128)(2,1)S(1)}, u32[]{:S(2)}, u32[]{:S(2)}) collective-permute-start(bf16[64,4608]{1,0:T(8,128)(2,1)S(1)} %copy-done.57), channel_id=1, source_target_pairs={{0,16},{4,20},{8,24},{12,28},{16,0},{20,4},{24,8},{28,12},{1,17},{... | collective-permute-start | bytes 1769480 | tf_op jit(solution)/shard_map/ppermute | solution.py:302
  127.9 16.5 %collective-permute-start.31 = (bf16[144,1152]{1,0:T(8,128)(2,1)}, bf16[144,1152]{1,0:T(8,128)(2,1)S(1)}, u32[]{:S(2)}, u32[]{:S(2)}) collective-permute-start(bf16[144,1152]{1,0:T(8,128)(2,1)} %collective-permute-done.19.far_ref), channel_id=1, source_target_pairs={{0,1},{1,0},{2,3},{3,2},{4,5},{5,4},{6,7},{7,6},{8,9},{9,8},{10,11... | collective-permute-start | bytes 995336 | tf_op jit(solution)/shard_map/ppermute | solution.py:306
  145.9 19.9 %collective-permute-start.32 = (bf16[576,4608]{1,0:T(8,128)(2,1)}, bf16[576,4608]{1,0:T(8,128)(2,1)S(1)}, u32[]{:S(2)}, u32[]{:S(2)}) collective-permute-start(bf16[576,4608]{1,0:T(8,128)(2,1)} %shard_map.369.mine.out_mine), channel_id=1, source_target_pairs={{0,4},{4,0},{8,12},{12,8},{16,20},{20,16},{24,28},{28,24},{1,5},{5... | collective-permute-start | bytes 15925256 | tf_op jit(solution)/shard_map/ppermute | solution.py:302
  146.4 19.3 %collective-permute-start.26 = (bf16[80,4608]{1,0:T(8,128)(2,1)S(1)}, bf16[80,4608]{1,0:T(8,128)(2,1)S(1)}, u32[]{:S(2)}, u32[]{:S(2)}) collective-permute-start(bf16[80,4608]{1,0:T(8,128)(2,1)S(1)} %copy-done.33), channel_id=1, source_target_pairs={{0,16},{4,20},{8,24},{12,28},{16,0},{20,4},{24,8},{28,12},{1,17},{... | collective-permute-start | bytes 2211848 | tf_op jit(solution)/shard_map/ppermute | solution.py:302
  147.6 35.4 %collective-permute-start.36 = (bf16[80,4608]{1,0:T(8,128)(2,1)S(1)}, bf16[80,4608]{1,0:T(8,128)(2,1)S(1)}, u32[]{:S(2)}, u32[]{:S(2)}) collective-permute-start(bf16[80,4608]{1,0:T(8,128)(2,1)S(1)} %collective-permute-done.28.top_x), channel_id=1, source_target_pairs={{0,16},{4,20},{8,24},{12,28},{16,0},{20,4},{24,8},{28,12},{1,17},{... | collective-permute-start | bytes 2211848 | tf_op jit(solution)/shard_map/ppermute | solution.py:302
  148.4 16.6 %collective-permute-start.27 = (bf16[64,4608]{1,0:T(8,128)(2,1)}, bf16[64,4608]{1,0:T(8,128)(2,1)}, u32[]{:S(2)}, u32[]{:S(2)}) collective-permute-start(bf16[64,4608]{1,0:T(8,128)(2,1)} %get-tuple-element.329.bottom), channel_id=1, source_target_pairs={{0,8},{4,12},{8,0},{12,4},{16,24},{20,28},{24,16},{28,20},{1,9},{5... | collective-permute-start | bytes 1769480 | tf_op jit(solution)/shard_map/ppermute | solution.py:302
  153.4 29.7 %collective-permute-start.37 = (bf16[64,4608]{1,0:T(8,128)(2,1)}, bf16[64,4608]{1,0:T(8,128)(2,1)}, u32[]{:S(2)}, u32[]{:S(2)}) collective-permute-start(bf16[64,4608]{1,0:T(8,128)(2,1)} %copy-done.59), channel_id=1, source_target_pairs={{0,8},{4,12},{8,0},{12,4},{16,24},{20,28},{24,16},{28,20},{1,9},{5... | collective-permute-start | bytes 1769480 | tf_op jit(solution)/shard_map/ppermute | solution.py:302
  189.3 31.5 %collective-permute-start.38 = (bf16[576,4608]{1,0:T(8,128)(2,1)}, bf16[576,4608]{1,0:T(8,128)(2,1)S(1)}, u32[]{:S(2)}, u32[]{:S(2)}) collective-permute-start(bf16[576,4608]{1,0:T(8,128)(2,1)} %shard_map.372.mine), channel_id=1, source_target_pairs={{0,4},{4,0},{8,12},{12,8},{16,20},{20,16},{24,28},{28,24},{1,5},{5... | collective-permute-start | bytes 15925256 | tf_op jit(solution)/shard_map/ppermute | solution.py:302
  189.3 17.8 %collective-permute-start.34 = (bf16[288,1152]{1,0:T(8,128)(2,1)S(1)}, bf16[288,1152]{1,0:T(8,128)(2,1)S(1)}, u32[]{:S(2)}, u32[]{:S(2)}) collective-permute-start(bf16[288,1152]{1,0:T(8,128)(2,1)S(1)} %copy-done.43), channel_id=1, source_target_pairs={{0,8},{4,12},{8,0},{12,4},{16,24},{20,28},{24,16},{28,20},{1,9},{5... | collective-permute-start | bytes 1990664 | tf_op jit(solution)/shard_map/ppermute | solution.py:302
  190.8 29.9 %collective-permute-start.35 = (bf16[288,1152]{1,0:T(8,128)(2,1)S(1)}, bf16[288,1152]{1,0:T(8,128)(2,1)}, u32[]{:S(2)}, u32[]{:S(2)}) collective-permute-start(bf16[288,1152]{1,0:T(8,128)(2,1)S(1)} %copy-done.44), channel_id=1, source_target_pairs={{0,16},{4,20},{8,24},{12,28},{16,0},{20,4},{24,8},{28,12},{1,17},{... | collective-permute-start | bytes 1990664 | tf_op jit(solution)/shard_map/ppermute | solution.py:302
  191.1 45.7 %collective-permute-start.42 = (bf16[288,1152]{1,0:T(8,128)(2,1)S(1)}, bf16[288,1152]{1,0:T(8,128)(2,1)}, u32[]{:S(2)}, u32[]{:S(2)}) collective-permute-start(bf16[288,1152]{1,0:T(8,128)(2,1)S(1)} %copy-done.43), channel_id=1, source_target_pairs={{0,16},{4,20},{8,24},{12,28},{16,0},{20,4},{24,8},{28,12},{1,17},{... | collective-permute-start | bytes 1990664 | tf_op jit(solution)/shard_map/ppermute | solution.py:302
  192.8 43.9 %collective-permute-start.43 = (bf16[288,1152]{1,0:T(8,128)(2,1)S(1)}, bf16[288,1152]{1,0:T(8,128)(2,1)}, u32[]{:S(2)}, u32[]{:S(2)}) collective-permute-start(bf16[288,1152]{1,0:T(8,128)(2,1)S(1)} %copy-done.44), channel_id=1, source_target_pairs={{0,8},{4,12},{8,0},{12,4},{16,24},{20,28},{24,16},{28,20},{1,9},{5... | collective-permute-start | bytes 1990664 | tf_op jit(solution)/shard_map/ppermute | solution.py:302
  207.1 29.7 %collective-permute-start.44 = (bf16[258,1152]{1,0:T(8,128)(2,1)S(1)}, bf16[258,1152]{1,0:T(8,128)(2,1)}, u32[]{:S(2)}, u32[]{:S(2)}) collective-permute-start(bf16[258,1152]{1,0:T(8,128)(2,1)S(1)} %copy-done.4), channel_id=1, source_target_pairs={{0,4},{4,0},{8,12},{12,8},{16,20},{20,16},{24,28},{28,24},{1,5},{5... | collective-permute-start | bytes 1783304 | tf_op jit(solution)/shard_map/ppermute | solution.py:302
  220.7 16.1 %collective-permute-start.45 = (bf16[576,384]{1,0:T(8,128)(2,1)}, bf16[576,384]{1,0:T(8,128)(2,1)}, u32[]{:S(2)}, u32[]{:S(2)}) collective-permute-start(bf16[576,384]{1,0:T(8,128)(2,1)} %get-tuple-element.366), channel_id=1, source_target_pairs={{0,4},{4,0},{8,12},{12,8},{16,20},{20,16},{24,28},{28,24},{1,5},{5... | collective-permute-start | bytes 1327112 | tf_op jit(solution)/shard_map/ppermute | solution.py:302
  237.1 17.1 %collective-permute-start.39 = (bf16[288,1152]{1,0:T(8,128)(2,1)S(1)}, bf16[288,1152]{1,0:T(8,128)(2,1)S(1)}, u32[]{:S(2)}, u32[]{:S(2)}) collective-permute-start(bf16[288,1152]{1,0:T(8,128)(2,1)S(1)} %collective-permute-done.34.top_x), channel_id=1, source_target_pairs={{0,16},{4,20},{8,24},{12,28},{16,0},{20,4},{24,8},{28,12},{1,17},{... | collective-permute-start | bytes 1990664 | tf_op jit(solution)/shard_map/ppermute | solution.py:302
  238.4 17.0 %collective-permute-start.40 = (bf16[288,1152]{1,0:T(8,128)(2,1)}, bf16[288,1152]{1,0:T(8,128)(2,1)S(1)}, u32[]{:S(2)}, u32[]{:S(2)}) collective-permute-start(bf16[288,1152]{1,0:T(8,128)(2,1)} %collective-permute-done.35.bottom_y), channel_id=1, source_target_pairs={{0,8},{4,12},{8,0},{12,4},{16,24},{20,28},{24,16},{28,20},{1,9},{5... | collective-permute-start | bytes 1990664 | tf_op jit(solution)/shard_map/ppermute | solution.py:302
  238.9 15.2 %collective-permute-start.41 = (bf16[576,384]{1,0:T(8,128)(2,1)}, bf16[576,384]{1,0:T(8,128)(2,1)S(1)}, u32[]{:S(2)}, u32[]{:S(2)}) collective-permute-start(bf16[576,384]{1,0:T(8,128)(2,1)} %get-tuple-element.364), channel_id=1, source_target_pairs={{0,4},{4,0},{8,12},{12,8},{16,20},{20,16},{24,28},{28,24},{1,5},{5... | collective-permute-start | bytes 1327112 | tf_op jit(solution)/shard_map/ppermute | solution.py:302
  261.4 22.2 %collective-permute-start.47 = (bf16[288,1152]{1,0:T(8,128)(2,1)}, bf16[288,1152]{1,0:T(8,128)(2,1)S(1)}, u32[]{:S(2)}, u32[]{:S(2)}) collective-permute-start(bf16[288,1152]{1,0:T(8,128)(2,1)} %get-tuple-element.387), channel_id=1, source_target_pairs={{0,8},{4,12},{8,0},{12,4},{16,24},{20,28},{24,16},{28,20},{1,9},{5... | collective-permute-start | bytes 1990664 | tf_op jit(solution)/shard_map/ppermute | solution.py:302
  262.3 21.3 %collective-permute-start.48 = (bf16[288,1152]{1,0:T(8,128)(2,1)}, bf16[288,1152]{1,0:T(8,128)(2,1)S(1)}, u32[]{:S(2)}, u32[]{:S(2)}) collective-permute-start(bf16[288,1152]{1,0:T(8,128)(2,1)} %get-tuple-element.388), channel_id=1, source_target_pairs={{0,16},{4,20},{8,24},{12,28},{16,0},{20,4},{24,8},{28,12},{1,17},{... | collective-permute-start | bytes 1990664 | tf_op jit(solution)/shard_map/ppermute | solution.py:302
  263.7 29.4 %collective-permute-start.49 = (bf16[288,1152]{1,0:T(8,128)(2,1)}, bf16[288,1152]{1,0:T(8,128)(2,1)S(1)}, u32[]{:S(2)}, u32[]{:S(2)}) collective-permute-start(bf16[288,1152]{1,0:T(8,128)(2,1)} %get-tuple-element.389), channel_id=1, source_target_pairs={{0,8},{4,12},{8,0},{12,4},{16,24},{20,28},{24,16},{28,20},{1,9},{5... | collective-permute-start | bytes 1990664 | tf_op jit(solution)/shard_map/ppermute | solution.py:302
  264.3 29.3 %collective-permute-start.50 = (bf16[288,1152]{1,0:T(8,128)(2,1)}, bf16[288,1152]{1,0:T(8,128)(2,1)}, u32[]{:S(2)}, u32[]{:S(2)}) collective-permute-start(bf16[288,1152]{1,0:T(8,128)(2,1)} %get-tuple-element.390), channel_id=1, source_target_pairs={{0,16},{4,20},{8,24},{12,28},{16,0},{20,4},{24,8},{28,12},{1,17},{... | collective-permute-start | bytes 1990664 | tf_op jit(solution)/shard_map/ppermute | solution.py:302
  293.8 17.8 %collective-permute-start.53 = (bf16[288,1152]{1,0:T(8,128)(2,1)S(1)}, bf16[288,1152]{1,0:T(8,128)(2,1)S(1)}, u32[]{:S(2)}, u32[]{:S(2)}) collective-permute-start(bf16[288,1152]{1,0:T(8,128)(2,1)S(1)} %add_convert_fusion.2), channel_id=1, source_target_pairs={{0,8},{4,12},{8,0},{12,4},{16,24},{20,28},{24,16},{28,20},{1,9},{5... | collective-permute-start | bytes 1990664 | tf_op jit(solution)/shard_map/ppermute | solution.py:302
  295.4 17.1 %collective-permute-start.52 = (bf16[288,1152]{1,0:T(8,128)(2,1)S(1)}, bf16[288,1152]{1,0:T(8,128)(2,1)S(1)}, u32[]{:S(2)}, u32[]{:S(2)}) collective-permute-start(bf16[288,1152]{1,0:T(8,128)(2,1)S(1)} %add_convert_fusion.3), channel_id=1, source_target_pairs={{0,16},{4,20},{8,24},{12,28},{16,0},{20,4},{24,8},{28,12},{1,17},{... | collective-permute-start | bytes 1990664 | tf_op jit(solution)/shard_map/ppermute | solution.py:302
  312.5 19.6 %collective-permute-start.55 = (bf16[80,4608]{1,0:T(8,128)(2,1)}, bf16[80,4608]{1,0:T(8,128)(2,1)S(1)}, u32[]{:S(2)}, u32[]{:S(2)}) collective-permute-start(bf16[80,4608]{1,0:T(8,128)(2,1)} %get-tuple-element.413), channel_id=1, source_target_pairs={{0,8},{4,12},{8,0},{12,4},{16,24},{20,28},{24,16},{28,20},{1,9},{5... | collective-permute-start | bytes 2211848 | tf_op jit(solution)/shard_map/ppermute | solution.py:302
  313.2 16.7 %collective-permute-start.56 = (bf16[64,4608]{1,0:T(8,128)(2,1)}, bf16[64,4608]{1,0:T(8,128)(2,1)S(1)}, u32[]{:S(2)}, u32[]{:S(2)}) collective-permute-start(bf16[64,4608]{1,0:T(8,128)(2,1)} %get-tuple-element.414), channel_id=1, source_target_pairs={{0,16},{4,20},{8,24},{12,28},{16,0},{20,4},{24,8},{28,12},{1,17},{... | collective-permute-start | bytes 1769480 | tf_op jit(solution)/shard_map/ppermute | solution.py:302
  314.8 33.5 %collective-permute-start.59 = (bf16[80,4608]{1,0:T(8,128)(2,1)}, bf16[80,4608]{1,0:T(8,128)(2,1)S(1)}, u32[]{:S(2)}, u32[]{:S(2)}) collective-permute-start(bf16[80,4608]{1,0:T(8,128)(2,1)} %get-tuple-element.436), channel_id=1, source_target_pairs={{0,8},{4,12},{8,0},{12,4},{16,24},{20,28},{24,16},{28,20},{1,9},{5... | collective-permute-start | bytes 2211848 | tf_op jit(solution)/shard_map/ppermute | solution.py:302
  332.1 16.2 %collective-permute-start.61 = (bf16[258,1152]{1,0:T(8,128)(2,1)}, bf16[258,1152]{1,0:T(8,128)(2,1)S(1)}, u32[]{:S(2)}, u32[]{:S(2)}) collective-permute-start(bf16[258,1152]{1,0:T(8,128)(2,1)} %get-tuple-element.438.refs_6_), channel_id=1, source_target_pairs={{0,4},{4,0},{8,12},{12,8},{16,20},{20,16},{24,28},{28,24},{1,5},{5... | collective-permute-start | bytes 1783304 | tf_op jit(solution)/shard_map/ppermute | solution.py:302
  332.1 16.1 %collective-permute-start.60 = (bf16[64,4608]{1,0:T(8,128)(2,1)S(1)}, bf16[64,4608]{1,0:T(8,128)(2,1)S(1)}, u32[]{:S(2)}, u32[]{:S(2)}) collective-permute-start(bf16[64,4608]{1,0:T(8,128)(2,1)S(1)} %copy-done.100), channel_id=1, source_target_pairs={{0,16},{4,20},{8,24},{12,28},{16,0},{20,4},{24,8},{28,12},{1,17},{... | collective-permute-start | bytes 1769480 | tf_op jit(solution)/shard_map/ppermute | solution.py:302
  349.5 21.4 %collective-permute-start.57 = (bf16[80,4608]{1,0:T(8,128)(2,1)S(1)}, bf16[80,4608]{1,0:T(8,128)(2,1)S(1)}, u32[]{:S(2)}, u32[]{:S(2)}) collective-permute-start(bf16[80,4608]{1,0:T(8,128)(2,1)S(1)} %add_convert_fusion.1), channel_id=1, source_target_pairs={{0,16},{4,20},{8,24},{12,28},{16,0},{20,4},{24,8},{28,12},{1,17},{... | collective-permute-start | bytes 2211848 | tf_op jit(solution)/shard_map/ppermute | solution.py:302
  351.0 19.8 %collective-permute-start.58 = (bf16[64,4608]{1,0:T(8,128)(2,1)S(1)}, bf16[64,4608]{1,0:T(8,128)(2,1)S(1)}, u32[]{:S(2)}, u32[]{:S(2)}) collective-permute-start(bf16[64,4608]{1,0:T(8,128)(2,1)S(1)} %add_convert_fusion.5), channel_id=1, source_target_pairs={{0,8},{4,12},{8,0},{12,4},{16,24},{20,28},{24,16},{28,20},{1,9},{5... | collective-permute-start | bytes 1769480 | tf_op jit(solution)/shard_map/ppermute | solution.py:302
  370.9 21.4 %collective-permute-start.63 = (bf16[80,4608]{1,0:T(8,128)(2,1)}, bf16[80,4608]{1,0:T(8,128)(2,1)S(1)}, u32[]{:S(2)}, u32[]{:S(2)}) collective-permute-start(bf16[80,4608]{1,0:T(8,128)(2,1)} %get-tuple-element.453), channel_id=1, source_target_pairs={{0,8},{4,12},{8,0},{12,4},{16,24},{20,28},{24,16},{28,20},{1,9},{5... | collective-permute-start | bytes 2211848 | tf_op jit(solution)/shard_map/ppermute | solution.py:302
  372.4 19.9 %collective-permute-start.64 = (bf16[64,4608]{1,0:T(8,128)(2,1)}, bf16[64,4608]{1,0:T(8,128)(2,1)S(1)}, u32[]{:S(2)}, u32[]{:S(2)}) collective-permute-start(bf16[64,4608]{1,0:T(8,128)(2,1)} %get-tuple-element.454), channel_id=1, source_target_pairs={{0,16},{4,20},{8,24},{12,28},{16,0},{20,4},{24,8},{28,12},{1,17},{... | collective-permute-start | bytes 1769480 | tf_op jit(solution)/shard_map/ppermute | solution.py:302
  373.2 18.6 %collective-permute-start.65 = (bf16[144,1152]{1,0:T(8,128)(2,1)S(1)}, bf16[144,1152]{1,0:T(8,128)(2,1)S(1)}, u32[]{:S(2)}, u32[]{:S(2)}) collective-permute-start(bf16[144,1152]{1,0:T(8,128)(2,1)S(1)} %copy-done.102), channel_id=1, source_target_pairs={{0,1},{1,0},{2,3},{3,2},{4,5},{5,4},{6,7},{7,6},{8,9},{9,8},{10,11... | collective-permute-start | bytes 995336 | tf_op jit(solution)/shard_map/ppermute | solution.py:306
  373.6 18.7 %collective-permute-start.66 = (bf16[144,1152]{1,0:T(8,128)(2,1)S(1)}, bf16[144,1152]{1,0:T(8,128)(2,1)S(1)}, u32[]{:S(2)}, u32[]{:S(2)}) collective-permute-start(bf16[144,1152]{1,0:T(8,128)(2,1)S(1)} %copy-done.101), channel_id=1, source_target_pairs={{0,1},{1,0},{2,3},{3,2},{4,5},{5,4},{6,7},{7,6},{8,9},{9,8},{10,11... | collective-permute-start | bytes 995336 | tf_op jit(solution)/shard_map/ppermute | solution.py:306
  375.5 30.8 %collective-permute-start.69 = (bf16[80,4608]{1,0:T(8,128)(2,1)}, bf16[80,4608]{1,0:T(8,128)(2,1)S(1)}, u32[]{:S(2)}, u32[]{:S(2)}) collective-permute-start(bf16[80,4608]{1,0:T(8,128)(2,1)} %get-tuple-element.464), channel_id=1, source_target_pairs={{0,8},{4,12},{8,0},{12,4},{16,24},{20,28},{24,16},{28,20},{1,9},{5... | collective-permute-start | bytes 2211848 | tf_op jit(solution)/shard_map/ppermute | solution.py:302
  393.1 15.9 %collective-permute-start.71 = (bf16[144,1152]{1,0:T(8,128)(2,1)}, bf16[144,1152]{1,0:T(8,128)(2,1)}, u32[]{:S(2)}, u32[]{:S(2)}) collective-permute-start(bf16[144,1152]{1,0:T(8,128)(2,1)} %add_convert_fusion.10), channel_id=1, source_target_pairs={{0,2},{1,3},{2,0},{3,1},{4,6},{5,7},{6,4},{7,5},{8,10},{9,11},{10,... | collective-permute-start | bytes 995336 | tf_op jit(solution)/shard_map/ppermute | solution.py:306
  393.1 15.9 %collective-permute-start.72 = (bf16[258,1152]{1,0:T(8,128)(2,1)S(1)}, bf16[258,1152]{1,0:T(8,128)(2,1)}, u32[]{:S(2)}, u32[]{:S(2)}) collective-permute-start(bf16[258,1152]{1,0:T(8,128)(2,1)S(1)} %copy-done.11), channel_id=1, source_target_pairs={{0,4},{4,0},{8,12},{12,8},{16,20},{20,16},{24,28},{28,24},{1,5},{5... | collective-permute-start | bytes 1783304 | tf_op jit(solution)/shard_map/ppermute | solution.py:302
  394.1 41.3 %collective-permute-start.68 = (bf16[64,4608]{1,0:T(8,128)(2,1)}, bf16[64,4608]{1,0:T(8,128)(2,1)}, u32[]{:S(2)}, u32[]{:S(2)}) collective-permute-start(bf16[64,4608]{1,0:T(8,128)(2,1)} %add_convert_fusion.4), channel_id=1, source_target_pairs={{0,8},{4,12},{8,0},{12,4},{16,24},{20,28},{24,16},{28,20},{1,9},{5... | collective-permute-start | bytes 1769480 | tf_op jit(solution)/shard_map/ppermute | solution.py:302
  405.6 29.8 %collective-permute-start.67 = (bf16[80,4608]{1,0:T(8,128)(2,1)}, bf16[80,4608]{1,0:T(8,128)(2,1)}, u32[]{:S(2)}, u32[]{:S(2)}) collective-permute-start(bf16[80,4608]{1,0:T(8,128)(2,1)} %add_convert_fusion), channel_id=1, source_target_pairs={{0,16},{4,20},{8,24},{12,28},{16,0},{20,4},{24,8},{28,12},{1,17},{... | collective-permute-start | bytes 2211848 | tf_op jit(solution)/shard_map/ppermute | solution.py:302
  409.0 26.4 %collective-permute-start.73 = (bf16[144,1152]{1,0:T(8,128)(2,1)}, bf16[144,1152]{1,0:T(8,128)(2,1)}, u32[]{:S(2)}, u32[]{:S(2)}) collective-permute-start(bf16[144,1152]{1,0:T(8,128)(2,1)} %get-tuple-element.482), channel_id=1, source_target_pairs={{0,1},{1,0},{2,3},{3,2},{4,5},{5,4},{6,7},{7,6},{8,9},{9,8},{10,11... | collective-permute-start | bytes 995336 | tf_op jit(solution)/shard_map/ppermute | solution.py:306
  409.0 26.4 %collective-permute-start.74 = (bf16[144,1152]{1,0:T(8,128)(2,1)}, bf16[144,1152]{1,0:T(8,128)(2,1)}, u32[]{:S(2)}, u32[]{:S(2)}) collective-permute-start(bf16[144,1152]{1,0:T(8,128)(2,1)} %get-tuple-element.483), channel_id=1, source_target_pairs={{0,1},{1,0},{2,3},{3,2},{4,5},{5,4},{6,7},{7,6},{8,9},{9,8},{10,11... | collective-permute-start | bytes 995336 | tf_op jit(solution)/shard_map/ppermute | solution.py:306
  411.1 24.3 %collective-permute-start.75 = (f32[12672]{0:T(1024)S(1)}, f32[12672]{0:T(1024)S(1)}, u32[]{:S(2)}, u32[]{:S(2)}) collective-permute-start(f32[12672]{0:T(1024)S(1)} %concatenate.70), channel_id=1, source_target_pairs={{0,4},{4,0},{8,12},{12,8},{16,20},{20,16},{24,28},{28,24},{1,5},{5... | collective-permute-start | bytes 152072 | tf_op jit(solution)/shard_map/ppermute | solution.py:302
  436.5 17.7 %collective-permute-start.80 = (bf16[144,1152]{1,0:T(8,128)(2,1)S(1)}, bf16[144,1152]{1,0:T(8,128)(2,1)S(1)}, u32[]{:S(2)}, u32[]{:S(2)}) collective-permute-start(bf16[144,1152]{1,0:T(8,128)(2,1)S(1)} %add_convert_fusion.9), channel_id=1, source_target_pairs={{0,2},{1,3},{2,0},{3,1},{4,6},{5,7},{6,4},{7,5},{8,10},{9,11},{10,... | collective-permute-start | bytes 995336 | tf_op jit(solution)/shard_map/ppermute | solution.py:306
  436.6 19.0 %collective-permute-start.76 = (bf16[144,1152]{1,0:T(8,128)(2,1)}, bf16[144,1152]{1,0:T(8,128)(2,1)S(1)}, u32[]{:S(2)}, u32[]{:S(2)}) collective-permute-start(bf16[144,1152]{1,0:T(8,128)(2,1)} %get-tuple-element.496), channel_id=1, source_target_pairs={{0,8},{4,12},{8,0},{12,4},{16,24},{20,28},{24,16},{28,20},{1,9},{5... | collective-permute-start | bytes 995336 | tf_op jit(solution)/shard_map/ppermute | solution.py:302
  438.0 17.6 %collective-permute-start.77 = (bf16[144,1152]{1,0:T(8,128)(2,1)}, bf16[144,1152]{1,0:T(8,128)(2,1)S(1)}, u32[]{:S(2)}, u32[]{:S(2)}) collective-permute-start(bf16[144,1152]{1,0:T(8,128)(2,1)} %get-tuple-element.497), channel_id=1, source_target_pairs={{0,16},{4,20},{8,24},{12,28},{16,0},{20,4},{24,8},{28,12},{1,17},{... | collective-permute-start | bytes 995336 | tf_op jit(solution)/shard_map/ppermute | solution.py:302
  438.8 16.9 %collective-permute-start.78 = (bf16[144,1152]{1,0:T(8,128)(2,1)}, bf16[144,1152]{1,0:T(8,128)(2,1)S(1)}, u32[]{:S(2)}, u32[]{:S(2)}) collective-permute-start(bf16[144,1152]{1,0:T(8,128)(2,1)} %get-tuple-element.498), channel_id=1, source_target_pairs={{0,8},{4,12},{8,0},{12,4},{16,24},{20,28},{24,16},{28,20},{1,9},{5... | collective-permute-start | bytes 995336 | tf_op jit(solution)/shard_map/ppermute | solution.py:302
  440.3 15.3 %collective-permute-start.79 = (bf16[144,1152]{1,0:T(8,128)(2,1)}, bf16[144,1152]{1,0:T(8,128)(2,1)S(1)}, u32[]{:S(2)}, u32[]{:S(2)}) collective-permute-start(bf16[144,1152]{1,0:T(8,128)(2,1)} %get-tuple-element.499), channel_id=1, source_target_pairs={{0,16},{4,20},{8,24},{12,28},{16,0},{20,4},{24,8},{28,12},{1,17},{... | collective-permute-start | bytes 995336 | tf_op jit(solution)/shard_map/ppermute | solution.py:302
  458.5 15.9 %collective-permute-start.84 = (bf16[144,1152]{1,0:T(8,128)(2,1)S(1)}, bf16[144,1152]{1,0:T(8,128)(2,1)S(1)}, u32[]{:S(2)}, u32[]{:S(2)}) collective-permute-start(bf16[144,1152]{1,0:T(8,128)(2,1)S(1)} %copy-done.103), channel_id=1, source_target_pairs={{0,1},{1,0},{2,3},{3,2},{4,5},{5,4},{6,7},{7,6},{8,9},{9,8},{10,11... | collective-permute-start | bytes 995336 | tf_op jit(solution)/shard_map/ppermute | solution.py:306
  475.5 20.1 %collective-permute-start.88 = (bf16[144,1152]{1,0:T(8,128)(2,1)}, bf16[144,1152]{1,0:T(8,128)(2,1)}, u32[]{:S(2)}, u32[]{:S(2)}) collective-permute-start(bf16[144,1152]{1,0:T(8,128)(2,1)} %add_convert_fusion.6), channel_id=1, source_target_pairs={{0,2},{1,3},{2,0},{3,1},{4,6},{5,7},{6,4},{7,5},{8,10},{9,11},{10,... | collective-permute-start | bytes 995336 | tf_op jit(solution)/shard_map/ppermute | solution.py:306
  (134 other events, 1342.3 us)

commit v3 on v0

--- a/solution.py
+++ b/solution.py
@@ -1,6 +1,8 @@
 import jax
 import jax.numpy as jnp
 from jax import lax
+from jax.experimental import pallas as pl
+from jax.experimental.pallas import tpu as pltpu
 from jax.sharding import PartitionSpec as P
 
 D = 1152
@@ -80,7 +82,7 @@
     return (weight - step_rate * (direction + weight_decay * weight), moment_new, square_new)
 
 
-def on_device(
+def general_device(
     inputs,
     skip_tokens,
     cotangent,
@@ -287,6 +289,988 @@
     )
 
 
+CORE = 1
+ACROSS = 2
+ALONG = 4
+PAD = 384
+VMEM_BYTES = 56 * 1024 * 1024
+LIGHT = pl.CostEstimate(flops=0, bytes_accessed=1024, transcendentals=0)
+PARAMS = pltpu.CompilerParams(vmem_limit_bytes=VMEM_BYTES)
+
+
+def swap_wide(value, bit):
+    return lax.ppermute(value, "wide", [(i, i ^ bit) for i in range(8)])
+
+
+def swap_narrow(value, bit):
+    return lax.ppermute(value, "narrow", [(i, i ^ bit) for i in range(4)])
+
+
+def together(*values):
+    return lax.optimization_barrier(values)
+
+
+def spot():
+    wide = lax.axis_index("wide")
+    narrow = lax.axis_index("narrow")
+    return (wide & 1, (wide >> 1) & 1, (wide >> 2) & 1, narrow & 1, narrow >> 1)
+
+
+def split_rows(rows):
+    return -(-rows // 32) * 16
+
+
+def column_blocks(kind, quarter):
+    if kind == "attend_output":
+        width = quarter // 8
+        order = [8 * part + 2 * n + p for part in range(3) for p in range(2) for n in range(4)]
+        blocks = [(block // 6, (block % 6) * width) for block in order]
+        return width, blocks + [(n, (6 + p) * width) for p in range(2) for n in range(4)]
+    width = quarter // 2
+    return width, [(n, p * width) for p in range(2) for n in range(4)]
+
+
+def fold(shard):
+    parts = max(1, shard.shape[0] // (D // 8))
+    height = shard.shape[0] // parts
+    return jnp.concatenate(
+        [shard[part * height : (part + 1) * height] for part in range(parts)], axis=1
+    )
+
+
+def unfold(value, rows):
+    parts = rows // value.shape[0]
+    quarter = value.shape[1] // parts
+    return jnp.concatenate(
+        [value[:, part * quarter : (part + 1) * quarter] for part in range(parts)], axis=0
+    )
+
+
+def arrange(kind, parts, shard, others, extra=0):
+    height = shard.shape[0] - extra
+    rows, quarter = parts * height, shard.shape[1] // parts
+    width, blocks = column_blocks(kind, quarter)
+
+    def kernel(*refs):
+        full, apart, held = refs[4], refs[5], refs[-1]
+        narrow = lax.axis_index("narrow")
+        for relative in range(4):
+            held[relative] = refs[relative][...]
+        for number in range(4):
+            value = held[narrow ^ number]
+            if extra:
+                apart[number] = value[height:]
+            for position, (owner, offset) in enumerate(blocks):
+                if owner == number:
+                    column = slice(position * width, (position + 1) * width)
+                    for part in range(parts):
+                        start = part * quarter + offset
+                        full[part * height : (part + 1) * height, column] = value[
+                            :height, start : start + width
+                        ]
+
+    outs = [jax.ShapeDtypeStruct((rows, 4 * quarter), jnp.bfloat16)]
+    if extra:
+        outs.append(jax.ShapeDtypeStruct((4, extra, shard.shape[1]), jnp.bfloat16))
+    return pl.pallas_call(
+        kernel,
+        out_shape=tuple(outs),
+        scratch_shapes=[pltpu.VMEM((4,) + shard.shape, jnp.bfloat16)],
+        compiler_params=PARAMS,
+        cost_estimate=LIGHT,
+    )(shard, *others)
+
+
+def weight_scratch(rows, columns):
+    return [pltpu.VMEM((rows, columns), jnp.bfloat16), pltpu.SemaphoreType.DMA((8,))]
+
+
+def fetch(refs, full, sems, columns=None):
+    wide = lax.axis_index("wide")
+    core, chip = wide & 1, wide >> 1
+    rows = full.shape[0] // 8
+    copies = []
+    for number, (ends, from_x, from_y) in enumerate((refs[:3], refs[3:])):
+        parity = core if number == 0 else 1 - core
+        own, far = ends.at[pl.ds(0, rows)], ends.at[pl.ds(rows, rows)]
+        for relative, piece in enumerate((own, from_x, from_y, far)):
+            if columns is not None:
+                piece = piece.at[:, columns]
+            start = pl.multiple_of((4 * parity + (chip ^ relative)) * rows, 16)
+            copies.append(
+                pltpu.make_async_copy(
+                    piece, full.at[pl.ds(start, rows)], sems.at[4 * number + relative]
+                )
+            )
+    for copy in copies:
+        copy.start()
+    for copy in copies:
+        copy.wait()
+
+
+def pair_gradient(lefts, rights):
+    height = lefts[0][0].shape[0]
+    rows = height // 4
+    split = split_rows(rows)
+    tokens = rights[0][0].shape[0]
+    widths = [right[0].shape[1] for right in rights]
+    tile = 384 if height > 576 else 1152
+    steps = [width // tile for width in widths]
+    starts = [sum(steps[:position]) for position in range(len(steps))]
+    count = len(lefts)
+
+    def kernel(*refs):
+        left_refs = refs[: 2 * count]
+        right_refs = refs[2 * count : 4 * count]
+        outs, (joint, beside) = refs[4 * count : 4 * count + 8], refs[4 * count + 8 :]
+        step = pl.program_id(0)
+        wide = lax.axis_index("wide")
+        across, along = (wide >> 1) & 1, (wide >> 2) & 1
+
+        @pl.when(step == 0)
+        def _():
+            joint[...] = jnp.zeros_like(joint)
+
+        for number in range(count):
+
+            @pl.when(step == starts[number])
+            def _():
+                beside[:, :PAD] = left_refs[2 * number][...]
+                beside[:, PAD:] = left_refs[2 * number + 1][...]
+
+            @pl.when((step >= starts[number]) & (step < starts[number] + steps[number]))
+            def _():
+                joint[:tokens] = right_refs[2 * number][...]
+                joint[PAD : PAD + tokens] = right_refs[2 * number + 1][...]
+                for y in range(2):
+                    for x in range(2):
+                        first_row = (2 * y + x) * rows
+                        total = jnp.dot(
+                            beside[first_row : first_row + rows],
+                            joint[...],
+                            preferred_element_type=jnp.float32,
+                        ).astype(jnp.bfloat16)
+
+                        for kept_x in range(2):
+                            for kept_y in range(2):
+
+                                @pl.when(
+                                    ((across == x) == (kept_x == 1))
+                                    & ((along == y) == (kept_y == 1))
+                                )
+                                def _():
+                                    outs[2 * (1 - kept_x) + (1 - kept_y)][...] = total[:split]
+                                    outs[4 + 2 * (1 - kept_y) + (1 - kept_x)][...] = total[split:]
+
+    def right_spec(number):
+        return pl.BlockSpec(
+            (tokens, tile),
+            lambda i: (0, jnp.clip(i - starts[number], 0, steps[number] - 1)),
+        )
+
+    in_specs = [pl.BlockSpec((height, PAD), lambda i: (0, 0))] * (2 * count)
+    operands = [left for pair in lefts for left in pair]
+    for number in range(count):
+        in_specs += [right_spec(number)] * 2
+        operands += list(rights[number])
+    top_spec = pl.BlockSpec((split, tile), lambda i: (0, i))
+    bottom_spec = pl.BlockSpec((rows - split, tile), lambda i: (0, i))
+    top_shape = jax.ShapeDtypeStruct((split, sum(widths)), jnp.bfloat16)
+    bottom_shape = jax.ShapeDtypeStruct((rows - split, sum(widths)), jnp.bfloat16)
+    outs = pl.pallas_call(
+        kernel,
+        grid=(sum(steps),),
+        in_specs=in_specs,
+        out_specs=(top_spec,) * 4 + (bottom_spec,) * 4,
+        out_shape=(top_shape,) * 4 + (bottom_shape,) * 4,
+        scratch_shapes=[
+            pltpu.VMEM((2 * PAD, tile), jnp.bfloat16),
+            pltpu.VMEM((height, 2 * PAD), jnp.bfloat16),
+        ],
+        compiler_params=PARAMS,
+        cost_estimate=LIGHT,
+    )(*operands)
+    return outs[:4], outs[4:]
+
+
+def unarrange(kind, parts, top, bottom):
+    split, columns = top[0].shape
+    rest = bottom[0].shape[0]
+    rows = split + rest
+    quarter = columns // 4
+    height = rows // parts
+    width, blocks = column_blocks(kind, quarter)
+
+    def kernel(*refs):
+        tops, bottoms = refs[:3], refs[3:6]
+        keep_ref, keep_far_ref, send_ref, send_far_ref, held = refs[6:]
+        narrow = lax.axis_index("narrow")
+        low_bit, high_bit = narrow & 1, narrow >> 1
+        held[:split] = add_low(*[ref[...] for ref in tops])
+        held[split:] = add_low(*[ref[...] for ref in bottoms])
+        for position, (owner, offset) in enumerate(blocks):
+            piece = held[:, position * width : (position + 1) * width]
+            for kept_low in range(2):
+                for kept_high in range(2):
+                    target = (keep_ref, keep_far_ref, send_ref, send_far_ref)[
+                        2 * (1 - kept_low) + (1 - kept_high)
+                    ]
+
+                    @pl.when(
+                        ((low_bit == (owner & 1)) == (kept_low == 1))
+                        & ((high_bit == (owner >> 1)) == (kept_high == 1))
+                    )
+                    def _():
+                        for part in range(parts):
+                            start = part * quarter + offset
+                            target[:, start : start + width] = piece[
+                                part * height : (part + 1) * height
+                            ]
+
+    shape = jax.ShapeDtypeStruct((height, parts * quarter), jnp.bfloat16)
+    return pl.pallas_call(
+        kernel,
+        out_shape=(shape,) * 4,
+        scratch_shapes=[pltpu.VMEM((rows, columns), jnp.bfloat16)],
+        compiler_params=PARAMS,
+        cost_estimate=LIGHT,
+    )(*top, *bottom)
+
+
+def add_low(*terms):
+    return sum(term.astype(jnp.float32) for term in terms).astype(jnp.bfloat16)
+
+
+def pick(value, index, dim=0):
+    return lax.dynamic_index_in_dim(value, index, dim, keepdims=False)
+
+
+def halves_of(value, core):
+    middle = value.shape[-1] // 2
+    first, second = value[..., :middle], value[..., middle:]
+    return jnp.where(core == 0, first, second), jnp.where(core == 0, second, first)
+
+
+def inner(value):
+    width = value.shape[-1] // 8
+    return jnp.concatenate(
+        [
+            value[..., (2 * n + p) * width : (2 * n + p + 1) * width]
+            for p in range(2)
+            for n in range(4)
+        ],
+        axis=-1,
+    )
+
+
+def outer(value):
+    width = value.shape[-1] // 8
+    return jnp.concatenate(
+        [
+            value[..., (4 * p + n) * width : (4 * p + n + 1) * width]
+            for n in range(4)
+            for p in range(2)
+        ],
+        axis=-1,
+    )
+
+
+def upright(value):
+    return jnp.pad(value, ((0, PAD - value.shape[0]), (0, 0))).T
+
+
+def both(parts, order):
+    if order == 0:
+        return swap_wide(parts[0], ACROSS), swap_wide(parts[1], ALONG)
+    return swap_wide(parts[0], ALONG), swap_wide(parts[1], ACROSS)
+
+
+KEEP_NEAR, KEEP_FAR, SEND_NEAR, SEND_FAR = range(4)
+
+
+def send(blocks, which):
+    return both((blocks[0][which], blocks[1][which]), 0)
+
+
+def forward(blocks, got):
+    return both(tuple(add_low(blocks[i][KEEP_FAR], got[i]) for i in range(2)), 1)
+
+
+def settle(kind, parts, blocks, got_near, got_last):
+    return unarrange(
+        kind, parts, *[(blocks[i][KEEP_NEAR], got_near[i], got_last[i]) for i in range(2)]
+    )
+
+
+def narrow_first(quarters):
+    return swap_narrow(quarters[SEND_FAR], 1), swap_narrow(quarters[SEND_NEAR], 1)
+
+
+def narrow_second(quarters, got):
+    return swap_narrow(add_low(quarters[KEEP_FAR], got[0]), 2)
+
+
+def finish(quarters, got, got_last):
+    return (
+        quarters[KEEP_NEAR].astype(jnp.float32)
+        + got[1].astype(jnp.float32)
+        + got_last.astype(jnp.float32)
+    )
+
+
+def across_narrow(shard):
+    return tuple(swap_narrow(shard, bit) for bit in (1, 2, 3))
+
+
+def gather_first(block):
+    return swap_wide(block, ACROSS), swap_wide(block, ALONG)
+
+
+def gather_second(first):
+    split = split_rows(first[0].shape[0])
+    return swap_wide(first[0][:split], ALONG), swap_wide(first[1][split:], ACROSS)
+
+
+def swap_sides(first):
+    return swap_wide(first[0], CORE), swap_wide(first[1], CORE)
+
+
+def ends_of(block, second):
+    return jnp.concatenate([block, second[0], second[1]], axis=0)
+
+
+def heavy(kernel, outs, scratch, weights, operands):
+    return pl.pallas_call(
+        kernel,
+        in_specs=[pl.BlockSpec(memory_space=pl.ANY)] * len(weights)
+        + [pl.BlockSpec(memory_space=pltpu.VMEM)] * len(operands),
+        out_shape=tuple(jax.ShapeDtypeStruct(shape, dtype) for shape, dtype in outs),
+        scratch_shapes=scratch,
+        compiler_params=PARAMS,
+        cost_estimate=LIGHT,
+    )(*weights, *operands)
+
+
+def dot_rows(left, right):
+    return lax.dot_general(left, right, (((1,), (1,)), ((), ())), preferred_element_type=jnp.float32)
+
+
+def dot_depth(left, right):
+    return lax.dot_general(left, right, (((0,), (0,)), ((), ())), preferred_element_type=jnp.float32)
+
+
+def store_upright(value, padded, mine, other):
+    features = value.shape[1]
+    padded[: value.shape[0]] = value
+    turned = padded[...].T.astype(jnp.bfloat16)
+    core = lax.axis_index("wide") & 1
+
+    @pl.when(core == 0)
+    def _():
+        mine[...] = turned[: features // 2]
+        other[...] = turned[features // 2 :]
+
+    @pl.when(core == 1)
+    def _():
+        other[...] = turned[: features // 2]
+        mine[...] = turned[features // 2 :]
+
+
+def merge_forward(joined, weight, bias, gain, shift):
+    length = joined.shape[0]
+
+    def kernel(*refs):
+        joined_ref, bias_ref, gain_ref, shift_ref = refs[6:10]
+        stream, entry, up_mine, up_other, full, sems, padded = refs[10:]
+        fetch(refs[:6], full, sems)
+        padded[...] = jnp.zeros_like(padded)
+        stream[...] = product(joined_ref[...], full[...]) + bias_ref[...]
+        normed = normalize(stream[...])[0]
+        value = (normed * gain_ref[...] + shift_ref[...]).astype(jnp.bfloat16)
+        entry[...] = value
+        store_upright(value.astype(jnp.float32), padded, up_mine, up_other)
+
+    return heavy(
+        kernel,
+        [
+            ((length, D), jnp.float32),
+            ((length, D), jnp.bfloat16),
+            ((D // 2, PAD), jnp.bfloat16),
+            ((D // 2, PAD), jnp.bfloat16),
+        ],
+        weight_scratch(2 * D, D) + [pltpu.VMEM((PAD, D), jnp.float32)],
+        weight,
+        (joined, bias, gain, shift),
+    )
+
+
+def attend_head(heads, head, chances_ref, slot):
+    at = head * HD
+    queries = heads[:, at : at + HD]
+    keys = heads[:, D + at : D + at + HD]
+    values = heads[:, 2 * D + at : 2 * D + at + HD]
+    logits = dot_rows(queries, keys) * HD ** (-0.5)
+    powers = jnp.exp(logits - jnp.max(logits, axis=-1, keepdims=True))
+    chances = powers / jnp.sum(powers, axis=-1, keepdims=True)
+    chances_ref[slot] = chances
+    return product(chances.astype(jnp.bfloat16), values).astype(jnp.bfloat16)
+
+
+def attend_first(entry, weight):
+    length = entry.shape[0]
+
+    def kernel(*refs):
+        entry_ref, heads, chances_ref, mix_ref, full, sems = refs[6:]
+        fetch(refs[:6], full, sems, pl.ds(0, 3 * D))
+        for part in range(3):
+            columns = slice(part * D, (part + 1) * D)
+            heads[:, columns] = product(entry_ref[...], full[:, columns]).astype(jnp.bfloat16)
+        for head in range(H // 2):
+            mix_ref[:, head * HD : (head + 1) * HD] = attend_head(heads, head, chances_ref, head)
+
+    return heavy(
+        kernel,
+        [
+            ((length, 3 * D), jnp.bfloat16),
+            ((H // 2, length, length), jnp.float32),
+            ((length, D // 2), jnp.bfloat16),
+        ],
+        weight_scratch(D, 3 * D),
+        weight,
+        (entry,),
+    )
+
+
+def attend_second(heads, mix_first, weight, stream_zero, bias, gain, shift):
+    length = heads.shape[0]
+    half = D // 2
+
+    def kernel(*refs):
+        heads_ref, first_ref, zero_ref, bias_ref, gain_ref, shift_ref = refs[6:12]
+        chances_ref, stream, value_ref, up_mine, up_other, full, sems, mixed, padded = refs[12:]
+        fetch(refs[:6], full, sems, pl.ds(3 * D, D))
+        padded[...] = jnp.zeros_like(padded)
+        mixed[:, :half] = first_ref[...]
+        for head in range(H // 2, H):
+            mixed[:, head * HD : (head + 1) * HD] = attend_head(
+                heads_ref, head, chances_ref, head - H // 2
+            )
+        stream[...] = zero_ref[...] + product(mixed[...], full[...]) + bias_ref[...]
+        store_upright(
+            mixed[...].astype(jnp.float32), padded, up_mine.at[pl.ds(0, half)], up_other.at[pl.ds(0, half)]
+        )
+        normed = normalize(stream[...])[0]
+        value = (normed * gain_ref[...] + shift_ref[...]).astype(jnp.bfloat16)
+        value_ref[...] = value
+        store_upright(
+            value.astype(jnp.float32), padded, up_mine.at[pl.ds(half, half)], up_other.at[pl.ds(half, half)]
+        )
+
+    return heavy(
+        kernel,
+        [
+            ((H // 2, length, length), jnp.float32),
+            ((length, D), jnp.float32),
+            ((length, D), jnp.bfloat16),
+            ((D, PAD), jnp.bfloat16),
+            ((D, PAD), jnp.bfloat16),
+        ],
+        weight_scratch(D, D)
+        + [pltpu.VMEM((length, D), jnp.bfloat16), pltpu.VMEM((PAD, D), jnp.float32)],
+        weight,
+        (heads, mix_first, stream_zero, bias, gain, shift),
+    )
+
+
+def expand_forward(entry, weight, bias):
+    length = entry.shape[0]
+
+    def kernel(*refs):
+        entry_ref, bias_ref = refs[6:8]
+        active_ref, slope_ref, up_mine, up_other, full, sems, padded = refs[8:]
+        core = lax.axis_index("wide") & 1
+        fetch(refs[:6], full, sems)
+        padded[...] = jnp.zeros_like(padded)
+        for step in range(FF // D):
+            columns = slice(step * D, (step + 1) * D)
+            value = product(entry_ref[...], full[:, columns]) + bias_ref[:, columns]
+            inside = 0.5 * (1.0 + lax.erf(value * (0.5**0.5)))
+            bell = jnp.exp(-0.5 * value * value) * (2.0 * jnp.pi) ** -0.5
+            active = (value * inside).astype(jnp.bfloat16)
+            slope_ref[:, columns] = inside + value * bell
+            active_ref[:, columns] = active
+            padded[:length] = active.astype(jnp.float32)
+            turned = padded[...].T.astype(jnp.bfloat16)
+            rows = slice((step % 2) * D, (step % 2 + 1) * D)
+
+            @pl.when(core == step // 2)
+            def _():
+                up_mine[rows] = turned
+
+            @pl.when(core != step // 2)
+            def _():
+                up_other[rows] = turned
+
+    return heavy(
+        kernel,
+        [
+            ((length, FF), jnp.bfloat16),
+            ((length, FF), jnp.float32),
+            ((FF // 2, PAD), jnp.bfloat16),
+            ((FF // 2, PAD), jnp.bfloat16),
+        ],
+        weight_scratch(D, FF) + [pltpu.VMEM((PAD, D), jnp.float32)],
+        weight,
+        (entry, bias),
+    )
+
+
+def hidden_backward(pulled, weight, slope):
+    length = pulled.shape[0]
+
+    def kernel(*refs):
+        pulled_ref, slope_ref, low_ref, sum_ref, full, sems = refs[6:]
+        fetch(refs[:6], full, sems)
+        for step in range(FF // D):
+            columns = slice(step * D, (step + 1) * D)
+            delta = dot_rows(pulled_ref[...], full[columns]) * slope_ref[:, columns]
+            low_ref[:, columns] = delta.astype(jnp.bfloat16)
+            sum_ref[:, columns] = jnp.sum(delta, axis=0, keepdims=True)
+
+    return heavy(
+        kernel,
+        [((length, FF), jnp.bfloat16), ((1, FF), jnp.float32)],
+        weight_scratch(FF, D),
+        weight,
+        (pulled, slope),
+    )
+
+
+def expand_backward(hidden_low, weight, mixed_weight, pulled, stream_one, gain):
+    length = pulled.shape[0]
+
+    def kernel(*refs):
+        hidden_ref, pulled_ref, stream_ref, gain_ref = refs[12:16]
+        one_ref, low_ref, sums, mix_ref, full, sems, output, output_sems = refs[16:]
+        fetch(refs[:6], full, sems)
+        fetch(refs[6:12], output, output_sems, pl.ds(3 * D, D))
+        value = dot_rows(hidden_ref[...], full[...])
+        normed, inverse = normalize(stream_ref[...])
+        upstream = pulled_ref[...].astype(jnp.float32)
+        one = upstream + norm_back(value * gain_ref[...], normed, inverse)
+        one_ref[...] = one
+        low_value = one.astype(jnp.bfloat16)
+        low_ref[...] = low_value
+        sums[0:1] = jnp.sum(one, axis=0, keepdims=True)
+        sums[1:2] = jnp.sum(value * normed, axis=0, keepdims=True)
+        sums[2:3] = jnp.sum(value, axis=0, keepdims=True)
+        sums[3:4] = jnp.sum(upstream, axis=0, keepdims=True)
+        mix_ref[...] = dot_rows(low_value, output[...]).astype(jnp.bfloat16)
+
+    return heavy(
+        kernel,
+        [
+            ((length, D), jnp.float32),
+            ((length, D), jnp.bfloat16),
+            ((4, D), jnp.float32),
+            ((length, D), jnp.bfloat16),
+        ],
+        weight_scratch(D, FF) + weight_scratch(D, D),
+        (*weight, *mixed_weight),
+        (hidden_low, pulled, stream_one, gain),
+    )
+
+
+def attend_backward(heads, chances_first, chances_second, delta_mixture):
+    length = heads.shape[0]
+    scale = HD ** (-0.5)
+
+    def kernel(heads_ref, first_ref, second_ref, delta_ref, mixed):
+        for head in range(H):
+            at = head * HD
+            queries = heads_ref[:, at : at + HD]
+            keys = heads_ref[:, D + at : D + at + HD]
+            values = heads_ref[:, 2 * D + at : 2 * D + at + HD]
+            delta = delta_ref[:, at : at + HD]
+            chances = (first_ref, second_ref)[head // (H // 2)][head % (H // 2)]
+            pull = dot_rows(delta, values)
+            inner_sum = jnp.sum(chances * pull, axis=-1, keepdims=True)
+            scores = (scale * (chances * (pull - inner_sum))).astype(jnp.bfloat16)
+            mixed[:, at : at + HD] = product(scores, keys).astype(jnp.bfloat16)
+            mixed[:, D + at : D + at + HD] = dot_depth(scores, queries).astype(jnp.bfloat16)
+            mixed[:, 2 * D + at : 2 * D + at + HD] = dot_depth(
+                chances.astype(jnp.bfloat16), delta
+            ).astype(jnp.bfloat16)
+
+    return heavy(
+        kernel,
+        [((length, 3 * D), jnp.bfloat16)],
+        [],
+        (),
+        (heads, chances_first, chances_second, delta_mixture),
+    )[0]
+
+
+def entry_backward(delta_mixed, weight, delta_one, stream_zero, gain):
+    length = delta_mixed.shape[0]
+
+    def kernel(*refs):
+        mixed_ref, one_ref, stream_ref, gain_ref, low_ref, sums, full, sems = refs[6:]
+        fetch(refs[:6], full, sems, pl.ds(0, 3 * D))
+        value = dot_rows(mixed_ref[...], full[...])
+        normed, inverse = normalize(stream_ref[...])
+        zero = one_ref[...] + norm_back(value * gain_ref[...], normed, inverse)
+        low_ref[...] = zero.astype(jnp.bfloat16)
+        sums[0:1] = jnp.sum(zero, axis=0, keepdims=True)
+        sums[1:2] = jnp.sum(value * normed, axis=0, keepdims=True)
+        sums[2:3] = jnp.sum(value, axis=0, keepdims=True)
+
+    return heavy(
+        kernel,
+        [((length, D), jnp.bfloat16), ((3, D), jnp.float32)],
+        weight_scratch(D, 3 * D),
+        weight,
+        (delta_mixed, delta_one, stream_zero, gain),
+    )
+
+
+def joined_backward(zero_low, weight):
+    length = zero_low.shape[0]
+    width = 2 * D // 8
+
+    def kernel(*refs):
+        zero_ref, first_ref, second_ref, full, sems = refs[6:]
+        fetch(refs[:6], full, sems)
+        for parity in range(2):
+            delta = dot_rows(zero_ref[...], full[parity * D : (parity + 1) * D])
+            delta = delta.astype(jnp.bfloat16)
+            for number in range(4):
+                target = (first_ref, second_ref)[number // 2]
+                column = (2 * (number % 2) + parity) * width
+                target[:, column : column + width] = delta[:, number * width : (number + 1) * width]
+
+    out = ((length, D), jnp.bfloat16)
+    return heavy(kernel, [out, out], weight_scratch(2 * D, D), weight, (zero_low,))
+
+
+def shrink_forward(active, weight, stream_one, bias):
+    length = active.shape[0]
+    width = D // 8
+
+    def kernel(*refs):
+        active_ref, stream_ref, bias_ref, out_ref, full, sems = refs[6:]
+        fetch(refs[:6], full, sems)
+        total = (
+            stream_ref[...] + product(active_ref[...], full[...]) + bias_ref[...]
+        ).astype(jnp.bfloat16)
+        for parity in range(2):
+            for number in range(4):
+                column = (2 * number + parity) * width
+                source = (4 * parity + number) * width
+                out_ref[:, column : column + width] = total[:, source : source + width]
+
+    return heavy(
+        kernel,
+        [((length, D), jnp.bfloat16)],
+        weight_scratch(FF, D),
+        weight,
+        (active, stream_one, bias),
+    )[0]
+
+
+def on_device(
+    inputs,
+    skip_tokens,
+    cotangent,
+    merge_weight,
+    merge_moment,
+    merge_square,
+    attend_weight,
+    attend_moment,
+    attend_square,
+    output_weight,
+    output_moment,
+    output_square,
+    expand_weight,
+    expand_moment,
+    expand_square,
+    shrink_weight,
+    shrink_moment,
+    shrink_square,
+    vectors,
+    vector_moment,
+    vector_square,
+):
+    high_bit, low_bit = spot()[4], spot()[3]
+    core = spot()[0]
+    low = jnp.bfloat16
+    columns = attend_weight.shape[1]
+
+    merge_low = fold(merge_weight.astype(low))
+    width = merge_low.shape[1]
+    count = vectors.shape[0]
+    vector_rows = jnp.pad(vectors.astype(low), (0, 16 * width - count)).reshape(16, width)
+    merge_low = jnp.concatenate([merge_low, vector_rows], axis=0)
+    merge_others = across_narrow(merge_low)
+    mixed_low = jnp.concatenate([attend_weight.astype(low), output_weight.astype(low)], axis=1)
+    joined = inner(jnp.concatenate([inputs[0], skip_tokens[0]], axis=-1))
+    joined_mine, joined_other = halves_of(joined, core)
+    pulled = inner(cotangent[0])
+    merge_others, mixed_low, joined, joined_mine, joined_other, pulled = together(
+        merge_others, mixed_low, joined, joined_mine, joined_other, pulled
+    )
+    merge_block, vector_parts = arrange("merge", 2, merge_low, merge_others, 16)
+    merge_first = gather_first(merge_block)
+    mixed_far = swap_narrow(mixed_low, 2)
+    mixed_near = swap_narrow(mixed_low, 1)
+    expand_low = expand_weight.astype(low)
+    merge_first, mixed_far, vector_parts, expand_low = together(
+        merge_first, mixed_far, vector_parts, expand_low
+    )
+    merge_second = gather_second(merge_first)
+    merge_sides = swap_sides(merge_first)
+    mixed_last = swap_narrow(mixed_far, 1)
+    shrink_low = fold(shrink_weight.astype(low))
+    pieces = unpack(vector_parts.reshape(4, -1)[:, :count].reshape(-1).astype(jnp.float32))
+    pieces = tuple(inner(piece)[None] for piece in pieces)
+    merge_second, merge_sides, mixed_near, mixed_last, shrink_low, pieces = together(
+        merge_second, merge_sides, mixed_near, mixed_last, shrink_low, pieces
+    )
+    skip_bias, gain_one, bias_one, output_bias, gain_two, bias_two, shrink_bias, expand_bias = pieces
+    mixed_block = arrange("attend_output", 1, mixed_low, (mixed_near, mixed_far, mixed_last))[0]
+    mixed_first = gather_first(mixed_block)
+    expand_far = swap_narrow(expand_low, 2)
+    expand_near = swap_narrow(expand_low, 1)
+    merge_ends = ends_of(merge_block, merge_second)
+    merge_pieces = (merge_ends, *merge_first, swap_wide(merge_ends, CORE), *merge_sides)
+    stream_zero, attend_input, attend_up, attend_up_other = merge_forward(
+        joined, merge_pieces, skip_bias, gain_one, bias_one
+    )
+    joined_up = upright(joined_mine)
+    joined_up_other = upright(joined_other)
+    (
+        mixed_first,
+        expand_far,
+        expand_near,
+        stream_zero,
+        attend_input,
+        attend_up_other,
+        joined_up,
+        joined_up_other,
+    ) = together(
+        mixed_first,
+        expand_far,
+        expand_near,
+        stream_zero,
+        attend_input,
+        attend_up_other,
+        joined_up,
+        joined_up_other,
+    )
+    mixed_second = gather_second(mixed_first)
+    mixed_sides = swap_sides(mixed_first)
+    expand_last = swap_narrow(expand_far, 1)
+    mixed_second, mixed_sides, expand_last = together(mixed_second, mixed_sides, expand_last)
+    expand_block = arrange("expand", 1, expand_low, (expand_near, expand_far, expand_last))[0]
+    expand_first = gather_first(expand_block)
+    shrink_far = swap_narrow(shrink_low, 2)
+    shrink_near = swap_narrow(shrink_low, 1)
+    mixed_ends = ends_of(mixed_block, mixed_second)
+    mixed_pieces = (mixed_ends, *mixed_first, swap_wide(mixed_ends, CORE), *mixed_sides)
+    heads, chances_first, mix_first = attend_first(attend_input, mixed_pieces)
+    expand_first, shrink_far, shrink_near, heads, mix_first = together(
+        expand_first, shrink_far, shrink_near, heads, mix_first
+    )
+    expand_second = gather_second(expand_first)
+    expand_sides = swap_sides(expand_first)
+    shrink_last = swap_narrow(shrink_far, 1)
+    chances_second, stream_one, expand_input, ups, ups_other = attend_second(
+        heads, mix_first, mixed_pieces, stream_zero, output_bias, gain_two, bias_two
+    )
+    expand_second, expand_sides, shrink_last, expand_input, ups_other = together(
+        expand_second, expand_sides, shrink_last, expand_input, ups_other
+    )
+    shrink_block = arrange("shrink", 4, shrink_low, (shrink_near, shrink_far, shrink_last))[0]
+    shrink_first = gather_first(shrink_block)
+    expand_ends = ends_of(expand_block, expand_second)
+    expand_pieces = (expand_ends, *expand_first, swap_wide(expand_ends, CORE), *expand_sides)
+    pulled_sibling = swap_wide(pulled, CORE)
+    active, slope, active_up, active_up_other = expand_forward(
+        expand_input, expand_pieces, expand_bias
+    )
+    shrink_first, pulled_sibling, active, slope, active_up, active_up_other = together(
+        shrink_first, pulled_sibling, active, slope, active_up, active_up_other
+    )
+    shrink_second = gather_second(shrink_first)
+    shrink_sides = swap_sides(shrink_first)
+    active_up_sibling = swap_wide(active_up_other, CORE)
+    shrink_blocks = pair_gradient([(active_up, active_up_sibling)], [(pulled, pulled_sibling)])
+    shrink_second, shrink_sides, shrink_blocks = together(
+        shrink_second, shrink_sides, shrink_blocks
+    )
+    shrink_far_got = send(shrink_blocks, SEND_FAR)
+    shrink_near_got = send(shrink_blocks, SEND_NEAR)
+    shrink_ends = ends_of(shrink_block, shrink_second)
+    shrink_pieces = (shrink_ends, *shrink_first, swap_wide(shrink_ends, CORE), *shrink_sides)
+    hidden_low, hidden_sum = hidden_backward(pulled, shrink_pieces, slope)
+    outputs = shrink_forward(active, shrink_pieces, stream_one, shrink_bias)[None]
+    shrink_far_got, shrink_near_got, hidden_low, hidden_sum, outputs, attend_up_other = together(
+        shrink_far_got, shrink_near_got, hidden_low, hidden_sum, outputs, attend_up_other
+    )
+    shrink_got_last = forward(shrink_blocks, shrink_far_got)
+    hidden_sibling = swap_wide(hidden_low, CORE)
+    ups_sibling = swap_wide(ups_other, CORE)
+    attend_up_sibling = swap_wide(attend_up_other, CORE)
+    half = D // 2
+    expand_blocks = pair_gradient(
+        [(ups[half:], ups_sibling[half:])], [(hidden_low, hidden_sibling)]
+    )
+    shrink_got_last, expand_blocks, hidden_low, attend_up_sibling, joined_up_other = together(
+        shrink_got_last, expand_blocks, hidden_low, attend_up_sibling, joined_up_other
+    )
+    expand_far_got = send(expand_blocks, SEND_FAR)
+    joined_sibling = swap_wide(joined_up_other, CORE)
+    delta_one, stream_low, sums_two, delta_mixture = expand_backward(
+        hidden_low, expand_pieces, mixed_pieces, pulled, stream_one, gain_two
+    )
+    expand_far_got, joined_sibling, stream_low, delta_mixture, expand_blocks = together(
+        expand_far_got, joined_sibling, stream_low, delta_mixture, expand_blocks
+    )
+    expand_near_got = send(expand_blocks, SEND_NEAR)
+    stream_sibling = swap_wide(stream_low, CORE)
+    delta_mixed = attend_backward(heads, chances_first, chances_second, delta_mixture)
+    expand_near_got, stream_sibling, delta_mixed = together(
+        expand_near_got, stream_sibling, delta_mixed
+    )
+    expand_got_last = forward(expand_blocks, expand_far_got)
+    mixed_sibling = swap_wide(delta_mixed, CORE)
+    shrink_quarters = settle("shrink", 4, shrink_blocks, shrink_near_got, shrink_got_last)
+    mixed_blocks = pair_gradient(
+        [(attend_up, attend_up_sibling), (ups[:half], ups_sibling[:half])],
+        [(delta_mixed, mixed_sibling), (stream_low, stream_sibling)],
+    )
+    expand_got_last, shrink_quarters, mixed_blocks, delta_mixed = together(
+        expand_got_last, shrink_quarters, mixed_blocks, delta_mixed
+    )
+    mixed_far_got = send(mixed_blocks, SEND_FAR)
+    shrink_got = narrow_first(shrink_quarters)
+    zero_low, sums_one = entry_backward(
+        delta_mixed, mixed_pieces, delta_one, stream_zero, gain_one
+    )
+    mixed_far_got, shrink_got, zero_low, sums_one, mixed_blocks = together(
+        mixed_far_got, shrink_got, zero_low, sums_one, mixed_blocks
+    )
+    mixed_near_got = send(mixed_blocks, SEND_NEAR)
+    shrink_end = narrow_second(shrink_quarters, shrink_got)
+    zero_sibling = swap_wide(zero_low, CORE)
+    expand_quarters = settle("expand", 1, expand_blocks, expand_near_got, expand_got_last)
+    input_gradient, skip_gradient = joined_backward(zero_low, merge_pieces)
+    (
+        mixed_near_got,
+        shrink_end,
+        zero_sibling,
+        expand_quarters,
+        zero_low,
+        input_gradient,
+        skip_gradient,
+    ) = together(
+        mixed_near_got,
+        shrink_end,
+        zero_sibling,
+        expand_quarters,
+        zero_low,
+        input_gradient,
+        skip_gradient,
+    )
+    mixed_got_last = forward(mixed_blocks, mixed_far_got)
+    expand_got = narrow_first(expand_quarters)
+    merge_blocks = pair_gradient([(joined_up, joined_sibling)], [(zero_low, zero_sibling)])
+    vector_total = jnp.concatenate(
+        [
+            outer(row)
+            for row in (
+                sums_one[0],
+                sums_one[1],
+                sums_one[2],
+                sums_two[0],
+                sums_two[1],
+                sums_two[2],
+                sums_two[3],
+                hidden_sum[0],
+            )
+        ]
+    )
+    mixed_got_last, expand_got, vector_total, merge_blocks, shrink_end = together(
+        mixed_got_last, expand_got, vector_total, merge_blocks, shrink_end
+    )
+    merge_far_got = send(merge_blocks, SEND_FAR)
+    merge_near_got = send(merge_blocks, SEND_NEAR)
+    expand_end = narrow_second(expand_quarters, expand_got)
+    mixed_quarters = settle("attend_output", 1, mixed_blocks, mixed_near_got, mixed_got_last)
+    shrink_new = adamw_update(
+        shrink_weight,
+        shrink_moment,
+        shrink_square,
+        unfold(finish(shrink_quarters, shrink_got, shrink_end), shrink_weight.shape[0]),
+        rate_shrink,
+    )
+    merge_far_got, merge_near_got, expand_end, mixed_quarters, vector_total, shrink_new = together(
+        merge_far_got, merge_near_got, expand_end, mixed_quarters, vector_total, shrink_new
+    )
+    merge_got_last = forward(merge_blocks, merge_far_got)
+    mixed_got = narrow_first(mixed_quarters)
+    vector_total = vector_total + swap_wide(vector_total, CORE)
+    vector_total = vector_total + swap_wide(vector_total, ACROSS)
+    merge_got_last, mixed_got, vector_total, expand_end = together(
+        merge_got_last, mixed_got, vector_total, expand_end
+    )
+    merge_quarters = settle("merge", 2, merge_blocks, merge_near_got, merge_got_last)
+    merge_got = narrow_first(merge_quarters)
+    mixed_end = narrow_second(mixed_quarters, mixed_got)
+    vector_total = vector_total + swap_wide(vector_total, ALONG)
+    expand_new = adamw_update(
+        expand_weight,
+        expand_moment,
+        expand_square,
+        finish(expand_quarters, expand_got, expand_end),
+        rate_expand,
+    )
+    merge_got, mixed_end, vector_total, expand_new = together(
+        merge_got, mixed_end, vector_total, expand_new
+    )
+    merge_end = narrow_second(merge_quarters, merge_got)
+    halves = vector_total.reshape(2, -1)
+    vector_total = pick(halves, high_bit) + swap_narrow(pick(halves, 1 - high_bit), 2)
+    halves = vector_total.reshape(2, -1)
+    vector_total = pick(halves, low_bit) + swap_narrow(pick(halves, 1 - low_bit), 1)
+    mixed_total = finish(mixed_quarters, mixed_got, mixed_end)
+    attend_new = adamw_update(
+        attend_weight, attend_moment, attend_square, mixed_total[:, :columns], rate_attend
+    )
+    output_new = adamw_update(
+        output_weight, output_moment, output_square, mixed_total[:, columns:], rate_output
+    )
+    merge_new = adamw_update(
+        merge_weight,
+        merge_moment,
+        merge_square,
+        unfold(finish(merge_quarters, merge_got, merge_end), merge_weight.shape[0]),
+        rate_merge,
+    )
+    vector_new = adamw_update(vectors, vector_moment, vector_square, vector_total, rate_vector)
+    return (
+        outputs,
+        input_gradient[None],
+        skip_gradient[None],
+        *merge_new,
+        *attend_new,
+        *output_new,
+        *expand_new,
+        *shrink_new,
+        *vector_new,
+    )
+
+
 def solution(mesh):
     in_specs = (
         P(("wide", "narrow"), None, None),
@@ -334,6 +1318,7 @@
         P("narrow"),
         P("narrow"),
     )
+    tuned = mesh.shape["wide"] == 8 and mesh.shape["narrow"] == 4
     return jax.shard_map(
-        on_device, mesh=mesh, in_specs=in_specs, out_specs=out_specs, check_vma=False
-    )
+        on_device if tuned else general_device, mesh=mesh, in_specs=in_specs, out_specs=out_specs, check_vma=False
+    )

time: 1200 us -> 499 us (0.42)
  waiting for transfers between devices: 799 us -> 125 us
  Pallas kernels: 0 us -> 198 us
  matrix products: 164 us -> 0 us
  blocking collectives: 140 us -> 0 us
  starting transfers between devices: 1.13 us -> 77 us
  between operations: 16.3 us -> 2.55 us
    reduce_scatter x6 -> x0, waiting for transfers between devices: 471 us -> none  [the longest x1 137 us: on_device(): lax.psum_scatter(shrink_gradient, 'wide', scatter_dimension=0, tiled=True)]
    all_gather x7 -> x0, waiting for transfers between devices: 203 us -> none  [the longest x1 62.3 us: on_device(): lax.all_gather(columns[3], 'wide', axis=0, tiled=True)]
    pallas_call x0 -> x22, Pallas kernels: none -> 198 us  [the longest x10 118 us: heavy(): pl.pallas_call(kernel, in_specs=[pl.BlockSpec(memory_space=pl.ANY)] * len...]
    dot_general x21 -> x0, matrix products: 164 us -> none  [the longest x5 47.2 us: weight_gradient(): lax.dot_general(flat_left, flat_right, (((0,), (0,)), ((), ())), preferre...]
    unnamed x21 -> x0, waiting for transfers between devices: 125 us -> none
    ppermute x0 -> x90, waiting for transfers between devices: none -> 125 us  [the longest x26 66 us: swap_narrow(): return lax.ppermute(value, 'narrow', [(i, i ^ bit) for i in range(4)])]
    all_gather x3 -> x0, blocking collectives: 78.3 us -> none  [the longest x1 32.1 us: on_device(): lax.all_gather(merge_low, 'narrow', axis=1, tiled=True)]
    ppermute x0 -> x90, starting transfers between devices: none -> 77 us  [the longest x64 48.7 us: swap_wide(): return lax.ppermute(value, 'wide', [(i, i ^ bit) for i in range(8)])]
  transfers between devices with their start and end apart: 17 -> 90, of which waited for: 14 -> 38; matrix products, arithmetic and copies ran while one was open for 17% -> 12% of each run, Pallas kernels for 0% -> 40%
where the time goes in v3:
time: 499 us; the launch traced here: 490 us
  Pallas kernels  198 us (40%)
  waiting for transfers between devices  125 us (25%)
  starting transfers between devices  77 us (15%)
  local copies, waits for them, and re-layouts  59 us (12%)
  other arithmetic  28.9 us (6%)
    pallas_call x10, Pallas kernels, heavy(): pl.pallas_call(kernel, in_specs=[pl.BlockSpec(memory_space=pl.ANY)] * len...  118 us
    ppermute x26, waiting for transfers between devices, swap_narrow(): return lax.ppermute(value, 'narrow', [(i, i ^ bit) for i in range(4)])  66 us
    ppermute x64, waiting for transfers between devices, swap_wide(): return lax.ppermute(value, 'wide', [(i, i ^ bit) for i in range(8)])  58.9 us
    ppermute x64, starting transfers between devices, swap_wide(): return lax.ppermute(value, 'wide', [(i, i ^ bit) for i in range(8)])  48.7 us
    pallas_call x4, Pallas kernels, pair_gradient(): pl.pallas_call(kernel, grid=(sum(steps),), in_specs=in_specs, out_specs=(...  44.6 us
    unnamed x225, local copies, waits for them, and re-layouts  28.5 us
    ppermute x26, starting transfers between devices, swap_narrow(): return lax.ppermute(value, 'narrow', [(i, i ^ bit) for i in range(4)])  28.3 us
    pallas_call x4, Pallas kernels, unarrange(): pl.pallas_call(kernel, out_shape=(shape,) * 4, scratch_shapes=[pltpu.VMEM...  21 us
  transfers between devices with their start and end apart: 90, of which 38 were waited for; matrix products, arithmetic and copies ran while one was open for 12% of the time, Pallas kernels for 40%

profile of v3, /device:TPU:0, one launch (start us, length us, event | category | flops | bytes accessed | tf_op | source)
XLA Modules:
  0.0 490.3 jit_solution(2306022330343988138)
XLA Ops:
  3.4 3.0 collective-permute-start
  6.4 2.6 collective-permute-start.1
  18.4 1.8 concatenate.75.refs_2_.refs_6_.refs_13_
  20.3 1.7 broadcast_select_fusion
  22.7 1.8 collective-permute-done.1.refs_2_
  24.4 2.6 shard_map.364
  31.6 4.6 collective-permute-start.5
  37.7 2.0 concatenate.76.refs_0_
  39.8 2.0 constant_dynamic-update-slice_fusion.10
  41.7 8.1 %collective-permute-done.5.refs_2_ = bf16[144,1152]{1,0:T(8,128)(2,1)} collective-permute-done((bf16[144,1152]{1,0:T(8,128)(2,1)}, bf16[144,1152]{1,0:T(8,128)(2,1)}, u32[]{:S(2)}, u32[]{:S(2)}) %collective-permute-start.5) | collective-permute-done | bytes 331808 | tf_op jit(solution)/shard_map/ppermute | solution.py:306
  59.2 3.0 collective-permute-done.6
  62.9 2.0 constant_dynamic-update-slice_fusion.9
  64.9 1.7 constant_dynamic-update-slice_fusion.8.refs_0_
  66.7 3.3 shard_map.365
  73.2 1.7 collective-permute-start.15
  74.9 2.6 copy.45.refs_6_
  77.5 2.9 pad_bitcast_fusion
  80.4 8.0 %shard_map.366 = (f32[258,1152]{1,0:T(8,128)}, bf16[258,1152]{1,0:T(8,128)(2,1)}, bf16[576,384]{1,0:T(8,128)(2,1)}, bf16[576,384]{1,0:T(8,128)(2,1)}) custom-call(bf16[576,1152]{1,0:T(8,128)(2,1)} %constant_dynamic-update-slice_fusion.8.refs_0_, bf16[288,1152]{1,0:T(8,128)(2,1)} %copy-done.22, bf16[288,1152]{1,0:T(8,128)(2,1)} %copy-done.23, ...), custom_call_target="tpu_custom_call" | custom-call | bytes 1024 | tf_op jit(solution)/shard_map/pallas_call | solution.py:643
  88.5 2.2 collective-permute-done.14.refs_2_
  90.7 11.0 %collective-permute-done.12.refs_1_.refs_7_ = bf16[144,4608]{1,0:T(8,128)(2,1)S(1)} collective-permute-done((bf16[144,4608]{1,0:T(8,128)(2,1)}, bf16[144,4608]{1,0:T(8,128)(2,1)S(1)}, u32[]{:S(2)}, u32[]{:S(2)}) %collective-permute-start.12) | collective-permute-done | bytes 1327136 | tf_op jit(solution)/shard_map/ppermute | solution.py:302
  106.0 9.1 %collective-permute-done.21.refs_3_ = bf16[144,1152]{1,0:T(8,128)(2,1)S(1)} collective-permute-done((bf16[144,1152]{1,0:T(8,128)(2,1)}, bf16[144,1152]{1,0:T(8,128)(2,1)S(1)}, u32[]{:S(2)}, u32[]{:S(2)}) %collective-permute-start.21) | collective-permute-done | bytes 331808 | tf_op jit(solution)/shard_map/ppermute | solution.py:306
  115.1 5.1 %collective-permute-done.18 = bf16[64,4608]{1,0:T(8,128)(2,1)S(1)} collective-permute-done((bf16[64,4608]{1,0:T(8,128)(2,1)S(1)}, bf16[64,4608]{1,0:T(8,128)(2,1)S(1)}, u32[]{:S(2)}, u32[]{:S(2)}) %collective-permute-start.18) | collective-permute-done | bytes 589856 | tf_op jit(solution)/shard_map/ppermute | solution.py:302
  120.1 1.8 collective-permute-done.17
  123.1 3.7 shard_map.367
  129.1 1.7 collective-permute-start.25
  132.4 11.1 %shard_map.368 = (bf16[258,3456]{1,0:T(8,128)(2,1)}, f32[8,258,258]{2,1,0:T(8,128)}, bf16[258,576]{1,0:T(8,128)(2,1)}) custom-call(bf16[288,4608]{1,0:T(8,128)(2,1)} %copy-done, bf16[144,4608]{1,0:T(8,128)(2,1)} %copy-done.2, bf16[144,4608]{1,0:T(8,128)(2,1)} %copy-done.3, bf16[288,4608]{1,0:T(8,128)(2,1)} %copy-done.1, bf16[144,4608]{1,0:T(8,128)(2,1)} %copy-done.6, ...), custom_call_target="tpu_custom_call" | custom-call | bytes 1024 | tf_op jit(solution)/shard_map/pallas_call | solution.py:643
  143.5 1.8 collective-permute-done.24.refs_2_
  145.3 12.3 %collective-permute-done.22.refs_1_ = bf16[144,4608]{1,0:T(8,128)(2,1)S(1)} collective-permute-done((bf16[144,4608]{1,0:T(8,128)(2,1)}, bf16[144,4608]{1,0:T(8,128)(2,1)S(1)}, u32[]{:S(2)}, u32[]{:S(2)}) %collective-permute-start.22) | collective-permute-done | bytes 1327136 | tf_op jit(solution)/shard_map/ppermute | solution.py:302
  163.1 13.9 %shard_map.369 = (f32[8,258,258]{2,1,0:T(8,128)}, f32[258,1152]{1,0:T(8,128)}, bf16[258,1152]{1,0:T(8,128)(2,1)}, bf16[1152,384]{1,0:T(8,128)(2,1)}, bf16[1152,384]{1,0:T(8,128)(2,1)}) custom-call(bf16[288,4608]{1,0:T(8,128)(2,1)} %copy-done, bf16[144,4608]{1,0:T(8,128)(2,1)} %copy-done.2, bf16[144,4608]{1,0:T(8,128)(2,1)} %copy-done.3, ...), custom_call_target="tpu_custom_call" | custom-call | bytes 1024 | tf_op jit(solution)/shard_map/pallas_call | solution.py:643
  179.9 4.3 shard_map.370
  188.6 16.2 %shard_map.371 = (bf16[258,4608]{1,0:T(8,128)(2,1)}, f32[258,4608]{1,0:T(8,128)}, bf16[2304,384]{1,0:T(8,128)(2,1)}, bf16[2304,384]{1,0:T(8,128)(2,1)}) custom-call(bf16[288,4608]{1,0:T(8,128)(2,1)} %copy-done.4, bf16[144,4608]{1,0:T(8,128)(2,1)} %copy-done.11, bf16[144,4608]{1,0:T(8,128)(2,1)} %collective-permute-done.23.refs_2_, ...), custom_call_target="tpu_custom_call" | custom-call | bytes 1024 | tf_op jit(solution)/shard_map/pallas_call | solution.py:643
  204.9 10.1 %collective-permute-done.32.refs_1_ = bf16[576,1152]{1,0:T(8,128)(2,1)S(1)} collective-permute-done((bf16[576,1152]{1,0:T(8,128)(2,1)}, bf16[576,1152]{1,0:T(8,128)(2,1)S(1)}, u32[]{:S(2)}, u32[]{:S(2)}) %collective-permute-start.32) | collective-permute-done | bytes 1327136 | tf_op jit(solution)/shard_map/ppermute | solution.py:302
  223.3 12.3 %shard_map.372 = (bf16[288,1152]{1,0:T(8,128)(2,1)}, bf16[288,1152]{1,0:T(8,128)(2,1)}, bf16[288,1152]{1,0:T(8,128)(2,1)}, bf16[288,1152]{1,0:T(8,128)(2,1)}, bf...) custom-call(bf16[2304,384]{1,0:T(8,128)(2,1)} %get-tuple-element.350, ...), custom_call_target="tpu_custom_call" | custom-call | bytes 1024 | tf_op jit(solution)/shard_map/pallas_call | solution.py:480
  237.6 2.4 pad_maximum_fusion.2.refs_0_
  246.7 11.9 %shard_map.373 = (bf16[258,4608]{1,0:T(8,128)(2,1)}, f32[1,4608]{1,0:T(1,128)}) custom-call(bf16[1152,1152]{1,0:T(8,128)(2,1)} %copy-done.5, bf16[576,1152]{1,0:T(8,128)(2,1)} %copy-done.12, bf16[576,1152]{1,0:T(8,128)(2,1)} %collective-permute-done.33.refs_2_, bf16[1152,1152]{1,0:T(8,128)(2,1)} %copy-done.8, bf16[576,1152]{1,0:T(8,128)(2,1)} %copy-done.20, ...), custom_call_target="tpu_custom_call" | custom-call | bytes 1024 | tf_op jit(solution)/shard_map/pallas_call | solution.py:643
  258.7 10.6 %shard_map.374 = bf16[258,1152]{1,0:T(8,128)(2,1)} custom-call(bf16[1152,1152]{1,0:T(8,128)(2,1)} %copy-done.5, bf16[576,1152]{1,0:T(8,128)(2,1)} %copy-done.12, bf16[576,1152]{1,0:T(8,128)(2,1)} %collective-permute-done.33.refs_2_, bf16[1152,1152]{1,0:T(8,128)(2,1)} %copy-done.8, bf16[576,1152]{1,0:T(8,128)(2,1)} %copy-done.20, ...), custom_call_target="tpu_custom_call" | custom-call | bytes 1024 | tf_op jit(solution)/shard_map/pallas_call | solution.py:643
  269.3 2.6 collective-permute-done.43.refs_1_
  276.5 1.8 collective-permute-done.48
  280.8 11.8 %shard_map.375 = (bf16[80,4608]{1,0:T(8,128)(2,1)}, bf16[80,4608]{1,0:T(8,128)(2,1)}, bf16[80,4608]{1,0:T(8,128)(2,1)}, bf16[80,4608]{1,0:T(8,128)(2,1)}, bf16[6...) custom-call(bf16[576,384]{1,0:T(8,128)(2,1)} %get-tuple-element.605.refs_0_,, ...), custom_call_target="tpu_custom_call" | custom-call | bytes 1024 | tf_op jit(solution)/shard_map/pallas_call | solution.py:480
  295.7 14.7 %shard_map.376 = (f32[258,1152]{1,0:T(8,128)}, bf16[258,1152]{1,0:T(8,128)(2,1)}, f32[4,1152]{1,0:T(4,128)}, bf16[258,1152]{1,0:T(8,128)(2,1)}) custom-call(bf16[288,4608]{1,0:T(8,128)(2,1)} %copy-done.4, bf16[144,4608]{1,0:T(8,128)(2,1)} %copy-done.11, bf16[144,4608]{1,0:T(8,128)(2,1)} %collective-permute-done.23.refs_2_, bf16[288,4608]{1,0:T(8,128)(2,1)} %copy-done.7, ...), custom_call_target="tpu_custom_call" | custom-call | bytes 1024 | tf_op jit(solution)/shard_map/pallas_call | solution.py:643
  310.7 2.0 collective-permute-done.51
  314.8 15.6 %shard_map.378.refs_4_.refs_6_ = bf16[258,3456]{1,0:T(8,128)(2,1)} custom-call(bf16[258,3456]{1,0:T(8,128)(2,1)} %get-tuple-element.328.refs_6_.heads_ref, f32[8,258,258]{2,1,0:T(8,128)} %get-tuple-element.425.first_ref, f32[8,258,258]{2,1,0:T(8,128)} %get-tuple-element.426.second_ref, bf16[258,1152]{1,0:T(8,128)(2,1)} %get-tuple-element.427.delta_ref), custom_call_target="tpu_custom_call" | custom-call | bytes 1024 | tf_op jit(solution)/shard_map/pallas_call | solution.py:643
  333.9 5.2 %shard_map.377 = (bf16[144,1152]{1,0:T(8,128)(2,1)}, bf16[144,1152]{1,0:T(8,128)(2,1)}, bf16[144,1152]{1,0:T(8,128)(2,1)}, bf16[144,1152]{1,0:T(8,128)(2,1)}) custom-call(bf16[288,1152]{1,0:T(8,128)(2,1)} %get-tuple-element.410.refs_0_, bf16[288,1152]{1,0:T(8,128)(2,1)} %copy-done.55, bf16[288,1152]{1,0:T(8,128)(2,1)} %copy-done.58, ...), custom_call_target="tpu_custom_call" | custom-call | bytes 1024 | tf_op jit(solution)/shard_map/pallas_call | solution.py:531
  340.5 12.4 %shard_map.379 = (bf16[80,4608]{1,0:T(8,128)(2,1)}, bf16[80,4608]{1,0:T(8,128)(2,1)}, bf16[80,4608]{1,0:T(8,128)(2,1)}, bf16[80,4608]{1,0:T(8,128)(2,1)}, bf16[6...) custom-call(bf16[576,384]{1,0:T(8,128)(2,1)} %get-tuple-element.420.refs_0_,, ...), custom_call_target="tpu_custom_call" | custom-call | bytes 1024 | tf_op jit(solution)/shard_map/pallas_call | solution.py:480
  358.0 9.7 %shard_map.380 = (bf16[258,1152]{1,0:T(8,128)(2,1)}, f32[3,1152]{1,0:T(4,128)}) custom-call(bf16[288,4608]{1,0:T(8,128)(2,1)} %copy-done, bf16[144,4608]{1,0:T(8,128)(2,1)} %copy-done.2, bf16[144,4608]{1,0:T(8,128)(2,1)} %copy-done.3, bf16[288,4608]{1,0:T(8,128)(2,1)} %copy-done.1, bf16[144,4608]{1,0:T(8,128)(2,1)} %copy-done.6, ...), custom_call_target="tpu_custom_call" | custom-call | bytes 1024 | tf_op jit(solution)/shard_map/pallas_call | solution.py:643
  367.7 4.5 collective-permute-done.63
  376.7 2.0 add_convert_fusion.4
  378.8 10.0 %collective-permute-done.66 = bf16[144,1152]{1,0:T(8,128)(2,1)S(1)} collective-permute-done((bf16[144,1152]{1,0:T(8,128)(2,1)S(1)}, bf16[144,1152]{1,0:T(8,128)(2,1)S(1)}, u32[]{:S(2)}, u32[]{:S(2)}) %collective-permute-start.66) | collective-permute-done | bytes 331808 | tf_op jit(solution)/shard_map/ppermute | solution.py:306
  389.7 5.0 %shard_map.381 = (bf16[144,1152]{1,0:T(8,128)(2,1)}, bf16[144,1152]{1,0:T(8,128)(2,1)}, bf16[144,1152]{1,0:T(8,128)(2,1)}, bf16[144,1152]{1,0:T(8,128)(2,1)}) custom-call(bf16[80,4608]{1,0:T(8,128)(2,1)} %get-tuple-element.457.refs_0_, bf16[80,4608]{1,0:T(8,128)(2,1)} %collective-permute-done.56.refs_1_, bf16[80,4608]{1,0:T(8,128)(2,1)} %copy-done.50, ...), custom_call_target="tpu_custom_call" | custom-call | bytes 1024 | tf_op jit(solution)/shard_map/pallas_call | solution.py:531
  394.7 6.5 %shard_map.382 = (bf16[258,1152]{1,0:T(8,128)(2,1)}, bf16[258,1152]{1,0:T(8,128)(2,1)}) custom-call(bf16[576,1152]{1,0:T(8,128)(2,1)} %constant_dynamic-update-slice_fusion.8.refs_0_, bf16[288,1152]{1,0:T(8,128)(2,1)} %copy-done.22, bf16[288,1152]{1,0:T(8,128)(2,1)} %copy-done.23, bf16[576,1152]{1,0:T(8,128)(2,1)} %collective-permute-done.16.refs_3_, ...), custom_call_target="tpu_custom_call" | custom-call | bytes 1024 | tf_op jit(solution)/shard_map/pallas_call | solution.py:643
  401.3 2.0 collective-permute-start.71
  404.3 8.1 %shard_map.383 = (bf16[144,1152]{1,0:T(8,128)(2,1)}, bf16[144,1152]{1,0:T(8,128)(2,1)}, bf16[144,1152]{1,0:T(8,128)(2,1)}, bf16[144,1152]{1,0:T(8,128)(2,1)}, bf...) custom-call(bf16[1152,384]{1,0:T(8,128)(2,1)} %get-tuple-element.480, ...), custom_call_target="tpu_custom_call" | custom-call | bytes 1024 | tf_op jit(solution)/shard_map/pallas_call | solution.py:480
  412.5 5.5 %collective-permute-done.71 = bf16[144,1152]{1,0:T(8,128)(2,1)} collective-permute-done((bf16[144,1152]{1,0:T(8,128)(2,1)}, bf16[144,1152]{1,0:T(8,128)(2,1)}, u32[]{:S(2)}, u32[]{:S(2)}) %collective-permute-start.71) | collective-permute-done | bytes 331808 | tf_op jit(solution)/shard_map/ppermute | solution.py:306
  421.7 1.7 collective-permute-start.74
  423.8 6.8 %shard_map.384 = (bf16[144,1152]{1,0:T(8,128)(2,1)}, bf16[144,1152]{1,0:T(8,128)(2,1)}, bf16[144,1152]{1,0:T(8,128)(2,1)}, bf16[144,1152]{1,0:T(8,128)(2,1)}) custom-call(bf16[80,4608]{1,0:T(8,128)(2,1)} %get-tuple-element.500.refs_0_, bf16[80,4608]{1,0:T(8,128)(2,1)} %collective-permute-done.64.refs_1_, bf16[80,4608]{1,0:T(8,128)(2,1)} %copy-done.49, ...), custom_call_target="tpu_custom_call" | custom-call | bytes 1024 | tf_op jit(solution)/shard_map/pallas_call | solution.py:531
  432.3 3.5 collective-permute-done.76
  438.9 1.7 collective-permute-start.77
  451.7 4.6 collective-permute-done.80
  458.3 3.9 shard_map.385
  464.3 2.7 multiply_subtract_fusion.1
  467.0 7.4 %collective-permute-done.83 = bf16[144,576]{1,0:T(8,128)(2,1)S(1)} collective-permute-done((bf16[144,576]{1,0:T(8,128)(2,1)}, bf16[144,576]{1,0:T(8,128)(2,1)S(1)}, u32[]{:S(2)}, u32[]{:S(2)}) %collective-permute-start.83) | collective-permute-done | bytes 165920 | tf_op jit(solution)/shard_map/ppermute | solution.py:306
  474.4 2.0 collective-permute-done.84
  477.4 2.9 collective-permute-start.87
  484.8 2.8 collective-permute-done.89
  (458 shorter events, 131.1 us)
Async XLA Ops:
  3.4 19.2 %collective-permute-start = (bf16[160,576]{1,0:T(8,128)(2,1)}, bf16[160,576]{1,0:T(8,128)(2,1)}, u32[]{:S(2)}, u32[]{:S(2)}) collective-permute-start(bf16[160,576]{1,0:T(8,128)(2,1)} %pad_maximum_fusion.8.refs_0_), channel_id=1, source_target_pairs={{0,1},{1,0},{2,3},{3,2},{4,5},{5,4},{6,7},{7,6},{8,9},{9,8},{10,11... | collective-permute-start | bytes 552968 | tf_op jit(solution)/shard_map/ppermute | solution.py:306
  6.4 18.0 %collective-permute-start.1 = (bf16[160,576]{1,0:T(8,128)(2,1)}, bf16[160,576]{1,0:T(8,128)(2,1)}, u32[]{:S(2)}, u32[]{:S(2)}) collective-permute-start(bf16[160,576]{1,0:T(8,128)(2,1)} %pad_maximum_fusion.8.refs_0_), channel_id=1, source_target_pairs={{0,2},{1,3},{2,0},{3,1},{4,6},{5,7},{6,4},{7,5},{8,10},{9,11},{10,... | collective-permute-start | bytes 552968 | tf_op jit(solution)/shard_map/ppermute | solution.py:306
  9.0 15.4 %collective-permute-start.2 = (bf16[160,576]{1,0:T(8,128)(2,1)}, bf16[160,576]{1,0:T(8,128)(2,1)}, u32[]{:S(2)}, u32[]{:S(2)}) collective-permute-start(bf16[160,576]{1,0:T(8,128)(2,1)} %pad_maximum_fusion.8.refs_0_), channel_id=1, source_target_pairs={{0,3},{1,2},{2,1},{3,0},{4,7},{5,6},{6,5},{7,4},{8,11},{9,10},{10,... | collective-permute-start | bytes 552968 | tf_op jit(solution)/shard_map/ppermute | solution.py:306
  27.1 22.7 %collective-permute-start.3 = (bf16[288,1152]{1,0:T(8,128)(2,1)}, bf16[288,1152]{1,0:T(8,128)(2,1)S(1)}, u32[]{:S(2)}, u32[]{:S(2)}) collective-permute-start(bf16[288,1152]{1,0:T(8,128)(2,1)} %get-tuple-element.288), channel_id=1, source_target_pairs={{0,8},{4,12},{8,0},{12,4},{16,24},{20,28},{24,16},{28,20},{1,9},{5... | collective-permute-start | bytes 1990664 | tf_op jit(solution)/shard_map/ppermute | solution.py:302
  28.6 21.2 %collective-permute-start.4 = (bf16[288,1152]{1,0:T(8,128)(2,1)}, bf16[288,1152]{1,0:T(8,128)(2,1)S(1)}, u32[]{:S(2)}, u32[]{:S(2)}) collective-permute-start(bf16[288,1152]{1,0:T(8,128)(2,1)} %get-tuple-element.288), channel_id=1, source_target_pairs={{0,16},{4,20},{8,24},{12,28},{16,0},{20,4},{24,8},{28,12},{1,17},{... | collective-permute-start | bytes 1990664 | tf_op jit(solution)/shard_map/ppermute | solution.py:302
  31.6 18.2 %collective-permute-start.5 = (bf16[144,1152]{1,0:T(8,128)(2,1)}, bf16[144,1152]{1,0:T(8,128)(2,1)}, u32[]{:S(2)}, u32[]{:S(2)}) collective-permute-start(bf16[144,1152]{1,0:T(8,128)(2,1)} %pad_maximum_fusion.7.refs_0_), channel_id=1, source_target_pairs={{0,2},{1,3},{2,0},{3,1},{4,6},{5,7},{6,4},{7,5},{8,10},{9,11},{10,... | collective-permute-start | bytes 995336 | tf_op jit(solution)/shard_map/ppermute | solution.py:306
  39.7 13.8 %collective-permute-start.10 = (bf16[144,1152]{1,0:T(8,128)(2,1)}, bf16[144,1152]{1,0:T(8,128)(2,1)}, u32[]{:S(2)}, u32[]{:S(2)}) collective-permute-start(bf16[144,1152]{1,0:T(8,128)(2,1)} %pad_maximum_fusion.7.refs_0_), channel_id=1, source_target_pairs={{0,1},{1,0},{2,3},{3,2},{4,5},{5,4},{6,7},{7,6},{8,9},{9,8},{10,11... | collective-permute-start | bytes 995336 | tf_op jit(solution)/shard_map/ppermute | solution.py:306
  66.7 13.8 %collective-permute-start.16 = (bf16[576,1152]{1,0:T(8,128)(2,1)}, bf16[576,1152]{1,0:T(8,128)(2,1)}, u32[]{:S(2)}, u32[]{:S(2)}) collective-permute-start(bf16[576,1152]{1,0:T(8,128)(2,1)} %constant_dynamic-update-slice_fusion.8.refs_0_), channel_id=1, source_target_pairs={{0,4},{4,0},{8,12},{12,8},{16,20},{20,16},{24,28},{28,24},{1,5},{5... | collective-permute-start | bytes 3981320 | tf_op jit(solution)/shard_map/ppermute | solution.py:302
  70.0 31.7 %collective-permute-start.12 = (bf16[144,4608]{1,0:T(8,128)(2,1)}, bf16[144,4608]{1,0:T(8,128)(2,1)S(1)}, u32[]{:S(2)}, u32[]{:S(2)}) collective-permute-start(bf16[144,4608]{1,0:T(8,128)(2,1)} %shard_map.365), channel_id=1, source_target_pairs={{0,8},{4,12},{8,0},{12,4},{16,24},{20,28},{24,16},{28,20},{1,9},{5... | collective-permute-start | bytes 3981320 | tf_op jit(solution)/shard_map/ppermute | solution.py:302
  71.5 31.5 %collective-permute-start.13 = (bf16[144,4608]{1,0:T(8,128)(2,1)}, bf16[144,4608]{1,0:T(8,128)(2,1)S(1)}, u32[]{:S(2)}, u32[]{:S(2)}) collective-permute-start(bf16[144,4608]{1,0:T(8,128)(2,1)} %shard_map.365), channel_id=1, source_target_pairs={{0,16},{4,20},{8,24},{12,28},{16,0},{20,4},{24,8},{28,12},{1,17},{... | collective-permute-start | bytes 3981320 | tf_op jit(solution)/shard_map/ppermute | solution.py:302
  73.0 17.7 %collective-permute-start.14 = (bf16[144,1152]{1,0:T(8,128)(2,1)}, bf16[144,1152]{1,0:T(8,128)(2,1)}, u32[]{:S(2)}, u32[]{:S(2)}) collective-permute-start(bf16[144,1152]{1,0:T(8,128)(2,1)} %convert_element_type.177.refs_0_), channel_id=1, source_target_pairs={{0,2},{1,3},{2,0},{3,1},{4,6},{5,7},{6,4},{7,5},{8,10},{9,11},{10,... | collective-permute-start | bytes 995336 | tf_op jit(solution)/shard_map/ppermute | solution.py:306
  73.2 17.5 %collective-permute-start.15 = (bf16[144,1152]{1,0:T(8,128)(2,1)}, bf16[144,1152]{1,0:T(8,128)(2,1)}, u32[]{:S(2)}, u32[]{:S(2)}) collective-permute-start(bf16[144,1152]{1,0:T(8,128)(2,1)} %convert_element_type.177.refs_0_), channel_id=1, source_target_pairs={{0,1},{1,0},{2,3},{3,2},{4,5},{5,4},{6,7},{7,6},{8,9},{9,8},{10,11... | collective-permute-start | bytes 995336 | tf_op jit(solution)/shard_map/ppermute | solution.py:306
  102.9 19.0 %collective-permute-start.19 = (bf16[144,4608]{1,0:T(8,128)(2,1)S(1)}, bf16[144,4608]{1,0:T(8,128)(2,1)S(1)}, u32[]{:S(2)}, u32[]{:S(2)}) collective-permute-start(bf16[144,4608]{1,0:T(8,128)(2,1)S(1)} %collective-permute-done.12.refs_1_.refs_7_), channel_id=1, source_target_pairs={{0,4},{4,0},{8,12},{12,8},{16,20},{20,16},{24,28},{28,24},{1,5},{5... | collective-permute-start | bytes 3981320 | tf_op jit(solution)/shard_map/ppermute | solution.py:302
  102.9 19.0 %collective-permute-start.20 = (bf16[144,4608]{1,0:T(8,128)(2,1)S(1)}, bf16[144,4608]{1,0:T(8,128)(2,1)}, u32[]{:S(2)}, u32[]{:S(2)}) collective-permute-start(bf16[144,4608]{1,0:T(8,128)(2,1)S(1)} %collective-permute-done.13.refs_2_.refs_8_), channel_id=1, source_target_pairs={{0,4},{4,0},{8,12},{12,8},{16,20},{20,16},{24,28},{28,24},{1,5},{5... | collective-permute-start | bytes 3981320 | tf_op jit(solution)/shard_map/ppermute | solution.py:302
  103.5 18.5 %collective-permute-start.17 = (bf16[80,4608]{1,0:T(8,128)(2,1)S(1)}, bf16[80,4608]{1,0:T(8,128)(2,1)S(1)}, u32[]{:S(2)}, u32[]{:S(2)}) collective-permute-start(bf16[80,4608]{1,0:T(8,128)(2,1)S(1)} %slice.933), channel_id=1, source_target_pairs={{0,16},{4,20},{8,24},{12,28},{16,0},{20,4},{24,8},{28,12},{1,17},{... | collective-permute-start | bytes 2211848 | tf_op jit(solution)/shard_map/ppermute | solution.py:302
  105.1 15.0 %collective-permute-start.18 = (bf16[64,4608]{1,0:T(8,128)(2,1)S(1)}, bf16[64,4608]{1,0:T(8,128)(2,1)S(1)}, u32[]{:S(2)}, u32[]{:S(2)}) collective-permute-start(bf16[64,4608]{1,0:T(8,128)(2,1)S(1)} %slice.934), channel_id=1, source_target_pairs={{0,8},{4,12},{8,0},{12,4},{16,24},{20,28},{24,16},{28,20},{1,9},{5... | collective-permute-start | bytes 1769480 | tf_op jit(solution)/shard_map/ppermute | solution.py:302
  126.8 30.8 %collective-permute-start.22 = (bf16[144,4608]{1,0:T(8,128)(2,1)}, bf16[144,4608]{1,0:T(8,128)(2,1)S(1)}, u32[]{:S(2)}, u32[]{:S(2)}) collective-permute-start(bf16[144,4608]{1,0:T(8,128)(2,1)} %shard_map.367), channel_id=1, source_target_pairs={{0,8},{4,12},{8,0},{12,4},{16,24},{20,28},{24,16},{28,20},{1,9},{5... | collective-permute-start | bytes 3981320 | tf_op jit(solution)/shard_map/ppermute | solution.py:302
  127.4 30.6 %collective-permute-start.23 = (bf16[144,4608]{1,0:T(8,128)(2,1)}, bf16[144,4608]{1,0:T(8,128)(2,1)}, u32[]{:S(2)}, u32[]{:S(2)}) collective-permute-start(bf16[144,4608]{1,0:T(8,128)(2,1)} %shard_map.367), channel_id=1, source_target_pairs={{0,16},{4,20},{8,24},{12,28},{16,0},{20,4},{24,8},{28,12},{1,17},{... | collective-permute-start | bytes 3981320 | tf_op jit(solution)/shard_map/ppermute | solution.py:302
  128.9 16.4 %collective-permute-start.24 = (bf16[144,1152]{1,0:T(8,128)(2,1)S(1)}, bf16[144,1152]{1,0:T(8,128)(2,1)S(1)}, u32[]{:S(2)}, u32[]{:S(2)}) collective-permute-start(bf16[144,1152]{1,0:T(8,128)(2,1)S(1)} %copy-done.36), channel_id=1, source_target_pairs={{0,2},{1,3},{2,0},{3,1},{4,6},{5,7},{6,4},{7,5},{8,10},{9,11},{10,... | collective-permute-start | bytes 995336 | tf_op jit(solution)/shard_map/ppermute | solution.py:306
  129.1 16.2 %collective-permute-start.25 = (bf16[144,1152]{1,0:T(8,128)(2,1)S(1)}, bf16[144,1152]{1,0:T(8,128)(2,1)}, u32[]{:S(2)}, u32[]{:S(2)}) collective-permute-start(bf16[144,1152]{1,0:T(8,128)(2,1)S(1)} %copy-done.36), channel_id=1, source_target_pairs={{0,1},{1,0},{2,3},{3,2},{4,5},{5,4},{6,7},{7,6},{8,9},{9,8},{10,11... | collective-permute-start | bytes 995336 | tf_op jit(solution)/shard_map/ppermute | solution.py:306
  158.0 19.1 %collective-permute-start.29 = (bf16[144,4608]{1,0:T(8,128)(2,1)S(1)}, bf16[144,4608]{1,0:T(8,128)(2,1)S(1)}, u32[]{:S(2)}, u32[]{:S(2)}) collective-permute-start(bf16[144,4608]{1,0:T(8,128)(2,1)S(1)} %collective-permute-done.22.refs_1_), channel_id=1, source_target_pairs={{0,4},{4,0},{8,12},{12,8},{16,20},{20,16},{24,28},{28,24},{1,5},{5... | collective-permute-start | bytes 3981320 | tf_op jit(solution)/shard_map/ppermute | solution.py:302
  158.0 19.1 %collective-permute-start.30 = (bf16[144,4608]{1,0:T(8,128)(2,1)}, bf16[144,4608]{1,0:T(8,128)(2,1)S(1)}, u32[]{:S(2)}, u32[]{:S(2)}) collective-permute-start(bf16[144,4608]{1,0:T(8,128)(2,1)} %collective-permute-done.23.refs_2_), channel_id=1, source_target_pairs={{0,4},{4,0},{8,12},{12,8},{16,20},{20,16},{24,28},{28,24},{1,5},{5... | collective-permute-start | bytes 3981320 | tf_op jit(solution)/shard_map/ppermute | solution.py:302
  158.5 18.5 %collective-permute-start.27 = (bf16[80,4608]{1,0:T(8,128)(2,1)S(1)}, bf16[80,4608]{1,0:T(8,128)(2,1)S(1)}, u32[]{:S(2)}, u32[]{:S(2)}) collective-permute-start(bf16[80,4608]{1,0:T(8,128)(2,1)S(1)} %slice.935), channel_id=1, source_target_pairs={{0,16},{4,20},{8,24},{12,28},{16,0},{20,4},{24,8},{28,12},{1,17},{... | collective-permute-start | bytes 2211848 | tf_op jit(solution)/shard_map/ppermute | solution.py:302
  161.2 15.8 %collective-permute-start.28 = (bf16[64,4608]{1,0:T(8,128)(2,1)S(1)}, bf16[64,4608]{1,0:T(8,128)(2,1)}, u32[]{:S(2)}, u32[]{:S(2)}) collective-permute-start(bf16[64,4608]{1,0:T(8,128)(2,1)S(1)} %slice.936), channel_id=1, source_target_pairs={{0,8},{4,12},{8,0},{12,4},{16,24},{20,28},{24,16},{28,20},{1,9},{5... | collective-permute-start | bytes 1769480 | tf_op jit(solution)/shard_map/ppermute | solution.py:302
  162.8 14.3 %collective-permute-start.31 = (bf16[144,1152]{1,0:T(8,128)(2,1)}, bf16[144,1152]{1,0:T(8,128)(2,1)}, u32[]{:S(2)}, u32[]{:S(2)}) collective-permute-start(bf16[144,1152]{1,0:T(8,128)(2,1)} %copy-done.88), channel_id=1, source_target_pairs={{0,1},{1,0},{2,3},{3,2},{4,5},{5,4},{6,7},{7,6},{8,9},{9,8},{10,11... | collective-permute-start | bytes 995336 | tf_op jit(solution)/shard_map/ppermute | solution.py:306
  184.2 30.9 %collective-permute-start.32 = (bf16[576,1152]{1,0:T(8,128)(2,1)}, bf16[576,1152]{1,0:T(8,128)(2,1)S(1)}, u32[]{:S(2)}, u32[]{:S(2)}) collective-permute-start(bf16[576,1152]{1,0:T(8,128)(2,1)} %shard_map.370), channel_id=1, source_target_pairs={{0,8},{4,12},{8,0},{12,4},{16,24},{20,28},{24,16},{28,20},{1,9},{5... | collective-permute-start | bytes 3981320 | tf_op jit(solution)/shard_map/ppermute | solution.py:302
  185.6 30.7 %collective-permute-start.33 = (bf16[576,1152]{1,0:T(8,128)(2,1)}, bf16[576,1152]{1,0:T(8,128)(2,1)}, u32[]{:S(2)}, u32[]{:S(2)}) collective-permute-start(bf16[576,1152]{1,0:T(8,128)(2,1)} %shard_map.370), channel_id=1, source_target_pairs={{0,16},{4,20},{8,24},{12,28},{16,0},{20,4},{24,8},{28,12},{1,17},{... | collective-permute-start | bytes 3981320 | tf_op jit(solution)/shard_map/ppermute | solution.py:302
  187.1 17.8 %collective-permute-start.34 = (bf16[258,1152]{1,0:T(8,128)(2,1)S(1)}, bf16[258,1152]{1,0:T(8,128)(2,1)S(1)}, u32[]{:S(2)}, u32[]{:S(2)}) collective-permute-start(bf16[258,1152]{1,0:T(8,128)(2,1)S(1)} %concatenate.75.refs_2_.refs_6_.refs_13_), channel_id=1, source_target_pairs={{0,4},{4,0},{8,12},{12,8},{16,20},{20,16},{24,28},{28,24},{1,5},{5... | collective-permute-start | bytes 1783304 | tf_op jit(solution)/shard_map/ppermute | solution.py:302
  216.3 21.3 %collective-permute-start.38 = (bf16[576,1152]{1,0:T(8,128)(2,1)S(1)}, bf16[576,1152]{1,0:T(8,128)(2,1)S(1)}, u32[]{:S(2)}, u32[]{:S(2)}) collective-permute-start(bf16[576,1152]{1,0:T(8,128)(2,1)S(1)} %collective-permute-done.32.refs_1_), channel_id=1, source_target_pairs={{0,4},{4,0},{8,12},{12,8},{16,20},{20,16},{24,28},{28,24},{1,5},{5... | collective-permute-start | bytes 3981320 | tf_op jit(solution)/shard_map/ppermute | solution.py:302
  216.8 20.8 %collective-permute-start.39 = (bf16[576,1152]{1,0:T(8,128)(2,1)}, bf16[576,1152]{1,0:T(8,128)(2,1)S(1)}, u32[]{:S(2)}, u32[]{:S(2)}) collective-permute-start(bf16[576,1152]{1,0:T(8,128)(2,1)} %collective-permute-done.33.refs_2_), channel_id=1, source_target_pairs={{0,4},{4,0},{8,12},{12,8},{16,20},{20,16},{24,28},{28,24},{1,5},{5... | collective-permute-start | bytes 3981320 | tf_op jit(solution)/shard_map/ppermute | solution.py:302
  218.8 17.7 %collective-permute-start.36 = (bf16[288,1152]{1,0:T(8,128)(2,1)}, bf16[288,1152]{1,0:T(8,128)(2,1)}, u32[]{:S(2)}, u32[]{:S(2)}) collective-permute-start(bf16[288,1152]{1,0:T(8,128)(2,1)} %slice.937), channel_id=1, source_target_pairs={{0,16},{4,20},{8,24},{12,28},{16,0},{20,4},{24,8},{28,12},{1,17},{... | collective-permute-start | bytes 1990664 | tf_op jit(solution)/shard_map/ppermute | solution.py:302
  220.4 17.1 %collective-permute-start.37 = (bf16[288,1152]{1,0:T(8,128)(2,1)S(1)}, bf16[288,1152]{1,0:T(8,128)(2,1)}, u32[]{:S(2)}, u32[]{:S(2)}) collective-permute-start(bf16[288,1152]{1,0:T(8,128)(2,1)S(1)} %slice.938), channel_id=1, source_target_pairs={{0,8},{4,12},{8,0},{12,4},{16,24},{20,28},{24,16},{28,20},{1,9},{5... | collective-permute-start | bytes 1990664 | tf_op jit(solution)/shard_map/ppermute | solution.py:302
  240.1 29.1 %collective-permute-start.41 = (bf16[288,1152]{1,0:T(8,128)(2,1)}, bf16[288,1152]{1,0:T(8,128)(2,1)S(1)}, u32[]{:S(2)}, u32[]{:S(2)}) collective-permute-start(bf16[288,1152]{1,0:T(8,128)(2,1)} %get-tuple-element.361), channel_id=1, source_target_pairs={{0,8},{4,12},{8,0},{12,4},{16,24},{20,28},{24,16},{28,20},{1,9},{5... | collective-permute-start | bytes 1990664 | tf_op jit(solution)/shard_map/ppermute | solution.py:302
  240.7 28.5 %collective-permute-start.42 = (bf16[288,1152]{1,0:T(8,128)(2,1)}, bf16[288,1152]{1,0:T(8,128)(2,1)S(1)}, u32[]{:S(2)}, u32[]{:S(2)}) collective-permute-start(bf16[288,1152]{1,0:T(8,128)(2,1)} %get-tuple-element.362), channel_id=1, source_target_pairs={{0,16},{4,20},{8,24},{12,28},{16,0},{20,4},{24,8},{28,12},{1,17},{... | collective-permute-start | bytes 1990664 | tf_op jit(solution)/shard_map/ppermute | solution.py:302
  241.3 30.6 %collective-permute-start.43 = (bf16[288,1152]{1,0:T(8,128)(2,1)}, bf16[288,1152]{1,0:T(8,128)(2,1)S(1)}, u32[]{:S(2)}, u32[]{:S(2)}) collective-permute-start(bf16[288,1152]{1,0:T(8,128)(2,1)} %get-tuple-element.363), channel_id=1, source_target_pairs={{0,8},{4,12},{8,0},{12,4},{16,24},{20,28},{24,16},{28,20},{1,9},{5... | collective-permute-start | bytes 1990664 | tf_op jit(solution)/shard_map/ppermute | solution.py:302
  242.7 29.4 %collective-permute-start.44 = (bf16[288,1152]{1,0:T(8,128)(2,1)}, bf16[288,1152]{1,0:T(8,128)(2,1)S(1)}, u32[]{:S(2)}, u32[]{:S(2)}) collective-permute-start(bf16[288,1152]{1,0:T(8,128)(2,1)} %get-tuple-element.364), channel_id=1, source_target_pairs={{0,16},{4,20},{8,24},{12,28},{16,0},{20,4},{24,8},{28,12},{1,17},{... | collective-permute-start | bytes 1990664 | tf_op jit(solution)/shard_map/ppermute | solution.py:302
  273.2 19.5 %collective-permute-start.47 = (bf16[288,1152]{1,0:T(8,128)(2,1)S(1)}, bf16[288,1152]{1,0:T(8,128)(2,1)S(1)}, u32[]{:S(2)}, u32[]{:S(2)}) collective-permute-start(bf16[288,1152]{1,0:T(8,128)(2,1)S(1)} %add_convert_fusion.2), channel_id=1, source_target_pairs={{0,8},{4,12},{8,0},{12,4},{16,24},{20,28},{24,16},{28,20},{1,9},{5... | collective-permute-start | bytes 1990664 | tf_op jit(solution)/shard_map/ppermute | solution.py:302
  274.9 17.8 %collective-permute-start.46 = (bf16[288,1152]{1,0:T(8,128)(2,1)S(1)}, bf16[288,1152]{1,0:T(8,128)(2,1)S(1)}, u32[]{:S(2)}, u32[]{:S(2)}) collective-permute-start(bf16[288,1152]{1,0:T(8,128)(2,1)S(1)} %add_convert_fusion.3), channel_id=1, source_target_pairs={{0,16},{4,20},{8,24},{12,28},{16,0},{20,4},{24,8},{28,12},{1,17},{... | collective-permute-start | bytes 1990664 | tf_op jit(solution)/shard_map/ppermute | solution.py:302
  275.5 17.1 %collective-permute-start.50 = (bf16[576,384]{1,0:T(8,128)(2,1)}, bf16[576,384]{1,0:T(8,128)(2,1)S(1)}, u32[]{:S(2)}, u32[]{:S(2)}) collective-permute-start(bf16[576,384]{1,0:T(8,128)(2,1)} %get-tuple-element.392), channel_id=1, source_target_pairs={{0,4},{4,0},{8,12},{12,8},{16,20},{20,16},{24,28},{28,24},{1,5},{5... | collective-permute-start | bytes 1327112 | tf_op jit(solution)/shard_map/ppermute | solution.py:302
  293.6 19.1 %collective-permute-start.53 = (bf16[1152,384]{1,0:T(8,128)(2,1)S(1)}, bf16[1152,384]{1,0:T(8,128)(2,1)S(1)}, u32[]{:S(2)}, u32[]{:S(2)}) collective-permute-start(bf16[1152,384]{1,0:T(8,128)(2,1)S(1)} %copy-done.37), channel_id=1, source_target_pairs={{0,4},{4,0},{8,12},{12,8},{16,20},{20,16},{24,28},{28,24},{1,5},{5... | collective-permute-start | bytes 2654216 | tf_op jit(solution)/shard_map/ppermute | solution.py:302
  293.7 19.0 %collective-permute-start.51 = (bf16[80,4608]{1,0:T(8,128)(2,1)}, bf16[80,4608]{1,0:T(8,128)(2,1)S(1)}, u32[]{:S(2)}, u32[]{:S(2)}) collective-permute-start(bf16[80,4608]{1,0:T(8,128)(2,1)} %get-tuple-element.394), channel_id=1, source_target_pairs={{0,8},{4,12},{8,0},{12,4},{16,24},{20,28},{24,16},{28,20},{1,9},{5... | collective-permute-start | bytes 2211848 | tf_op jit(solution)/shard_map/ppermute | solution.py:302
  295.2 15.5 %collective-permute-start.52 = (bf16[64,4608]{1,0:T(8,128)(2,1)}, bf16[64,4608]{1,0:T(8,128)(2,1)S(1)}, u32[]{:S(2)}, u32[]{:S(2)}) collective-permute-start(bf16[64,4608]{1,0:T(8,128)(2,1)} %get-tuple-element.395), channel_id=1, source_target_pairs={{0,16},{4,20},{8,24},{12,28},{16,0},{20,4},{24,8},{28,12},{1,17},{... | collective-permute-start | bytes 1769480 | tf_op jit(solution)/shard_map/ppermute | solution.py:302
  312.7 18.1 %collective-permute-start.56 = (bf16[80,4608]{1,0:T(8,128)(2,1)S(1)}, bf16[80,4608]{1,0:T(8,128)(2,1)}, u32[]{:S(2)}, u32[]{:S(2)}) collective-permute-start(bf16[80,4608]{1,0:T(8,128)(2,1)S(1)} %copy-done.103), channel_id=1, source_target_pairs={{0,8},{4,12},{8,0},{12,4},{16,24},{20,28},{24,16},{28,20},{1,9},{5... | collective-permute-start | bytes 2211848 | tf_op jit(solution)/shard_map/ppermute | solution.py:302
  314.2 16.2 %collective-permute-start.58 = (bf16[258,1152]{1,0:T(8,128)(2,1)}, bf16[258,1152]{1,0:T(8,128)(2,1)S(1)}, u32[]{:S(2)}, u32[]{:S(2)}) collective-permute-start(bf16[258,1152]{1,0:T(8,128)(2,1)} %get-tuple-element.424.refs_6_), channel_id=1, source_target_pairs={{0,4},{4,0},{8,12},{12,8},{16,20},{20,16},{24,28},{28,24},{1,5},{5... | collective-permute-start | bytes 1783304 | tf_op jit(solution)/shard_map/ppermute | solution.py:302
  314.2 16.1 %collective-permute-start.57 = (bf16[64,4608]{1,0:T(8,128)(2,1)}, bf16[64,4608]{1,0:T(8,128)(2,1)S(1)}, u32[]{:S(2)}, u32[]{:S(2)}) collective-permute-start(bf16[64,4608]{1,0:T(8,128)(2,1)} %get-tuple-element.423), channel_id=1, source_target_pairs={{0,16},{4,20},{8,24},{12,28},{16,0},{20,4},{24,8},{28,12},{1,17},{... | collective-permute-start | bytes 1769480 | tf_op jit(solution)/shard_map/ppermute | solution.py:302
  331.6 21.4 %collective-permute-start.54 = (bf16[80,4608]{1,0:T(8,128)(2,1)S(1)}, bf16[80,4608]{1,0:T(8,128)(2,1)S(1)}, u32[]{:S(2)}, u32[]{:S(2)}) collective-permute-start(bf16[80,4608]{1,0:T(8,128)(2,1)S(1)} %add_convert_fusion.1), channel_id=1, source_target_pairs={{0,16},{4,20},{8,24},{12,28},{16,0},{20,4},{24,8},{28,12},{1,17},{... | collective-permute-start | bytes 2211848 | tf_op jit(solution)/shard_map/ppermute | solution.py:302
  333.3 19.7 %collective-permute-start.55 = (bf16[64,4608]{1,0:T(8,128)(2,1)S(1)}, bf16[64,4608]{1,0:T(8,128)(2,1)S(1)}, u32[]{:S(2)}, u32[]{:S(2)}) collective-permute-start(bf16[64,4608]{1,0:T(8,128)(2,1)S(1)} %add_convert_fusion.5), channel_id=1, source_target_pairs={{0,8},{4,12},{8,0},{12,4},{16,24},{20,28},{24,16},{28,20},{1,9},{5... | collective-permute-start | bytes 1769480 | tf_op jit(solution)/shard_map/ppermute | solution.py:302
  353.0 19.2 %collective-permute-start.60 = (bf16[80,4608]{1,0:T(8,128)(2,1)}, bf16[80,4608]{1,0:T(8,128)(2,1)S(1)}, u32[]{:S(2)}, u32[]{:S(2)}) collective-permute-start(bf16[80,4608]{1,0:T(8,128)(2,1)} %get-tuple-element.438), channel_id=1, source_target_pairs={{0,8},{4,12},{8,0},{12,4},{16,24},{20,28},{24,16},{28,20},{1,9},{5... | collective-permute-start | bytes 2211848 | tf_op jit(solution)/shard_map/ppermute | solution.py:302
  354.5 17.7 %collective-permute-start.61 = (bf16[64,4608]{1,0:T(8,128)(2,1)}, bf16[64,4608]{1,0:T(8,128)(2,1)}, u32[]{:S(2)}, u32[]{:S(2)}) collective-permute-start(bf16[64,4608]{1,0:T(8,128)(2,1)} %get-tuple-element.439), channel_id=1, source_target_pairs={{0,16},{4,20},{8,24},{12,28},{16,0},{20,4},{24,8},{28,12},{1,17},{... | collective-permute-start | bytes 1769480 | tf_op jit(solution)/shard_map/ppermute | solution.py:302
  357.1 15.2 %collective-permute-start.63 = (bf16[144,1152]{1,0:T(8,128)(2,1)}, bf16[144,1152]{1,0:T(8,128)(2,1)S(1)}, u32[]{:S(2)}, u32[]{:S(2)}) collective-permute-start(bf16[144,1152]{1,0:T(8,128)(2,1)} %get-tuple-element.441), channel_id=1, source_target_pairs={{0,1},{1,0},{2,3},{3,2},{4,5},{5,4},{6,7},{7,6},{8,9},{9,8},{10,11... | collective-permute-start | bytes 995336 | tf_op jit(solution)/shard_map/ppermute | solution.py:306
  372.4 16.3 %collective-permute-start.66 = (bf16[144,1152]{1,0:T(8,128)(2,1)S(1)}, bf16[144,1152]{1,0:T(8,128)(2,1)S(1)}, u32[]{:S(2)}, u32[]{:S(2)}) collective-permute-start(bf16[144,1152]{1,0:T(8,128)(2,1)S(1)} %add_convert_fusion.10), channel_id=1, source_target_pairs={{0,2},{1,3},{2,0},{3,1},{4,6},{5,7},{6,4},{7,5},{8,10},{9,11},{10,... | collective-permute-start | bytes 995336 | tf_op jit(solution)/shard_map/ppermute | solution.py:306
  373.6 27.6 %collective-permute-start.64 = (bf16[80,4608]{1,0:T(8,128)(2,1)S(1)}, bf16[80,4608]{1,0:T(8,128)(2,1)}, u32[]{:S(2)}, u32[]{:S(2)}) collective-permute-start(bf16[80,4608]{1,0:T(8,128)(2,1)S(1)} %copy-done.102), channel_id=1, source_target_pairs={{0,8},{4,12},{8,0},{12,4},{16,24},{20,28},{24,16},{28,20},{1,9},{5... | collective-permute-start | bytes 2211848 | tf_op jit(solution)/shard_map/ppermute | solution.py:302
  374.4 26.9 %collective-permute-start.67 = (bf16[258,1152]{1,0:T(8,128)(2,1)}, bf16[258,1152]{1,0:T(8,128)(2,1)}, u32[]{:S(2)}, u32[]{:S(2)}) collective-permute-start(bf16[258,1152]{1,0:T(8,128)(2,1)} %get-tuple-element.482.refs_6_.refs_2_), channel_id=1, source_target_pairs={{0,4},{4,0},{8,12},{12,8},{16,20},{20,16},{24,28},{28,24},{1,5},{5... | collective-permute-start | bytes 1783304 | tf_op jit(solution)/shard_map/ppermute | solution.py:302
  374.4 26.8 %collective-permute-start.65 = (bf16[64,4608]{1,0:T(8,128)(2,1)S(1)}, bf16[64,4608]{1,0:T(8,128)(2,1)}, u32[]{:S(2)}, u32[]{:S(2)}) collective-permute-start(bf16[64,4608]{1,0:T(8,128)(2,1)S(1)} %copy-done.104), channel_id=1, source_target_pairs={{0,16},{4,20},{8,24},{12,28},{16,0},{20,4},{24,8},{28,12},{1,17},{... | collective-permute-start | bytes 1769480 | tf_op jit(solution)/shard_map/ppermute | solution.py:302
  375.5 36.9 %collective-permute-start.68 = (bf16[80,4608]{1,0:T(8,128)(2,1)S(1)}, bf16[80,4608]{1,0:T(8,128)(2,1)S(1)}, u32[]{:S(2)}, u32[]{:S(2)}) collective-permute-start(bf16[80,4608]{1,0:T(8,128)(2,1)S(1)} %add_convert_fusion), channel_id=1, source_target_pairs={{0,16},{4,20},{8,24},{12,28},{16,0},{20,4},{24,8},{28,12},{1,17},{... | collective-permute-start | bytes 2211848 | tf_op jit(solution)/shard_map/ppermute | solution.py:302
  388.7 23.7 %collective-permute-start.69 = (bf16[64,4608]{1,0:T(8,128)(2,1)}, bf16[64,4608]{1,0:T(8,128)(2,1)}, u32[]{:S(2)}, u32[]{:S(2)}) collective-permute-start(bf16[64,4608]{1,0:T(8,128)(2,1)} %add_convert_fusion.4), channel_id=1, source_target_pairs={{0,8},{4,12},{8,0},{12,4},{16,24},{20,28},{24,16},{28,20},{1,9},{5... | collective-permute-start | bytes 1769480 | tf_op jit(solution)/shard_map/ppermute | solution.py:302
  401.3 16.6 %collective-permute-start.71 = (bf16[144,1152]{1,0:T(8,128)(2,1)}, bf16[144,1152]{1,0:T(8,128)(2,1)}, u32[]{:S(2)}, u32[]{:S(2)}) collective-permute-start(bf16[144,1152]{1,0:T(8,128)(2,1)} %get-tuple-element.476), channel_id=1, source_target_pairs={{0,1},{1,0},{2,3},{3,2},{4,5},{5,4},{6,7},{7,6},{8,9},{9,8},{10,11... | collective-permute-start | bytes 995336 | tf_op jit(solution)/shard_map/ppermute | solution.py:306
  419.4 16.3 %collective-permute-start.76 = (bf16[144,1152]{1,0:T(8,128)(2,1)S(1)}, bf16[144,1152]{1,0:T(8,128)(2,1)S(1)}, u32[]{:S(2)}, u32[]{:S(2)}) collective-permute-start(bf16[144,1152]{1,0:T(8,128)(2,1)S(1)} %add_convert_fusion.9), channel_id=1, source_target_pairs={{0,2},{1,3},{2,0},{3,1},{4,6},{5,7},{6,4},{7,5},{8,10},{9,11},{10,... | collective-permute-start | bytes 995336 | tf_op jit(solution)/shard_map/ppermute | solution.py:306
  419.8 16.0 %collective-permute-start.72 = (bf16[144,1152]{1,0:T(8,128)(2,1)}, bf16[144,1152]{1,0:T(8,128)(2,1)S(1)}, u32[]{:S(2)}, u32[]{:S(2)}) collective-permute-start(bf16[144,1152]{1,0:T(8,128)(2,1)} %get-tuple-element.494), channel_id=1, source_target_pairs={{0,8},{4,12},{8,0},{12,4},{16,24},{20,28},{24,16},{28,20},{1,9},{5... | collective-permute-start | bytes 995336 | tf_op jit(solution)/shard_map/ppermute | solution.py:302
  420.4 15.3 %collective-permute-start.73 = (bf16[144,1152]{1,0:T(8,128)(2,1)}, bf16[144,1152]{1,0:T(8,128)(2,1)S(1)}, u32[]{:S(2)}, u32[]{:S(2)}) collective-permute-start(bf16[144,1152]{1,0:T(8,128)(2,1)} %get-tuple-element.495), channel_id=1, source_target_pairs={{0,16},{4,20},{8,24},{12,28},{16,0},{20,4},{24,8},{28,12},{1,17},{... | collective-permute-start | bytes 995336 | tf_op jit(solution)/shard_map/ppermute | solution.py:302
  421.7 14.1 %collective-permute-start.74 = (bf16[144,1152]{1,0:T(8,128)(2,1)}, bf16[144,1152]{1,0:T(8,128)(2,1)S(1)}, u32[]{:S(2)}, u32[]{:S(2)}) collective-permute-start(bf16[144,1152]{1,0:T(8,128)(2,1)} %get-tuple-element.496), channel_id=1, source_target_pairs={{0,8},{4,12},{8,0},{12,4},{16,24},{20,28},{24,16},{28,20},{1,9},{5... | collective-permute-start | bytes 995336 | tf_op jit(solution)/shard_map/ppermute | solution.py:302
  436.8 13.3 %collective-permute-start.78 = (bf16[144,1152]{1,0:T(8,128)(2,1)}, bf16[144,1152]{1,0:T(8,128)(2,1)}, u32[]{:S(2)}, u32[]{:S(2)}) collective-permute-start(bf16[144,1152]{1,0:T(8,128)(2,1)} %add_convert_fusion.7), channel_id=1, source_target_pairs={{0,8},{4,12},{8,0},{12,4},{16,24},{20,28},{24,16},{28,20},{1,9},{5... | collective-permute-start | bytes 995336 | tf_op jit(solution)/shard_map/ppermute | solution.py:302
  442.1 14.2 %collective-permute-start.80 = (bf16[144,1152]{1,0:T(8,128)(2,1)}, bf16[144,1152]{1,0:T(8,128)(2,1)S(1)}, u32[]{:S(2)}, u32[]{:S(2)}) collective-permute-start(bf16[144,1152]{1,0:T(8,128)(2,1)} %get-tuple-element.520), channel_id=1, source_target_pairs={{0,1},{1,0},{2,3},{3,2},{4,5},{5,4},{6,7},{7,6},{8,9},{9,8},{10,11... | collective-permute-start | bytes 995336 | tf_op jit(solution)/shard_map/ppermute | solution.py:306
  457.6 18.7 %collective-permute-start.85 = (bf16[144,1152]{1,0:T(8,128)(2,1)S(1)}, bf16[144,1152]{1,0:T(8,128)(2,1)S(1)}, u32[]{:S(2)}, u32[]{:S(2)}) collective-permute-start(bf16[144,1152]{1,0:T(8,128)(2,1)S(1)} %add_convert_fusion.6), channel_id=1, source_target_pairs={{0,2},{1,3},{2,0},{3,1},{4,6},{5,7},{6,4},{7,5},{8,10},{9,11},{10,... | collective-permute-start | bytes 995336 | tf_op jit(solution)/shard_map/ppermute | solution.py:306
  (131 other events, 1306.3 us)

commit v4 on v3

--- a/solution.py
+++ b/solution.py
@@ -381,51 +381,58 @@
     )(shard, *others)
 
 
-def weight_scratch(rows, columns):
-    return [pltpu.VMEM((rows, columns), jnp.bfloat16), pltpu.SemaphoreType.DMA((8,))]
-
-
-def fetch(refs, full, sems, columns=None):
-    wide = lax.axis_index("wide")
-    core, chip = wide & 1, wide >> 1
-    rows = full.shape[0] // 8
-    copies = []
-    for number, (ends, from_x, from_y) in enumerate((refs[:3], refs[3:])):
-        parity = core if number == 0 else 1 - core
-        own, far = ends.at[pl.ds(0, rows)], ends.at[pl.ds(rows, rows)]
-        for relative, piece in enumerate((own, from_x, from_y, far)):
-            if columns is not None:
-                piece = piece.at[:, columns]
-            start = pl.multiple_of((4 * parity + (chip ^ relative)) * rows, 16)
-            copies.append(
-                pltpu.make_async_copy(
-                    piece, full.at[pl.ds(start, rows)], sems.at[4 * number + relative]
-                )
-            )
-    for copy in copies:
-        copy.start()
-    for copy in copies:
-        copy.wait()
-
-
-def pair_gradient(lefts, rights):
+def weight_scratch(rows, columns, chunks=1):
+    return [pltpu.VMEM((rows, columns), jnp.bfloat16), pltpu.SemaphoreType.DMA((chunks, 8))]
+
+
+class Fetch:
+    def __init__(self, refs, full, sems, first=0):
+        wide = lax.axis_index("wide")
+        core, chip = wide & 1, wide >> 1
+        rows = full.shape[0] // 8
+        chunks = sems.shape[0]
+        width = full.shape[1] // chunks
+        self.copies = []
+        for chunk in range(chunks):
+            group = []
+            for number, (ends, from_x, from_y) in enumerate((refs[:3], refs[3:])):
+                parity = core if number == 0 else 1 - core
+                own, far = ends.at[pl.ds(0, rows)], ends.at[pl.ds(rows, rows)]
+                for relative, piece in enumerate((own, from_x, from_y, far)):
+                    start = pl.multiple_of((4 * parity + (chip ^ relative)) * rows, 16)
+                    group.append(
+                        pltpu.make_async_copy(
+                            piece.at[:, pl.ds(first + chunk * width, width)],
+                            full.at[pl.ds(start, rows), pl.ds(chunk * width, width)],
+                            sems.at[chunk, 4 * number + relative],
+                        )
+                    )
+            self.copies.append(group)
+        for group in self.copies:
+            for copy in group:
+                copy.start()
+
+    def wait(self, chunk=0):
+        for copy in self.copies[chunk]:
+            copy.wait()
+
+
+def pair_gradient(lefts, right):
     height = lefts[0][0].shape[0]
     rows = height // 4
     split = split_rows(rows)
-    tokens = rights[0][0].shape[0]
-    widths = [right[0].shape[1] for right in rights]
+    tokens, columns = right[0].shape
     tile = 384 if height > 576 else 1152
-    steps = [width // tile for width in widths]
-    starts = [sum(steps[:position]) for position in range(len(steps))]
     count = len(lefts)
+    ends = [sum(width for _, _, width in lefts[: number + 1]) // tile for number in range(count)]
+    starts = [0] + ends[:-1]
 
     def kernel(*refs):
         left_refs = refs[: 2 * count]
-        right_refs = refs[2 * count : 4 * count]
-        outs, (joint, beside) = refs[4 * count : 4 * count + 8], refs[4 * count + 8 :]
+        right_ref, sibling_ref = refs[2 * count : 2 * count + 2]
+        outs = refs[2 * count + 2 : 2 * count + 6]
+        joint, beside, total = refs[2 * count + 6 :]
         step = pl.program_id(0)
-        wide = lax.axis_index("wide")
-        across, along = (wide >> 1) & 1, (wide >> 2) & 1
 
         @pl.when(step == 0)
         def _():
@@ -438,103 +445,102 @@
                 beside[:, :PAD] = left_refs[2 * number][...]
                 beside[:, PAD:] = left_refs[2 * number + 1][...]
 
-            @pl.when((step >= starts[number]) & (step < starts[number] + steps[number]))
-            def _():
-                joint[:tokens] = right_refs[2 * number][...]
-                joint[PAD : PAD + tokens] = right_refs[2 * number + 1][...]
-                for y in range(2):
-                    for x in range(2):
-                        first_row = (2 * y + x) * rows
-                        total = jnp.dot(
-                            beside[first_row : first_row + rows],
-                            joint[...],
-                            preferred_element_type=jnp.float32,
-                        ).astype(jnp.bfloat16)
-
-                        for kept_x in range(2):
-                            for kept_y in range(2):
-
-                                @pl.when(
-                                    ((across == x) == (kept_x == 1))
-                                    & ((along == y) == (kept_y == 1))
-                                )
-                                def _():
-                                    outs[2 * (1 - kept_x) + (1 - kept_y)][...] = total[:split]
-                                    outs[4 + 2 * (1 - kept_y) + (1 - kept_x)][...] = total[split:]
-
-    def right_spec(number):
-        return pl.BlockSpec(
-            (tokens, tile),
-            lambda i: (0, jnp.clip(i - starts[number], 0, steps[number] - 1)),
-        )
-
-    in_specs = [pl.BlockSpec((height, PAD), lambda i: (0, 0))] * (2 * count)
-    operands = [left for pair in lefts for left in pair]
-    for number in range(count):
-        in_specs += [right_spec(number)] * 2
-        operands += list(rights[number])
-    top_spec = pl.BlockSpec((split, tile), lambda i: (0, i))
-    bottom_spec = pl.BlockSpec((rows - split, tile), lambda i: (0, i))
-    top_shape = jax.ShapeDtypeStruct((split, sum(widths)), jnp.bfloat16)
-    bottom_shape = jax.ShapeDtypeStruct((rows - split, sum(widths)), jnp.bfloat16)
+        joint[:tokens] = right_ref[...]
+        joint[PAD : PAD + tokens] = sibling_ref[...]
+        total[...] = jnp.dot(
+            beside[...], joint[...], preferred_element_type=jnp.float32
+        ).astype(jnp.bfloat16)
+        part_blocks(total, rows, outs)
+
+    whole = pl.BlockSpec((height, PAD), lambda i: (0, 0))
+    part = lambda size: pl.BlockSpec((size, tile), lambda i: (0, i))
+    pair = lambda size: pl.BlockSpec((2, size, tile), lambda i: (0, 0, i))
     outs = pl.pallas_call(
         kernel,
-        grid=(sum(steps),),
-        in_specs=in_specs,
-        out_specs=(top_spec,) * 4 + (bottom_spec,) * 4,
-        out_shape=(top_shape,) * 4 + (bottom_shape,) * 4,
+        grid=(columns // tile,),
+        in_specs=[whole] * (2 * count) + [part(tokens)] * 2,
+        out_specs=(pair(split), pair(split), pair(rows - split), pair(rows - split)),
+        out_shape=block_shapes(rows, columns),
         scratch_shapes=[
             pltpu.VMEM((2 * PAD, tile), jnp.bfloat16),
             pltpu.VMEM((height, 2 * PAD), jnp.bfloat16),
+            pltpu.VMEM((height, tile), jnp.bfloat16),
         ],
         compiler_params=PARAMS,
         cost_estimate=LIGHT,
-    )(*operands)
-    return outs[:4], outs[4:]
-
-
-def unarrange(kind, parts, top, bottom):
-    split, columns = top[0].shape
-    rest = bottom[0].shape[0]
+    )(*[left for pair_of in lefts for left in pair_of[:2]], *right)
+    return outs
+
+
+def block_shapes(rows, columns):
+    split = split_rows(rows)
+    top = jax.ShapeDtypeStruct((2, split, columns), jnp.bfloat16)
+    bottom = jax.ShapeDtypeStruct((2, rows - split, columns), jnp.bfloat16)
+    return top, top, bottom, bottom
+
+
+def part_blocks(total, rows, outs):
+    wide = lax.axis_index("wide")
+    across, along = (wide >> 1) & 1, (wide >> 2) & 1
+    split = split_rows(rows)
+    for kept_x in range(2):
+        for kept_y in range(2):
+            x = across if kept_x else 1 - across
+            y = along if kept_y else 1 - along
+            start = pl.multiple_of((2 * y + x) * rows, 16)
+            outs[1 - kept_x][1 - kept_y] = total[pl.ds(start, split)]
+            outs[3 - kept_y][1 - kept_x] = total[
+                pl.ds(pl.multiple_of(start + split, 16), rows - split)
+            ]
+
+
+def unarrange(kind, parts, blocks, got, got_last):
+    split, columns = got_last[0].shape
+    rest = got_last[1].shape[0]
     rows = split + rest
     quarter = columns // 4
     height = rows // parts
-    width, blocks = column_blocks(kind, quarter)
+    width, column_parts = column_blocks(kind, quarter)
 
     def kernel(*refs):
         tops, bottoms = refs[:3], refs[3:6]
-        keep_ref, keep_far_ref, send_ref, send_far_ref, held = refs[6:]
+        outs, held = refs[6:10], refs[10]
         narrow = lax.axis_index("narrow")
         low_bit, high_bit = narrow & 1, narrow >> 1
-        held[:split] = add_low(*[ref[...] for ref in tops])
-        held[split:] = add_low(*[ref[...] for ref in bottoms])
-        for position, (owner, offset) in enumerate(blocks):
-            piece = held[:, position * width : (position + 1) * width]
-            for kept_low in range(2):
-                for kept_high in range(2):
-                    target = (keep_ref, keep_far_ref, send_ref, send_far_ref)[
-                        2 * (1 - kept_low) + (1 - kept_high)
-                    ]
-
-                    @pl.when(
-                        ((low_bit == (owner & 1)) == (kept_low == 1))
-                        & ((high_bit == (owner >> 1)) == (kept_high == 1))
-                    )
-                    def _():
-                        for part in range(parts):
-                            start = part * quarter + offset
-                            target[:, start : start + width] = piece[
-                                part * height : (part + 1) * height
-                            ]
-
+        held[:split] = add_low(tops[0][...], tops[1][...], tops[2][...])
+        held[split:] = add_low(bottoms[0][...], bottoms[1][...], bottoms[2][...])
+        for owner in range(4):
+            for which in range(4):
+                low_same, high_same = 1 - which // 2, 1 - which % 2
+
+                @pl.when(
+                    ((low_bit == (owner & 1)) == (low_same == 1))
+                    & ((high_bit == (owner >> 1)) == (high_same == 1))
+                )
+                def _():
+                    for position, (quarter_of, offset) in enumerate(column_parts):
+                        if quarter_of == owner:
+                            piece = held[:, position * width : (position + 1) * width]
+                            for part in range(parts):
+                                start = part * quarter + offset
+                                outs[which][:, start : start + width] = piece[
+                                    part * height : (part + 1) * height
+                                ]
+
+    near = lambda size: pl.BlockSpec((None, size, columns), lambda i: (0, 0, 0))
+    full = lambda size, width: pl.BlockSpec((size, width), lambda i: (0, 0))
     shape = jax.ShapeDtypeStruct((height, parts * quarter), jnp.bfloat16)
     return pl.pallas_call(
         kernel,
+        grid=(1,),
+        in_specs=[near(split), near(split), full(split, columns)]
+        + [near(rest), near(rest), full(rest, columns)],
+        out_specs=(full(height, parts * quarter),) * 4,
         out_shape=(shape,) * 4,
         scratch_shapes=[pltpu.VMEM((rows, columns), jnp.bfloat16)],
         compiler_params=PARAMS,
         cost_estimate=LIGHT,
-    )(*top, *bottom)
+    )(blocks[0], got[0], got_last[0], blocks[2], got[1], got_last[1])
 
 
 def add_low(*terms):
@@ -579,26 +585,17 @@
     return jnp.pad(value, ((0, PAD - value.shape[0]), (0, 0))).T
 
 
-def both(parts, order):
-    if order == 0:
-        return swap_wide(parts[0], ACROSS), swap_wide(parts[1], ALONG)
-    return swap_wide(parts[0], ALONG), swap_wide(parts[1], ACROSS)
-
-
 KEEP_NEAR, KEEP_FAR, SEND_NEAR, SEND_FAR = range(4)
 
 
-def send(blocks, which):
-    return both((blocks[0][which], blocks[1][which]), 0)
+def send(blocks):
+    return swap_wide(blocks[1], ACROSS), swap_wide(blocks[3], ALONG)
 
 
 def forward(blocks, got):
-    return both(tuple(add_low(blocks[i][KEEP_FAR], got[i]) for i in range(2)), 1)
-
-
-def settle(kind, parts, blocks, got_near, got_last):
-    return unarrange(
-        kind, parts, *[(blocks[i][KEEP_NEAR], got_near[i], got_last[i]) for i in range(2)]
+    return (
+        swap_wide(add_low(blocks[0][1], got[0][1]), ALONG),
+        swap_wide(add_low(blocks[2][1], got[1][1]), ACROSS),
     )
 
 
@@ -637,6 +634,18 @@
 
 def ends_of(block, second):
     return jnp.concatenate([block, second[0], second[1]], axis=0)
+
+
+def direct_narrow(quarters):
+    return (
+        swap_narrow(quarters[KEEP_FAR], 2),
+        swap_narrow(quarters[SEND_NEAR], 1),
+        swap_narrow(quarters[SEND_FAR], 3),
+    )
+
+
+def direct_sum(quarters, got):
+    return sum(term.astype(jnp.float32) for term in (quarters[KEEP_NEAR], *got))
 
 
 def heavy(kernel, outs, scratch, weights, operands):
@@ -682,8 +691,9 @@
     def kernel(*refs):
         joined_ref, bias_ref, gain_ref, shift_ref = refs[6:10]
         stream, entry, up_mine, up_other, full, sems, padded = refs[10:]
-        fetch(refs[:6], full, sems)
+        weight_in = Fetch(refs[:6], full, sems)
         padded[...] = jnp.zeros_like(padded)
+        weight_in.wait()
         stream[...] = product(joined_ref[...], full[...]) + bias_ref[...]
         normed = normalize(stream[...])[0]
         value = (normed * gain_ref[...] + shift_ref[...]).astype(jnp.bfloat16)
@@ -716,26 +726,30 @@
     return product(chances.astype(jnp.bfloat16), values).astype(jnp.bfloat16)
 
 
+FIRST = 12
+
+
 def attend_first(entry, weight):
     length = entry.shape[0]
 
     def kernel(*refs):
         entry_ref, heads, chances_ref, mix_ref, full, sems = refs[6:]
-        fetch(refs[:6], full, sems, pl.ds(0, 3 * D))
+        weight_in = Fetch(refs[:6], full, sems)
         for part in range(3):
+            weight_in.wait(part)
             columns = slice(part * D, (part + 1) * D)
             heads[:, columns] = product(entry_ref[...], full[:, columns]).astype(jnp.bfloat16)
-        for head in range(H // 2):
+        for head in range(FIRST):
             mix_ref[:, head * HD : (head + 1) * HD] = attend_head(heads, head, chances_ref, head)
 
     return heavy(
         kernel,
         [
             ((length, 3 * D), jnp.bfloat16),
-            ((H // 2, length, length), jnp.float32),
-            ((length, D // 2), jnp.bfloat16),
+            ((FIRST, length, length), jnp.float32),
+            ((length, FIRST * HD), jnp.bfloat16),
         ],
-        weight_scratch(D, 3 * D),
+        weight_scratch(D, 3 * D, 3),
         weight,
         (entry,),
     )
@@ -748,13 +762,14 @@
     def kernel(*refs):
         heads_ref, first_ref, zero_ref, bias_ref, gain_ref, shift_ref = refs[6:12]
         chances_ref, stream, value_ref, up_mine, up_other, full, sems, mixed, padded = refs[12:]
-        fetch(refs[:6], full, sems, pl.ds(3 * D, D))
+        weight_in = Fetch(refs[:6], full, sems, 3 * D)
         padded[...] = jnp.zeros_like(padded)
-        mixed[:, :half] = first_ref[...]
-        for head in range(H // 2, H):
+        mixed[:, : FIRST * HD] = first_ref[...]
+        for head in range(FIRST, H):
             mixed[:, head * HD : (head + 1) * HD] = attend_head(
-                heads_ref, head, chances_ref, head - H // 2
+                heads_ref, head, chances_ref, head - FIRST
             )
+        weight_in.wait()
         stream[...] = zero_ref[...] + product(mixed[...], full[...]) + bias_ref[...]
         store_upright(
             mixed[...].astype(jnp.float32), padded, up_mine.at[pl.ds(0, half)], up_other.at[pl.ds(0, half)]
@@ -769,7 +784,7 @@
     return heavy(
         kernel,
         [
-            ((H // 2, length, length), jnp.float32),
+            ((H - FIRST, length, length), jnp.float32),
             ((length, D), jnp.float32),
             ((length, D), jnp.bfloat16),
             ((D, PAD), jnp.bfloat16),
@@ -789,10 +804,11 @@
         entry_ref, bias_ref = refs[6:8]
         active_ref, slope_ref, up_mine, up_other, full, sems, padded = refs[8:]
         core = lax.axis_index("wide") & 1
-        fetch(refs[:6], full, sems)
+        weight_in = Fetch(refs[:6], full, sems)
         padded[...] = jnp.zeros_like(padded)
         for step in range(FF // D):
             columns = slice(step * D, (step + 1) * D)
+            weight_in.wait(step)
             value = product(entry_ref[...], full[:, columns]) + bias_ref[:, columns]
             inside = 0.5 * (1.0 + lax.erf(value * (0.5**0.5)))
             bell = jnp.exp(-0.5 * value * value) * (2.0 * jnp.pi) ** -0.5
@@ -819,7 +835,7 @@
             ((FF // 2, PAD), jnp.bfloat16),
             ((FF // 2, PAD), jnp.bfloat16),
         ],
-        weight_scratch(D, FF) + [pltpu.VMEM((PAD, D), jnp.float32)],
+        weight_scratch(D, FF, FF // D) + [pltpu.VMEM((PAD, D), jnp.float32)],
         weight,
         (entry, bias),
     )
@@ -830,7 +846,7 @@
 
     def kernel(*refs):
         pulled_ref, slope_ref, low_ref, sum_ref, full, sems = refs[6:]
-        fetch(refs[:6], full, sems)
+        Fetch(refs[:6], full, sems).wait()
         for step in range(FF // D):
             columns = slice(step * D, (step + 1) * D)
             delta = dot_rows(pulled_ref[...], full[columns]) * slope_ref[:, columns]
@@ -851,10 +867,15 @@
 
     def kernel(*refs):
         hidden_ref, pulled_ref, stream_ref, gain_ref = refs[12:16]
-        one_ref, low_ref, sums, mix_ref, full, sems, output, output_sems = refs[16:]
-        fetch(refs[:6], full, sems)
-        fetch(refs[6:12], output, output_sems, pl.ds(3 * D, D))
-        value = dot_rows(hidden_ref[...], full[...])
+        one_ref, low_ref, sums, mix_ref, full, sems, output, output_sems, delta = refs[16:]
+        weight_in = Fetch(refs[:6], full, sems)
+        output_in = Fetch(refs[6:12], output, output_sems, 3 * D)
+        for step in range(FF // D):
+            columns = slice(step * D, (step + 1) * D)
+            weight_in.wait(step)
+            part = dot_rows(hidden_ref[:, columns], full[:, columns])
+            delta[...] = part if step == 0 else delta[...] + part
+        value = delta[...]
         normed, inverse = normalize(stream_ref[...])
         upstream = pulled_ref[...].astype(jnp.float32)
         one = upstream + norm_back(value * gain_ref[...], normed, inverse)
@@ -865,6 +886,7 @@
         sums[1:2] = jnp.sum(value * normed, axis=0, keepdims=True)
         sums[2:3] = jnp.sum(value, axis=0, keepdims=True)
         sums[3:4] = jnp.sum(upstream, axis=0, keepdims=True)
+        output_in.wait()
         mix_ref[...] = dot_rows(low_value, output[...]).astype(jnp.bfloat16)
 
     return heavy(
@@ -875,24 +897,27 @@
             ((4, D), jnp.float32),
             ((length, D), jnp.bfloat16),
         ],
-        weight_scratch(D, FF) + weight_scratch(D, D),
+        weight_scratch(D, FF, FF // D)
+        + weight_scratch(D, D)
+        + [pltpu.VMEM((length, D), jnp.float32)],
         (*weight, *mixed_weight),
         (hidden_low, pulled, stream_one, gain),
     )
 
 
-def attend_backward(heads, chances_first, chances_second, delta_mixture):
+def attend_backward(heads, chances_first, chances_second, delta_mixture, stream_low):
     length = heads.shape[0]
     scale = HD ** (-0.5)
 
-    def kernel(heads_ref, first_ref, second_ref, delta_ref, mixed):
+    def kernel(heads_ref, first_ref, second_ref, delta_ref, stream_ref, mixed):
+        mixed[:, 3 * D :] = stream_ref[...]
         for head in range(H):
             at = head * HD
             queries = heads_ref[:, at : at + HD]
             keys = heads_ref[:, D + at : D + at + HD]
             values = heads_ref[:, 2 * D + at : 2 * D + at + HD]
             delta = delta_ref[:, at : at + HD]
-            chances = (first_ref, second_ref)[head // (H // 2)][head % (H // 2)]
+            chances = first_ref[head] if head < FIRST else second_ref[head - FIRST]
             pull = dot_rows(delta, values)
             inner_sum = jnp.sum(chances * pull, axis=-1, keepdims=True)
             scores = (scale * (chances * (pull - inner_sum))).astype(jnp.bfloat16)
@@ -904,10 +929,10 @@
 
     return heavy(
         kernel,
-        [((length, 3 * D), jnp.bfloat16)],
+        [((length, 4 * D), jnp.bfloat16)],
         [],
         (),
-        (heads, chances_first, chances_second, delta_mixture),
+        (heads, chances_first, chances_second, delta_mixture, stream_low),
     )[0]
 
 
@@ -915,9 +940,14 @@
     length = delta_mixed.shape[0]
 
     def kernel(*refs):
-        mixed_ref, one_ref, stream_ref, gain_ref, low_ref, sums, full, sems = refs[6:]
-        fetch(refs[:6], full, sems, pl.ds(0, 3 * D))
-        value = dot_rows(mixed_ref[...], full[...])
+        mixed_ref, one_ref, stream_ref, gain_ref, low_ref, sums, full, sems, delta = refs[6:]
+        weight_in = Fetch(refs[:6], full, sems)
+        for step in range(3):
+            columns = slice(step * D, (step + 1) * D)
+            weight_in.wait(step)
+            part = dot_rows(mixed_ref[:, columns], full[:, columns])
+            delta[...] = part if step == 0 else delta[...] + part
+        value = delta[...]
         normed, inverse = normalize(stream_ref[...])
         zero = one_ref[...] + norm_back(value * gain_ref[...], normed, inverse)
         low_ref[...] = zero.astype(jnp.bfloat16)
@@ -928,7 +958,7 @@
     return heavy(
         kernel,
         [((length, D), jnp.bfloat16), ((3, D), jnp.float32)],
-        weight_scratch(D, 3 * D),
+        weight_scratch(D, 3 * D, 3) + [pltpu.VMEM((length, D), jnp.float32)],
         weight,
         (delta_mixed, delta_one, stream_zero, gain),
     )
@@ -940,7 +970,7 @@
 
     def kernel(*refs):
         zero_ref, first_ref, second_ref, full, sems = refs[6:]
-        fetch(refs[:6], full, sems)
+        Fetch(refs[:6], full, sems).wait()
         for parity in range(2):
             delta = dot_rows(zero_ref[...], full[parity * D : (parity + 1) * D])
             delta = delta.astype(jnp.bfloat16)
@@ -959,7 +989,7 @@
 
     def kernel(*refs):
         active_ref, stream_ref, bias_ref, out_ref, full, sems = refs[6:]
-        fetch(refs[:6], full, sems)
+        Fetch(refs[:6], full, sems).wait()
         total = (
             stream_ref[...] + product(active_ref[...], full[...]) + bias_ref[...]
         ).astype(jnp.bfloat16)
@@ -1070,8 +1100,8 @@
     mixed_second = gather_second(mixed_first)
     mixed_sides = swap_sides(mixed_first)
     expand_last = swap_narrow(expand_far, 1)
-    mixed_second, mixed_sides, expand_last = together(mixed_second, mixed_sides, expand_last)
     expand_block = arrange("expand", 1, expand_low, (expand_near, expand_far, expand_last))[0]
+    mixed_second, mixed_sides, expand_block = together(mixed_second, mixed_sides, expand_block)
     expand_first = gather_first(expand_block)
     shrink_far = swap_narrow(shrink_low, 2)
     shrink_near = swap_narrow(shrink_low, 1)
@@ -1087,10 +1117,10 @@
     chances_second, stream_one, expand_input, ups, ups_other = attend_second(
         heads, mix_first, mixed_pieces, stream_zero, output_bias, gain_two, bias_two
     )
-    expand_second, expand_sides, shrink_last, expand_input, ups_other = together(
-        expand_second, expand_sides, shrink_last, expand_input, ups_other
-    )
     shrink_block = arrange("shrink", 4, shrink_low, (shrink_near, shrink_far, shrink_last))[0]
+    expand_second, expand_sides, shrink_block, expand_input, ups_other = together(
+        expand_second, expand_sides, shrink_block, expand_input, ups_other
+    )
     shrink_first = gather_first(shrink_block)
     expand_ends = ends_of(expand_block, expand_second)
     expand_pieces = (expand_ends, *expand_first, swap_wide(expand_ends, CORE), *expand_sides)
@@ -1104,87 +1134,84 @@
     shrink_second = gather_second(shrink_first)
     shrink_sides = swap_sides(shrink_first)
     active_up_sibling = swap_wide(active_up_other, CORE)
-    shrink_blocks = pair_gradient([(active_up, active_up_sibling)], [(pulled, pulled_sibling)])
+    shrink_blocks = pair_gradient([(active_up, active_up_sibling, D)], (pulled, pulled_sibling))
     shrink_second, shrink_sides, shrink_blocks = together(
         shrink_second, shrink_sides, shrink_blocks
     )
-    shrink_far_got = send(shrink_blocks, SEND_FAR)
-    shrink_near_got = send(shrink_blocks, SEND_NEAR)
+    shrink_got = send(shrink_blocks)
     shrink_ends = ends_of(shrink_block, shrink_second)
     shrink_pieces = (shrink_ends, *shrink_first, swap_wide(shrink_ends, CORE), *shrink_sides)
+    ups_sibling = swap_wide(ups_other, CORE)
+    attend_up_sibling = swap_wide(attend_up_other, CORE)
     hidden_low, hidden_sum = hidden_backward(pulled, shrink_pieces, slope)
     outputs = shrink_forward(active, shrink_pieces, stream_one, shrink_bias)[None]
-    shrink_far_got, shrink_near_got, hidden_low, hidden_sum, outputs, attend_up_other = together(
-        shrink_far_got, shrink_near_got, hidden_low, hidden_sum, outputs, attend_up_other
-    )
-    shrink_got_last = forward(shrink_blocks, shrink_far_got)
+    shrink_got, ups_sibling, attend_up_sibling, hidden_low, hidden_sum, outputs, joined_up_other = (
+        together(
+            shrink_got,
+            ups_sibling,
+            attend_up_sibling,
+            hidden_low,
+            hidden_sum,
+            outputs,
+            joined_up_other,
+        )
+    )
+    shrink_got_last = forward(shrink_blocks, shrink_got)
     hidden_sibling = swap_wide(hidden_low, CORE)
-    ups_sibling = swap_wide(ups_other, CORE)
-    attend_up_sibling = swap_wide(attend_up_other, CORE)
     half = D // 2
     expand_blocks = pair_gradient(
-        [(ups[half:], ups_sibling[half:])], [(hidden_low, hidden_sibling)]
-    )
-    shrink_got_last, expand_blocks, hidden_low, attend_up_sibling, joined_up_other = together(
-        shrink_got_last, expand_blocks, hidden_low, attend_up_sibling, joined_up_other
-    )
-    expand_far_got = send(expand_blocks, SEND_FAR)
+        [(ups[half:], ups_sibling[half:], FF)], (hidden_low, hidden_sibling)
+    )
+    shrink_got_last, expand_blocks, hidden_low, joined_up_other = together(
+        shrink_got_last, expand_blocks, hidden_low, joined_up_other
+    )
+    expand_got = send(expand_blocks)
     joined_sibling = swap_wide(joined_up_other, CORE)
     delta_one, stream_low, sums_two, delta_mixture = expand_backward(
         hidden_low, expand_pieces, mixed_pieces, pulled, stream_one, gain_two
     )
-    expand_far_got, joined_sibling, stream_low, delta_mixture, expand_blocks = together(
-        expand_far_got, joined_sibling, stream_low, delta_mixture, expand_blocks
-    )
-    expand_near_got = send(expand_blocks, SEND_NEAR)
-    stream_sibling = swap_wide(stream_low, CORE)
-    delta_mixed = attend_backward(heads, chances_first, chances_second, delta_mixture)
-    expand_near_got, stream_sibling, delta_mixed = together(
-        expand_near_got, stream_sibling, delta_mixed
-    )
-    expand_got_last = forward(expand_blocks, expand_far_got)
+    delta_mixed = attend_backward(heads, chances_first, chances_second, delta_mixture, stream_low)
+    shrink_quarters = unarrange("shrink", 4, shrink_blocks, shrink_got, shrink_got_last)
+    expand_got, joined_sibling, delta_mixed, shrink_quarters = together(
+        expand_got, joined_sibling, delta_mixed, shrink_quarters
+    )
+    expand_got_last = forward(expand_blocks, expand_got)
     mixed_sibling = swap_wide(delta_mixed, CORE)
-    shrink_quarters = settle("shrink", 4, shrink_blocks, shrink_near_got, shrink_got_last)
+    shrink_narrow = narrow_first(shrink_quarters)
     mixed_blocks = pair_gradient(
-        [(attend_up, attend_up_sibling), (ups[:half], ups_sibling[:half])],
-        [(delta_mixed, mixed_sibling), (stream_low, stream_sibling)],
-    )
-    expand_got_last, shrink_quarters, mixed_blocks, delta_mixed = together(
-        expand_got_last, shrink_quarters, mixed_blocks, delta_mixed
-    )
-    mixed_far_got = send(mixed_blocks, SEND_FAR)
-    shrink_got = narrow_first(shrink_quarters)
+        [(attend_up, attend_up_sibling, 3 * D), (ups[:half], ups_sibling[:half], D)],
+        (delta_mixed, mixed_sibling),
+    )
+    expand_got_last, shrink_narrow, mixed_blocks, delta_mixed, moments = together(
+        expand_got_last,
+        shrink_narrow,
+        mixed_blocks,
+        delta_mixed,
+        (shrink_weight, shrink_moment, shrink_square),
+    )
+    mixed_got = send(mixed_blocks)
+    shrink_end = narrow_second(shrink_quarters, shrink_narrow)
+    expand_quarters = unarrange("expand", 1, expand_blocks, expand_got, expand_got_last)
+    expand_narrow = narrow_first(expand_quarters)
     zero_low, sums_one = entry_backward(
         delta_mixed, mixed_pieces, delta_one, stream_zero, gain_one
     )
-    mixed_far_got, shrink_got, zero_low, sums_one, mixed_blocks = together(
-        mixed_far_got, shrink_got, zero_low, sums_one, mixed_blocks
-    )
-    mixed_near_got = send(mixed_blocks, SEND_NEAR)
-    shrink_end = narrow_second(shrink_quarters, shrink_got)
+    input_gradient, skip_gradient = joined_backward(zero_low, merge_pieces)
+    mixed_got, shrink_end, expand_narrow, zero_low, sums_one, input_gradient, skip_gradient = (
+        together(
+            mixed_got,
+            shrink_end,
+            expand_narrow,
+            zero_low,
+            sums_one,
+            input_gradient,
+            skip_gradient,
+        )
+    )
+    mixed_got_last = forward(mixed_blocks, mixed_got)
+    expand_end = narrow_second(expand_quarters, expand_narrow)
     zero_sibling = swap_wide(zero_low, CORE)
-    expand_quarters = settle("expand", 1, expand_blocks, expand_near_got, expand_got_last)
-    input_gradient, skip_gradient = joined_backward(zero_low, merge_pieces)
-    (
-        mixed_near_got,
-        shrink_end,
-        zero_sibling,
-        expand_quarters,
-        zero_low,
-        input_gradient,
-        skip_gradient,
-    ) = together(
-        mixed_near_got,
-        shrink_end,
-        zero_sibling,
-        expand_quarters,
-        zero_low,
-        input_gradient,
-        skip_gradient,
-    )
-    mixed_got_last = forward(mixed_blocks, mixed_far_got)
-    expand_got = narrow_first(expand_quarters)
-    merge_blocks = pair_gradient([(joined_up, joined_sibling)], [(zero_low, zero_sibling)])
+    merge_blocks = pair_gradient([(joined_up, joined_sibling, D)], (zero_low, zero_sibling))
     vector_total = jnp.concatenate(
         [
             outer(row)
@@ -1200,61 +1227,56 @@
             )
         ]
     )
-    mixed_got_last, expand_got, vector_total, merge_blocks, shrink_end = together(
-        mixed_got_last, expand_got, vector_total, merge_blocks, shrink_end
-    )
-    merge_far_got = send(merge_blocks, SEND_FAR)
-    merge_near_got = send(merge_blocks, SEND_NEAR)
-    expand_end = narrow_second(expand_quarters, expand_got)
-    mixed_quarters = settle("attend_output", 1, mixed_blocks, mixed_near_got, mixed_got_last)
-    shrink_new = adamw_update(
-        shrink_weight,
-        shrink_moment,
-        shrink_square,
-        unfold(finish(shrink_quarters, shrink_got, shrink_end), shrink_weight.shape[0]),
-        rate_shrink,
-    )
-    merge_far_got, merge_near_got, expand_end, mixed_quarters, vector_total, shrink_new = together(
-        merge_far_got, merge_near_got, expand_end, mixed_quarters, vector_total, shrink_new
-    )
-    merge_got_last = forward(merge_blocks, merge_far_got)
-    mixed_got = narrow_first(mixed_quarters)
+    mixed_got_last, expand_end, vector_total, merge_blocks, shrink_end = together(
+        mixed_got_last, expand_end, vector_total, merge_blocks, shrink_end
+    )
+    merge_got = send(merge_blocks)
+    mixed_quarters = unarrange("attend_output", 1, mixed_blocks, mixed_got, mixed_got_last)
+    mixed_narrow = narrow_first(mixed_quarters)
     vector_total = vector_total + swap_wide(vector_total, CORE)
+    merge_got, mixed_narrow, vector_total, expand_end, shrink_end = together(
+        merge_got, mixed_narrow, vector_total, expand_end, shrink_end
+    )
+    merge_got_last = forward(merge_blocks, merge_got)
+    mixed_end = narrow_second(mixed_quarters, mixed_narrow)
     vector_total = vector_total + swap_wide(vector_total, ACROSS)
-    merge_got_last, mixed_got, vector_total, expand_end = together(
-        merge_got_last, mixed_got, vector_total, expand_end
-    )
-    merge_quarters = settle("merge", 2, merge_blocks, merge_near_got, merge_got_last)
-    merge_got = narrow_first(merge_quarters)
-    mixed_end = narrow_second(mixed_quarters, mixed_got)
     vector_total = vector_total + swap_wide(vector_total, ALONG)
+    shrink_sum = unfold(
+        finish(shrink_quarters, shrink_narrow, shrink_end), shrink_weight.shape[0]
+    )
+    shrink_new = adamw_update(*[moment.T for moment in moments], shrink_sum.T, rate_shrink)
+    shrink_new = [new.T for new in shrink_new]
+    merge_got_last, mixed_end, vector_total, shrink_new, expand_end = together(
+        merge_got_last, mixed_end, vector_total, shrink_new, expand_end
+    )
+    merge_quarters = unarrange("merge", 2, merge_blocks, merge_got, merge_got_last)
+    merge_narrow = direct_narrow(merge_quarters)
+    halves = vector_total.reshape(2, -1)
+    vector_total = pick(halves, high_bit) + swap_narrow(pick(halves, 1 - high_bit), 2)
+    halves = vector_total.reshape(2, -1)
+    vector_total = pick(halves, low_bit) + swap_narrow(pick(halves, 1 - low_bit), 1)
     expand_new = adamw_update(
         expand_weight,
         expand_moment,
         expand_square,
-        finish(expand_quarters, expand_got, expand_end),
+        finish(expand_quarters, expand_narrow, expand_end),
         rate_expand,
     )
-    merge_got, mixed_end, vector_total, expand_new = together(
-        merge_got, mixed_end, vector_total, expand_new
-    )
-    merge_end = narrow_second(merge_quarters, merge_got)
-    halves = vector_total.reshape(2, -1)
-    vector_total = pick(halves, high_bit) + swap_narrow(pick(halves, 1 - high_bit), 2)
-    halves = vector_total.reshape(2, -1)
-    vector_total = pick(halves, low_bit) + swap_narrow(pick(halves, 1 - low_bit), 1)
-    mixed_total = finish(mixed_quarters, mixed_got, mixed_end)
+    mixed_total = finish(mixed_quarters, mixed_narrow, mixed_end)
     attend_new = adamw_update(
         attend_weight, attend_moment, attend_square, mixed_total[:, :columns], rate_attend
     )
     output_new = adamw_update(
         output_weight, output_moment, output_square, mixed_total[:, columns:], rate_output
+    )
+    merge_narrow, vector_total, expand_new, attend_new, output_new = together(
+        merge_narrow, vector_total, expand_new, attend_new, output_new
     )
     merge_new = adamw_update(
         merge_weight,
         merge_moment,
         merge_square,
-        unfold(finish(merge_quarters, merge_got, merge_end), merge_weight.shape[0]),
+        unfold(direct_sum(merge_quarters, merge_narrow), merge_weight.shape[0]),
         rate_merge,
     )
     vector_new = adamw_update(vectors, vector_moment, vector_square, vector_total, rate_vector)

time: 499 us -> 479 us (0.960)
  Pallas kernels: 198 us -> 180 us
  local copies, waits for them, and re-layouts: 59 us -> 76.6 us
  waiting for transfers between devices: 125 us -> 110 us
    ppermute x26, waiting for transfers between devices: 66 us -> 45.1 us  [swap_narrow(): return lax.ppermute(value, 'narrow', [(i, i ^ bit) for i in range(4)])]
    pallas_call x8, Pallas kernels: 65.6 us -> 53.1 us  [the longest x4 36 us: pair_gradient(): pl.pallas_call(kernel, grid=(columns // tile,), in_specs=[whole] * (2 * c...]
    ppermute x64 -> x55, starting transfers between devices: 48.7 us -> 40.7 us  [swap_wide(): return lax.ppermute(value, 'wide', [(i, i ^ bit) for i in range(8)])]
    ppermute x26, starting transfers between devices: 28.3 us -> 34.7 us  [swap_narrow(): return lax.ppermute(value, 'narrow', [(i, i ^ bit) for i in range(4)])]
    ppermute x64 -> x55, waiting for transfers between devices: 58.9 us -> 65.2 us  [swap_wide(): return lax.ppermute(value, 'wide', [(i, i ^ bit) for i in range(8)])]
    optimization_barrier x1 -> x4, local copies, waits for them, and re-layouts: 2.6 us -> 7.74 us  [together(): return lax.optimization_barrier(values)]
    unnamed x225 -> x213, local copies, waits for them, and re-layouts: 28.5 us -> 28 us
  transfers between devices with their start and end apart: 90 -> 81, of which waited for: 38 -> 34; matrix products, arithmetic and copies ran while one was open for 12% -> 16% of each run, Pallas kernels for 40% -> 38%
where the time goes in v4:
time: 479 us; the launch traced here: 471 us
  Pallas kernels  180 us (38%)
  waiting for transfers between devices  110 us (23%)
  local copies, waits for them, and re-layouts  76.6 us (16%)
  starting transfers between devices  75.4 us (16%)
  other arithmetic  26.9 us (6%)
    pallas_call x10, Pallas kernels, heavy(): pl.pallas_call(kernel, in_specs=[pl.BlockSpec(memory_space=pl.ANY)] * len...  114 us
    ppermute x55, waiting for transfers between devices, swap_wide(): return lax.ppermute(value, 'wide', [(i, i ^ bit) for i in range(8)])  65.2 us
    ppermute x26, waiting for transfers between devices, swap_narrow(): return lax.ppermute(value, 'narrow', [(i, i ^ bit) for i in range(4)])  45.1 us
    ppermute x55, starting transfers between devices, swap_wide(): return lax.ppermute(value, 'wide', [(i, i ^ bit) for i in range(8)])  40.7 us
    pallas_call x4, Pallas kernels, pair_gradient(): pl.pallas_call(kernel, grid=(columns // tile,), in_specs=[whole] * (2 * c...  36 us
    ppermute x26, starting transfers between devices, swap_narrow(): return lax.ppermute(value, 'narrow', [(i, i ^ bit) for i in range(4)])  34.7 us
    unnamed x213, local copies, waits for them, and re-layouts  28 us
    pallas_call x4, Pallas kernels, unarrange(): pl.pallas_call(kernel, grid=(1,), in_specs=[near(split), near(split), ful...  17.1 us
  transfers between devices with their start and end apart: 81, of which 34 were waited for; matrix products, arithmetic and copies ran while one was open for 16% of the time, Pallas kernels for 38%

profile of v4, /device:TPU:0, one launch (start us, length us, event | category | flops | bytes accessed | tf_op | source)
XLA Modules:
  0.0 470.9 jit_solution(4747592142818025784)
XLA Ops:
  3.4 3.0 collective-permute-start
  6.4 2.6 collective-permute-start.1
  18.4 2.3 concatenate.75.refs_2_.refs_6_.refs_13_
  20.7 2.7 broadcast_select_fusion
  24.4 2.6 shard_map.364
  30.3 4.6 collective-permute-start.5
  38.8 9.8 %collective-permute-done.5.refs_2_ = bf16[144,1152]{1,0:T(8,128)(2,1)} collective-permute-done((bf16[144,1152]{1,0:T(8,128)(2,1)}, bf16[144,1152]{1,0:T(8,128)(2,1)}, u32[]{:S(2)}, u32[]{:S(2)}) %collective-permute-start.5) | collective-permute-done | bytes 331808 | tf_op jit(solution)/shard_map/ppermute | solution.py:306
  62.9 1.7 constant_dynamic-update-slice_fusion.8.refs_0_
  64.7 3.3 shard_map.365
  71.8 1.7 collective-permute-start.15
  73.5 2.6 copy.57.refs_6_
  76.1 2.9 pad_bitcast_fusion
  79.0 8.3 %shard_map.366 = (f32[258,1152]{1,0:T(8,128)}, bf16[258,1152]{1,0:T(8,128)(2,1)}, bf16[576,384]{1,0:T(8,128)(2,1)}, bf16[576,384]{1,0:T(8,128)(2,1)}) custom-call(bf16[576,1152]{1,0:T(8,128)(2,1)} %constant_dynamic-update-slice_fusion.8.refs_0_, bf16[288,1152]{1,0:T(8,128)(2,1)} %copy-done.18, bf16[288,1152]{1,0:T(8,128)(2,1)} %copy-done.19, ...), custom_call_target="tpu_custom_call" | custom-call | bytes 1024 | tf_op jit(solution)/shard_map/pallas_call | solution.py:652
  88.6 11.1 %collective-permute-done.12.refs_1_.refs_7_ = bf16[144,4608]{1,0:T(8,128)(2,1)S(1)} collective-permute-done((bf16[144,4608]{1,0:T(8,128)(2,1)}, bf16[144,4608]{1,0:T(8,128)(2,1)S(1)}, u32[]{:S(2)}, u32[]{:S(2)}) %collective-permute-start.12) | collective-permute-done | bytes 1327136 | tf_op jit(solution)/shard_map/ppermute | solution.py:302
  104.1 9.2 %collective-permute-done.21.refs_3_ = bf16[144,1152]{1,0:T(8,128)(2,1)} collective-permute-done((bf16[144,1152]{1,0:T(8,128)(2,1)}, bf16[144,1152]{1,0:T(8,128)(2,1)}, u32[]{:S(2)}, u32[]{:S(2)}) %collective-permute-start.21) | collective-permute-done | bytes 331808 | tf_op jit(solution)/shard_map/ppermute | solution.py:306
  113.2 2.7 shard_map.367
  116.0 2.2 collective-permute-done.18
  118.2 1.8 collective-permute-done.17
  124.2 1.7 collective-permute-start.25
  127.8 14.1 %shard_map.368 = (bf16[258,3456]{1,0:T(8,128)(2,1)}, f32[12,258,258]{2,1,0:T(8,128)}, bf16[258,864]{1,0:T(8,128)(2,1)}) custom-call(bf16[288,4608]{1,0:T(8,128)(2,1)} %copy-done, bf16[144,4608]{1,0:T(8,128)(2,1)} %copy-done.2, bf16[144,4608]{1,0:T(8,128)(2,1)} %copy-done.3, bf16[288,4608]{1,0:T(8,128)(2,1)} %copy-done.1, bf16[144,4608]{1,0:T(8,128)(2,1)} %copy-done.4, ...), custom_call_target="tpu_custom_call" | custom-call | bytes 1024 | tf_op jit(solution)/shard_map/pallas_call | solution.py:652
  141.9 11.2 %collective-permute-done.22.refs_1_ = bf16[144,4608]{1,0:T(8,128)(2,1)S(1)} collective-permute-done((bf16[144,4608]{1,0:T(8,128)(2,1)}, bf16[144,4608]{1,0:T(8,128)(2,1)S(1)}, u32[]{:S(2)}, u32[]{:S(2)}) %collective-permute-start.22) | collective-permute-done | bytes 1327136 | tf_op jit(solution)/shard_map/ppermute | solution.py:302
  156.4 1.9 slice.984
  161.6 10.8 %shard_map.370 = (f32[4,258,258]{2,1,0:T(8,128)}, f32[258,1152]{1,0:T(8,128)}, bf16[258,1152]{1,0:T(8,128)(2,1)}, bf16[1152,384]{1,0:T(8,128)(2,1)}, bf16[1152,384]{1,0:T(8,128)(2,1)}) custom-call(bf16[288,4608]{1,0:T(8,128)(2,1)} %copy-done, bf16[144,4608]{1,0:T(8,128)(2,1)} %copy-done.2, bf16[144,4608]{1,0:T(8,128)(2,1)} %copy-done.3, ...), custom_call_target="tpu_custom_call" | custom-call | bytes 1024 | tf_op jit(solution)/shard_map/pallas_call | solution.py:652
  173.1 3.4 shard_map.369
  180.3 3.8 collective-permute-done.35.refs_3_
  185.7 14.4 %shard_map.371 = (bf16[258,4608]{1,0:T(8,128)(2,1)}, f32[258,4608]{1,0:T(8,128)}, bf16[2304,384]{1,0:T(8,128)(2,1)}, bf16[2304,384]{1,0:T(8,128)(2,1)}) custom-call(bf16[288,4608]{1,0:T(8,128)(2,1)} %copy-done.5, bf16[144,4608]{1,0:T(8,128)(2,1)} %copy-done.11, bf16[144,4608]{1,0:T(8,128)(2,1)} %collective-permute-done.23.refs_2_, ...), custom_call_target="tpu_custom_call" | custom-call | bytes 1024 | tf_op jit(solution)/shard_map/pallas_call | solution.py:652
  200.1 10.9 %collective-permute-done.32.refs_1_ = bf16[576,1152]{1,0:T(8,128)(2,1)S(1)} collective-permute-done((bf16[576,1152]{1,0:T(8,128)(2,1)}, bf16[576,1152]{1,0:T(8,128)(2,1)S(1)}, u32[]{:S(2)}, u32[]{:S(2)}) %collective-permute-start.32) | collective-permute-done | bytes 1327136 | tf_op jit(solution)/shard_map/ppermute | solution.py:302
  212.7 2.0 slice.986
  218.2 10.6 %shard_map.372 = (bf16[2,288,1152]{2,1,0:T(8,128)(2,1)}, bf16[2,288,1152]{2,1,0:T(8,128)(2,1)}, bf16[2,288,1152]{2,1,0:T(8,128)(2,1)}, bf16[2,288,1152]{2,1,0:T(8,128)(2,1)}) custom-call(bf16[2304,384]{1,0:T(8,128)(2,1)} %get-tuple-element.298.refs_0_, bf16[2304,384]{1,0:T(8,128)(2,1)} %collective-permute-done.40.refs_1_, ...), custom_call_target="tpu_custom_call" | custom-call | bytes 1024 | tf_op jit(solution)/shard_map/pallas_call | solution.py:458
  228.7 3.5 collective-permute-done.36
  241.8 12.0 %shard_map.373 = (bf16[258,4608]{1,0:T(8,128)(2,1)}, f32[1,4608]{1,0:T(1,128)}) custom-call(bf16[1152,1152]{1,0:T(8,128)(2,1)} %copy-done.6, bf16[576,1152]{1,0:T(8,128)(2,1)} %copy-done.12, bf16[576,1152]{1,0:T(8,128)(2,1)} %collective-permute-done.33.refs_2_, bf16[1152,1152]{1,0:T(8,128)(2,1)} %copy-done.8, bf16[576,1152]{1,0:T(8,128)(2,1)} %copy-done.16, ...), custom_call_target="tpu_custom_call" | custom-call | bytes 1024 | tf_op jit(solution)/shard_map/pallas_call | solution.py:652
  253.9 10.6 %shard_map.374 = bf16[258,1152]{1,0:T(8,128)(2,1)} custom-call(bf16[1152,1152]{1,0:T(8,128)(2,1)} %copy-done.6, bf16[576,1152]{1,0:T(8,128)(2,1)} %copy-done.12, bf16[576,1152]{1,0:T(8,128)(2,1)} %collective-permute-done.33.refs_2_, bf16[1152,1152]{1,0:T(8,128)(2,1)} %copy-done.8, bf16[576,1152]{1,0:T(8,128)(2,1)} %copy-done.16, ...), custom_call_target="tpu_custom_call" | custom-call | bytes 1024 | tf_op jit(solution)/shard_map/pallas_call | solution.py:652
  264.5 2.7 collective-permute-done.41.refs_1_
  273.5 2.1 fusion.24
  277.1 9.3 %shard_map.375 = (bf16[2,80,4608]{2,1,0:T(8,128)(2,1)}, bf16[2,80,4608]{2,1,0:T(8,128)(2,1)}, bf16[2,64,4608]{2,1,0:T(8,128)(2,1)}, bf16[2,64,4608]{2,1,0:T(8,128)(2,1)}) custom-call(bf16[576,384]{1,0:T(8,128)(2,1)} %get-tuple-element.522.refs_0_, bf16[576,384]{1,0:T(8,128)(2,1)} %get-tuple-element.520.refs_1_, ...), custom_call_target="tpu_custom_call" | custom-call | bytes 1024 | tf_op jit(solution)/shard_map/pallas_call | solution.py:458
  291.2 4.9 %shard_map.378 = (bf16[144,1152]{1,0:T(8,128)(2,1)}, bf16[144,1152]{1,0:T(8,128)(2,1)}, bf16[144,1152]{1,0:T(8,128)(2,1)}, bf16[144,1152]{1,0:T(8,128)(2,1)}) custom-call(bf16[2,288,1152]{2,1,0:T(8,128)(2,1)} %get-tuple-element.321.refs_0_, bf16[2,288,1152]{2,1,0:T(8,128)(2,1)} %copy-done.28, bf16[288,1152]{1,0:T(8,128)(2,1)} %copy-done.59, ...), custom_call_target="tpu_custom_call" | custom-call | bytes 1024 | tf_op jit(solution)/shard_map/pallas_call | solution.py:533
  296.1 12.3 %shard_map.376 = (f32[258,1152]{1,0:T(8,128)}, bf16[258,1152]{1,0:T(8,128)(2,1)}, f32[4,1152]{1,0:T(4,128)}, bf16[258,1152]{1,0:T(8,128)(2,1)}) custom-call(bf16[288,4608]{1,0:T(8,128)(2,1)} %copy-done.5, bf16[144,4608]{1,0:T(8,128)(2,1)} %copy-done.11, bf16[144,4608]{1,0:T(8,128)(2,1)} %collective-permute-done.23.refs_2_, bf16[288,4608]{1,0:T(8,128)(2,1)} %copy-done.7, ...), custom_call_target="tpu_custom_call" | custom-call | bytes 1024 | tf_op jit(solution)/shard_map/pallas_call | solution.py:652
  308.4 16.0 %shard_map.377.refs_4_.refs_6_ = bf16[258,4608]{1,0:T(8,128)(2,1)} custom-call(bf16[258,3456]{1,0:T(8,128)(2,1)} %get-tuple-element.276.refs_6_.heads_ref, f32[12,258,258]{2,1,0:T(8,128)} %get-tuple-element.337.first_ref, f32[4,258,258]{2,1,0:T(8,128)} %get-tuple-element.338.second_ref, bf16[258,1152]{1,0:T(8,128)(2,1)} %get-tuple-element.340.delta_ref, ...), custom_call_target="tpu_custom_call" | custom-call | bytes 1024 | tf_op jit(solution)/shard_map/pallas_call | solution.py:652
  328.2 1.7 collective-permute-start.54
  331.8 9.7 %shard_map.379 = (bf16[2,80,4608]{2,1,0:T(8,128)(2,1)}, bf16[2,80,4608]{2,1,0:T(8,128)(2,1)}, bf16[2,64,4608]{2,1,0:T(8,128)(2,1)}, bf16[2,64,4608]{2,1,0:T(8,128)(2,1)}) custom-call(bf16[576,384]{1,0:T(8,128)(2,1)} %get-tuple-element.353.refs_0_, bf16[576,384]{1,0:T(8,128)(2,1)} %collective-permute-done.44.refs_1_, ...), custom_call_target="tpu_custom_call" | custom-call | bytes 1024 | tf_op jit(solution)/shard_map/pallas_call | solution.py:458
  341.5 3.2 collective-permute-done.55
  349.1 4.2 shard_map.380
  353.3 1.7 collective-permute-start.60
  355.5 2.3 collective-permute-start.59
  359.2 9.4 %shard_map.381 = (bf16[258,1152]{1,0:T(8,128)(2,1)}, f32[3,1152]{1,0:T(4,128)}) custom-call(bf16[288,4608]{1,0:T(8,128)(2,1)} %copy-done, bf16[144,4608]{1,0:T(8,128)(2,1)} %copy-done.2, bf16[144,4608]{1,0:T(8,128)(2,1)} %copy-done.3, bf16[288,4608]{1,0:T(8,128)(2,1)} %copy-done.1, bf16[144,4608]{1,0:T(8,128)(2,1)} %copy-done.4, ...), custom_call_target="tpu_custom_call" | custom-call | bytes 1024 | tf_op jit(solution)/shard_map/pallas_call | solution.py:652
  368.7 6.6 %shard_map.382 = (bf16[258,1152]{1,0:T(8,128)(2,1)}, bf16[258,1152]{1,0:T(8,128)(2,1)}) custom-call(bf16[576,1152]{1,0:T(8,128)(2,1)} %constant_dynamic-update-slice_fusion.8.refs_0_, bf16[288,1152]{1,0:T(8,128)(2,1)} %copy-done.18, bf16[288,1152]{1,0:T(8,128)(2,1)} %copy-done.19, bf16[576,1152]{1,0:T(8,128)(2,1)} %collective-permute-done.16.refs_3_, ...), custom_call_target="tpu_custom_call" | custom-call | bytes 1024 | tf_op jit(solution)/shard_map/pallas_call | solution.py:652
  375.5 3.6 collective-permute-done.57.refs_1_
  381.8 1.6 collective-permute-start.62
  383.6 2.3 collective-permute-start.64
  387.0 6.4 %shard_map.383 = (bf16[2,144,1152]{2,1,0:T(8,128)(2,1)}, bf16[2,144,1152]{2,1,0:T(8,128)(2,1)}, bf16[2,144,1152]{2,1,0:T(8,128)(2,1)}, bf16[2,144,1152]{2,1,0:T(8,128)(2,1)}) custom-call(bf16[1152,384]{1,0:T(8,128)(2,1)} %get-tuple-element.385.refs_0_, bf16[1152,384]{1,0:T(8,128)(2,1)} %copy-done.52, bf16[258,1152]{1,0:T(8,128)(2,1)} %get-tuple-element.387.refs_6_.refs_2_, ...), custom_call_target="tpu_custom_call" | custom-call | bytes 1024 | tf_op jit(solution)/shard_map/pallas_call | solution.py:458
  393.4 7.8 %collective-permute-done.64 = bf16[144,1152]{1,0:T(8,128)(2,1)S(1)} collective-permute-done((bf16[144,1152]{1,0:T(8,128)(2,1)S(1)}, bf16[144,1152]{1,0:T(8,128)(2,1)S(1)}, u32[]{:S(2)}, u32[]{:S(2)}) %collective-permute-start.64) | collective-permute-done | bytes 331808 | tf_op jit(solution)/shard_map/ppermute | solution.py:306
  403.8 4.7 shard_map.384
  412.0 2.4 copy.61
  415.7 3.8 collective-permute-done.68
  419.5 4.6 collective-permute-done.69
  424.2 1.7 convert_add_fusion.2
  428.1 2.3 collective-permute-start.73
  434.1 5.3 %collective-permute-done.75 = f32[12672]{0:T(1024)S(1)} collective-permute-done((f32[12672]{0:T(1024)S(1)}, f32[12672]{0:T(1024)S(1)}, u32[]{:S(2)}, u32[]{:S(2)}) %collective-permute-start.75) | collective-permute-done | bytes 50720 | tf_op jit(solution)/shard_map/ppermute | solution.py:302
  439.4 4.0 collective-permute-done.73
  443.8 3.3 shard_map.385
  447.1 2.9 collective-permute-start.76
  450.0 1.9 collective-permute-start.78
  453.2 1.7 multiply_subtract_fusion
  461.0 2.1 multiply_subtract_fusion.3
  (430 shorter events, 134.2 us)
Async XLA Ops:
  3.4 20.7 %collective-permute-start = (bf16[160,576]{1,0:T(8,128)(2,1)}, bf16[160,576]{1,0:T(8,128)(2,1)}, u32[]{:S(2)}, u32[]{:S(2)}) collective-permute-start(bf16[160,576]{1,0:T(8,128)(2,1)} %pad_maximum_fusion.6.refs_0_), channel_id=1, source_target_pairs={{0,1},{1,0},{2,3},{3,2},{4,5},{5,4},{6,7},{7,6},{8,9},{9,8},{10,11... | collective-permute-start | bytes 552968 | tf_op jit(solution)/shard_map/ppermute | solution.py:306
  6.4 18.0 %collective-permute-start.1 = (bf16[160,576]{1,0:T(8,128)(2,1)}, bf16[160,576]{1,0:T(8,128)(2,1)}, u32[]{:S(2)}, u32[]{:S(2)}) collective-permute-start(bf16[160,576]{1,0:T(8,128)(2,1)} %pad_maximum_fusion.6.refs_0_), channel_id=1, source_target_pairs={{0,2},{1,3},{2,0},{3,1},{4,6},{5,7},{6,4},{7,5},{8,10},{9,11},{10,... | collective-permute-start | bytes 552968 | tf_op jit(solution)/shard_map/ppermute | solution.py:306
  9.0 15.4 %collective-permute-start.2 = (bf16[160,576]{1,0:T(8,128)(2,1)}, bf16[160,576]{1,0:T(8,128)(2,1)}, u32[]{:S(2)}, u32[]{:S(2)}) collective-permute-start(bf16[160,576]{1,0:T(8,128)(2,1)} %pad_maximum_fusion.6.refs_0_), channel_id=1, source_target_pairs={{0,3},{1,2},{2,1},{3,0},{4,7},{5,6},{6,5},{7,4},{8,11},{9,10},{10,... | collective-permute-start | bytes 552968 | tf_op jit(solution)/shard_map/ppermute | solution.py:306
  27.1 21.5 %collective-permute-start.3 = (bf16[288,1152]{1,0:T(8,128)(2,1)}, bf16[288,1152]{1,0:T(8,128)(2,1)S(1)}, u32[]{:S(2)}, u32[]{:S(2)}) collective-permute-start(bf16[288,1152]{1,0:T(8,128)(2,1)} %get-tuple-element.237), channel_id=1, source_target_pairs={{0,8},{4,12},{8,0},{12,4},{16,24},{20,28},{24,16},{28,20},{1,9},{5... | collective-permute-start | bytes 1990664 | tf_op jit(solution)/shard_map/ppermute | solution.py:302
  28.6 20.0 %collective-permute-start.4 = (bf16[288,1152]{1,0:T(8,128)(2,1)}, bf16[288,1152]{1,0:T(8,128)(2,1)S(1)}, u32[]{:S(2)}, u32[]{:S(2)}) collective-permute-start(bf16[288,1152]{1,0:T(8,128)(2,1)} %get-tuple-element.237), channel_id=1, source_target_pairs={{0,16},{4,20},{8,24},{12,28},{16,0},{20,4},{24,8},{28,12},{1,17},{... | collective-permute-start | bytes 1990664 | tf_op jit(solution)/shard_map/ppermute | solution.py:302
  30.3 18.2 %collective-permute-start.5 = (bf16[144,1152]{1,0:T(8,128)(2,1)}, bf16[144,1152]{1,0:T(8,128)(2,1)}, u32[]{:S(2)}, u32[]{:S(2)}) collective-permute-start(bf16[144,1152]{1,0:T(8,128)(2,1)} %pad_maximum_fusion.5.refs_0_), channel_id=1, source_target_pairs={{0,2},{1,3},{2,0},{3,1},{4,6},{5,7},{6,4},{7,5},{8,10},{9,11},{10,... | collective-permute-start | bytes 995336 | tf_op jit(solution)/shard_map/ppermute | solution.py:306
  37.8 14.8 %collective-permute-start.10 = (bf16[144,1152]{1,0:T(8,128)(2,1)}, bf16[144,1152]{1,0:T(8,128)(2,1)}, u32[]{:S(2)}, u32[]{:S(2)}) collective-permute-start(bf16[144,1152]{1,0:T(8,128)(2,1)} %pad_maximum_fusion.5.refs_0_), channel_id=1, source_target_pairs={{0,1},{1,0},{2,3},{3,2},{4,5},{5,4},{6,7},{7,6},{8,9},{9,8},{10,11... | collective-permute-start | bytes 995336 | tf_op jit(solution)/shard_map/ppermute | solution.py:306
  48.9 13.1 %collective-permute-start.8 = (bf16[288,1152]{1,0:T(8,128)(2,1)S(1)}, bf16[288,1152]{1,0:T(8,128)(2,1)S(1)}, u32[]{:S(2)}, u32[]{:S(2)}) collective-permute-start(bf16[288,1152]{1,0:T(8,128)(2,1)S(1)} %collective-permute-done.3.refs_1_), channel_id=1, source_target_pairs={{0,4},{4,0},{8,12},{12,8},{16,20},{20,16},{24,28},{28,24},{1,5},{5... | collective-permute-start | bytes 1990664 | tf_op jit(solution)/shard_map/ppermute | solution.py:302
  64.7 14.3 %collective-permute-start.16 = (bf16[576,1152]{1,0:T(8,128)(2,1)}, bf16[576,1152]{1,0:T(8,128)(2,1)}, u32[]{:S(2)}, u32[]{:S(2)}) collective-permute-start(bf16[576,1152]{1,0:T(8,128)(2,1)} %constant_dynamic-update-slice_fusion.8.refs_0_), channel_id=1, source_target_pairs={{0,4},{4,0},{8,12},{12,8},{16,20},{20,16},{24,28},{28,24},{1,5},{5... | collective-permute-start | bytes 3981320 | tf_op jit(solution)/shard_map/ppermute | solution.py:302
  68.0 31.7 %collective-permute-start.12 = (bf16[144,4608]{1,0:T(8,128)(2,1)}, bf16[144,4608]{1,0:T(8,128)(2,1)S(1)}, u32[]{:S(2)}, u32[]{:S(2)}) collective-permute-start(bf16[144,4608]{1,0:T(8,128)(2,1)} %shard_map.365), channel_id=1, source_target_pairs={{0,8},{4,12},{8,0},{12,4},{16,24},{20,28},{24,16},{28,20},{1,9},{5... | collective-permute-start | bytes 3981320 | tf_op jit(solution)/shard_map/ppermute | solution.py:302
  69.5 31.5 %collective-permute-start.13 = (bf16[144,4608]{1,0:T(8,128)(2,1)}, bf16[144,4608]{1,0:T(8,128)(2,1)S(1)}, u32[]{:S(2)}, u32[]{:S(2)}) collective-permute-start(bf16[144,4608]{1,0:T(8,128)(2,1)} %shard_map.365), channel_id=1, source_target_pairs={{0,16},{4,20},{8,24},{12,28},{16,0},{20,4},{24,8},{28,12},{1,17},{... | collective-permute-start | bytes 3981320 | tf_op jit(solution)/shard_map/ppermute | solution.py:302
  71.0 17.6 %collective-permute-start.14 = (bf16[144,1152]{1,0:T(8,128)(2,1)}, bf16[144,1152]{1,0:T(8,128)(2,1)S(1)}, u32[]{:S(2)}, u32[]{:S(2)}) collective-permute-start(bf16[144,1152]{1,0:T(8,128)(2,1)} %convert_element_type.211.refs_0_), channel_id=1, source_target_pairs={{0,2},{1,3},{2,0},{3,1},{4,6},{5,7},{6,4},{7,5},{8,10},{9,11},{10,... | collective-permute-start | bytes 995336 | tf_op jit(solution)/shard_map/ppermute | solution.py:306
  71.8 16.8 %collective-permute-start.15 = (bf16[144,1152]{1,0:T(8,128)(2,1)}, bf16[144,1152]{1,0:T(8,128)(2,1)}, u32[]{:S(2)}, u32[]{:S(2)}) collective-permute-start(bf16[144,1152]{1,0:T(8,128)(2,1)} %convert_element_type.211.refs_0_), channel_id=1, source_target_pairs={{0,1},{1,0},{2,3},{3,2},{4,5},{5,4},{6,7},{7,6},{8,9},{9,8},{10,11... | collective-permute-start | bytes 995336 | tf_op jit(solution)/shard_map/ppermute | solution.py:306
  101.0 19.0 %collective-permute-start.19 = (bf16[144,4608]{1,0:T(8,128)(2,1)S(1)}, bf16[144,4608]{1,0:T(8,128)(2,1)S(1)}, u32[]{:S(2)}, u32[]{:S(2)}) collective-permute-start(bf16[144,4608]{1,0:T(8,128)(2,1)S(1)} %collective-permute-done.12.refs_1_.refs_7_), channel_id=1, source_target_pairs={{0,4},{4,0},{8,12},{12,8},{16,20},{20,16},{24,28},{28,24},{1,5},{5... | collective-permute-start | bytes 3981320 | tf_op jit(solution)/shard_map/ppermute | solution.py:302
  101.0 20.1 %collective-permute-start.20 = (bf16[144,4608]{1,0:T(8,128)(2,1)S(1)}, bf16[144,4608]{1,0:T(8,128)(2,1)}, u32[]{:S(2)}, u32[]{:S(2)}) collective-permute-start(bf16[144,4608]{1,0:T(8,128)(2,1)S(1)} %collective-permute-done.13.refs_2_.refs_8_), channel_id=1, source_target_pairs={{0,4},{4,0},{8,12},{12,8},{16,20},{20,16},{24,28},{28,24},{1,5},{5... | collective-permute-start | bytes 3981320 | tf_op jit(solution)/shard_map/ppermute | solution.py:302
  101.5 18.5 %collective-permute-start.17 = (bf16[80,4608]{1,0:T(8,128)(2,1)S(1)}, bf16[80,4608]{1,0:T(8,128)(2,1)S(1)}, u32[]{:S(2)}, u32[]{:S(2)}) collective-permute-start(bf16[80,4608]{1,0:T(8,128)(2,1)S(1)} %slice.981), channel_id=1, source_target_pairs={{0,16},{4,20},{8,24},{12,28},{16,0},{20,4},{24,8},{28,12},{1,17},{... | collective-permute-start | bytes 2211848 | tf_op jit(solution)/shard_map/ppermute | solution.py:302
  103.2 15.0 %collective-permute-start.18 = (bf16[64,4608]{1,0:T(8,128)(2,1)S(1)}, bf16[64,4608]{1,0:T(8,128)(2,1)S(1)}, u32[]{:S(2)}, u32[]{:S(2)}) collective-permute-start(bf16[64,4608]{1,0:T(8,128)(2,1)S(1)} %slice.982), channel_id=1, source_target_pairs={{0,8},{4,12},{8,0},{12,4},{16,24},{20,28},{24,16},{28,20},{1,9},{5... | collective-permute-start | bytes 1769480 | tf_op jit(solution)/shard_map/ppermute | solution.py:302
  121.4 31.8 %collective-permute-start.22 = (bf16[144,4608]{1,0:T(8,128)(2,1)}, bf16[144,4608]{1,0:T(8,128)(2,1)S(1)}, u32[]{:S(2)}, u32[]{:S(2)}) collective-permute-start(bf16[144,4608]{1,0:T(8,128)(2,1)} %shard_map.367), channel_id=1, source_target_pairs={{0,8},{4,12},{8,0},{12,4},{16,24},{20,28},{24,16},{28,20},{1,9},{5... | collective-permute-start | bytes 3981320 | tf_op jit(solution)/shard_map/ppermute | solution.py:302
  122.0 31.5 %collective-permute-start.23 = (bf16[144,4608]{1,0:T(8,128)(2,1)}, bf16[144,4608]{1,0:T(8,128)(2,1)}, u32[]{:S(2)}, u32[]{:S(2)}) collective-permute-start(bf16[144,4608]{1,0:T(8,128)(2,1)} %shard_map.367), channel_id=1, source_target_pairs={{0,16},{4,20},{8,24},{12,28},{16,0},{20,4},{24,8},{28,12},{1,17},{... | collective-permute-start | bytes 3981320 | tf_op jit(solution)/shard_map/ppermute | solution.py:302
  123.5 18.4 %collective-permute-start.24 = (bf16[144,1152]{1,0:T(8,128)(2,1)S(1)}, bf16[144,1152]{1,0:T(8,128)(2,1)S(1)}, u32[]{:S(2)}, u32[]{:S(2)}) collective-permute-start(bf16[144,1152]{1,0:T(8,128)(2,1)S(1)} %concatenate.76.refs_0_), channel_id=1, source_target_pairs={{0,2},{1,3},{2,0},{3,1},{4,6},{5,7},{6,4},{7,5},{8,10},{9,11},{10,... | collective-permute-start | bytes 995336 | tf_op jit(solution)/shard_map/ppermute | solution.py:306
  124.2 17.7 %collective-permute-start.25 = (bf16[144,1152]{1,0:T(8,128)(2,1)S(1)}, bf16[144,1152]{1,0:T(8,128)(2,1)S(1)}, u32[]{:S(2)}, u32[]{:S(2)}) collective-permute-start(bf16[144,1152]{1,0:T(8,128)(2,1)S(1)} %concatenate.76.refs_0_), channel_id=1, source_target_pairs={{0,1},{1,0},{2,3},{3,2},{4,5},{5,4},{6,7},{7,6},{8,9},{9,8},{10,11... | collective-permute-start | bytes 995336 | tf_op jit(solution)/shard_map/ppermute | solution.py:306
  153.5 23.0 %collective-permute-start.29 = (bf16[144,4608]{1,0:T(8,128)(2,1)S(1)}, bf16[144,4608]{1,0:T(8,128)(2,1)S(1)}, u32[]{:S(2)}, u32[]{:S(2)}) collective-permute-start(bf16[144,4608]{1,0:T(8,128)(2,1)S(1)} %collective-permute-done.22.refs_1_), channel_id=1, source_target_pairs={{0,4},{4,0},{8,12},{12,8},{16,20},{20,16},{24,28},{28,24},{1,5},{5... | collective-permute-start | bytes 3981320 | tf_op jit(solution)/shard_map/ppermute | solution.py:302
  153.5 23.0 %collective-permute-start.30 = (bf16[144,4608]{1,0:T(8,128)(2,1)}, bf16[144,4608]{1,0:T(8,128)(2,1)S(1)}, u32[]{:S(2)}, u32[]{:S(2)}) collective-permute-start(bf16[144,4608]{1,0:T(8,128)(2,1)} %collective-permute-done.23.refs_2_), channel_id=1, source_target_pairs={{0,4},{4,0},{8,12},{12,8},{16,20},{20,16},{24,28},{28,24},{1,5},{5... | collective-permute-start | bytes 3981320 | tf_op jit(solution)/shard_map/ppermute | solution.py:302
  154.9 21.6 %collective-permute-start.27 = (bf16[80,4608]{1,0:T(8,128)(2,1)}, bf16[80,4608]{1,0:T(8,128)(2,1)S(1)}, u32[]{:S(2)}, u32[]{:S(2)}) collective-permute-start(bf16[80,4608]{1,0:T(8,128)(2,1)} %slice.983), channel_id=1, source_target_pairs={{0,16},{4,20},{8,24},{12,28},{16,0},{20,4},{24,8},{28,12},{1,17},{... | collective-permute-start | bytes 2211848 | tf_op jit(solution)/shard_map/ppermute | solution.py:302
  158.3 14.0 %collective-permute-start.31 = (bf16[144,1152]{1,0:T(8,128)(2,1)S(1)}, bf16[144,1152]{1,0:T(8,128)(2,1)S(1)}, u32[]{:S(2)}, u32[]{:S(2)}) collective-permute-start(bf16[144,1152]{1,0:T(8,128)(2,1)S(1)} %collective-permute-done.24.refs_2_), channel_id=1, source_target_pairs={{0,1},{1,0},{2,3},{3,2},{4,5},{5,4},{6,7},{7,6},{8,9},{9,8},{10,11... | collective-permute-start | bytes 995336 | tf_op jit(solution)/shard_map/ppermute | solution.py:306
  158.6 17.8 %collective-permute-start.28 = (bf16[64,4608]{1,0:T(8,128)(2,1)}, bf16[64,4608]{1,0:T(8,128)(2,1)}, u32[]{:S(2)}, u32[]{:S(2)}) collective-permute-start(bf16[64,4608]{1,0:T(8,128)(2,1)} %slice.984), channel_id=1, source_target_pairs={{0,8},{4,12},{8,0},{12,4},{16,24},{20,28},{24,16},{28,20},{1,9},{5... | collective-permute-start | bytes 1769480 | tf_op jit(solution)/shard_map/ppermute | solution.py:302
  179.2 31.8 %collective-permute-start.32 = (bf16[576,1152]{1,0:T(8,128)(2,1)}, bf16[576,1152]{1,0:T(8,128)(2,1)S(1)}, u32[]{:S(2)}, u32[]{:S(2)}) collective-permute-start(bf16[576,1152]{1,0:T(8,128)(2,1)} %shard_map.369), channel_id=1, source_target_pairs={{0,8},{4,12},{8,0},{12,4},{16,24},{20,28},{24,16},{28,20},{1,9},{5... | collective-permute-start | bytes 3981320 | tf_op jit(solution)/shard_map/ppermute | solution.py:302
  179.8 31.5 %collective-permute-start.33 = (bf16[576,1152]{1,0:T(8,128)(2,1)}, bf16[576,1152]{1,0:T(8,128)(2,1)}, u32[]{:S(2)}, u32[]{:S(2)}) collective-permute-start(bf16[576,1152]{1,0:T(8,128)(2,1)} %shard_map.369), channel_id=1, source_target_pairs={{0,16},{4,20},{8,24},{12,28},{16,0},{20,4},{24,8},{28,12},{1,17},{... | collective-permute-start | bytes 3981320 | tf_op jit(solution)/shard_map/ppermute | solution.py:302
  180.3 19.7 %collective-permute-start.34 = (bf16[258,1152]{1,0:T(8,128)(2,1)S(1)}, bf16[258,1152]{1,0:T(8,128)(2,1)S(1)}, u32[]{:S(2)}, u32[]{:S(2)}) collective-permute-start(bf16[258,1152]{1,0:T(8,128)(2,1)S(1)} %copy-done.9), channel_id=1, source_target_pairs={{0,4},{4,0},{8,12},{12,8},{16,20},{20,16},{24,28},{28,24},{1,5},{5... | collective-permute-start | bytes 1783304 | tf_op jit(solution)/shard_map/ppermute | solution.py:302
  211.3 21.2 %collective-permute-start.38 = (bf16[576,1152]{1,0:T(8,128)(2,1)S(1)}, bf16[576,1152]{1,0:T(8,128)(2,1)S(1)}, u32[]{:S(2)}, u32[]{:S(2)}) collective-permute-start(bf16[576,1152]{1,0:T(8,128)(2,1)S(1)} %collective-permute-done.32.refs_1_), channel_id=1, source_target_pairs={{0,4},{4,0},{8,12},{12,8},{16,20},{20,16},{24,28},{28,24},{1,5},{5... | collective-permute-start | bytes 3981320 | tf_op jit(solution)/shard_map/ppermute | solution.py:302
  211.8 20.7 %collective-permute-start.39 = (bf16[576,1152]{1,0:T(8,128)(2,1)}, bf16[576,1152]{1,0:T(8,128)(2,1)S(1)}, u32[]{:S(2)}, u32[]{:S(2)}) collective-permute-start(bf16[576,1152]{1,0:T(8,128)(2,1)} %collective-permute-done.33.refs_2_), channel_id=1, source_target_pairs={{0,4},{4,0},{8,12},{12,8},{16,20},{20,16},{24,28},{28,24},{1,5},{5... | collective-permute-start | bytes 3981320 | tf_op jit(solution)/shard_map/ppermute | solution.py:302
  214.7 17.5 %collective-permute-start.36 = (bf16[288,1152]{1,0:T(8,128)(2,1)}, bf16[288,1152]{1,0:T(8,128)(2,1)S(1)}, u32[]{:S(2)}, u32[]{:S(2)}) collective-permute-start(bf16[288,1152]{1,0:T(8,128)(2,1)} %slice.985), channel_id=1, source_target_pairs={{0,16},{4,20},{8,24},{12,28},{16,0},{20,4},{24,8},{28,12},{1,17},{... | collective-permute-start | bytes 1990664 | tf_op jit(solution)/shard_map/ppermute | solution.py:302
  215.2 17.4 %collective-permute-start.37 = (bf16[288,1152]{1,0:T(8,128)(2,1)}, bf16[288,1152]{1,0:T(8,128)(2,1)}, u32[]{:S(2)}, u32[]{:S(2)}) collective-permute-start(bf16[288,1152]{1,0:T(8,128)(2,1)} %slice.986), channel_id=1, source_target_pairs={{0,8},{4,12},{8,0},{12,4},{16,24},{20,28},{24,16},{28,20},{1,9},{5... | collective-permute-start | bytes 1990664 | tf_op jit(solution)/shard_map/ppermute | solution.py:302
  235.4 31.8 %collective-permute-start.41 = (bf16[2,288,1152]{2,1,0:T(8,128)(2,1)}, bf16[2,288,1152]{2,1,0:T(8,128)(2,1)S(1)}, u32[]{:S(2)}, u32[]{:S(2)}) collective-permute-start(bf16[2,288,1152]{2,1,0:T(8,128)(2,1)} %get-tuple-element.305), channel_id=1, source_target_pairs={{0,8},{4,12},{8,0},{12,4},{16,24},{20,28},{24,16},{28,20},{1,9},{5... | collective-permute-start | bytes 3981320 | tf_op jit(solution)/shard_map/ppermute | solution.py:302
  237.0 31.4 %collective-permute-start.42 = (bf16[2,288,1152]{2,1,0:T(8,128)(2,1)}, bf16[2,288,1152]{2,1,0:T(8,128)(2,1)S(1)}, u32[]{:S(2)}, u32[]{:S(2)}) collective-permute-start(bf16[2,288,1152]{2,1,0:T(8,128)(2,1)} %get-tuple-element.306), channel_id=1, source_target_pairs={{0,16},{4,20},{8,24},{12,28},{16,0},{20,4},{24,8},{28,12},{1,17},{... | collective-permute-start | bytes 3981320 | tf_op jit(solution)/shard_map/ppermute | solution.py:302
  238.5 26.0 %collective-permute-start.43 = (bf16[1152,384]{1,0:T(8,128)(2,1)}, bf16[1152,384]{1,0:T(8,128)(2,1)}, u32[]{:S(2)}, u32[]{:S(2)}) collective-permute-start(bf16[1152,384]{1,0:T(8,128)(2,1)} %get-tuple-element.307), channel_id=1, source_target_pairs={{0,4},{4,0},{8,12},{12,8},{16,20},{20,16},{24,28},{28,24},{1,5},{5... | collective-permute-start | bytes 2654216 | tf_op jit(solution)/shard_map/ppermute | solution.py:302
  238.5 26.0 %collective-permute-start.44 = (bf16[576,384]{1,0:T(8,128)(2,1)}, bf16[576,384]{1,0:T(8,128)(2,1)}, u32[]{:S(2)}, u32[]{:S(2)}) collective-permute-start(bf16[576,384]{1,0:T(8,128)(2,1)} %get-tuple-element.308), channel_id=1, source_target_pairs={{0,4},{4,0},{8,12},{12,8},{16,20},{20,16},{24,28},{28,24},{1,5},{5... | collective-permute-start | bytes 1327112 | tf_op jit(solution)/shard_map/ppermute | solution.py:302
  269.4 17.5 %collective-permute-start.47 = (bf16[288,1152]{1,0:T(8,128)(2,1)}, bf16[288,1152]{1,0:T(8,128)(2,1)S(1)}, u32[]{:S(2)}, u32[]{:S(2)}) collective-permute-start(bf16[288,1152]{1,0:T(8,128)(2,1)} %fusion.10), channel_id=1, source_target_pairs={{0,8},{4,12},{8,0},{12,4},{16,24},{20,28},{24,16},{28,20},{1,9},{5... | collective-permute-start | bytes 1990664 | tf_op jit(solution)/shard_map/ppermute | solution.py:302
  270.9 17.2 %collective-permute-start.46 = (bf16[288,1152]{1,0:T(8,128)(2,1)}, bf16[288,1152]{1,0:T(8,128)(2,1)S(1)}, u32[]{:S(2)}, u32[]{:S(2)}) collective-permute-start(bf16[288,1152]{1,0:T(8,128)(2,1)} %fusion.9), channel_id=1, source_target_pairs={{0,16},{4,20},{8,24},{12,28},{16,0},{20,4},{24,8},{28,12},{1,17},{... | collective-permute-start | bytes 1990664 | tf_op jit(solution)/shard_map/ppermute | solution.py:302
  288.2 36.3 %collective-permute-start.49 = (bf16[2,80,4608]{2,1,0:T(8,128)(2,1)}, bf16[2,80,4608]{2,1,0:T(8,128)(2,1)S(1)}, u32[]{:S(2)}, u32[]{:S(2)}) collective-permute-start(bf16[2,80,4608]{2,1,0:T(8,128)(2,1)} %get-tuple-element.334), channel_id=1, source_target_pairs={{0,8},{4,12},{8,0},{12,4},{16,24},{20,28},{24,16},{28,20},{1,9},{5... | collective-permute-start | bytes 4423688 | tf_op jit(solution)/shard_map/ppermute | solution.py:302
  289.7 34.8 %collective-permute-start.50 = (bf16[2,64,4608]{2,1,0:T(8,128)(2,1)}, bf16[2,64,4608]{2,1,0:T(8,128)(2,1)S(1)}, u32[]{:S(2)}, u32[]{:S(2)}) collective-permute-start(bf16[2,64,4608]{2,1,0:T(8,128)(2,1)} %get-tuple-element.335), channel_id=1, source_target_pairs={{0,16},{4,20},{8,24},{12,28},{16,0},{20,4},{24,8},{28,12},{1,17},{... | collective-permute-start | bytes 3538952 | tf_op jit(solution)/shard_map/ppermute | solution.py:302
  291.2 33.3 %collective-permute-start.51 = (bf16[1152,384]{1,0:T(8,128)(2,1)S(1)}, bf16[1152,384]{1,0:T(8,128)(2,1)S(1)}, u32[]{:S(2)}, u32[]{:S(2)}) collective-permute-start(bf16[1152,384]{1,0:T(8,128)(2,1)S(1)} %copy-done.51), channel_id=1, source_target_pairs={{0,4},{4,0},{8,12},{12,8},{16,20},{20,16},{24,28},{28,24},{1,5},{5... | collective-permute-start | bytes 2654216 | tf_op jit(solution)/shard_map/ppermute | solution.py:302
  326.9 18.6 %collective-permute-start.52 = (bf16[80,4608]{1,0:T(8,128)(2,1)}, bf16[80,4608]{1,0:T(8,128)(2,1)S(1)}, u32[]{:S(2)}, u32[]{:S(2)}) collective-permute-start(bf16[80,4608]{1,0:T(8,128)(2,1)} %fusion.6), channel_id=1, source_target_pairs={{0,16},{4,20},{8,24},{12,28},{16,0},{20,4},{24,8},{28,12},{1,17},{... | collective-permute-start | bytes 2211848 | tf_op jit(solution)/shard_map/ppermute | solution.py:302
  327.6 17.1 %collective-permute-start.53 = (bf16[64,4608]{1,0:T(8,128)(2,1)S(1)}, bf16[64,4608]{1,0:T(8,128)(2,1)S(1)}, u32[]{:S(2)}, u32[]{:S(2)}) collective-permute-start(bf16[64,4608]{1,0:T(8,128)(2,1)S(1)} %fusion.11), channel_id=1, source_target_pairs={{0,8},{4,12},{8,0},{12,4},{16,24},{20,28},{24,16},{28,20},{1,9},{5... | collective-permute-start | bytes 1769480 | tf_op jit(solution)/shard_map/ppermute | solution.py:302
  328.2 13.3 %collective-permute-start.54 = (bf16[144,1152]{1,0:T(8,128)(2,1)}, bf16[144,1152]{1,0:T(8,128)(2,1)S(1)}, u32[]{:S(2)}, u32[]{:S(2)}) collective-permute-start(bf16[144,1152]{1,0:T(8,128)(2,1)} %get-tuple-element.351), channel_id=1, source_target_pairs={{0,1},{1,0},{2,3},{3,2},{4,5},{5,4},{6,7},{7,6},{8,9},{9,8},{10,11... | collective-permute-start | bytes 995336 | tf_op jit(solution)/shard_map/ppermute | solution.py:306
  329.9 14.7 %collective-permute-start.55 = (bf16[144,1152]{1,0:T(8,128)(2,1)S(1)}, bf16[144,1152]{1,0:T(8,128)(2,1)S(1)}, u32[]{:S(2)}, u32[]{:S(2)}) collective-permute-start(bf16[144,1152]{1,0:T(8,128)(2,1)S(1)} %copy-done.97), channel_id=1, source_target_pairs={{0,1},{1,0},{2,3},{3,2},{4,5},{5,4},{6,7},{7,6},{8,9},{9,8},{10,11... | collective-permute-start | bytes 995336 | tf_op jit(solution)/shard_map/ppermute | solution.py:306
  345.5 33.6 %collective-permute-start.57 = (bf16[2,80,4608]{2,1,0:T(8,128)(2,1)}, bf16[2,80,4608]{2,1,0:T(8,128)(2,1)S(1)}, u32[]{:S(2)}, u32[]{:S(2)}) collective-permute-start(bf16[2,80,4608]{2,1,0:T(8,128)(2,1)} %get-tuple-element.360), channel_id=1, source_target_pairs={{0,8},{4,12},{8,0},{12,4},{16,24},{20,28},{24,16},{28,20},{1,9},{5... | collective-permute-start | bytes 4423688 | tf_op jit(solution)/shard_map/ppermute | solution.py:302
  346.9 28.6 %collective-permute-start.58 = (bf16[2,64,4608]{2,1,0:T(8,128)(2,1)}, bf16[2,64,4608]{2,1,0:T(8,128)(2,1)S(1)}, u32[]{:S(2)}, u32[]{:S(2)}) collective-permute-start(bf16[2,64,4608]{2,1,0:T(8,128)(2,1)} %get-tuple-element.361), channel_id=1, source_target_pairs={{0,16},{4,20},{8,24},{12,28},{16,0},{20,4},{24,8},{28,12},{1,17},{... | collective-permute-start | bytes 3538952 | tf_op jit(solution)/shard_map/ppermute | solution.py:302
  353.3 21.9 %collective-permute-start.60 = (bf16[144,1152]{1,0:T(8,128)(2,1)}, bf16[144,1152]{1,0:T(8,128)(2,1)S(1)}, u32[]{:S(2)}, u32[]{:S(2)}) collective-permute-start(bf16[144,1152]{1,0:T(8,128)(2,1)} %get-tuple-element.366), channel_id=1, source_target_pairs={{0,1},{1,0},{2,3},{3,2},{4,5},{5,4},{6,7},{7,6},{8,9},{9,8},{10,11... | collective-permute-start | bytes 995336 | tf_op jit(solution)/shard_map/ppermute | solution.py:306
  355.1 20.4 %collective-permute-start.61 = (bf16[144,1152]{1,0:T(8,128)(2,1)}, bf16[144,1152]{1,0:T(8,128)(2,1)S(1)}, u32[]{:S(2)}, u32[]{:S(2)}) collective-permute-start(bf16[144,1152]{1,0:T(8,128)(2,1)} %get-tuple-element.367), channel_id=1, source_target_pairs={{0,1},{1,0},{2,3},{3,2},{4,5},{5,4},{6,7},{7,6},{8,9},{9,8},{10,11... | collective-permute-start | bytes 995336 | tf_op jit(solution)/shard_map/ppermute | solution.py:306
  355.5 20.0 %collective-permute-start.59 = (bf16[144,1152]{1,0:T(8,128)(2,1)S(1)}, bf16[144,1152]{1,0:T(8,128)(2,1)S(1)}, u32[]{:S(2)}, u32[]{:S(2)}) collective-permute-start(bf16[144,1152]{1,0:T(8,128)(2,1)S(1)} %add_convert_fusion.10), channel_id=1, source_target_pairs={{0,2},{1,3},{2,0},{3,1},{4,6},{5,7},{6,4},{7,5},{8,10},{9,11},{10,... | collective-permute-start | bytes 995336 | tf_op jit(solution)/shard_map/ppermute | solution.py:306
  380.1 21.2 %collective-permute-start.63 = (bf16[64,4608]{1,0:T(8,128)(2,1)}, bf16[64,4608]{1,0:T(8,128)(2,1)S(1)}, u32[]{:S(2)}, u32[]{:S(2)}) collective-permute-start(bf16[64,4608]{1,0:T(8,128)(2,1)} %fusion.12), channel_id=1, source_target_pairs={{0,8},{4,12},{8,0},{12,4},{16,24},{20,28},{24,16},{28,20},{1,9},{5... | collective-permute-start | bytes 1769480 | tf_op jit(solution)/shard_map/ppermute | solution.py:302
  381.8 19.4 %collective-permute-start.62 = (bf16[80,4608]{1,0:T(8,128)(2,1)}, bf16[80,4608]{1,0:T(8,128)(2,1)S(1)}, u32[]{:S(2)}, u32[]{:S(2)}) collective-permute-start(bf16[80,4608]{1,0:T(8,128)(2,1)} %fusion.7), channel_id=1, source_target_pairs={{0,16},{4,20},{8,24},{12,28},{16,0},{20,4},{24,8},{28,12},{1,17},{... | collective-permute-start | bytes 2211848 | tf_op jit(solution)/shard_map/ppermute | solution.py:302
  383.6 17.7 %collective-permute-start.64 = (bf16[144,1152]{1,0:T(8,128)(2,1)S(1)}, bf16[144,1152]{1,0:T(8,128)(2,1)S(1)}, u32[]{:S(2)}, u32[]{:S(2)}) collective-permute-start(bf16[144,1152]{1,0:T(8,128)(2,1)S(1)} %add_convert_fusion.9), channel_id=1, source_target_pairs={{0,2},{1,3},{2,0},{3,1},{4,6},{5,7},{6,4},{7,5},{8,10},{9,11},{10,... | collective-permute-start | bytes 995336 | tf_op jit(solution)/shard_map/ppermute | solution.py:306
  402.0 22.1 %collective-permute-start.66 = (bf16[2,144,1152]{2,1,0:T(8,128)(2,1)}, bf16[2,144,1152]{2,1,0:T(8,128)(2,1)S(1)}, u32[]{:S(2)}, u32[]{:S(2)}) collective-permute-start(bf16[2,144,1152]{2,1,0:T(8,128)(2,1)} %get-tuple-element.394), channel_id=1, source_target_pairs={{0,8},{4,12},{8,0},{12,4},{16,24},{20,28},{24,16},{28,20},{1,9},{5... | collective-permute-start | bytes 1990664 | tf_op jit(solution)/shard_map/ppermute | solution.py:302
  402.5 21.6 %collective-permute-start.67 = (bf16[2,144,1152]{2,1,0:T(8,128)(2,1)}, bf16[2,144,1152]{2,1,0:T(8,128)(2,1)S(1)}, u32[]{:S(2)}, u32[]{:S(2)}) collective-permute-start(bf16[2,144,1152]{2,1,0:T(8,128)(2,1)} %get-tuple-element.395), channel_id=1, source_target_pairs={{0,16},{4,20},{8,24},{12,28},{16,0},{20,4},{24,8},{28,12},{1,17},{... | collective-permute-start | bytes 1990664 | tf_op jit(solution)/shard_map/ppermute | solution.py:302
  409.2 14.9 %collective-permute-start.69 = (bf16[144,1152]{1,0:T(8,128)(2,1)}, bf16[144,1152]{1,0:T(8,128)(2,1)}, u32[]{:S(2)}, u32[]{:S(2)}) collective-permute-start(bf16[144,1152]{1,0:T(8,128)(2,1)} %get-tuple-element.399), channel_id=1, source_target_pairs={{0,1},{1,0},{2,3},{3,2},{4,5},{5,4},{6,7},{7,6},{8,9},{9,8},{10,11... | collective-permute-start | bytes 995336 | tf_op jit(solution)/shard_map/ppermute | solution.py:306
  428.1 15.3 %collective-permute-start.73 = (bf16[144,1152]{1,0:T(8,128)(2,1)S(1)}, bf16[144,1152]{1,0:T(8,128)(2,1)}, u32[]{:S(2)}, u32[]{:S(2)}) collective-permute-start(bf16[144,1152]{1,0:T(8,128)(2,1)S(1)} %add_convert_fusion.6), channel_id=1, source_target_pairs={{0,2},{1,3},{2,0},{3,1},{4,6},{5,7},{6,4},{7,5},{8,10},{9,11},{10,... | collective-permute-start | bytes 995336 | tf_op jit(solution)/shard_map/ppermute | solution.py:306
  430.4 13.0 %collective-permute-start.72 = (bf16[144,1152]{1,0:T(8,128)(2,1)S(1)}, bf16[144,1152]{1,0:T(8,128)(2,1)}, u32[]{:S(2)}, u32[]{:S(2)}) collective-permute-start(bf16[144,1152]{1,0:T(8,128)(2,1)S(1)} %fusion.16), channel_id=1, source_target_pairs={{0,8},{4,12},{8,0},{12,4},{16,24},{20,28},{24,16},{28,20},{1,9},{5... | collective-permute-start | bytes 995336 | tf_op jit(solution)/shard_map/ppermute | solution.py:302
  431.2 12.3 %collective-permute-start.71 = (bf16[144,1152]{1,0:T(8,128)(2,1)S(1)}, bf16[144,1152]{1,0:T(8,128)(2,1)}, u32[]{:S(2)}, u32[]{:S(2)}) collective-permute-start(bf16[144,1152]{1,0:T(8,128)(2,1)S(1)} %fusion.15), channel_id=1, source_target_pairs={{0,16},{4,20},{8,24},{12,28},{16,0},{20,4},{24,8},{28,12},{1,17},{... | collective-permute-start | bytes 995336 | tf_op jit(solution)/shard_map/ppermute | solution.py:302
  443.7 12.6 %collective-permute-start.79 = (f32[6336]{0:T(1024)S(1)}, f32[6336]{0:T(1024)S(1)}, u32[]{:S(2)}, u32[]{:S(2)}) collective-permute-start(f32[6336]{0:T(1024)S(1)} %get-tuple-element.487), channel_id=1, source_target_pairs={{0,2},{1,3},{2,0},{3,1},{4,6},{5,7},{6,4},{7,5},{8,10},{9,11},{10,... | collective-permute-start | bytes 76040 | tf_op jit(solution)/shard_map/ppermute | solution.py:306
  447.1 20.3 %collective-permute-start.76 = (bf16[144,576]{1,0:T(8,128)(2,1)}, bf16[144,576]{1,0:T(8,128)(2,1)}, u32[]{:S(2)}, u32[]{:S(2)}) collective-permute-start(bf16[144,576]{1,0:T(8,128)(2,1)} %get-tuple-element.419), channel_id=1, source_target_pairs={{0,2},{1,3},{2,0},{3,1},{4,6},{5,7},{6,4},{7,5},{8,10},{9,11},{10,... | collective-permute-start | bytes 497672 | tf_op jit(solution)/shard_map/ppermute | solution.py:306
  450.0 17.4 %collective-permute-start.77 = (bf16[144,576]{1,0:T(8,128)(2,1)}, bf16[144,576]{1,0:T(8,128)(2,1)}, u32[]{:S(2)}, u32[]{:S(2)}) collective-permute-start(bf16[144,576]{1,0:T(8,128)(2,1)} %get-tuple-element.420), channel_id=1, source_target_pairs={{0,1},{1,0},{2,3},{3,2},{4,5},{5,4},{6,7},{7,6},{8,9},{9,8},{10,11... | collective-permute-start | bytes 497672 | tf_op jit(solution)/shard_map/ppermute | solution.py:306
  450.0 17.4 %collective-permute-start.78 = (bf16[144,576]{1,0:T(8,128)(2,1)}, bf16[144,576]{1,0:T(8,128)(2,1)}, u32[]{:S(2)}, u32[]{:S(2)}) collective-permute-start(bf16[144,576]{1,0:T(8,128)(2,1)} %get-tuple-element.421), channel_id=1, source_target_pairs={{0,3},{1,2},{2,1},{3,0},{4,7},{5,6},{6,5},{7,4},{8,11},{9,10},{10,... | collective-permute-start | bytes 497672 | tf_op jit(solution)/shard_map/ppermute | solution.py:306
  (115 other events, 825.5 us)

commit v5 on v4

--- a/solution.py
+++ b/solution.py
@@ -316,8 +316,17 @@
     return (wide & 1, (wide >> 1) & 1, (wide >> 2) & 1, narrow & 1, narrow >> 1)
 
 
-def split_rows(rows):
-    return -(-rows // 32) * 16
+def split_shapes(rows, columns):
+    if columns == FF:
+        return (rows, columns // 2), True
+    return (rows // 2, columns), False
+
+
+def split_block(value):
+    shape, by_columns = split_shapes(*value.shape[-2:])
+    if by_columns:
+        return value[..., : shape[1]], value[..., shape[1] :]
+    return value[..., : shape[0], :], value[..., shape[0] :, :]
 
 
 def column_blocks(kind, quarter):
@@ -418,13 +427,12 @@
 
 
 def pair_gradient(lefts, right):
-    height = lefts[0][0].shape[0]
+    height = lefts[0][4]
     rows = height // 4
-    split = split_rows(rows)
     tokens, columns = right[0].shape
     tile = 384 if height > 576 else 1152
     count = len(lefts)
-    ends = [sum(width for _, _, width in lefts[: number + 1]) // tile for number in range(count)]
+    ends = [sum(left[2] for left in lefts[: number + 1]) // tile for number in range(count)]
     starts = [0] + ends[:-1]
 
     def kernel(*refs):
@@ -450,16 +458,23 @@
         total[...] = jnp.dot(
             beside[...], joint[...], preferred_element_type=jnp.float32
         ).astype(jnp.bfloat16)
-        part_blocks(total, rows, outs)
-
-    whole = pl.BlockSpec((height, PAD), lambda i: (0, 0))
+        by_columns = split_shapes(rows, columns)[1]
+        part_blocks(total, rows, outs, step < columns // tile // 2 if by_columns else None)
+
+    whole = lambda place: pl.BlockSpec((height, PAD), lambda i: (place, 0))
     part = lambda size: pl.BlockSpec((size, tile), lambda i: (0, i))
-    pair = lambda size: pl.BlockSpec((2, size, tile), lambda i: (0, 0, i))
+    shape, by_columns = split_shapes(rows, columns)
+    half = columns // tile // 2
+    if by_columns:
+        top = pl.BlockSpec((2, rows, tile), lambda i: (0, 0, jnp.minimum(i, half - 1)))
+        bottom = pl.BlockSpec((2, rows, tile), lambda i: (0, 0, jnp.maximum(i - half, 0)))
+    else:
+        top = bottom = pl.BlockSpec((2, shape[0], tile), lambda i: (0, 0, i))
     outs = pl.pallas_call(
         kernel,
         grid=(columns // tile,),
-        in_specs=[whole] * (2 * count) + [part(tokens)] * 2,
-        out_specs=(pair(split), pair(split), pair(rows - split), pair(rows - split)),
+        in_specs=[whole(left[3]) for left in lefts for _ in range(2)] + [part(tokens)] * 2,
+        out_specs=(top, top, bottom, bottom),
         out_shape=block_shapes(rows, columns),
         scratch_shapes=[
             pltpu.VMEM((2 * PAD, tile), jnp.bfloat16),
@@ -473,31 +488,39 @@
 
 
 def block_shapes(rows, columns):
-    split = split_rows(rows)
-    top = jax.ShapeDtypeStruct((2, split, columns), jnp.bfloat16)
-    bottom = jax.ShapeDtypeStruct((2, rows - split, columns), jnp.bfloat16)
-    return top, top, bottom, bottom
-
-
-def part_blocks(total, rows, outs):
+    shape = split_shapes(rows, columns)[0]
+    return (jax.ShapeDtypeStruct((2,) + shape, jnp.bfloat16),) * 4
+
+
+def part_blocks(total, rows, outs, first_half):
     wide = lax.axis_index("wide")
     across, along = (wide >> 1) & 1, (wide >> 2) & 1
-    split = split_rows(rows)
+    half = rows // 2
     for kept_x in range(2):
         for kept_y in range(2):
             x = across if kept_x else 1 - across
             y = along if kept_y else 1 - along
             start = pl.multiple_of((2 * y + x) * rows, 16)
-            outs[1 - kept_x][1 - kept_y] = total[pl.ds(start, split)]
-            outs[3 - kept_y][1 - kept_x] = total[
-                pl.ds(pl.multiple_of(start + split, 16), rows - split)
-            ]
+            top, bottom = outs[1 - kept_x], outs[3 - kept_y]
+            if first_half is None:
+                top[1 - kept_y] = total[pl.ds(start, half)]
+                bottom[1 - kept_x] = total[pl.ds(pl.multiple_of(start + half, 16), half)]
+                continue
+
+            @pl.when(first_half)
+            def _():
+                top[1 - kept_y] = total[pl.ds(start, rows)]
+
+            @pl.when(jnp.logical_not(first_half))
+            def _():
+                bottom[1 - kept_x] = total[pl.ds(start, rows)]
 
 
 def unarrange(kind, parts, blocks, got, got_last):
-    split, columns = got_last[0].shape
-    rest = got_last[1].shape[0]
-    rows = split + rest
+    by_columns = got_last[0].shape[1] == FF // 2
+    part_rows, part_columns = got_last[0].shape
+    rows = part_rows if by_columns else 2 * part_rows
+    columns = 2 * part_columns if by_columns else part_columns
     quarter = columns // 4
     height = rows // parts
     width, column_parts = column_blocks(kind, quarter)
@@ -507,8 +530,14 @@
         outs, held = refs[6:10], refs[10]
         narrow = lax.axis_index("narrow")
         low_bit, high_bit = narrow & 1, narrow >> 1
-        held[:split] = add_low(tops[0][...], tops[1][...], tops[2][...])
-        held[split:] = add_low(bottoms[0][...], bottoms[1][...], bottoms[2][...])
+        top = add_low(tops[0][...], tops[1][...], tops[2][...])
+        bottom = add_low(bottoms[0][...], bottoms[1][...], bottoms[2][...])
+        if by_columns:
+            held[:, :part_columns] = top
+            held[:, part_columns:] = bottom
+        else:
+            held[:part_rows] = top
+            held[part_rows:] = bottom
         for owner in range(4):
             for which in range(4):
                 low_same, high_same = 1 - which // 2, 1 - which % 2
@@ -527,14 +556,13 @@
                                     part * height : (part + 1) * height
                                 ]
 
-    near = lambda size: pl.BlockSpec((None, size, columns), lambda i: (0, 0, 0))
+    near = pl.BlockSpec((None, part_rows, part_columns), lambda i: (0, 0, 0))
     full = lambda size, width: pl.BlockSpec((size, width), lambda i: (0, 0))
     shape = jax.ShapeDtypeStruct((height, parts * quarter), jnp.bfloat16)
     return pl.pallas_call(
         kernel,
         grid=(1,),
-        in_specs=[near(split), near(split), full(split, columns)]
-        + [near(rest), near(rest), full(rest, columns)],
+        in_specs=[near, near, full(part_rows, part_columns)] * 2,
         out_specs=(full(height, parts * quarter),) * 4,
         out_shape=(shape,) * 4,
         scratch_shapes=[pltpu.VMEM((rows, columns), jnp.bfloat16)],
@@ -624,8 +652,10 @@
 
 
 def gather_second(first):
-    split = split_rows(first[0].shape[0])
-    return swap_wide(first[0][:split], ALONG), swap_wide(first[1][split:], ACROSS)
+    return (
+        swap_wide(split_block(first[0])[0], ALONG),
+        swap_wide(split_block(first[1])[1], ACROSS),
+    )
 
 
 def swap_sides(first):
@@ -633,19 +663,74 @@
 
 
 def ends_of(block, second):
-    return jnp.concatenate([block, second[0], second[1]], axis=0)
-
-
-def direct_narrow(quarters):
-    return (
-        swap_narrow(quarters[KEEP_FAR], 2),
-        swap_narrow(quarters[SEND_NEAR], 1),
-        swap_narrow(quarters[SEND_FAR], 3),
-    )
-
-
-def direct_sum(quarters, got):
-    return sum(term.astype(jnp.float32) for term in (quarters[KEEP_NEAR], *got))
+    if split_shapes(*block.shape)[1]:
+        return jnp.concatenate([block, jnp.concatenate(second, axis=1)], axis=0)
+    return jnp.concatenate([block, *second], axis=0)
+
+
+def line_gradient(lefts, rights, rights_sibling):
+    tokens, height = lefts[0].shape
+    width = rights.shape[2]
+    rows = height // 4
+
+    def kernel(*refs):
+        right_ref, sibling_ref = refs[8:10]
+        outs, total = refs[10:14], refs[14]
+        chip = lax.axis_index("wide") >> 1
+        for number in range(8):
+            right = (right_ref, sibling_ref)[number // 4][number % 4]
+            part = lax.dot_general(
+                right,
+                refs[number][...],
+                (((0,), (0,)), ((), ())),
+                preferred_element_type=jnp.float32,
+            )
+            total[...] = part if number == 0 else total[...] + part
+        for owner in range(4):
+            block = total[:, owner * rows : (owner + 1) * rows].T.astype(jnp.bfloat16)
+            for relative in range(4):
+
+                @pl.when((chip ^ relative) == owner)
+                def _():
+                    outs[relative][:, :width] = block[: rows // 2]
+                    outs[relative][:, width:] = block[rows // 2 :]
+
+    shape = jax.ShapeDtypeStruct((rows // 2, 2 * width), jnp.bfloat16)
+    return pl.pallas_call(
+        kernel,
+        out_shape=(shape,) * 4,
+        scratch_shapes=[pltpu.VMEM((width, height), jnp.float32)],
+        compiler_params=PARAMS,
+        cost_estimate=LIGHT,
+    )(*lefts, rights, rights_sibling)
+
+
+def turned_update(weight, moment, square, terms, parts, step_rate):
+    rows, quarter = weight.shape
+    height = rows // parts
+
+    def kernel(*refs):
+        weight_ref, moment_ref, square_ref = refs[: 3]
+        total = sum(ref[...].astype(jnp.float32) for ref in refs[3 : 3 + len(terms)])
+        outs, gradient = refs[3 + len(terms) : 6 + len(terms)], refs[-1]
+        for part in range(parts):
+            gradient[part * height : (part + 1) * height] = total[
+                :, part * quarter : (part + 1) * quarter
+            ]
+        new = adamw_update(
+            weight_ref[...], moment_ref[...], square_ref[...], gradient[...].T, step_rate
+        )
+        for out, value in zip(outs, new):
+            out[...] = value
+
+    new = pl.pallas_call(
+        kernel,
+        out_shape=(jax.ShapeDtypeStruct((quarter, rows), jnp.float32),) * 3,
+        scratch_shapes=[pltpu.VMEM((rows, quarter), jnp.float32)],
+        compiler_params=PARAMS,
+        cost_estimate=LIGHT,
+    )(weight.T, moment.T, square.T, *terms)
+    return tuple(value.T for value in new)
 
 
 def heavy(kernel, outs, scratch, weights, operands):
@@ -938,9 +1023,11 @@
 
 def entry_backward(delta_mixed, weight, delta_one, stream_zero, gain):
     length = delta_mixed.shape[0]
+    width = D // 8
 
     def kernel(*refs):
-        mixed_ref, one_ref, stream_ref, gain_ref, low_ref, sums, full, sems, delta = refs[6:]
+        mixed_ref, one_ref, stream_ref, gain_ref, low_ref, sums = refs[6:12]
+        quarters, (full, sems, delta) = refs[12:16], refs[16:]
         weight_in = Fetch(refs[:6], full, sems)
         for step in range(3):
             columns = slice(step * D, (step + 1) * D)
@@ -950,14 +1037,28 @@
         value = delta[...]
         normed, inverse = normalize(stream_ref[...])
         zero = one_ref[...] + norm_back(value * gain_ref[...], normed, inverse)
-        low_ref[...] = zero.astype(jnp.bfloat16)
+        zero_low = zero.astype(jnp.bfloat16)
+        low_ref[...] = zero_low
+        narrow = lax.axis_index("narrow")
+        for owner in range(4):
+            for relative in range(4):
+
+                @pl.when((narrow ^ relative) == owner)
+                def _():
+                    for parity in range(2):
+                        start = (4 * parity + owner) * width
+                        quarters[relative][:, parity * width : (parity + 1) * width] = zero_low[
+                            :, start : start + width
+                        ]
+
         sums[0:1] = jnp.sum(zero, axis=0, keepdims=True)
         sums[1:2] = jnp.sum(value * normed, axis=0, keepdims=True)
         sums[2:3] = jnp.sum(value, axis=0, keepdims=True)
 
     return heavy(
         kernel,
-        [((length, D), jnp.bfloat16), ((3, D), jnp.float32)],
+        [((length, D), jnp.bfloat16), ((3, D), jnp.float32)]
+        + [((length, D // 4), jnp.bfloat16)] * 4,
         weight_scratch(D, 3 * D, 3) + [pltpu.VMEM((length, D), jnp.float32)],
         weight,
         (delta_mixed, delta_one, stream_zero, gain),
@@ -1031,7 +1132,6 @@
     vector_moment,
     vector_square,
 ):
-    high_bit, low_bit = spot()[4], spot()[3]
     core = spot()[0]
     low = jnp.bfloat16
     columns = attend_weight.shape[1]
@@ -1054,9 +1154,11 @@
     mixed_far = swap_narrow(mixed_low, 2)
     mixed_near = swap_narrow(mixed_low, 1)
     expand_low = expand_weight.astype(low)
-    merge_first, mixed_far, vector_parts, expand_low = together(
-        merge_first, mixed_far, vector_parts, expand_low
-    )
+    known_sibling = swap_wide(jnp.concatenate([joined_other, pulled], axis=1), CORE)
+    merge_first, mixed_far, vector_parts, expand_low, known_sibling = together(
+        merge_first, mixed_far, vector_parts, expand_low, known_sibling
+    )
+    joined_sibling, pulled_sibling = known_sibling[:, :D], known_sibling[:, D:]
     merge_second = gather_second(merge_first)
     merge_sides = swap_sides(merge_first)
     mixed_last = swap_narrow(mixed_far, 1)
@@ -1076,26 +1178,8 @@
     stream_zero, attend_input, attend_up, attend_up_other = merge_forward(
         joined, merge_pieces, skip_bias, gain_one, bias_one
     )
-    joined_up = upright(joined_mine)
-    joined_up_other = upright(joined_other)
-    (
-        mixed_first,
-        expand_far,
-        expand_near,
-        stream_zero,
-        attend_input,
-        attend_up_other,
-        joined_up,
-        joined_up_other,
-    ) = together(
-        mixed_first,
-        expand_far,
-        expand_near,
-        stream_zero,
-        attend_input,
-        attend_up_other,
-        joined_up,
-        joined_up_other,
+    mixed_first, expand_far, expand_near, stream_zero, attend_input, attend_up_other = together(
+        mixed_first, expand_far, expand_near, stream_zero, attend_input, attend_up_other
     )
     mixed_second = gather_second(mixed_first)
     mixed_sides = swap_sides(mixed_first)
@@ -1118,100 +1202,114 @@
         heads, mix_first, mixed_pieces, stream_zero, output_bias, gain_two, bias_two
     )
     shrink_block = arrange("shrink", 4, shrink_low, (shrink_near, shrink_far, shrink_last))[0]
-    expand_second, expand_sides, shrink_block, expand_input, ups_other = together(
-        expand_second, expand_sides, shrink_block, expand_input, ups_other
+    (
+        expand_second,
+        expand_sides,
+        shrink_block,
+        expand_input,
+        ups_other,
+        joined_mine,
+        joined_sibling,
+    ) = together(
+        expand_second,
+        expand_sides,
+        shrink_block,
+        expand_input,
+        ups_other,
+        joined_mine,
+        joined_sibling,
     )
     shrink_first = gather_first(shrink_block)
     expand_ends = ends_of(expand_block, expand_second)
     expand_pieces = (expand_ends, *expand_first, swap_wide(expand_ends, CORE), *expand_sides)
-    pulled_sibling = swap_wide(pulled, CORE)
+    joined_far = swap_narrow(joined_mine, 2)
+    joined_near = swap_narrow(joined_mine, 1)
     active, slope, active_up, active_up_other = expand_forward(
         expand_input, expand_pieces, expand_bias
     )
-    shrink_first, pulled_sibling, active, slope, active_up, active_up_other = together(
-        shrink_first, pulled_sibling, active, slope, active_up, active_up_other
+    shrink_first, joined_far, joined_near, active, slope, active_up, active_up_other = together(
+        shrink_first, joined_far, joined_near, active, slope, active_up, active_up_other
     )
     shrink_second = gather_second(shrink_first)
     shrink_sides = swap_sides(shrink_first)
     active_up_sibling = swap_wide(active_up_other, CORE)
-    shrink_blocks = pair_gradient([(active_up, active_up_sibling, D)], (pulled, pulled_sibling))
-    shrink_second, shrink_sides, shrink_blocks = together(
-        shrink_second, shrink_sides, shrink_blocks
+    shrink_blocks = pair_gradient([(active_up, active_up_sibling, D, 0, FF // 2)], (pulled, pulled_sibling))
+    shrink_second, shrink_sides, shrink_blocks, joined_far, joined_sibling, ups_other = together(
+        shrink_second, shrink_sides, shrink_blocks, joined_far, joined_sibling, ups_other
     )
     shrink_got = send(shrink_blocks)
     shrink_ends = ends_of(shrink_block, shrink_second)
     shrink_pieces = (shrink_ends, *shrink_first, swap_wide(shrink_ends, CORE), *shrink_sides)
-    ups_sibling = swap_wide(ups_other, CORE)
-    attend_up_sibling = swap_wide(attend_up_other, CORE)
+    sibling_far = swap_narrow(joined_sibling, 2)
+    joined_last = swap_narrow(joined_far, 1)
     hidden_low, hidden_sum = hidden_backward(pulled, shrink_pieces, slope)
     outputs = shrink_forward(active, shrink_pieces, stream_one, shrink_bias)[None]
-    shrink_got, ups_sibling, attend_up_sibling, hidden_low, hidden_sum, outputs, joined_up_other = (
-        together(
-            shrink_got,
-            ups_sibling,
-            attend_up_sibling,
-            hidden_low,
-            hidden_sum,
-            outputs,
-            joined_up_other,
-        )
+    (
+        shrink_got,
+        sibling_far,
+        joined_last,
+        hidden_low,
+        hidden_sum,
+        outputs,
+        joined_sibling,
+        ups_other,
+        attend_up_other,
+    ) = together(
+        shrink_got,
+        sibling_far,
+        joined_last,
+        hidden_low,
+        hidden_sum,
+        outputs,
+        joined_sibling,
+        ups_other,
+        attend_up_other,
     )
     shrink_got_last = forward(shrink_blocks, shrink_got)
     hidden_sibling = swap_wide(hidden_low, CORE)
+    ups_sibling = swap_wide(ups_other, CORE)
+    sibling_near = swap_narrow(joined_sibling, 1)
     half = D // 2
     expand_blocks = pair_gradient(
-        [(ups[half:], ups_sibling[half:], FF)], (hidden_low, hidden_sibling)
-    )
-    shrink_got_last, expand_blocks, hidden_low, joined_up_other = together(
-        shrink_got_last, expand_blocks, hidden_low, joined_up_other
+        [(ups, ups_sibling, FF, 1, half)], (hidden_low, hidden_sibling)
+    )
+    shrink_got_last, sibling_near, expand_blocks, hidden_low, sibling_far = together(
+        shrink_got_last, sibling_near, expand_blocks, hidden_low, sibling_far
     )
     expand_got = send(expand_blocks)
-    joined_sibling = swap_wide(joined_up_other, CORE)
+    sibling_last = swap_narrow(sibling_far, 1)
+    attend_up_sibling = swap_wide(attend_up_other, CORE)
     delta_one, stream_low, sums_two, delta_mixture = expand_backward(
         hidden_low, expand_pieces, mixed_pieces, pulled, stream_one, gain_two
     )
     delta_mixed = attend_backward(heads, chances_first, chances_second, delta_mixture, stream_low)
-    shrink_quarters = unarrange("shrink", 4, shrink_blocks, shrink_got, shrink_got_last)
-    expand_got, joined_sibling, delta_mixed, shrink_quarters = together(
-        expand_got, joined_sibling, delta_mixed, shrink_quarters
+    expand_got, sibling_last, delta_mixed, attend_up_sibling = together(
+        expand_got, sibling_last, delta_mixed, attend_up_sibling
     )
     expand_got_last = forward(expand_blocks, expand_got)
     mixed_sibling = swap_wide(delta_mixed, CORE)
+    shrink_quarters = unarrange("shrink", 4, shrink_blocks, shrink_got, shrink_got_last)
     shrink_narrow = narrow_first(shrink_quarters)
     mixed_blocks = pair_gradient(
-        [(attend_up, attend_up_sibling, 3 * D), (ups[:half], ups_sibling[:half], D)],
+        [(attend_up, attend_up_sibling, 3 * D, 0, half), (ups, ups_sibling, D, 0, half)],
         (delta_mixed, mixed_sibling),
     )
-    expand_got_last, shrink_narrow, mixed_blocks, delta_mixed, moments = together(
-        expand_got_last,
-        shrink_narrow,
-        mixed_blocks,
-        delta_mixed,
-        (shrink_weight, shrink_moment, shrink_square),
+    expand_got_last, shrink_narrow, mixed_blocks, delta_mixed = together(
+        expand_got_last, shrink_narrow, mixed_blocks, delta_mixed
     )
     mixed_got = send(mixed_blocks)
-    shrink_end = narrow_second(shrink_quarters, shrink_narrow)
     expand_quarters = unarrange("expand", 1, expand_blocks, expand_got, expand_got_last)
     expand_narrow = narrow_first(expand_quarters)
-    zero_low, sums_one = entry_backward(
+    shrink_end = narrow_second(shrink_quarters, shrink_narrow)
+    zero_low, sums_one, *zero_quarters = entry_backward(
         delta_mixed, mixed_pieces, delta_one, stream_zero, gain_one
     )
+    mixed_got, expand_narrow, zero_low, sums_one, zero_quarters, shrink_end = together(
+        mixed_got, expand_narrow, zero_low, sums_one, zero_quarters, shrink_end
+    )
+    mixed_got_last = forward(mixed_blocks, mixed_got)
+    zero_got = tuple(swap_narrow(zero_quarters[bit], bit) for bit in (1, 2, 3))
     input_gradient, skip_gradient = joined_backward(zero_low, merge_pieces)
-    mixed_got, shrink_end, expand_narrow, zero_low, sums_one, input_gradient, skip_gradient = (
-        together(
-            mixed_got,
-            shrink_end,
-            expand_narrow,
-            zero_low,
-            sums_one,
-            input_gradient,
-            skip_gradient,
-        )
-    )
-    mixed_got_last = forward(mixed_blocks, mixed_got)
-    expand_end = narrow_second(expand_quarters, expand_narrow)
-    zero_sibling = swap_wide(zero_low, CORE)
-    merge_blocks = pair_gradient([(joined_up, joined_sibling, D)], (zero_low, zero_sibling))
     vector_total = jnp.concatenate(
         [
             outer(row)
@@ -1227,34 +1325,48 @@
             )
         ]
     )
-    mixed_got_last, expand_end, vector_total, merge_blocks, shrink_end = together(
-        mixed_got_last, expand_end, vector_total, merge_blocks, shrink_end
-    )
-    merge_got = send(merge_blocks)
+    vector_total = vector_total + swap_wide(vector_total, CORE)
+    mixed_got_last, zero_got, vector_total, input_gradient, skip_gradient, shrink_end = together(
+        mixed_got_last, zero_got, vector_total, input_gradient, skip_gradient, shrink_end
+    )
     mixed_quarters = unarrange("attend_output", 1, mixed_blocks, mixed_got, mixed_got_last)
     mixed_narrow = narrow_first(mixed_quarters)
-    vector_total = vector_total + swap_wide(vector_total, CORE)
-    merge_got, mixed_narrow, vector_total, expand_end, shrink_end = together(
-        merge_got, mixed_narrow, vector_total, expand_end, shrink_end
-    )
-    merge_got_last = forward(merge_blocks, merge_got)
+    expand_end = narrow_second(expand_quarters, expand_narrow)
+    zero_line = jnp.stack([zero_quarters[0], *zero_got])
+    zero_line_sibling = swap_wide(zero_line, CORE)
+    merge_blocks = line_gradient(
+        (
+            joined_mine,
+            joined_near,
+            joined_far,
+            joined_last,
+            joined_sibling,
+            sibling_near,
+            sibling_far,
+            sibling_last,
+        ),
+        zero_line,
+        zero_line_sibling,
+    )
+    vector_total = vector_total + swap_wide(vector_total, ACROSS)
+    mixed_narrow, merge_blocks, vector_total, shrink_end, expand_end = together(
+        mixed_narrow, merge_blocks, vector_total, shrink_end, expand_end
+    )
+    vector_total = vector_total + swap_wide(vector_total, ALONG)
     mixed_end = narrow_second(mixed_quarters, mixed_narrow)
-    vector_total = vector_total + swap_wide(vector_total, ACROSS)
-    vector_total = vector_total + swap_wide(vector_total, ALONG)
-    shrink_sum = unfold(
-        finish(shrink_quarters, shrink_narrow, shrink_end), shrink_weight.shape[0]
-    )
-    shrink_new = adamw_update(*[moment.T for moment in moments], shrink_sum.T, rate_shrink)
-    shrink_new = [new.T for new in shrink_new]
-    merge_got_last, mixed_end, vector_total, shrink_new, expand_end = together(
-        merge_got_last, mixed_end, vector_total, shrink_new, expand_end
-    )
-    merge_quarters = unarrange("merge", 2, merge_blocks, merge_got, merge_got_last)
-    merge_narrow = direct_narrow(merge_quarters)
-    halves = vector_total.reshape(2, -1)
-    vector_total = pick(halves, high_bit) + swap_narrow(pick(halves, 1 - high_bit), 2)
-    halves = vector_total.reshape(2, -1)
-    vector_total = pick(halves, low_bit) + swap_narrow(pick(halves, 1 - low_bit), 1)
+    merge_got = (
+        swap_wide(merge_blocks[1], ACROSS),
+        swap_wide(merge_blocks[2], ALONG),
+        swap_wide(merge_blocks[3], ACROSS + ALONG),
+    )
+    shrink_new = turned_update(
+        shrink_weight,
+        shrink_moment,
+        shrink_square,
+        (shrink_quarters[KEEP_NEAR], shrink_narrow[1], shrink_end),
+        4,
+        rate_shrink,
+    )
     expand_new = adamw_update(
         expand_weight,
         expand_moment,
@@ -1262,22 +1374,28 @@
         finish(expand_quarters, expand_narrow, expand_end),
         rate_expand,
     )
-    mixed_total = finish(mixed_quarters, mixed_narrow, mixed_end)
-    attend_new = adamw_update(
-        attend_weight, attend_moment, attend_square, mixed_total[:, :columns], rate_attend
-    )
-    output_new = adamw_update(
-        output_weight, output_moment, output_square, mixed_total[:, columns:], rate_output
-    )
-    merge_narrow, vector_total, expand_new, attend_new, output_new = together(
-        merge_narrow, vector_total, expand_new, attend_new, output_new
-    )
+    merge_sum = sum(term.astype(jnp.float32) for term in (merge_blocks[0], *merge_got))
     merge_new = adamw_update(
         merge_weight,
         merge_moment,
         merge_square,
-        unfold(direct_sum(merge_quarters, merge_narrow), merge_weight.shape[0]),
+        unfold(merge_sum, merge_weight.shape[0]),
         rate_merge,
+    )
+    merge_new, mixed_end, vector_total, shrink_new, expand_new = together(
+        merge_new, mixed_end, vector_total, shrink_new, expand_new
+    )
+    vector_parts = vector_total.reshape(4, -1)
+    narrow = lax.axis_index("narrow")
+    vector_total = pick(vector_parts, narrow)
+    for bit in (1, 2, 3):
+        vector_total = vector_total + swap_narrow(pick(vector_parts, narrow ^ bit), bit)
+    mixed_total = finish(mixed_quarters, mixed_narrow, mixed_end)
+    attend_new = adamw_update(
+        attend_weight, attend_moment, attend_square, mixed_total[:, :columns], rate_attend
+    )
+    output_new = adamw_update(
+        output_weight, output_moment, output_square, mixed_total[:, columns:], rate_output
     )
     vector_new = adamw_update(vectors, vector_moment, vector_square, vector_total, rate_vector)
     return (

time: 479 us -> 471 us (0.983)
  local copies, waits for them, and re-layouts: 76.6 us -> 53.7 us
  waiting for transfers between devices: 110 us -> 122 us
  other arithmetic: 26.9 us -> 20.8 us
  starting transfers between devices: 75.4 us -> 81.1 us
    ppermute x26 -> x33, waiting for transfers between devices: 45.1 us -> 78.4 us  [swap_narrow(): return lax.ppermute(value, 'narrow', [(i, i ^ bit) for i in range(4)])]
    ppermute x55 -> x53, waiting for transfers between devices: 65.2 us -> 43.5 us  [swap_wide(): return lax.ppermute(value, 'wide', [(i, i ^ bit) for i in range(8)])]
    ppermute x26 -> x33, starting transfers between devices: 34.7 us -> 43.6 us  [swap_narrow(): return lax.ppermute(value, 'narrow', [(i, i ^ bit) for i in range(4)])]
    optimization_barrier x4 -> x0, local copies, waits for them, and re-layouts: 7.74 us -> none  [together(): return lax.optimization_barrier(values)]
    unnamed x213 -> x197, local copies, waits for them, and re-layouts: 28 us -> 22.7 us
    concatenate x10 -> x12, local copies, waits for them, and re-layouts: 5.11 us -> 10.1 us  [inner(): jnp.concatenate([value[..., (2 * n + p) * width:(2 * n + p + 1) * width]...]
    slice x10 -> x9, local copies, waits for them, and re-layouts: 10.4 us -> 5.98 us  [the longest x4 3.44 us: split_block(): return (value[..., :shape[0], :], value[..., shape[0]:, :])]
    ppermute x55 -> x53, starting transfers between devices: 40.7 us -> 37.5 us  [swap_wide(): return lax.ppermute(value, 'wide', [(i, i ^ bit) for i in range(8)])]
  transfers between devices with their start and end apart: 81 -> 86, of which waited for: 34 -> 38; matrix products, arithmetic and copies ran while one was open for 16% -> 9% of each run, Pallas kernels for 38% -> 40%
where the time goes in v5:
time: 471 us; the launch traced here: 463 us
  Pallas kernels  184 us (39%)
  waiting for transfers between devices  122 us (26%)
  starting transfers between devices  81.1 us (17%)
  local copies, waits for them, and re-layouts  53.7 us (11%)
  other arithmetic  20.8 us (4%)
    pallas_call x10, Pallas kernels, heavy(): pl.pallas_call(kernel, in_specs=[pl.BlockSpec(memory_space=pl.ANY)] * len...  115 us
    ppermute x33, waiting for transfers between devices, swap_narrow(): return lax.ppermute(value, 'narrow', [(i, i ^ bit) for i in range(4)])  78.4 us
    ppermute x33, starting transfers between devices, swap_narrow(): return lax.ppermute(value, 'narrow', [(i, i ^ bit) for i in range(4)])  43.6 us
    ppermute x53, waiting for transfers between devices, swap_wide(): return lax.ppermute(value, 'wide', [(i, i ^ bit) for i in range(8)])  43.5 us
    ppermute x53, starting transfers between devices, swap_wide(): return lax.ppermute(value, 'wide', [(i, i ^ bit) for i in range(8)])  37.5 us
    pallas_call x3, Pallas kernels, pair_gradient(): pl.pallas_call(kernel, grid=(columns // tile,), in_specs=[whole(left[3])...  30.4 us
    unnamed x197, local copies, waits for them, and re-layouts  22.7 us
    pallas_call x3, Pallas kernels, unarrange(): pl.pallas_call(kernel, grid=(1,), in_specs=[near, near, full(part_rows, p...  13.6 us
  transfers between devices with their start and end apart: 86, of which 38 were waited for; matrix products, arithmetic and copies ran while one was open for 9% of the time, Pallas kernels for 40%

profile of v5, /device:TPU:0, one launch (start us, length us, event | category | flops | bytes accessed | tf_op | source)
XLA Modules:
  0.0 463.5 jit_solution(6355071714966186667)
XLA Ops:
  3.5 3.0 collective-permute-start
  6.5 2.6 collective-permute-start.1
  9.7 1.6 concatenate.79
  11.2 1.6 concatenate.80
  12.8 3.2 concatenate.78.refs_6_
  18.1 1.7 concatenate.81.refs_2_.refs_6_.refs_13_
  20.7 3.8 collective-permute-done.1.refs_2_
  25.7 2.7 shard_map.364
  31.6 4.6 collective-permute-start.5
  39.5 12.1 %collective-permute-done.5.refs_2_ = bf16[144,1152]{1,0:T(8,128)(2,1)} collective-permute-done((bf16[144,1152]{1,0:T(8,128)(2,1)}, bf16[144,1152]{1,0:T(8,128)(2,1)}, u32[]{:S(2)}, u32[]{:S(2)}) %collective-permute-start.5) | collective-permute-done | bytes 331808 | tf_op jit(solution)/shard_map/ppermute | solution.py:306
  65.1 2.0 constant_dynamic-update-slice_fusion.1
  67.1 1.7 constant_dynamic-update-slice_fusion.refs_0_
  68.9 3.3 shard_map.365
  75.4 1.7 collective-permute-start.16
  78.2 8.3 %shard_map.366 = (f32[258,1152]{1,0:T(8,128)}, bf16[258,1152]{1,0:T(8,128)(2,1)}, bf16[576,384]{1,0:T(8,128)(2,1)}, bf16[576,384]{1,0:T(8,128)(2,1)}) custom-call(bf16[576,1152]{1,0:T(8,128)(2,1)} %constant_dynamic-update-slice_fusion.refs_0_, bf16[288,1152]{1,0:T(8,128)(2,1)} %copy-done.22, bf16[288,1152]{1,0:T(8,128)(2,1)} %copy-done.23, ...), custom_call_target="tpu_custom_call" | custom-call | bytes 1024 | tf_op jit(solution)/shard_map/pallas_call | solution.py:737
  86.5 6.1 %collective-permute-done.15.refs_2_ = bf16[144,1152]{1,0:T(8,128)(2,1)S(1)} collective-permute-done((bf16[144,1152]{1,0:T(8,128)(2,1)S(1)}, bf16[144,1152]{1,0:T(8,128)(2,1)S(1)}, u32[]{:S(2)}, u32[]{:S(2)}) %collective-permute-start.15) | collective-permute-done | bytes 331808 | tf_op jit(solution)/shard_map/ppermute | solution.py:306
  92.6 11.3 %collective-permute-done.13.refs_1_.refs_7_ = bf16[144,4608]{1,0:T(8,128)(2,1)S(1)} collective-permute-done((bf16[144,4608]{1,0:T(8,128)(2,1)}, bf16[144,4608]{1,0:T(8,128)(2,1)S(1)}, u32[]{:S(2)}, u32[]{:S(2)}) %collective-permute-start.13) | collective-permute-done | bytes 1327136 | tf_op jit(solution)/shard_map/ppermute | solution.py:302
  108.7 8.9 %collective-permute-done.22.refs_3_ = bf16[144,1152]{1,0:T(8,128)(2,1)} collective-permute-done((bf16[144,1152]{1,0:T(8,128)(2,1)}, bf16[144,1152]{1,0:T(8,128)(2,1)}, u32[]{:S(2)}, u32[]{:S(2)}) %collective-permute-start.22) | collective-permute-done | bytes 331808 | tf_op jit(solution)/shard_map/ppermute | solution.py:306
  117.6 2.8 shard_map.367
  120.4 2.3 collective-permute-done.18
  128.6 1.7 collective-permute-done.27.refs_3_.refs_9_
  131.7 14.1 %shard_map.368 = (bf16[258,3456]{1,0:T(8,128)(2,1)}, f32[12,258,258]{2,1,0:T(8,128)}, bf16[258,864]{1,0:T(8,128)(2,1)}) custom-call(bf16[288,4608]{1,0:T(8,128)(2,1)} %copy-done, bf16[144,4608]{1,0:T(8,128)(2,1)} %copy-done.2, bf16[144,4608]{1,0:T(8,128)(2,1)} %copy-done.3, bf16[288,4608]{1,0:T(8,128)(2,1)} %copy-done.1, bf16[144,4608]{1,0:T(8,128)(2,1)} %copy-done.5, ...), custom_call_target="tpu_custom_call" | custom-call | bytes 1024 | tf_op jit(solution)/shard_map/pallas_call | solution.py:737
  145.8 11.2 %collective-permute-done.23.refs_1_ = bf16[144,4608]{1,0:T(8,128)(2,1)S(1)} collective-permute-done((bf16[144,4608]{1,0:T(8,128)(2,1)}, bf16[144,4608]{1,0:T(8,128)(2,1)S(1)}, u32[]{:S(2)}, u32[]{:S(2)}) %collective-permute-start.23) | collective-permute-done | bytes 1327136 | tf_op jit(solution)/shard_map/ppermute | solution.py:302
  160.6 2.4 fusion.16
  163.0 10.7 %shard_map.370 = (f32[4,258,258]{2,1,0:T(8,128)}, f32[258,1152]{1,0:T(8,128)}, bf16[258,1152]{1,0:T(8,128)(2,1)}, bf16[1152,384]{1,0:T(8,128)(2,1)}, bf16[1152,384]{1,0:T(8,128)(2,1)}) custom-call(bf16[288,4608]{1,0:T(8,128)(2,1)} %copy-done, bf16[144,4608]{1,0:T(8,128)(2,1)} %copy-done.2, bf16[144,4608]{1,0:T(8,128)(2,1)} %copy-done.3, ...), custom_call_target="tpu_custom_call" | custom-call | bytes 1024 | tf_op jit(solution)/shard_map/pallas_call | solution.py:737
  174.5 3.4 shard_map.369
  181.8 1.5 collective-permute-start.34
  183.4 1.6 collective-permute-start.35
  187.5 14.3 %shard_map.371 = (bf16[258,4608]{1,0:T(8,128)(2,1)}, f32[258,4608]{1,0:T(8,128)}, bf16[2304,384]{1,0:T(8,128)(2,1)}, bf16[2304,384]{1,0:T(8,128)(2,1)}) custom-call(bf16[288,4608]{1,0:T(8,128)(2,1)} %copy-done.4, bf16[144,4608]{1,0:T(8,128)(2,1)} %copy-done.11, bf16[144,4608]{1,0:T(8,128)(2,1)} %copy-done.12, bf16[288,4608]{1,0:T(8,128)(2,1)} %copy-done.8, ...), custom_call_target="tpu_custom_call" | custom-call | bytes 1024 | tf_op jit(solution)/shard_map/pallas_call | solution.py:737
  201.8 11.3 %collective-permute-done.35.refs_2_ = bf16[258,1152]{1,0:T(8,128)(2,1)} collective-permute-done((bf16[258,1152]{1,0:T(8,128)(2,1)}, bf16[258,1152]{1,0:T(8,128)(2,1)}, u32[]{:S(2)}, u32[]{:S(2)}) %collective-permute-start.35) | collective-permute-done | bytes 594464 | tf_op jit(solution)/shard_map/ppermute | solution.py:306
  219.8 10.6 %shard_map.372 = (bf16[2,288,1152]{2,1,0:T(8,128)(2,1)}, bf16[2,288,1152]{2,1,0:T(8,128)(2,1)}, bf16[2,288,1152]{2,1,0:T(8,128)(2,1)}, bf16[2,288,1152]{2,1,0:T(8,128)(2,1)}) custom-call(bf16[2304,384]{1,0:T(8,128)(2,1)} %get-tuple-element.299.refs_0_, bf16[2304,384]{1,0:T(8,128)(2,1)} %collective-permute-done.42.refs_1_, bf16[258,1152]{1,0:T(8,128)(2,1)} %copy-done.7, ...), custom_call_target="tpu_custom_call" | custom-call | bytes 1024 | tf_op jit(solution)/shard_map/pallas_call | solution.py:473
  230.4 2.8 collective-permute-done.38
  234.4 1.7 constant_dynamic-update-slice_fusion.4
  239.2 1.8 collective-permute-start.45
  243.8 12.1 %shard_map.373 = (bf16[258,4608]{1,0:T(8,128)(2,1)}, f32[1,4608]{1,0:T(1,128)}) custom-call(bf16[1152,1152]{1,0:T(8,128)(2,1)} %copy-done.6, bf16[576,1152]{1,0:T(8,128)(2,1)} %copy-done.13, bf16[576,1152]{1,0:T(8,128)(2,1)} %copy-done.14, bf16[1152,1152]{1,0:T(8,128)(2,1)} %copy-done.9, bf16[576,1152]{1,0:T(8,128)(2,1)} %copy-done.20, ...), custom_call_target="tpu_custom_call" | custom-call | bytes 1024 | tf_op jit(solution)/shard_map/pallas_call | solution.py:737
  255.9 10.7 %shard_map.374 = bf16[258,1152]{1,0:T(8,128)(2,1)} custom-call(bf16[1152,1152]{1,0:T(8,128)(2,1)} %copy-done.6, bf16[576,1152]{1,0:T(8,128)(2,1)} %copy-done.13, bf16[576,1152]{1,0:T(8,128)(2,1)} %copy-done.14, bf16[1152,1152]{1,0:T(8,128)(2,1)} %copy-done.9, bf16[576,1152]{1,0:T(8,128)(2,1)} %copy-done.20, bf16[576,1152]{1,0:T(8,128)(2,1)} %copy-done.21, ...), custom_call_target="tpu_custom_call" | custom-call | bytes 1024 | tf_op jit(solution)/shard_map/pallas_call | solution.py:737
  266.6 2.3 collective-permute-done.45.refs_6_
  274.4 1.7 collective-permute-start.50
  277.9 10.0 %shard_map.375 = (bf16[2,144,2304]{2,1,0:T(8,128)(2,1)}, bf16[2,144,2304]{2,1,0:T(8,128)(2,1)}, bf16[2,144,2304]{2,1,0:T(8,128)(2,1)}, bf16[2,144,2304]{2,1,0:T(8,128)(2,1)}) custom-call(bf16[1152,384]{1,0:T(8,128)(2,1)} %get-tuple-element.330.refs_0_.refs_2_, bf16[1152,384]{1,0:T(8,128)(2,1)} %copy-done.24, ...), custom_call_target="tpu_custom_call" | custom-call | bytes 1024 | tf_op jit(solution)/shard_map/pallas_call | solution.py:473
  287.9 2.2 collective-permute-done.50.refs_5_
  295.2 12.3 %shard_map.376 = (f32[258,1152]{1,0:T(8,128)}, bf16[258,1152]{1,0:T(8,128)(2,1)}, f32[4,1152]{1,0:T(4,128)}, bf16[258,1152]{1,0:T(8,128)(2,1)}) custom-call(bf16[288,4608]{1,0:T(8,128)(2,1)} %copy-done.4, bf16[144,4608]{1,0:T(8,128)(2,1)} %copy-done.11, bf16[144,4608]{1,0:T(8,128)(2,1)} %copy-done.12, bf16[288,4608]{1,0:T(8,128)(2,1)} %copy-done.8, ...), custom_call_target="tpu_custom_call" | custom-call | bytes 1024 | tf_op jit(solution)/shard_map/pallas_call | solution.py:737
  307.5 16.0 %shard_map.377.refs_4_.refs_6_ = bf16[258,4608]{1,0:T(8,128)(2,1)} custom-call(bf16[258,3456]{1,0:T(8,128)(2,1)} %get-tuple-element.275.refs_6_.heads_ref, f32[12,258,258]{2,1,0:T(8,128)} %get-tuple-element.342.first_ref, f32[4,258,258]{2,1,0:T(8,128)} %get-tuple-element.343.second_ref, bf16[258,1152]{1,0:T(8,128)(2,1)} %get-tuple-element.345.delta_ref, ...), custom_call_target="tpu_custom_call" | custom-call | bytes 1024 | tf_op jit(solution)/shard_map/pallas_call | solution.py:737
  329.4 4.5 shard_map.378
  334.1 1.7 collective-permute-start.60
  337.4 9.8 %shard_map.379 = (bf16[2,144,2304]{2,1,0:T(8,128)(2,1)}, bf16[2,144,2304]{2,1,0:T(8,128)(2,1)}, bf16[2,144,2304]{2,1,0:T(8,128)(2,1)}, bf16[2,144,2304]{2,1,0:T(8,128)(2,1)}) custom-call(bf16[576,384]{1,0:T(8,128)(2,1)} %get-tuple-element.355.refs_0_, bf16[576,384]{1,0:T(8,128)(2,1)} %copy-done.71, bf16[1152,384]{1,0:T(8,128)(2,1)} %get-tuple-element.330.refs_0_.refs_2_, ...), custom_call_target="tpu_custom_call" | custom-call | bytes 1024 | tf_op jit(solution)/shard_map/pallas_call | solution.py:473
  347.2 3.1 collective-permute-done.60.refs_4_
  353.4 4.4 shard_map.380
  360.0 10.4 %shard_map.381 = (bf16[258,1152]{1,0:T(8,128)(2,1)}, f32[3,1152]{1,0:T(4,128)}, bf16[258,288]{1,0:T(8,128)(2,1)}, bf16[258,288]{1,0:T(8,128)(2,1)}, bf16[258,288]{1,0:T(8,128)(2,1)}, /*index=5*/bf16[258,288]{1,0:T(8,128)(2,1)}) custom-call(bf16[288,4608]{1,0:T(8,128)(2,1)} %copy-done, bf16[144,4608]{1,0:T(8,128)(2,1)} %copy-done.2, ...), custom_call_target="tpu_custom_call" | custom-call | bytes 1024 | tf_op jit(solution)/shard_map/pallas_call | solution.py:737
  370.5 4.2 collective-permute-done.64
  374.7 4.6 collective-permute-done.65
  387.3 2.4 collective-permute-start.71
  389.7 6.5 %shard_map.382 = (bf16[258,1152]{1,0:T(8,128)(2,1)}, bf16[258,1152]{1,0:T(8,128)(2,1)}) custom-call(bf16[576,1152]{1,0:T(8,128)(2,1)} %constant_dynamic-update-slice_fusion.refs_0_, bf16[288,1152]{1,0:T(8,128)(2,1)} %copy-done.22, bf16[288,1152]{1,0:T(8,128)(2,1)} %copy-done.23, bf16[576,1152]{1,0:T(8,128)(2,1)} %copy-done.16, bf16[288,1152]{1,0:T(8,128)(2,1)} %copy-done.40, ...), custom_call_target="tpu_custom_call" | custom-call | bytes 1024 | tf_op jit(solution)/shard_map/pallas_call | solution.py:737
  396.3 7.5 %collective-permute-done.70 = bf16[258,288]{1,0:T(8,128)(2,1)S(1)} collective-permute-done((bf16[258,288]{1,0:T(8,128)(2,1)}, bf16[258,288]{1,0:T(8,128)(2,1)S(1)}, u32[]{:S(2)}, u32[]{:S(2)}) %collective-permute-start.70) | collective-permute-done | bytes 148640 | tf_op jit(solution)/shard_map/ppermute | solution.py:306
  405.1 4.4 collective-permute-start.77
  409.5 4.7 %shard_map.383 = (bf16[144,1152]{1,0:T(8,128)(2,1)}, bf16[144,1152]{1,0:T(8,128)(2,1)}, bf16[144,1152]{1,0:T(8,128)(2,1)}, bf16[144,1152]{1,0:T(8,128)(2,1)}) custom-call(bf16[2,144,2304]{2,1,0:T(8,128)(2,1)} %get-tuple-element.362.refs_0_, bf16[2,144,2304]{2,1,0:T(8,128)(2,1)} %copy-done.27, bf16[144,2304]{1,0:T(8,128)(2,1)} %copy-done.55, ...), custom_call_target="tpu_custom_call" | custom-call | bytes 1024 | tf_op jit(solution)/shard_map/pallas_call | solution.py:562
  414.2 2.0 collective-permute-start.74
  417.5 2.9 collective-permute-done.76
  421.4 8.1 %shard_map.384 = (bf16[144,576]{1,0:T(8,128)(2,1)}, bf16[144,576]{1,0:T(8,128)(2,1)}, bf16[144,576]{1,0:T(8,128)(2,1)}, bf16[144,576]{1,0:T(8,128)(2,1)}) custom-call(bf16[258,1152]{1,0:T(8,128)(2,1)} %get-tuple-element.286.refs_0_, bf16[258,1152]{1,0:T(8,128)(2,1)} %collective-permute-done.36.refs_1_, bf16[258,1152]{1,0:T(8,128)(2,1)} %collective-permute-done.35.refs_2_, ...), custom_call_target="tpu_custom_call" | custom-call | bytes 1024 | tf_op jit(solution)/shard_map/pallas_call | solution.py:699
  430.2 6.2 %collective-permute-done.74 = bf16[144,1152]{1,0:T(8,128)(2,1)S(1)} collective-permute-done((bf16[144,1152]{1,0:T(8,128)(2,1)}, bf16[144,1152]{1,0:T(8,128)(2,1)S(1)}, u32[]{:S(2)}, u32[]{:S(2)}) %collective-permute-start.74) | collective-permute-done | bytes 331808 | tf_op jit(solution)/shard_map/ppermute | solution.py:306
  441.9 1.7 multiply_subtract_fusion
  443.6 4.0 shard_map.385
  450.4 3.8 collective-permute-done.81
  454.5 2.3 collective-permute-start.84
  456.8 2.1 collective-permute-start.85
  (414 shorter events, 118.2 us)
Async XLA Ops:
  3.5 17.2 %collective-permute-start = (bf16[160,576]{1,0:T(8,128)(2,1)}, bf16[160,576]{1,0:T(8,128)(2,1)}, u32[]{:S(2)}, u32[]{:S(2)}) collective-permute-start(bf16[160,576]{1,0:T(8,128)(2,1)} %pad_maximum_fusion.4.refs_0_), channel_id=1, source_target_pairs={{0,1},{1,0},{2,3},{3,2},{4,5},{5,4},{6,7},{7,6},{8,9},{9,8},{10,11... | collective-permute-start | bytes 552968 | tf_op jit(solution)/shard_map/ppermute | solution.py:306
  6.5 18.0 %collective-permute-start.1 = (bf16[160,576]{1,0:T(8,128)(2,1)}, bf16[160,576]{1,0:T(8,128)(2,1)}, u32[]{:S(2)}, u32[]{:S(2)}) collective-permute-start(bf16[160,576]{1,0:T(8,128)(2,1)} %pad_maximum_fusion.4.refs_0_), channel_id=1, source_target_pairs={{0,2},{1,3},{2,0},{3,1},{4,6},{5,7},{6,4},{7,5},{8,10},{9,11},{10,... | collective-permute-start | bytes 552968 | tf_op jit(solution)/shard_map/ppermute | solution.py:306
  9.1 15.4 %collective-permute-start.2 = (bf16[160,576]{1,0:T(8,128)(2,1)}, bf16[160,576]{1,0:T(8,128)(2,1)}, u32[]{:S(2)}, u32[]{:S(2)}) collective-permute-start(bf16[160,576]{1,0:T(8,128)(2,1)} %pad_maximum_fusion.4.refs_0_), channel_id=1, source_target_pairs={{0,3},{1,2},{2,1},{3,0},{4,7},{5,6},{6,5},{7,4},{8,11},{9,10},{10,... | collective-permute-start | bytes 552968 | tf_op jit(solution)/shard_map/ppermute | solution.py:306
  25.7 26.0 %collective-permute-start.6 = (bf16[258,2304]{1,0:T(8,128)(2,1)}, bf16[258,2304]{1,0:T(8,128)(2,1)}, u32[]{:S(2)}, u32[]{:S(2)}) collective-permute-start(bf16[258,2304]{1,0:T(8,128)(2,1)} %pad_maximum_fusion), channel_id=1, source_target_pairs={{0,4},{4,0},{8,12},{12,8},{16,20},{20,16},{24,28},{28,24},{1,5},{5... | collective-permute-start | bytes 3566600 | tf_op jit(solution)/shard_map/ppermute | solution.py:302
  28.3 23.3 %collective-permute-start.3 = (bf16[288,1152]{1,0:T(8,128)(2,1)}, bf16[288,1152]{1,0:T(8,128)(2,1)S(1)}, u32[]{:S(2)}, u32[]{:S(2)}) collective-permute-start(bf16[288,1152]{1,0:T(8,128)(2,1)} %get-tuple-element.236), channel_id=1, source_target_pairs={{0,8},{4,12},{8,0},{12,4},{16,24},{20,28},{24,16},{28,20},{1,9},{5... | collective-permute-start | bytes 1990664 | tf_op jit(solution)/shard_map/ppermute | solution.py:302
  29.8 21.8 %collective-permute-start.4 = (bf16[288,1152]{1,0:T(8,128)(2,1)}, bf16[288,1152]{1,0:T(8,128)(2,1)S(1)}, u32[]{:S(2)}, u32[]{:S(2)}) collective-permute-start(bf16[288,1152]{1,0:T(8,128)(2,1)} %get-tuple-element.236), channel_id=1, source_target_pairs={{0,16},{4,20},{8,24},{12,28},{16,0},{20,4},{24,8},{28,12},{1,17},{... | collective-permute-start | bytes 1990664 | tf_op jit(solution)/shard_map/ppermute | solution.py:302
  31.6 20.0 %collective-permute-start.5 = (bf16[144,1152]{1,0:T(8,128)(2,1)}, bf16[144,1152]{1,0:T(8,128)(2,1)}, u32[]{:S(2)}, u32[]{:S(2)}) collective-permute-start(bf16[144,1152]{1,0:T(8,128)(2,1)} %pad_maximum_fusion.3.refs_0_), channel_id=1, source_target_pairs={{0,2},{1,3},{2,0},{3,1},{4,6},{5,7},{6,4},{7,5},{8,10},{9,11},{10,... | collective-permute-start | bytes 995336 | tf_op jit(solution)/shard_map/ppermute | solution.py:306
  38.5 17.1 %collective-permute-start.11 = (bf16[144,1152]{1,0:T(8,128)(2,1)}, bf16[144,1152]{1,0:T(8,128)(2,1)}, u32[]{:S(2)}, u32[]{:S(2)}) collective-permute-start(bf16[144,1152]{1,0:T(8,128)(2,1)} %pad_maximum_fusion.3.refs_0_), channel_id=1, source_target_pairs={{0,1},{1,0},{2,3},{3,2},{4,5},{5,4},{6,7},{7,6},{8,9},{9,8},{10,11... | collective-permute-start | bytes 995336 | tf_op jit(solution)/shard_map/ppermute | solution.py:306
  52.0 13.1 %collective-permute-start.10 = (bf16[288,1152]{1,0:T(8,128)(2,1)S(1)}, bf16[288,1152]{1,0:T(8,128)(2,1)S(1)}, u32[]{:S(2)}, u32[]{:S(2)}) collective-permute-start(bf16[288,1152]{1,0:T(8,128)(2,1)S(1)} %collective-permute-done.4.refs_2_), channel_id=1, source_target_pairs={{0,4},{4,0},{8,12},{12,8},{16,20},{20,16},{24,28},{28,24},{1,5},{5... | collective-permute-start | bytes 1990664 | tf_op jit(solution)/shard_map/ppermute | solution.py:302
  53.5 11.6 %collective-permute-start.9 = (bf16[288,1152]{1,0:T(8,128)(2,1)S(1)}, bf16[288,1152]{1,0:T(8,128)(2,1)S(1)}, u32[]{:S(2)}, u32[]{:S(2)}) collective-permute-start(bf16[288,1152]{1,0:T(8,128)(2,1)S(1)} %collective-permute-done.3.refs_1_), channel_id=1, source_target_pairs={{0,4},{4,0},{8,12},{12,8},{16,20},{20,16},{24,28},{28,24},{1,5},{5... | collective-permute-start | bytes 1990664 | tf_op jit(solution)/shard_map/ppermute | solution.py:302
  72.2 31.8 %collective-permute-start.13 = (bf16[144,4608]{1,0:T(8,128)(2,1)}, bf16[144,4608]{1,0:T(8,128)(2,1)S(1)}, u32[]{:S(2)}, u32[]{:S(2)}) collective-permute-start(bf16[144,4608]{1,0:T(8,128)(2,1)} %shard_map.365), channel_id=1, source_target_pairs={{0,8},{4,12},{8,0},{12,4},{16,24},{20,28},{24,16},{28,20},{1,9},{5... | collective-permute-start | bytes 3981320 | tf_op jit(solution)/shard_map/ppermute | solution.py:302
  73.7 31.5 %collective-permute-start.14 = (bf16[144,4608]{1,0:T(8,128)(2,1)}, bf16[144,4608]{1,0:T(8,128)(2,1)S(1)}, u32[]{:S(2)}, u32[]{:S(2)}) collective-permute-start(bf16[144,4608]{1,0:T(8,128)(2,1)} %shard_map.365), channel_id=1, source_target_pairs={{0,16},{4,20},{8,24},{12,28},{16,0},{20,4},{24,8},{28,12},{1,17},{... | collective-permute-start | bytes 3981320 | tf_op jit(solution)/shard_map/ppermute | solution.py:302
  75.2 17.4 %collective-permute-start.15 = (bf16[144,1152]{1,0:T(8,128)(2,1)S(1)}, bf16[144,1152]{1,0:T(8,128)(2,1)S(1)}, u32[]{:S(2)}, u32[]{:S(2)}) collective-permute-start(bf16[144,1152]{1,0:T(8,128)(2,1)S(1)} %convert_element_type.171.refs_0_), channel_id=1, source_target_pairs={{0,2},{1,3},{2,0},{3,1},{4,6},{5,7},{6,4},{7,5},{8,10},{9,11},{10,... | collective-permute-start | bytes 995336 | tf_op jit(solution)/shard_map/ppermute | solution.py:306
  75.4 17.2 %collective-permute-start.16 = (bf16[144,1152]{1,0:T(8,128)(2,1)S(1)}, bf16[144,1152]{1,0:T(8,128)(2,1)S(1)}, u32[]{:S(2)}, u32[]{:S(2)}) collective-permute-start(bf16[144,1152]{1,0:T(8,128)(2,1)S(1)} %convert_element_type.171.refs_0_), channel_id=1, source_target_pairs={{0,1},{1,0},{2,3},{3,2},{4,5},{5,4},{6,7},{7,6},{8,9},{9,8},{10,11... | collective-permute-start | bytes 995336 | tf_op jit(solution)/shard_map/ppermute | solution.py:306
  105.2 18.8 %collective-permute-start.20 = (bf16[144,4608]{1,0:T(8,128)(2,1)S(1)}, bf16[144,4608]{1,0:T(8,128)(2,1)S(1)}, u32[]{:S(2)}, u32[]{:S(2)}) collective-permute-start(bf16[144,4608]{1,0:T(8,128)(2,1)S(1)} %collective-permute-done.13.refs_1_.refs_7_), channel_id=1, source_target_pairs={{0,4},{4,0},{8,12},{12,8},{16,20},{20,16},{24,28},{28,24},{1,5},{5... | collective-permute-start | bytes 3981320 | tf_op jit(solution)/shard_map/ppermute | solution.py:302
  105.2 19.8 %collective-permute-start.21 = (bf16[144,4608]{1,0:T(8,128)(2,1)S(1)}, bf16[144,4608]{1,0:T(8,128)(2,1)}, u32[]{:S(2)}, u32[]{:S(2)}) collective-permute-start(bf16[144,4608]{1,0:T(8,128)(2,1)S(1)} %collective-permute-done.14.refs_2_.refs_8_), channel_id=1, source_target_pairs={{0,4},{4,0},{8,12},{12,8},{16,20},{20,16},{24,28},{28,24},{1,5},{5... | collective-permute-start | bytes 3981320 | tf_op jit(solution)/shard_map/ppermute | solution.py:302
  106.2 16.5 %collective-permute-start.18 = (bf16[144,2304]{1,0:T(8,128)(2,1)S(1)}, bf16[144,2304]{1,0:T(8,128)(2,1)S(1)}, u32[]{:S(2)}, u32[]{:S(2)}) collective-permute-start(bf16[144,2304]{1,0:T(8,128)(2,1)S(1)} %slice.951), channel_id=1, source_target_pairs={{0,16},{4,20},{8,24},{12,28},{16,0},{20,4},{24,8},{28,12},{1,17},{... | collective-permute-start | bytes 1990664 | tf_op jit(solution)/shard_map/ppermute | solution.py:302
  107.8 16.2 %collective-permute-start.19 = (bf16[144,2304]{1,0:T(8,128)(2,1)S(1)}, bf16[144,2304]{1,0:T(8,128)(2,1)S(1)}, u32[]{:S(2)}, u32[]{:S(2)}) collective-permute-start(bf16[144,2304]{1,0:T(8,128)(2,1)S(1)} %slice.952), channel_id=1, source_target_pairs={{0,8},{4,12},{8,0},{12,4},{16,24},{20,28},{24,16},{28,20},{1,9},{5... | collective-permute-start | bytes 1990664 | tf_op jit(solution)/shard_map/ppermute | solution.py:302
  125.3 31.8 %collective-permute-start.23 = (bf16[144,4608]{1,0:T(8,128)(2,1)}, bf16[144,4608]{1,0:T(8,128)(2,1)S(1)}, u32[]{:S(2)}, u32[]{:S(2)}) collective-permute-start(bf16[144,4608]{1,0:T(8,128)(2,1)} %shard_map.367), channel_id=1, source_target_pairs={{0,8},{4,12},{8,0},{12,4},{16,24},{20,28},{24,16},{28,20},{1,9},{5... | collective-permute-start | bytes 3981320 | tf_op jit(solution)/shard_map/ppermute | solution.py:302
  126.1 31.4 %collective-permute-start.24 = (bf16[144,4608]{1,0:T(8,128)(2,1)}, bf16[144,4608]{1,0:T(8,128)(2,1)S(1)}, u32[]{:S(2)}, u32[]{:S(2)}) collective-permute-start(bf16[144,4608]{1,0:T(8,128)(2,1)} %shard_map.367), channel_id=1, source_target_pairs={{0,16},{4,20},{8,24},{12,28},{16,0},{20,4},{24,8},{28,12},{1,17},{... | collective-permute-start | bytes 3981320 | tf_op jit(solution)/shard_map/ppermute | solution.py:302
  126.6 19.2 %collective-permute-start.25 = (bf16[144,1152]{1,0:T(8,128)(2,1)S(1)}, bf16[144,1152]{1,0:T(8,128)(2,1)}, u32[]{:S(2)}, u32[]{:S(2)}) collective-permute-start(bf16[144,1152]{1,0:T(8,128)(2,1)S(1)} %concatenate.83.refs_0_), channel_id=1, source_target_pairs={{0,2},{1,3},{2,0},{3,1},{4,6},{5,7},{6,4},{7,5},{8,10},{9,11},{10,... | collective-permute-start | bytes 995336 | tf_op jit(solution)/shard_map/ppermute | solution.py:306
  127.6 18.2 %collective-permute-start.26 = (bf16[144,1152]{1,0:T(8,128)(2,1)S(1)}, bf16[144,1152]{1,0:T(8,128)(2,1)}, u32[]{:S(2)}, u32[]{:S(2)}) collective-permute-start(bf16[144,1152]{1,0:T(8,128)(2,1)S(1)} %concatenate.83.refs_0_), channel_id=1, source_target_pairs={{0,1},{1,0},{2,3},{3,2},{4,5},{5,4},{6,7},{7,6},{8,9},{9,8},{10,11... | collective-permute-start | bytes 995336 | tf_op jit(solution)/shard_map/ppermute | solution.py:306
  157.5 20.3 %collective-permute-start.30 = (bf16[144,4608]{1,0:T(8,128)(2,1)S(1)}, bf16[144,4608]{1,0:T(8,128)(2,1)S(1)}, u32[]{:S(2)}, u32[]{:S(2)}) collective-permute-start(bf16[144,4608]{1,0:T(8,128)(2,1)S(1)} %collective-permute-done.23.refs_1_), channel_id=1, source_target_pairs={{0,4},{4,0},{8,12},{12,8},{16,20},{20,16},{24,28},{28,24},{1,5},{5... | collective-permute-start | bytes 3981320 | tf_op jit(solution)/shard_map/ppermute | solution.py:302
  157.5 20.4 %collective-permute-start.31 = (bf16[144,4608]{1,0:T(8,128)(2,1)S(1)}, bf16[144,4608]{1,0:T(8,128)(2,1)S(1)}, u32[]{:S(2)}, u32[]{:S(2)}) collective-permute-start(bf16[144,4608]{1,0:T(8,128)(2,1)S(1)} %collective-permute-done.24.refs_2_), channel_id=1, source_target_pairs={{0,4},{4,0},{8,12},{12,8},{16,20},{20,16},{24,28},{28,24},{1,5},{5... | collective-permute-start | bytes 3981320 | tf_op jit(solution)/shard_map/ppermute | solution.py:302
  158.6 19.3 %collective-permute-start.28 = (bf16[144,2304]{1,0:T(8,128)(2,1)S(1)}, bf16[144,2304]{1,0:T(8,128)(2,1)S(1)}, u32[]{:S(2)}, u32[]{:S(2)}) collective-permute-start(bf16[144,2304]{1,0:T(8,128)(2,1)S(1)} %slice.953), channel_id=1, source_target_pairs={{0,16},{4,20},{8,24},{12,28},{16,0},{20,4},{24,8},{28,12},{1,17},{... | collective-permute-start | bytes 1990664 | tf_op jit(solution)/shard_map/ppermute | solution.py:302
  159.1 18.8 %collective-permute-start.29 = (bf16[144,2304]{1,0:T(8,128)(2,1)S(1)}, bf16[144,2304]{1,0:T(8,128)(2,1)S(1)}, u32[]{:S(2)}, u32[]{:S(2)}) collective-permute-start(bf16[144,2304]{1,0:T(8,128)(2,1)S(1)} %slice.954), channel_id=1, source_target_pairs={{0,8},{4,12},{8,0},{12,4},{16,24},{20,28},{24,16},{28,20},{1,9},{5... | collective-permute-start | bytes 1990664 | tf_op jit(solution)/shard_map/ppermute | solution.py:302
  160.4 13.4 %collective-permute-start.32 = (bf16[144,1152]{1,0:T(8,128)(2,1)}, bf16[144,1152]{1,0:T(8,128)(2,1)S(1)}, u32[]{:S(2)}, u32[]{:S(2)}) collective-permute-start(bf16[144,1152]{1,0:T(8,128)(2,1)} %collective-permute-done.25.refs_2_), channel_id=1, source_target_pairs={{0,1},{1,0},{2,3},{3,2},{4,5},{5,4},{6,7},{7,6},{8,9},{9,8},{10,11... | collective-permute-start | bytes 995336 | tf_op jit(solution)/shard_map/ppermute | solution.py:306
  181.0 32.1 %collective-permute-start.33 = (bf16[576,1152]{1,0:T(8,128)(2,1)}, bf16[576,1152]{1,0:T(8,128)(2,1)S(1)}, u32[]{:S(2)}, u32[]{:S(2)}) collective-permute-start(bf16[576,1152]{1,0:T(8,128)(2,1)} %shard_map.369), channel_id=1, source_target_pairs={{0,8},{4,12},{8,0},{12,4},{16,24},{20,28},{24,16},{28,20},{1,9},{5... | collective-permute-start | bytes 3981320 | tf_op jit(solution)/shard_map/ppermute | solution.py:302
  181.8 31.4 %collective-permute-start.34 = (bf16[576,1152]{1,0:T(8,128)(2,1)}, bf16[576,1152]{1,0:T(8,128)(2,1)S(1)}, u32[]{:S(2)}, u32[]{:S(2)}) collective-permute-start(bf16[576,1152]{1,0:T(8,128)(2,1)} %shard_map.369), channel_id=1, source_target_pairs={{0,16},{4,20},{8,24},{12,28},{16,0},{20,4},{24,8},{28,12},{1,17},{... | collective-permute-start | bytes 3981320 | tf_op jit(solution)/shard_map/ppermute | solution.py:302
  183.4 29.8 %collective-permute-start.35 = (bf16[258,1152]{1,0:T(8,128)(2,1)}, bf16[258,1152]{1,0:T(8,128)(2,1)}, u32[]{:S(2)}, u32[]{:S(2)}) collective-permute-start(bf16[258,1152]{1,0:T(8,128)(2,1)} %get-tuple-element.286.refs_0_), channel_id=1, source_target_pairs={{0,2},{1,3},{2,0},{3,1},{4,6},{5,7},{6,4},{7,5},{8,10},{9,11},{10,... | collective-permute-start | bytes 1783304 | tf_op jit(solution)/shard_map/ppermute | solution.py:306
  185.0 28.1 %collective-permute-start.36 = (bf16[258,1152]{1,0:T(8,128)(2,1)}, bf16[258,1152]{1,0:T(8,128)(2,1)}, u32[]{:S(2)}, u32[]{:S(2)}) collective-permute-start(bf16[258,1152]{1,0:T(8,128)(2,1)} %get-tuple-element.286.refs_0_), channel_id=1, source_target_pairs={{0,1},{1,0},{2,3},{3,2},{4,5},{5,4},{6,7},{7,6},{8,9},{9,8},{10,11... | collective-permute-start | bytes 1783304 | tf_op jit(solution)/shard_map/ppermute | solution.py:306
  213.2 21.2 %collective-permute-start.40 = (bf16[576,1152]{1,0:T(8,128)(2,1)S(1)}, bf16[576,1152]{1,0:T(8,128)(2,1)S(1)}, u32[]{:S(2)}, u32[]{:S(2)}) collective-permute-start(bf16[576,1152]{1,0:T(8,128)(2,1)S(1)} %collective-permute-done.33.refs_1_), channel_id=1, source_target_pairs={{0,4},{4,0},{8,12},{12,8},{16,20},{20,16},{24,28},{28,24},{1,5},{5... | collective-permute-start | bytes 3981320 | tf_op jit(solution)/shard_map/ppermute | solution.py:302
  213.7 20.7 %collective-permute-start.41 = (bf16[576,1152]{1,0:T(8,128)(2,1)S(1)}, bf16[576,1152]{1,0:T(8,128)(2,1)S(1)}, u32[]{:S(2)}, u32[]{:S(2)}) collective-permute-start(bf16[576,1152]{1,0:T(8,128)(2,1)S(1)} %collective-permute-done.34.refs_2_), channel_id=1, source_target_pairs={{0,4},{4,0},{8,12},{12,8},{16,20},{20,16},{24,28},{28,24},{1,5},{5... | collective-permute-start | bytes 3981320 | tf_op jit(solution)/shard_map/ppermute | solution.py:302
  215.7 17.4 %collective-permute-start.38 = (bf16[288,1152]{1,0:T(8,128)(2,1)}, bf16[288,1152]{1,0:T(8,128)(2,1)}, u32[]{:S(2)}, u32[]{:S(2)}) collective-permute-start(bf16[288,1152]{1,0:T(8,128)(2,1)} %slice.956), channel_id=1, source_target_pairs={{0,16},{4,20},{8,24},{12,28},{16,0},{20,4},{24,8},{28,12},{1,17},{... | collective-permute-start | bytes 1990664 | tf_op jit(solution)/shard_map/ppermute | solution.py:302
  217.1 17.4 %collective-permute-start.39 = (bf16[288,1152]{1,0:T(8,128)(2,1)}, bf16[288,1152]{1,0:T(8,128)(2,1)}, u32[]{:S(2)}, u32[]{:S(2)}) collective-permute-start(bf16[288,1152]{1,0:T(8,128)(2,1)} %slice.957), channel_id=1, source_target_pairs={{0,8},{4,12},{8,0},{12,4},{16,24},{20,28},{24,16},{28,20},{1,9},{5... | collective-permute-start | bytes 1990664 | tf_op jit(solution)/shard_map/ppermute | solution.py:302
  237.4 31.8 %collective-permute-start.43 = (bf16[2,288,1152]{2,1,0:T(8,128)(2,1)}, bf16[2,288,1152]{2,1,0:T(8,128)(2,1)S(1)}, u32[]{:S(2)}, u32[]{:S(2)}) collective-permute-start(bf16[2,288,1152]{2,1,0:T(8,128)(2,1)} %get-tuple-element.308), channel_id=1, source_target_pairs={{0,8},{4,12},{8,0},{12,4},{16,24},{20,28},{24,16},{28,20},{1,9},{5... | collective-permute-start | bytes 3981320 | tf_op jit(solution)/shard_map/ppermute | solution.py:302
  238.7 31.5 %collective-permute-start.44 = (bf16[2,288,1152]{2,1,0:T(8,128)(2,1)}, bf16[2,288,1152]{2,1,0:T(8,128)(2,1)}, u32[]{:S(2)}, u32[]{:S(2)}) collective-permute-start(bf16[2,288,1152]{2,1,0:T(8,128)(2,1)} %get-tuple-element.309), channel_id=1, source_target_pairs={{0,16},{4,20},{8,24},{12,28},{16,0},{20,4},{24,8},{28,12},{1,17},{... | collective-permute-start | bytes 3981320 | tf_op jit(solution)/shard_map/ppermute | solution.py:302
  239.2 29.7 %collective-permute-start.45 = (bf16[258,1152]{1,0:T(8,128)(2,1)}, bf16[258,1152]{1,0:T(8,128)(2,1)S(1)}, u32[]{:S(2)}, u32[]{:S(2)}) collective-permute-start(bf16[258,1152]{1,0:T(8,128)(2,1)} %get-tuple-element.329.refs_4_), channel_id=1, source_target_pairs={{0,2},{1,3},{2,0},{3,1},{4,6},{5,7},{6,4},{7,5},{8,10},{9,11},{10,... | collective-permute-start | bytes 1783304 | tf_op jit(solution)/shard_map/ppermute | solution.py:306
  241.0 27.9 %collective-permute-start.46 = (bf16[258,1152]{1,0:T(8,128)(2,1)}, bf16[258,1152]{1,0:T(8,128)(2,1)}, u32[]{:S(2)}, u32[]{:S(2)}) collective-permute-start(bf16[258,1152]{1,0:T(8,128)(2,1)} %collective-permute-done.35.refs_2_), channel_id=1, source_target_pairs={{0,1},{1,0},{2,3},{3,2},{4,5},{5,4},{6,7},{7,6},{8,9},{9,8},{10,11... | collective-permute-start | bytes 1783304 | tf_op jit(solution)/shard_map/ppermute | solution.py:306
  272.1 18.1 %collective-permute-start.49 = (bf16[288,1152]{1,0:T(8,128)(2,1)S(1)}, bf16[288,1152]{1,0:T(8,128)(2,1)S(1)}, u32[]{:S(2)}, u32[]{:S(2)}) collective-permute-start(bf16[288,1152]{1,0:T(8,128)(2,1)S(1)} %fusion.2), channel_id=1, source_target_pairs={{0,8},{4,12},{8,0},{12,4},{16,24},{20,28},{24,16},{28,20},{1,9},{5... | collective-permute-start | bytes 1990664 | tf_op jit(solution)/shard_map/ppermute | solution.py:302
  273.9 16.8 %collective-permute-start.48 = (bf16[288,1152]{1,0:T(8,128)(2,1)}, bf16[288,1152]{1,0:T(8,128)(2,1)S(1)}, u32[]{:S(2)}, u32[]{:S(2)}) collective-permute-start(bf16[288,1152]{1,0:T(8,128)(2,1)} %fusion.1), channel_id=1, source_target_pairs={{0,16},{4,20},{8,24},{12,28},{16,0},{20,4},{24,8},{28,12},{1,17},{... | collective-permute-start | bytes 1990664 | tf_op jit(solution)/shard_map/ppermute | solution.py:302
  274.4 15.8 %collective-permute-start.50 = (bf16[258,1152]{1,0:T(8,128)(2,1)}, bf16[258,1152]{1,0:T(8,128)(2,1)S(1)}, u32[]{:S(2)}, u32[]{:S(2)}) collective-permute-start(bf16[258,1152]{1,0:T(8,128)(2,1)} %get-tuple-element.329.refs_4_), channel_id=1, source_target_pairs={{0,1},{1,0},{2,3},{3,2},{4,5},{5,4},{6,7},{7,6},{8,9},{9,8},{10,11... | collective-permute-start | bytes 1783304 | tf_op jit(solution)/shard_map/ppermute | solution.py:306
  291.5 32.0 %collective-permute-start.53 = (bf16[2,144,2304]{2,1,0:T(8,128)(2,1)}, bf16[2,144,2304]{2,1,0:T(8,128)(2,1)S(1)}, u32[]{:S(2)}, u32[]{:S(2)}) collective-permute-start(bf16[2,144,2304]{2,1,0:T(8,128)(2,1)} %get-tuple-element.339), channel_id=1, source_target_pairs={{0,8},{4,12},{8,0},{12,4},{16,24},{20,28},{24,16},{28,20},{1,9},{5... | collective-permute-start | bytes 3981320 | tf_op jit(solution)/shard_map/ppermute | solution.py:302
  292.8 31.7 %collective-permute-start.54 = (bf16[2,144,2304]{2,1,0:T(8,128)(2,1)}, bf16[2,144,2304]{2,1,0:T(8,128)(2,1)S(1)}, u32[]{:S(2)}, u32[]{:S(2)}) collective-permute-start(bf16[2,144,2304]{2,1,0:T(8,128)(2,1)} %get-tuple-element.340), channel_id=1, source_target_pairs={{0,16},{4,20},{8,24},{12,28},{16,0},{20,4},{24,8},{28,12},{1,17},{... | collective-permute-start | bytes 3981320 | tf_op jit(solution)/shard_map/ppermute | solution.py:302
  293.9 29.6 %collective-permute-start.55 = (bf16[258,1152]{1,0:T(8,128)(2,1)S(1)}, bf16[258,1152]{1,0:T(8,128)(2,1)S(1)}, u32[]{:S(2)}, u32[]{:S(2)}) collective-permute-start(bf16[258,1152]{1,0:T(8,128)(2,1)S(1)} %copy-done.64), channel_id=1, source_target_pairs={{0,1},{1,0},{2,3},{3,2},{4,5},{5,4},{6,7},{7,6},{8,9},{9,8},{10,11... | collective-permute-start | bytes 1783304 | tf_op jit(solution)/shard_map/ppermute | solution.py:306
  295.2 28.3 %collective-permute-start.56 = (bf16[576,384]{1,0:T(8,128)(2,1)S(1)}, bf16[576,384]{1,0:T(8,128)(2,1)S(1)}, u32[]{:S(2)}, u32[]{:S(2)}) collective-permute-start(bf16[576,384]{1,0:T(8,128)(2,1)S(1)} %copy-done.95), channel_id=1, source_target_pairs={{0,4},{4,0},{8,12},{12,8},{16,20},{20,16},{24,28},{28,24},{1,5},{5... | collective-permute-start | bytes 1327112 | tf_op jit(solution)/shard_map/ppermute | solution.py:302
  326.2 24.1 %collective-permute-start.58 = (bf16[144,2304]{1,0:T(8,128)(2,1)}, bf16[144,2304]{1,0:T(8,128)(2,1)S(1)}, u32[]{:S(2)}, u32[]{:S(2)}) collective-permute-start(bf16[144,2304]{1,0:T(8,128)(2,1)} %fusion.4), channel_id=1, source_target_pairs={{0,8},{4,12},{8,0},{12,4},{16,24},{20,28},{24,16},{28,20},{1,9},{5... | collective-permute-start | bytes 1990664 | tf_op jit(solution)/shard_map/ppermute | solution.py:302
  328.0 22.4 %collective-permute-start.57 = (bf16[144,2304]{1,0:T(8,128)(2,1)}, bf16[144,2304]{1,0:T(8,128)(2,1)S(1)}, u32[]{:S(2)}, u32[]{:S(2)}) collective-permute-start(bf16[144,2304]{1,0:T(8,128)(2,1)} %fusion.3), channel_id=1, source_target_pairs={{0,16},{4,20},{8,24},{12,28},{16,0},{20,4},{24,8},{28,12},{1,17},{... | collective-permute-start | bytes 1990664 | tf_op jit(solution)/shard_map/ppermute | solution.py:302
  333.8 13.3 %collective-permute-start.59 = (bf16[144,1152]{1,0:T(8,128)(2,1)}, bf16[144,1152]{1,0:T(8,128)(2,1)S(1)}, u32[]{:S(2)}, u32[]{:S(2)}) collective-permute-start(bf16[144,1152]{1,0:T(8,128)(2,1)} %get-tuple-element.353), channel_id=1, source_target_pairs={{0,1},{1,0},{2,3},{3,2},{4,5},{5,4},{6,7},{7,6},{8,9},{9,8},{10,11... | collective-permute-start | bytes 995336 | tf_op jit(solution)/shard_map/ppermute | solution.py:306
  334.1 16.2 %collective-permute-start.60 = (bf16[144,1152]{1,0:T(8,128)(2,1)}, bf16[144,1152]{1,0:T(8,128)(2,1)S(1)}, u32[]{:S(2)}, u32[]{:S(2)}) collective-permute-start(bf16[144,1152]{1,0:T(8,128)(2,1)} %get-tuple-element.354), channel_id=1, source_target_pairs={{0,1},{1,0},{2,3},{3,2},{4,5},{5,4},{6,7},{7,6},{8,9},{9,8},{10,11... | collective-permute-start | bytes 995336 | tf_op jit(solution)/shard_map/ppermute | solution.py:306
  350.3 29.8 %collective-permute-start.62 = (bf16[2,144,2304]{2,1,0:T(8,128)(2,1)}, bf16[2,144,2304]{2,1,0:T(8,128)(2,1)S(1)}, u32[]{:S(2)}, u32[]{:S(2)}) collective-permute-start(bf16[2,144,2304]{2,1,0:T(8,128)(2,1)} %get-tuple-element.363), channel_id=1, source_target_pairs={{0,8},{4,12},{8,0},{12,4},{16,24},{20,28},{24,16},{28,20},{1,9},{5... | collective-permute-start | bytes 3981320 | tf_op jit(solution)/shard_map/ppermute | solution.py:302
  351.7 29.5 %collective-permute-start.63 = (bf16[2,144,2304]{2,1,0:T(8,128)(2,1)}, bf16[2,144,2304]{2,1,0:T(8,128)(2,1)S(1)}, u32[]{:S(2)}, u32[]{:S(2)}) collective-permute-start(bf16[2,144,2304]{2,1,0:T(8,128)(2,1)} %get-tuple-element.364), channel_id=1, source_target_pairs={{0,16},{4,20},{8,24},{12,28},{16,0},{20,4},{24,8},{28,12},{1,17},{... | collective-permute-start | bytes 3981320 | tf_op jit(solution)/shard_map/ppermute | solution.py:302
  352.4 18.1 %collective-permute-start.66 = (bf16[144,1152]{1,0:T(8,128)(2,1)S(1)}, bf16[144,1152]{1,0:T(8,128)(2,1)S(1)}, u32[]{:S(2)}, u32[]{:S(2)}) collective-permute-start(bf16[144,1152]{1,0:T(8,128)(2,1)S(1)} %add_convert_fusion.8), channel_id=1, source_target_pairs={{0,2},{1,3},{2,0},{3,1},{4,6},{5,7},{6,4},{7,5},{8,10},{9,11},{10,... | collective-permute-start | bytes 995336 | tf_op jit(solution)/shard_map/ppermute | solution.py:306
  357.7 16.9 %collective-permute-start.64 = (bf16[144,1152]{1,0:T(8,128)(2,1)}, bf16[144,1152]{1,0:T(8,128)(2,1)S(1)}, u32[]{:S(2)}, u32[]{:S(2)}) collective-permute-start(bf16[144,1152]{1,0:T(8,128)(2,1)} %get-tuple-element.367), channel_id=1, source_target_pairs={{0,1},{1,0},{2,3},{3,2},{4,5},{5,4},{6,7},{7,6},{8,9},{9,8},{10,11... | collective-permute-start | bytes 995336 | tf_op jit(solution)/shard_map/ppermute | solution.py:306
  358.8 20.5 %collective-permute-start.65 = (bf16[144,1152]{1,0:T(8,128)(2,1)}, bf16[144,1152]{1,0:T(8,128)(2,1)S(1)}, u32[]{:S(2)}, u32[]{:S(2)}) collective-permute-start(bf16[144,1152]{1,0:T(8,128)(2,1)} %get-tuple-element.368), channel_id=1, source_target_pairs={{0,1},{1,0},{2,3},{3,2},{4,5},{5,4},{6,7},{7,6},{8,9},{9,8},{10,11... | collective-permute-start | bytes 995336 | tf_op jit(solution)/shard_map/ppermute | solution.py:306
  382.3 21.5 %collective-permute-start.68 = (bf16[144,2304]{1,0:T(8,128)(2,1)}, bf16[144,2304]{1,0:T(8,128)(2,1)S(1)}, u32[]{:S(2)}, u32[]{:S(2)}) collective-permute-start(bf16[144,2304]{1,0:T(8,128)(2,1)} %fusion.6), channel_id=1, source_target_pairs={{0,8},{4,12},{8,0},{12,4},{16,24},{20,28},{24,16},{28,20},{1,9},{5... | collective-permute-start | bytes 1990664 | tf_op jit(solution)/shard_map/ppermute | solution.py:302
  384.0 19.8 %collective-permute-start.67 = (bf16[144,2304]{1,0:T(8,128)(2,1)}, bf16[144,2304]{1,0:T(8,128)(2,1)S(1)}, u32[]{:S(2)}, u32[]{:S(2)}) collective-permute-start(bf16[144,2304]{1,0:T(8,128)(2,1)} %fusion.5), channel_id=1, source_target_pairs={{0,16},{4,20},{8,24},{12,28},{16,0},{20,4},{24,8},{28,12},{1,17},{... | collective-permute-start | bytes 1990664 | tf_op jit(solution)/shard_map/ppermute | solution.py:302
  386.1 17.7 %collective-permute-start.70 = (bf16[258,288]{1,0:T(8,128)(2,1)}, bf16[258,288]{1,0:T(8,128)(2,1)S(1)}, u32[]{:S(2)}, u32[]{:S(2)}) collective-permute-start(bf16[258,288]{1,0:T(8,128)(2,1)} %get-tuple-element.383), channel_id=1, source_target_pairs={{0,2},{1,3},{2,0},{3,1},{4,6},{5,7},{6,4},{7,5},{8,10},{9,11},{10,... | collective-permute-start | bytes 445832 | tf_op jit(solution)/shard_map/ppermute | solution.py:306
  387.3 16.5 %collective-permute-start.71 = (bf16[258,288]{1,0:T(8,128)(2,1)}, bf16[258,288]{1,0:T(8,128)(2,1)S(1)}, u32[]{:S(2)}, u32[]{:S(2)}) collective-permute-start(bf16[258,288]{1,0:T(8,128)(2,1)} %get-tuple-element.384), channel_id=1, source_target_pairs={{0,3},{1,2},{2,1},{3,0},{4,7},{5,6},{6,5},{7,4},{8,11},{9,10},{10,... | collective-permute-start | bytes 445832 | tf_op jit(solution)/shard_map/ppermute | solution.py:306
  404.8 15.6 %collective-permute-start.75 = (bf16[4,258,288]{2,0,1:T(4,128)(2,1)S(1)}, bf16[4,258,288]{2,0,1:T(4,128)(2,1)S(1)}, u32[]{:S(2)}, u32[]{:S(2)}) collective-permute-start(bf16[4,258,288]{2,0,1:T(4,128)(2,1)S(1)} %copy.44), channel_id=1, source_target_pairs={{0,4},{4,0},{8,12},{12,8},{16,20},{20,16},{24,28},{28,24},{1,5},{5... | collective-permute-start | bytes 1783304 | tf_op jit(solution)/shard_map/ppermute | solution.py:302
  405.1 24.4 %collective-permute-start.77 = (bf16[144,1152]{1,0:T(8,128)(2,1)S(1)}, bf16[144,1152]{1,0:T(8,128)(2,1)S(1)}, u32[]{:S(2)}, u32[]{:S(2)}) collective-permute-start(bf16[144,1152]{1,0:T(8,128)(2,1)S(1)} %add_convert_fusion.7), channel_id=1, source_target_pairs={{0,2},{1,3},{2,0},{3,1},{4,6},{5,7},{6,4},{7,5},{8,10},{9,11},{10,... | collective-permute-start | bytes 995336 | tf_op jit(solution)/shard_map/ppermute | solution.py:306
  414.2 16.0 %collective-permute-start.73 = (bf16[144,1152]{1,0:T(8,128)(2,1)}, bf16[144,1152]{1,0:T(8,128)(2,1)S(1)}, u32[]{:S(2)}, u32[]{:S(2)}) collective-permute-start(bf16[144,1152]{1,0:T(8,128)(2,1)} %get-tuple-element.396), channel_id=1, source_target_pairs={{0,1},{1,0},{2,3},{3,2},{4,5},{5,4},{6,7},{7,6},{8,9},{9,8},{10,11... | collective-permute-start | bytes 995336 | tf_op jit(solution)/shard_map/ppermute | solution.py:306
  414.2 22.2 %collective-permute-start.74 = (bf16[144,1152]{1,0:T(8,128)(2,1)}, bf16[144,1152]{1,0:T(8,128)(2,1)S(1)}, u32[]{:S(2)}, u32[]{:S(2)}) collective-permute-start(bf16[144,1152]{1,0:T(8,128)(2,1)} %get-tuple-element.397), channel_id=1, source_target_pairs={{0,1},{1,0},{2,3},{3,2},{4,5},{5,4},{6,7},{7,6},{8,9},{9,8},{10,11... | collective-permute-start | bytes 995336 | tf_op jit(solution)/shard_map/ppermute | solution.py:306
  437.5 16.7 %collective-permute-start.81 = (bf16[144,1152]{1,0:T(8,128)(2,1)S(1)}, bf16[144,1152]{1,0:T(8,128)(2,1)S(1)}, u32[]{:S(2)}, u32[]{:S(2)}) collective-permute-start(bf16[144,1152]{1,0:T(8,128)(2,1)S(1)} %add_convert_fusion.6), channel_id=1, source_target_pairs={{0,2},{1,3},{2,0},{3,1},{4,6},{5,7},{6,4},{7,5},{8,10},{9,11},{10,... | collective-permute-start | bytes 995336 | tf_op jit(solution)/shard_map/ppermute | solution.py:306
  (118 other events, 941.2 us)

commit v6 on v5

--- a/solution.py
+++ b/solution.py
@@ -293,6 +293,7 @@
 ACROSS = 2
 ALONG = 4
 PAD = 384
+VECTOR_ROWS = 11
 VMEM_BYTES = 56 * 1024 * 1024
 LIGHT = pl.CostEstimate(flops=0, bytes_accessed=1024, transcendentals=0)
 PARAMS = pltpu.CompilerParams(vmem_limit_bytes=VMEM_BYTES)
@@ -665,7 +666,7 @@
 def ends_of(block, second):
     if split_shapes(*block.shape)[1]:
         return jnp.concatenate([block, jnp.concatenate(second, axis=1)], axis=0)
-    return jnp.concatenate([block, *second], axis=0)
+    return jnp.stack([block, jnp.concatenate(second, axis=0)]).reshape(-1, block.shape[1])
 
 
 def line_gradient(lefts, rights, rights_sibling):
@@ -678,7 +679,7 @@
         outs, total = refs[10:14], refs[14]
         chip = lax.axis_index("wide") >> 1
         for number in range(8):
-            right = (right_ref, sibling_ref)[number // 4][number % 4]
+            right = (right_ref, sibling_ref)[number // 4][number % 4, :tokens]
             part = lax.dot_general(
                 right,
                 refs[number][...],
@@ -686,16 +687,26 @@
                 preferred_element_type=jnp.float32,
             )
             total[...] = part if number == 0 else total[...] + part
+        sums = sum(
+            ref[number, tokens:].astype(jnp.float32)
+            for ref in (right_ref, sibling_ref)
+            for number in range(4)
+        )
+        for ref in outs:
+            for row in range(VECTOR_ROWS):
+                ref[rows // 2 + row // 2, (row % 2) * width : (row % 2 + 1) * width] = sums[
+                    row
+                ].astype(jnp.bfloat16)
         for owner in range(4):
             block = total[:, owner * rows : (owner + 1) * rows].T.astype(jnp.bfloat16)
             for relative in range(4):
 
                 @pl.when((chip ^ relative) == owner)
                 def _():
-                    outs[relative][:, :width] = block[: rows // 2]
-                    outs[relative][:, width:] = block[rows // 2 :]
-
-    shape = jax.ShapeDtypeStruct((rows // 2, 2 * width), jnp.bfloat16)
+                    outs[relative][: rows // 2, :width] = block[: rows // 2]
+                    outs[relative][: rows // 2, width:] = block[rows // 2 :]
+
+    shape = jax.ShapeDtypeStruct((rows // 2 + 16, 2 * width), jnp.bfloat16)
     return pl.pallas_call(
         kernel,
         out_shape=(shape,) * 4,
@@ -1021,13 +1032,14 @@
     )[0]
 
 
-def entry_backward(delta_mixed, weight, delta_one, stream_zero, gain):
+def entry_backward(delta_mixed, weight, delta_one, stream_zero, gain, sums_two, hidden_sum):
     length = delta_mixed.shape[0]
     width = D // 8
+    tall = -(-(length + VECTOR_ROWS) // 16) * 16
 
     def kernel(*refs):
-        mixed_ref, one_ref, stream_ref, gain_ref, low_ref, sums = refs[6:12]
-        quarters, (full, sems, delta) = refs[12:16], refs[16:]
+        mixed_ref, one_ref, stream_ref, gain_ref, sums_ref, hidden_ref, low_ref = refs[6:13]
+        quarters, (full, sems, delta, held) = refs[13:17], refs[17:]
         weight_in = Fetch(refs[:6], full, sems)
         for step in range(3):
             columns = slice(step * D, (step + 1) * D)
@@ -1039,6 +1051,19 @@
         zero = one_ref[...] + norm_back(value * gain_ref[...], normed, inverse)
         zero_low = zero.astype(jnp.bfloat16)
         low_ref[...] = zero_low
+        sums = [jnp.sum(part, axis=0, keepdims=True) for part in (zero, value * normed, value)]
+        sums += [sums_ref[row : row + 1] for row in range(4)]
+        held[...] = jnp.zeros_like(held)
+        for block in range(VECTOR_ROWS * 8):
+            owner, place = block // (2 * VECTOR_ROWS), block % (2 * VECTOR_ROWS)
+            if block < 56:
+                source, wide = sums[block // 8], block % 8
+                start = (4 * (wide % 2) + wide // 2) * width
+            else:
+                source, wide = hidden_ref, (block - 56) // 4
+                start = (4 * (wide % 2) + wide // 2) * 4 * width + (block % 4) * width
+            columns = slice((place % 2) * width, (place % 2 + 1) * width)
+            held[owner, place // 2 : place // 2 + 1, columns] = source[:, start : start + width]
         narrow = lax.axis_index("narrow")
         for owner in range(4):
             for relative in range(4):
@@ -1047,21 +1072,18 @@
                 def _():
                     for parity in range(2):
                         start = (4 * parity + owner) * width
-                        quarters[relative][:, parity * width : (parity + 1) * width] = zero_low[
-                            :, start : start + width
-                        ]
-
-        sums[0:1] = jnp.sum(zero, axis=0, keepdims=True)
-        sums[1:2] = jnp.sum(value * normed, axis=0, keepdims=True)
-        sums[2:3] = jnp.sum(value, axis=0, keepdims=True)
+                        quarters[relative][:length, parity * width : (parity + 1) * width] = (
+                            zero_low[:, start : start + width]
+                        )
+                    quarters[relative][length:] = held[owner, : tall - length].astype(jnp.bfloat16)
 
     return heavy(
         kernel,
-        [((length, D), jnp.bfloat16), ((3, D), jnp.float32)]
-        + [((length, D // 4), jnp.bfloat16)] * 4,
-        weight_scratch(D, 3 * D, 3) + [pltpu.VMEM((length, D), jnp.float32)],
+        [((length, D), jnp.bfloat16)] + [((tall, D // 4), jnp.bfloat16)] * 4,
+        weight_scratch(D, 3 * D, 3)
+        + [pltpu.VMEM((length, D), jnp.float32), pltpu.VMEM((4, 16, D // 4), jnp.float32)],
         weight,
-        (delta_mixed, delta_one, stream_zero, gain),
+        (delta_mixed, delta_one, stream_zero, gain, sums_two, hidden_sum),
     )
 
 
@@ -1301,33 +1323,17 @@
     expand_quarters = unarrange("expand", 1, expand_blocks, expand_got, expand_got_last)
     expand_narrow = narrow_first(expand_quarters)
     shrink_end = narrow_second(shrink_quarters, shrink_narrow)
-    zero_low, sums_one, *zero_quarters = entry_backward(
-        delta_mixed, mixed_pieces, delta_one, stream_zero, gain_one
-    )
-    mixed_got, expand_narrow, zero_low, sums_one, zero_quarters, shrink_end = together(
-        mixed_got, expand_narrow, zero_low, sums_one, zero_quarters, shrink_end
+    zero_low, *zero_quarters = entry_backward(
+        delta_mixed, mixed_pieces, delta_one, stream_zero, gain_one, sums_two, hidden_sum
+    )
+    mixed_got, expand_narrow, zero_low, zero_quarters, shrink_end = together(
+        mixed_got, expand_narrow, zero_low, zero_quarters, shrink_end
     )
     mixed_got_last = forward(mixed_blocks, mixed_got)
     zero_got = tuple(swap_narrow(zero_quarters[bit], bit) for bit in (1, 2, 3))
     input_gradient, skip_gradient = joined_backward(zero_low, merge_pieces)
-    vector_total = jnp.concatenate(
-        [
-            outer(row)
-            for row in (
-                sums_one[0],
-                sums_one[1],
-                sums_one[2],
-                sums_two[0],
-                sums_two[1],
-                sums_two[2],
-                sums_two[3],
-                hidden_sum[0],
-            )
-        ]
-    )
-    vector_total = vector_total + swap_wide(vector_total, CORE)
-    mixed_got_last, zero_got, vector_total, input_gradient, skip_gradient, shrink_end = together(
-        mixed_got_last, zero_got, vector_total, input_gradient, skip_gradient, shrink_end
+    mixed_got_last, zero_got, input_gradient, skip_gradient, shrink_end = together(
+        mixed_got_last, zero_got, input_gradient, skip_gradient, shrink_end
     )
     mixed_quarters = unarrange("attend_output", 1, mixed_blocks, mixed_got, mixed_got_last)
     mixed_narrow = narrow_first(mixed_quarters)
@@ -1348,11 +1354,9 @@
         zero_line,
         zero_line_sibling,
     )
-    vector_total = vector_total + swap_wide(vector_total, ACROSS)
-    mixed_narrow, merge_blocks, vector_total, shrink_end, expand_end = together(
-        mixed_narrow, merge_blocks, vector_total, shrink_end, expand_end
-    )
-    vector_total = vector_total + swap_wide(vector_total, ALONG)
+    mixed_narrow, merge_blocks, shrink_end, expand_end = together(
+        mixed_narrow, merge_blocks, shrink_end, expand_end
+    )
     mixed_end = narrow_second(mixed_quarters, mixed_narrow)
     merge_got = (
         swap_wide(merge_blocks[1], ACROSS),
@@ -1374,22 +1378,20 @@
         finish(expand_quarters, expand_narrow, expand_end),
         rate_expand,
     )
+    tall = merge_blocks[0].shape[0] - 16
     merge_sum = sum(term.astype(jnp.float32) for term in (merge_blocks[0], *merge_got))
     merge_new = adamw_update(
         merge_weight,
         merge_moment,
         merge_square,
-        unfold(merge_sum, merge_weight.shape[0]),
+        unfold(merge_sum[:tall], merge_weight.shape[0]),
         rate_merge,
     )
-    merge_new, mixed_end, vector_total, shrink_new, expand_new = together(
-        merge_new, mixed_end, vector_total, shrink_new, expand_new
-    )
-    vector_parts = vector_total.reshape(4, -1)
-    narrow = lax.axis_index("narrow")
-    vector_total = pick(vector_parts, narrow)
-    for bit in (1, 2, 3):
-        vector_total = vector_total + swap_narrow(pick(vector_parts, narrow ^ bit), bit)
+    vector_total = merge_sum[tall:].reshape(-1)[: vectors.shape[0]]
+    vector_new = adamw_update(vectors, vector_moment, vector_square, vector_total, rate_vector)
+    merge_new, mixed_end, vector_new, shrink_new, expand_new = together(
+        merge_new, mixed_end, vector_new, shrink_new, expand_new
+    )
     mixed_total = finish(mixed_quarters, mixed_narrow, mixed_end)
     attend_new = adamw_update(
         attend_weight, attend_moment, attend_square, mixed_total[:, :columns], rate_attend
@@ -1397,7 +1399,6 @@
     output_new = adamw_update(
         output_weight, output_moment, output_square, mixed_total[:, columns:], rate_output
     )
-    vector_new = adamw_update(vectors, vector_moment, vector_square, vector_total, rate_vector)
     return (
         outputs,
         input_gradient[None],

time: 471 us -> 456 us (0.968)
  local copies, waits for them, and re-layouts: 53.7 us -> 40.6 us
  starting transfers between devices: 81.1 us -> 75.1 us
    unnamed x197 -> x201, local copies, waits for them, and re-layouts: 22.7 us -> 16.7 us
    another operation x0 -> x4, other arithmetic: none -> 5.75 us  [ends_of(): jnp.stack([block, jnp.concatenate(second, axis=0)])]
    ppermute x33 -> x30, starting transfers between devices: 43.6 us -> 38.5 us  [swap_narrow(): return lax.ppermute(value, 'narrow', [(i, i ^ bit) for i in range(4)])]
    ppermute x33 -> x30, waiting for transfers between devices: 78.4 us -> 81.6 us  [swap_narrow(): return lax.ppermute(value, 'narrow', [(i, i ^ bit) for i in range(4)])]
    ppermute x53 -> x50, waiting for transfers between devices: 43.5 us -> 41.2 us  [swap_wide(): return lax.ppermute(value, 'wide', [(i, i ^ bit) for i in range(8)])]
    ppermute x53 -> x50, starting transfers between devices: 37.5 us -> 36.6 us  [swap_wide(): return lax.ppermute(value, 'wide', [(i, i ^ bit) for i in range(8)])]
  transfers between devices with their start and end apart: 86 -> 80, of which waited for: 38 -> 39; matrix products, arithmetic and copies ran while one was open for 9% -> 7% of each run, Pallas kernels for 40% -> 41%
where the time goes in v6:
time: 456 us; the launch traced here: 448 us
  Pallas kernels  184 us (40%)
  waiting for transfers between devices  123 us (27%)
  starting transfers between devices  75.1 us (16%)
  local copies, waits for them, and re-layouts  40.6 us (9%)
  other arithmetic  23.3 us (5%)
    pallas_call x10, Pallas kernels, heavy(): pl.pallas_call(kernel, in_specs=[pl.BlockSpec(memory_space=pl.ANY)] * len...  115 us
    ppermute x30, waiting for transfers between devices, swap_narrow(): return lax.ppermute(value, 'narrow', [(i, i ^ bit) for i in range(4)])  81.6 us
    ppermute x50, waiting for transfers between devices, swap_wide(): return lax.ppermute(value, 'wide', [(i, i ^ bit) for i in range(8)])  41.2 us
    ppermute x30, starting transfers between devices, swap_narrow(): return lax.ppermute(value, 'narrow', [(i, i ^ bit) for i in range(4)])  38.5 us
    ppermute x50, starting transfers between devices, swap_wide(): return lax.ppermute(value, 'wide', [(i, i ^ bit) for i in range(8)])  36.6 us
    pallas_call x3, Pallas kernels, pair_gradient(): pl.pallas_call(kernel, grid=(columns // tile,), in_specs=[whole(left[3])...  30.4 us
    unnamed x201, local copies, waits for them, and re-layouts  16.7 us
    pallas_call x3, Pallas kernels, unarrange(): pl.pallas_call(kernel, grid=(1,), in_specs=[near, near, full(part_rows, p...  13.6 us
  transfers between devices with their start and end apart: 80, of which 39 were waited for; matrix products, arithmetic and copies ran while one was open for 7% of the time, Pallas kernels for 41%

profile of v6, /device:TPU:0, one launch (start us, length us, event | category | flops | bytes accessed | tf_op | source)
XLA Modules:
  0.0 448.3 jit_solution(17025177423613250954)
XLA Ops:
  3.5 3.0 collective-permute-start
  6.5 2.6 collective-permute-start.1
  9.7 1.6 concatenate.76
  11.2 1.6 concatenate.77
  12.8 3.2 concatenate.75.refs_6_
  18.5 1.7 concatenate.78.refs_2_.refs_6_.refs_13_
  21.1 3.4 collective-permute-done.1.refs_2_
  25.6 2.7 shard_map.364
  31.3 4.5 %collective-permute-start.5 = (bf16[144,1152]{1,0:T(8,128)(2,1)}, bf16[144,1152]{1,0:T(8,128)(2,1)}, u32[]{:S(2)}, u32[]{:S(2)}) collective-permute-start(bf16[144,1152]{1,0:T(8,128)(2,1)} %pad_maximum_fusion.5.refs_0_), channel_id=1, source_target_pairs={{0,2},{1,3},{2,0},{3,1},{4,6},{5,7},{6,4},{7,5},{8,10},{9,11},{10,... | collective-permute-start | bytes 995336 | tf_op jit(solution)/shard_map/ppermute | solution.py:307
  36.6 14.7 %collective-permute-done.5.refs_2_ = bf16[144,1152]{1,0:T(8,128)(2,1)} collective-permute-done((bf16[144,1152]{1,0:T(8,128)(2,1)}, bf16[144,1152]{1,0:T(8,128)(2,1)}, u32[]{:S(2)}, u32[]{:S(2)}) %collective-permute-start.5) | collective-permute-done | bytes 331808 | tf_op jit(solution)/shard_map/ppermute | solution.py:307
  64.8 1.6 maximum_bitcast_fusion.1
  66.7 3.7 shard_map.365
  73.7 1.6 collective-permute-start.16
  76.3 8.3 %shard_map.366 = (f32[258,1152]{1,0:T(8,128)}, bf16[258,1152]{1,0:T(8,128)(2,1)}, bf16[576,384]{1,0:T(8,128)(2,1)}, bf16[576,384]{1,0:T(8,128)(2,1)}) custom-call(bf16[576,1152]{1,0:T(8,128)(2,1)} %bitcast.40, bf16[288,1152]{1,0:T(8,128)(2,1)} %copy-done.22, bf16[288,1152]{1,0:T(8,128)(2,1)} %copy-done.23, bf16[576,1152]{1,0:T(8,128)(2,1)} %copy-done.16, ...), custom_call_target="tpu_custom_call" | custom-call | bytes 1024 | tf_op jit(solution)/shard_map/pallas_call | solution.py:748
  84.6 5.8 %collective-permute-done.15.refs_2_ = bf16[144,1152]{1,0:T(8,128)(2,1)S(1)} collective-permute-done((bf16[144,1152]{1,0:T(8,128)(2,1)S(1)}, bf16[144,1152]{1,0:T(8,128)(2,1)S(1)}, u32[]{:S(2)}, u32[]{:S(2)}) %collective-permute-start.15) | collective-permute-done | bytes 331808 | tf_op jit(solution)/shard_map/ppermute | solution.py:307
  90.4 11.3 %collective-permute-done.13.refs_1_.refs_7_ = bf16[144,4608]{1,0:T(8,128)(2,1)S(1)} collective-permute-done((bf16[144,4608]{1,0:T(8,128)(2,1)}, bf16[144,4608]{1,0:T(8,128)(2,1)S(1)}, u32[]{:S(2)}, u32[]{:S(2)}) %collective-permute-start.13) | collective-permute-done | bytes 1327136 | tf_op jit(solution)/shard_map/ppermute | solution.py:303
  106.5 8.3 %collective-permute-done.22.refs_3_ = bf16[144,1152]{1,0:T(8,128)(2,1)S(1)} collective-permute-done((bf16[144,1152]{1,0:T(8,128)(2,1)S(1)}, bf16[144,1152]{1,0:T(8,128)(2,1)S(1)}, u32[]{:S(2)}, u32[]{:S(2)}) %collective-permute-start.22) | collective-permute-done | bytes 331808 | tf_op jit(solution)/shard_map/ppermute | solution.py:307
  115.6 2.9 shard_map.367
  118.4 2.1 collective-permute-done.18
  127.3 2.0 collective-permute-done.27.refs_3_.refs_9_
  130.8 14.1 %shard_map.368 = (bf16[258,3456]{1,0:T(8,128)(2,1)}, f32[12,258,258]{2,1,0:T(8,128)}, bf16[258,864]{1,0:T(8,128)(2,1)}) custom-call(bf16[288,4608]{1,0:T(8,128)(2,1)} %copy-done, bf16[144,4608]{1,0:T(8,128)(2,1)} %copy-done.2, bf16[144,4608]{1,0:T(8,128)(2,1)} %copy-done.3, bf16[288,4608]{1,0:T(8,128)(2,1)} %copy-done.1, bf16[144,4608]{1,0:T(8,128)(2,1)} %copy-done.6, ...), custom_call_target="tpu_custom_call" | custom-call | bytes 1024 | tf_op jit(solution)/shard_map/pallas_call | solution.py:748
  144.9 11.2 %collective-permute-done.23.refs_1_ = bf16[144,4608]{1,0:T(8,128)(2,1)S(1)} collective-permute-done((bf16[144,4608]{1,0:T(8,128)(2,1)}, bf16[144,4608]{1,0:T(8,128)(2,1)S(1)}, u32[]{:S(2)}, u32[]{:S(2)}) %collective-permute-start.23) | collective-permute-done | bytes 1327136 | tf_op jit(solution)/shard_map/ppermute | solution.py:303
  159.8 2.4 fusion.16
  162.2 10.8 %shard_map.370 = (f32[4,258,258]{2,1,0:T(8,128)}, f32[258,1152]{1,0:T(8,128)}, bf16[258,1152]{1,0:T(8,128)(2,1)}, bf16[1152,384]{1,0:T(8,128)(2,1)}, bf16[1152,384]{1,0:T(8,128)(2,1)}) custom-call(bf16[288,4608]{1,0:T(8,128)(2,1)} %copy-done, bf16[144,4608]{1,0:T(8,128)(2,1)} %copy-done.2, bf16[144,4608]{1,0:T(8,128)(2,1)} %copy-done.3, ...), custom_call_target="tpu_custom_call" | custom-call | bytes 1024 | tf_op jit(solution)/shard_map/pallas_call | solution.py:748
  173.7 3.3 shard_map.369
  182.4 1.5 collective-permute-start.35
  185.1 1.5 copy-done.9
  186.6 14.3 %shard_map.371 = (bf16[258,4608]{1,0:T(8,128)(2,1)}, f32[258,4608]{1,0:T(8,128)}, bf16[2304,384]{1,0:T(8,128)(2,1)}, bf16[2304,384]{1,0:T(8,128)(2,1)}) custom-call(bf16[288,4608]{1,0:T(8,128)(2,1)} %copy-done.4, bf16[144,4608]{1,0:T(8,128)(2,1)} %copy-done.12, bf16[144,4608]{1,0:T(8,128)(2,1)} %copy-done.13, bf16[288,4608]{1,0:T(8,128)(2,1)} %copy-done.9, ...), custom_call_target="tpu_custom_call" | custom-call | bytes 1024 | tf_op jit(solution)/shard_map/pallas_call | solution.py:748
  201.0 11.2 %collective-permute-done.35.refs_2_ = bf16[258,1152]{1,0:T(8,128)(2,1)} collective-permute-done((bf16[258,1152]{1,0:T(8,128)(2,1)}, bf16[258,1152]{1,0:T(8,128)(2,1)}, u32[]{:S(2)}, u32[]{:S(2)}) %collective-permute-start.35) | collective-permute-done | bytes 594464 | tf_op jit(solution)/shard_map/ppermute | solution.py:307
  216.7 1.6 collective-permute-done.42.refs_1_
  219.6 10.6 %shard_map.372 = (bf16[2,288,1152]{2,1,0:T(8,128)(2,1)}, bf16[2,288,1152]{2,1,0:T(8,128)(2,1)}, bf16[2,288,1152]{2,1,0:T(8,128)(2,1)}, bf16[2,288,1152]{2,1,0:T(8,128)(2,1)}) custom-call(bf16[2304,384]{1,0:T(8,128)(2,1)} %get-tuple-element.297.refs_0_, bf16[2304,384]{1,0:T(8,128)(2,1)} %copy-done.49, bf16[258,1152]{1,0:T(8,128)(2,1)} %copy-done.7, ...), custom_call_target="tpu_custom_call" | custom-call | bytes 1024 | tf_op jit(solution)/shard_map/pallas_call | solution.py:474
  232.6 2.4 maximum_bitcast_fusion
  235.0 1.7 pad_maximum_fusion
  238.6 1.7 collective-permute-start.45
  243.1 12.0 %shard_map.373 = (bf16[258,4608]{1,0:T(8,128)(2,1)}, f32[1,4608]{1,0:T(1,128)}) custom-call(bf16[1152,1152]{1,0:T(8,128)(2,1)} %bitcast.37, bf16[576,1152]{1,0:T(8,128)(2,1)} %copy-done.14, bf16[576,1152]{1,0:T(8,128)(2,1)} %copy-done.15, bf16[1152,1152]{1,0:T(8,128)(2,1)} %copy-done.10, bf16[576,1152]{1,0:T(8,128)(2,1)} %copy-done.20, ...), custom_call_target="tpu_custom_call" | custom-call | bytes 1024 | tf_op jit(solution)/shard_map/pallas_call | solution.py:748
  255.1 10.6 %shard_map.374 = bf16[258,1152]{1,0:T(8,128)(2,1)} custom-call(bf16[1152,1152]{1,0:T(8,128)(2,1)} %bitcast.38, bf16[576,1152]{1,0:T(8,128)(2,1)} %copy-done.14, bf16[576,1152]{1,0:T(8,128)(2,1)} %copy-done.15, bf16[1152,1152]{1,0:T(8,128)(2,1)} %copy-done.10, bf16[576,1152]{1,0:T(8,128)(2,1)} %copy-done.20, bf16[576,1152]{1,0:T(8,128)(2,1)} %copy-done.21, ...), custom_call_target="tpu_custom_call" | custom-call | bytes 1024 | tf_op jit(solution)/shard_map/pallas_call | solution.py:748
  265.7 2.4 collective-permute-done.45.refs_6_
  272.9 1.7 collective-permute-start.50
  275.5 1.6 copy-done.42
  277.1 9.9 %shard_map.375 = (bf16[2,144,2304]{2,1,0:T(8,128)(2,1)}, bf16[2,144,2304]{2,1,0:T(8,128)(2,1)}, bf16[2,144,2304]{2,1,0:T(8,128)(2,1)}, bf16[2,144,2304]{2,1,0:T(8,128)(2,1)}) custom-call(bf16[1152,384]{1,0:T(8,128)(2,1)} %get-tuple-element.328.refs_0_.refs_2_, bf16[1152,384]{1,0:T(8,128)(2,1)} %copy-done.24, ...), custom_call_target="tpu_custom_call" | custom-call | bytes 1024 | tf_op jit(solution)/shard_map/pallas_call | solution.py:474
  291.7 1.7 collective-permute-start.55
  293.4 12.3 %shard_map.376 = (f32[258,1152]{1,0:T(8,128)}, bf16[258,1152]{1,0:T(8,128)(2,1)}, f32[4,1152]{1,0:T(4,128)}, bf16[258,1152]{1,0:T(8,128)(2,1)}) custom-call(bf16[288,4608]{1,0:T(8,128)(2,1)} %copy-done.4, bf16[144,4608]{1,0:T(8,128)(2,1)} %copy-done.12, bf16[144,4608]{1,0:T(8,128)(2,1)} %copy-done.13, bf16[288,4608]{1,0:T(8,128)(2,1)} %copy-done.9, ...), custom_call_target="tpu_custom_call" | custom-call | bytes 1024 | tf_op jit(solution)/shard_map/pallas_call | solution.py:748
  305.7 16.0 %shard_map.377.refs_4_.refs_6_ = bf16[258,4608]{1,0:T(8,128)(2,1)} custom-call(bf16[258,3456]{1,0:T(8,128)(2,1)} %get-tuple-element.273.refs_6_.heads_ref, f32[12,258,258]{2,1,0:T(8,128)} %get-tuple-element.340.first_ref, f32[4,258,258]{2,1,0:T(8,128)} %get-tuple-element.341.second_ref, bf16[258,1152]{1,0:T(8,128)(2,1)} %get-tuple-element.343.delta_ref, ...), custom_call_target="tpu_custom_call" | custom-call | bytes 1024 | tf_op jit(solution)/shard_map/pallas_call | solution.py:748
  324.9 4.5 shard_map.378
  329.7 1.7 collective-permute-start.60
  331.4 9.9 %shard_map.379 = (bf16[2,144,2304]{2,1,0:T(8,128)(2,1)}, bf16[2,144,2304]{2,1,0:T(8,128)(2,1)}, bf16[2,144,2304]{2,1,0:T(8,128)(2,1)}, bf16[2,144,2304]{2,1,0:T(8,128)(2,1)}) custom-call(bf16[576,384]{1,0:T(8,128)(2,1)} %get-tuple-element.353.refs_0_, bf16[576,384]{1,0:T(8,128)(2,1)} %copy-done.77, bf16[1152,384]{1,0:T(8,128)(2,1)} %get-tuple-element.328.refs_0_.refs_2_, ...), custom_call_target="tpu_custom_call" | custom-call | bytes 1024 | tf_op jit(solution)/shard_map/pallas_call | solution.py:474
  341.3 5.3 %collective-permute-done.60.refs_4_ = bf16[144,1152]{1,0:T(8,128)(2,1)S(1)} collective-permute-done((bf16[144,1152]{1,0:T(8,128)(2,1)}, bf16[144,1152]{1,0:T(8,128)(2,1)S(1)}, u32[]{:S(2)}, u32[]{:S(2)}) %collective-permute-start.60) | collective-permute-done | bytes 331808 | tf_op jit(solution)/shard_map/ppermute | solution.py:307
  349.7 4.4 shard_map.380
  356.1 10.6 %shard_map.381 = (bf16[258,1152]{1,0:T(8,128)(2,1)}, bf16[272,288]{1,0:T(8,128)(2,1)}, bf16[272,288]{1,0:T(8,128)(2,1)}, bf16[272,288]{1,0:T(8,128)(2,1)}, bf16[272,288]{1,0:T(8,128)(2,1)}) custom-call(bf16[288,4608]{1,0:T(8,128)(2,1)} %copy-done, bf16[144,4608]{1,0:T(8,128)(2,1)} %copy-done.2, bf16[144,4608]{1,0:T(8,128)(2,1)} %copy-done.3, ...), custom_call_target="tpu_custom_call" | custom-call | bytes 1024 | tf_op jit(solution)/shard_map/pallas_call | solution.py:748
  366.7 5.0 %collective-permute-done.64 = bf16[144,1152]{1,0:T(8,128)(2,1)S(1)} collective-permute-done((bf16[144,1152]{1,0:T(8,128)(2,1)}, bf16[144,1152]{1,0:T(8,128)(2,1)S(1)}, u32[]{:S(2)}, u32[]{:S(2)}) %collective-permute-start.64) | collective-permute-done | bytes 331808 | tf_op jit(solution)/shard_map/ppermute | solution.py:307
  371.7 4.9 %collective-permute-done.65 = bf16[144,1152]{1,0:T(8,128)(2,1)S(1)} collective-permute-done((bf16[144,1152]{1,0:T(8,128)(2,1)}, bf16[144,1152]{1,0:T(8,128)(2,1)S(1)}, u32[]{:S(2)}, u32[]{:S(2)}) %collective-permute-start.65) | collective-permute-done | bytes 331808 | tf_op jit(solution)/shard_map/ppermute | solution.py:307
  381.3 1.5 collective-permute-start.70
  382.9 2.6 collective-permute-start.71
  385.5 6.5 %shard_map.382 = (bf16[258,1152]{1,0:T(8,128)(2,1)}, bf16[258,1152]{1,0:T(8,128)(2,1)}) custom-call(bf16[576,1152]{1,0:T(8,128)(2,1)} %bitcast.41, bf16[288,1152]{1,0:T(8,128)(2,1)} %copy-done.22, bf16[288,1152]{1,0:T(8,128)(2,1)} %copy-done.23, bf16[576,1152]{1,0:T(8,128)(2,1)} %copy-done.16, bf16[288,1152]{1,0:T(8,128)(2,1)} %copy-done.41, ...), custom_call_target="tpu_custom_call" | custom-call | bytes 1024 | tf_op jit(solution)/shard_map/pallas_call | solution.py:748
  392.0 5.7 %collective-permute-done.70 = bf16[272,288]{1,0:T(8,128)(2,1)S(1)} collective-permute-done((bf16[272,288]{1,0:T(8,128)(2,1)S(1)}, bf16[272,288]{1,0:T(8,128)(2,1)S(1)}, u32[]{:S(2)}, u32[]{:S(2)}) %collective-permute-start.70) | collective-permute-done | bytes 156704 | tf_op jit(solution)/shard_map/ppermute | solution.py:307
  398.7 3.4 collective-permute-start.75
  402.1 4.7 %shard_map.383 = (bf16[144,1152]{1,0:T(8,128)(2,1)}, bf16[144,1152]{1,0:T(8,128)(2,1)}, bf16[144,1152]{1,0:T(8,128)(2,1)}, bf16[144,1152]{1,0:T(8,128)(2,1)}) custom-call(bf16[2,144,2304]{2,1,0:T(8,128)(2,1)} %get-tuple-element.360.refs_0_, bf16[2,144,2304]{2,1,0:T(8,128)(2,1)} %copy-done.33, bf16[144,2304]{1,0:T(8,128)(2,1)} %copy-done.62, ...), custom_call_target="tpu_custom_call" | custom-call | bytes 1024 | tf_op jit(solution)/shard_map/pallas_call | solution.py:563
  406.9 2.0 collective-permute-start.73
  409.8 8.1 %shard_map.384 = (bf16[160,576]{1,0:T(8,128)(2,1)}, bf16[160,576]{1,0:T(8,128)(2,1)}, bf16[160,576]{1,0:T(8,128)(2,1)}, bf16[160,576]{1,0:T(8,128)(2,1)}) custom-call(bf16[258,1152]{1,0:T(8,128)(2,1)} %get-tuple-element.284.refs_0_, bf16[258,1152]{1,0:T(8,128)(2,1)} %collective-permute-done.36.refs_1_, bf16[258,1152]{1,0:T(8,128)(2,1)} %collective-permute-done.35.refs_2_, ...), custom_call_target="tpu_custom_call" | custom-call | bytes 1024 | tf_op jit(solution)/shard_map/pallas_call | solution.py:710
  417.9 5.1 %collective-permute-done.72 = bf16[144,1152]{1,0:T(8,128)(2,1)S(1)} collective-permute-done((bf16[144,1152]{1,0:T(8,128)(2,1)}, bf16[144,1152]{1,0:T(8,128)(2,1)S(1)}, u32[]{:S(2)}, u32[]{:S(2)}) %collective-permute-start.72) | collective-permute-done | bytes 331808 | tf_op jit(solution)/shard_map/ppermute | solution.py:307
  423.0 5.8 %collective-permute-done.73 = bf16[144,1152]{1,0:T(8,128)(2,1)S(1)} collective-permute-done((bf16[144,1152]{1,0:T(8,128)(2,1)}, bf16[144,1152]{1,0:T(8,128)(2,1)S(1)}, u32[]{:S(2)}, u32[]{:S(2)}) %collective-permute-start.73) | collective-permute-done | bytes 331808 | tf_op jit(solution)/shard_map/ppermute | solution.py:307
  433.0 1.7 multiply_subtract_fusion
  434.8 4.0 shard_map.385
  442.9 2.3 collective-permute-done.79
  (397 shorter events, 103.0 us)
Async XLA Ops:
  3.5 17.6 %collective-permute-start = (bf16[160,576]{1,0:T(8,128)(2,1)}, bf16[160,576]{1,0:T(8,128)(2,1)}, u32[]{:S(2)}, u32[]{:S(2)}) collective-permute-start(bf16[160,576]{1,0:T(8,128)(2,1)} %pad_maximum_fusion.6.refs_0_), channel_id=1, source_target_pairs={{0,1},{1,0},{2,3},{3,2},{4,5},{5,4},{6,7},{7,6},{8,9},{9,8},{10,11... | collective-permute-start | bytes 552968 | tf_op jit(solution)/shard_map/ppermute | solution.py:307
  6.5 18.0 %collective-permute-start.1 = (bf16[160,576]{1,0:T(8,128)(2,1)}, bf16[160,576]{1,0:T(8,128)(2,1)}, u32[]{:S(2)}, u32[]{:S(2)}) collective-permute-start(bf16[160,576]{1,0:T(8,128)(2,1)} %pad_maximum_fusion.6.refs_0_), channel_id=1, source_target_pairs={{0,2},{1,3},{2,0},{3,1},{4,6},{5,7},{6,4},{7,5},{8,10},{9,11},{10,... | collective-permute-start | bytes 552968 | tf_op jit(solution)/shard_map/ppermute | solution.py:307
  9.1 15.4 %collective-permute-start.2 = (bf16[160,576]{1,0:T(8,128)(2,1)}, bf16[160,576]{1,0:T(8,128)(2,1)}, u32[]{:S(2)}, u32[]{:S(2)}) collective-permute-start(bf16[160,576]{1,0:T(8,128)(2,1)} %pad_maximum_fusion.6.refs_0_), channel_id=1, source_target_pairs={{0,3},{1,2},{2,1},{3,0},{4,7},{5,6},{6,5},{7,4},{8,11},{9,10},{10,... | collective-permute-start | bytes 552968 | tf_op jit(solution)/shard_map/ppermute | solution.py:307
  25.6 25.6 %collective-permute-start.6 = (bf16[258,2304]{1,0:T(8,128)(2,1)}, bf16[258,2304]{1,0:T(8,128)(2,1)}, u32[]{:S(2)}, u32[]{:S(2)}) collective-permute-start(bf16[258,2304]{1,0:T(8,128)(2,1)} %pad_maximum_fusion.2), channel_id=1, source_target_pairs={{0,4},{4,0},{8,12},{12,8},{16,20},{20,16},{24,28},{28,24},{1,5},{5... | collective-permute-start | bytes 3566600 | tf_op jit(solution)/shard_map/ppermute | solution.py:303
  28.3 22.9 %collective-permute-start.3 = (bf16[288,1152]{1,0:T(8,128)(2,1)}, bf16[288,1152]{1,0:T(8,128)(2,1)S(1)}, u32[]{:S(2)}, u32[]{:S(2)}) collective-permute-start(bf16[288,1152]{1,0:T(8,128)(2,1)} %get-tuple-element.234), channel_id=1, source_target_pairs={{0,8},{4,12},{8,0},{12,4},{16,24},{20,28},{24,16},{28,20},{1,9},{5... | collective-permute-start | bytes 1990664 | tf_op jit(solution)/shard_map/ppermute | solution.py:303
  29.8 21.4 %collective-permute-start.4 = (bf16[288,1152]{1,0:T(8,128)(2,1)}, bf16[288,1152]{1,0:T(8,128)(2,1)S(1)}, u32[]{:S(2)}, u32[]{:S(2)}) collective-permute-start(bf16[288,1152]{1,0:T(8,128)(2,1)} %get-tuple-element.234), channel_id=1, source_target_pairs={{0,16},{4,20},{8,24},{12,28},{16,0},{20,4},{24,8},{28,12},{1,17},{... | collective-permute-start | bytes 1990664 | tf_op jit(solution)/shard_map/ppermute | solution.py:303
  31.3 19.9 %collective-permute-start.5 = (bf16[144,1152]{1,0:T(8,128)(2,1)}, bf16[144,1152]{1,0:T(8,128)(2,1)}, u32[]{:S(2)}, u32[]{:S(2)}) collective-permute-start(bf16[144,1152]{1,0:T(8,128)(2,1)} %pad_maximum_fusion.5.refs_0_), channel_id=1, source_target_pairs={{0,2},{1,3},{2,0},{3,1},{4,6},{5,7},{6,4},{7,5},{8,10},{9,11},{10,... | collective-permute-start | bytes 995336 | tf_op jit(solution)/shard_map/ppermute | solution.py:307
  36.5 18.8 %collective-permute-start.11 = (bf16[144,1152]{1,0:T(8,128)(2,1)}, bf16[144,1152]{1,0:T(8,128)(2,1)}, u32[]{:S(2)}, u32[]{:S(2)}) collective-permute-start(bf16[144,1152]{1,0:T(8,128)(2,1)} %pad_maximum_fusion.5.refs_0_), channel_id=1, source_target_pairs={{0,1},{1,0},{2,3},{3,2},{4,5},{5,4},{6,7},{7,6},{8,9},{9,8},{10,11... | collective-permute-start | bytes 995336 | tf_op jit(solution)/shard_map/ppermute | solution.py:307
  51.6 13.1 %collective-permute-start.10 = (bf16[288,1152]{1,0:T(8,128)(2,1)S(1)}, bf16[288,1152]{1,0:T(8,128)(2,1)S(1)}, u32[]{:S(2)}, u32[]{:S(2)}) collective-permute-start(bf16[288,1152]{1,0:T(8,128)(2,1)S(1)} %collective-permute-done.4.refs_2_), channel_id=1, source_target_pairs={{0,4},{4,0},{8,12},{12,8},{16,20},{20,16},{24,28},{28,24},{1,5},{5... | collective-permute-start | bytes 1990664 | tf_op jit(solution)/shard_map/ppermute | solution.py:303
  53.2 11.6 %collective-permute-start.9 = (bf16[288,1152]{1,0:T(8,128)(2,1)S(1)}, bf16[288,1152]{1,0:T(8,128)(2,1)S(1)}, u32[]{:S(2)}, u32[]{:S(2)}) collective-permute-start(bf16[288,1152]{1,0:T(8,128)(2,1)S(1)} %collective-permute-done.3.refs_1_), channel_id=1, source_target_pairs={{0,4},{4,0},{8,12},{12,8},{16,20},{20,16},{24,28},{28,24},{1,5},{5... | collective-permute-start | bytes 1990664 | tf_op jit(solution)/shard_map/ppermute | solution.py:303
  70.4 31.3 %collective-permute-start.13 = (bf16[144,4608]{1,0:T(8,128)(2,1)}, bf16[144,4608]{1,0:T(8,128)(2,1)S(1)}, u32[]{:S(2)}, u32[]{:S(2)}) collective-permute-start(bf16[144,4608]{1,0:T(8,128)(2,1)} %shard_map.365), channel_id=1, source_target_pairs={{0,8},{4,12},{8,0},{12,4},{16,24},{20,28},{24,16},{28,20},{1,9},{5... | collective-permute-start | bytes 3981320 | tf_op jit(solution)/shard_map/ppermute | solution.py:303
  71.9 31.1 %collective-permute-start.14 = (bf16[144,4608]{1,0:T(8,128)(2,1)}, bf16[144,4608]{1,0:T(8,128)(2,1)S(1)}, u32[]{:S(2)}, u32[]{:S(2)}) collective-permute-start(bf16[144,4608]{1,0:T(8,128)(2,1)} %shard_map.365), channel_id=1, source_target_pairs={{0,16},{4,20},{8,24},{12,28},{16,0},{20,4},{24,8},{28,12},{1,17},{... | collective-permute-start | bytes 3981320 | tf_op jit(solution)/shard_map/ppermute | solution.py:303
  73.4 17.0 %collective-permute-start.15 = (bf16[144,1152]{1,0:T(8,128)(2,1)S(1)}, bf16[144,1152]{1,0:T(8,128)(2,1)S(1)}, u32[]{:S(2)}, u32[]{:S(2)}) collective-permute-start(bf16[144,1152]{1,0:T(8,128)(2,1)S(1)} %convert_element_type.171.refs_0_), channel_id=1, source_target_pairs={{0,2},{1,3},{2,0},{3,1},{4,6},{5,7},{6,4},{7,5},{8,10},{9,11},{10,... | collective-permute-start | bytes 995336 | tf_op jit(solution)/shard_map/ppermute | solution.py:307
  73.7 16.7 %collective-permute-start.16 = (bf16[144,1152]{1,0:T(8,128)(2,1)S(1)}, bf16[144,1152]{1,0:T(8,128)(2,1)S(1)}, u32[]{:S(2)}, u32[]{:S(2)}) collective-permute-start(bf16[144,1152]{1,0:T(8,128)(2,1)S(1)} %convert_element_type.171.refs_0_), channel_id=1, source_target_pairs={{0,1},{1,0},{2,3},{3,2},{4,5},{5,4},{6,7},{7,6},{8,9},{9,8},{10,11... | collective-permute-start | bytes 995336 | tf_op jit(solution)/shard_map/ppermute | solution.py:307
  102.9 18.9 %collective-permute-start.20 = (bf16[144,4608]{1,0:T(8,128)(2,1)S(1)}, bf16[144,4608]{1,0:T(8,128)(2,1)S(1)}, u32[]{:S(2)}, u32[]{:S(2)}) collective-permute-start(bf16[144,4608]{1,0:T(8,128)(2,1)S(1)} %collective-permute-done.13.refs_1_.refs_7_), channel_id=1, source_target_pairs={{0,4},{4,0},{8,12},{12,8},{16,20},{20,16},{24,28},{28,24},{1,5},{5... | collective-permute-start | bytes 3981320 | tf_op jit(solution)/shard_map/ppermute | solution.py:303
  102.9 19.9 %collective-permute-start.21 = (bf16[144,4608]{1,0:T(8,128)(2,1)S(1)}, bf16[144,4608]{1,0:T(8,128)(2,1)}, u32[]{:S(2)}, u32[]{:S(2)}) collective-permute-start(bf16[144,4608]{1,0:T(8,128)(2,1)S(1)} %collective-permute-done.14.refs_2_.refs_8_), channel_id=1, source_target_pairs={{0,4},{4,0},{8,12},{12,8},{16,20},{20,16},{24,28},{28,24},{1,5},{5... | collective-permute-start | bytes 3981320 | tf_op jit(solution)/shard_map/ppermute | solution.py:303
  104.0 16.5 %collective-permute-start.18 = (bf16[144,2304]{1,0:T(8,128)(2,1)S(1)}, bf16[144,2304]{1,0:T(8,128)(2,1)}, u32[]{:S(2)}, u32[]{:S(2)}) collective-permute-start(bf16[144,2304]{1,0:T(8,128)(2,1)S(1)} %slice.513), channel_id=1, source_target_pairs={{0,16},{4,20},{8,24},{12,28},{16,0},{20,4},{24,8},{28,12},{1,17},{... | collective-permute-start | bytes 1990664 | tf_op jit(solution)/shard_map/ppermute | solution.py:303
  105.6 16.2 %collective-permute-start.19 = (bf16[144,2304]{1,0:T(8,128)(2,1)S(1)}, bf16[144,2304]{1,0:T(8,128)(2,1)}, u32[]{:S(2)}, u32[]{:S(2)}) collective-permute-start(bf16[144,2304]{1,0:T(8,128)(2,1)S(1)} %slice.514), channel_id=1, source_target_pairs={{0,8},{4,12},{8,0},{12,4},{16,24},{20,28},{24,16},{28,20},{1,9},{5... | collective-permute-start | bytes 1990664 | tf_op jit(solution)/shard_map/ppermute | solution.py:303
  124.4 31.8 %collective-permute-start.23 = (bf16[144,4608]{1,0:T(8,128)(2,1)}, bf16[144,4608]{1,0:T(8,128)(2,1)S(1)}, u32[]{:S(2)}, u32[]{:S(2)}) collective-permute-start(bf16[144,4608]{1,0:T(8,128)(2,1)} %shard_map.367), channel_id=1, source_target_pairs={{0,8},{4,12},{8,0},{12,4},{16,24},{20,28},{24,16},{28,20},{1,9},{5... | collective-permute-start | bytes 3981320 | tf_op jit(solution)/shard_map/ppermute | solution.py:303
  125.0 31.4 %collective-permute-start.24 = (bf16[144,4608]{1,0:T(8,128)(2,1)}, bf16[144,4608]{1,0:T(8,128)(2,1)S(1)}, u32[]{:S(2)}, u32[]{:S(2)}) collective-permute-start(bf16[144,4608]{1,0:T(8,128)(2,1)} %shard_map.367), channel_id=1, source_target_pairs={{0,16},{4,20},{8,24},{12,28},{16,0},{20,4},{24,8},{28,12},{1,17},{... | collective-permute-start | bytes 3981320 | tf_op jit(solution)/shard_map/ppermute | solution.py:303
  125.5 19.4 %collective-permute-start.25 = (bf16[144,1152]{1,0:T(8,128)(2,1)S(1)}, bf16[144,1152]{1,0:T(8,128)(2,1)}, u32[]{:S(2)}, u32[]{:S(2)}) collective-permute-start(bf16[144,1152]{1,0:T(8,128)(2,1)S(1)} %concatenate.80.refs_0_), channel_id=1, source_target_pairs={{0,2},{1,3},{2,0},{3,1},{4,6},{5,7},{6,4},{7,5},{8,10},{9,11},{10,... | collective-permute-start | bytes 995336 | tf_op jit(solution)/shard_map/ppermute | solution.py:307
  126.8 18.1 %collective-permute-start.26 = (bf16[144,1152]{1,0:T(8,128)(2,1)S(1)}, bf16[144,1152]{1,0:T(8,128)(2,1)}, u32[]{:S(2)}, u32[]{:S(2)}) collective-permute-start(bf16[144,1152]{1,0:T(8,128)(2,1)S(1)} %concatenate.80.refs_0_), channel_id=1, source_target_pairs={{0,1},{1,0},{2,3},{3,2},{4,5},{5,4},{6,7},{7,6},{8,9},{9,8},{10,11... | collective-permute-start | bytes 995336 | tf_op jit(solution)/shard_map/ppermute | solution.py:307
  156.4 20.6 %collective-permute-start.30 = (bf16[144,4608]{1,0:T(8,128)(2,1)S(1)}, bf16[144,4608]{1,0:T(8,128)(2,1)S(1)}, u32[]{:S(2)}, u32[]{:S(2)}) collective-permute-start(bf16[144,4608]{1,0:T(8,128)(2,1)S(1)} %collective-permute-done.23.refs_1_), channel_id=1, source_target_pairs={{0,4},{4,0},{8,12},{12,8},{16,20},{20,16},{24,28},{28,24},{1,5},{5... | collective-permute-start | bytes 3981320 | tf_op jit(solution)/shard_map/ppermute | solution.py:303
  156.4 20.6 %collective-permute-start.31 = (bf16[144,4608]{1,0:T(8,128)(2,1)S(1)}, bf16[144,4608]{1,0:T(8,128)(2,1)S(1)}, u32[]{:S(2)}, u32[]{:S(2)}) collective-permute-start(bf16[144,4608]{1,0:T(8,128)(2,1)S(1)} %collective-permute-done.24.refs_2_), channel_id=1, source_target_pairs={{0,4},{4,0},{8,12},{12,8},{16,20},{20,16},{24,28},{28,24},{1,5},{5... | collective-permute-start | bytes 3981320 | tf_op jit(solution)/shard_map/ppermute | solution.py:303
  157.7 19.3 %collective-permute-start.28 = (bf16[144,2304]{1,0:T(8,128)(2,1)S(1)}, bf16[144,2304]{1,0:T(8,128)(2,1)S(1)}, u32[]{:S(2)}, u32[]{:S(2)}) collective-permute-start(bf16[144,2304]{1,0:T(8,128)(2,1)S(1)} %slice.515), channel_id=1, source_target_pairs={{0,16},{4,20},{8,24},{12,28},{16,0},{20,4},{24,8},{28,12},{1,17},{... | collective-permute-start | bytes 1990664 | tf_op jit(solution)/shard_map/ppermute | solution.py:303
  158.2 18.8 %collective-permute-start.29 = (bf16[144,2304]{1,0:T(8,128)(2,1)S(1)}, bf16[144,2304]{1,0:T(8,128)(2,1)S(1)}, u32[]{:S(2)}, u32[]{:S(2)}) collective-permute-start(bf16[144,2304]{1,0:T(8,128)(2,1)S(1)} %slice.516), channel_id=1, source_target_pairs={{0,8},{4,12},{8,0},{12,4},{16,24},{20,28},{24,16},{28,20},{1,9},{5... | collective-permute-start | bytes 1990664 | tf_op jit(solution)/shard_map/ppermute | solution.py:303
  159.5 13.5 %collective-permute-start.32 = (bf16[144,1152]{1,0:T(8,128)(2,1)}, bf16[144,1152]{1,0:T(8,128)(2,1)S(1)}, u32[]{:S(2)}, u32[]{:S(2)}) collective-permute-start(bf16[144,1152]{1,0:T(8,128)(2,1)} %collective-permute-done.25.refs_2_), channel_id=1, source_target_pairs={{0,1},{1,0},{2,3},{3,2},{4,5},{5,4},{6,7},{7,6},{8,9},{9,8},{10,11... | collective-permute-start | bytes 995336 | tf_op jit(solution)/shard_map/ppermute | solution.py:307
  180.1 32.1 %collective-permute-start.33 = (bf16[576,1152]{1,0:T(8,128)(2,1)}, bf16[576,1152]{1,0:T(8,128)(2,1)S(1)}, u32[]{:S(2)}, u32[]{:S(2)}) collective-permute-start(bf16[576,1152]{1,0:T(8,128)(2,1)} %shard_map.369), channel_id=1, source_target_pairs={{0,8},{4,12},{8,0},{12,4},{16,24},{20,28},{24,16},{28,20},{1,9},{5... | collective-permute-start | bytes 3981320 | tf_op jit(solution)/shard_map/ppermute | solution.py:303
  180.9 31.4 %collective-permute-start.34 = (bf16[576,1152]{1,0:T(8,128)(2,1)}, bf16[576,1152]{1,0:T(8,128)(2,1)S(1)}, u32[]{:S(2)}, u32[]{:S(2)}) collective-permute-start(bf16[576,1152]{1,0:T(8,128)(2,1)} %shard_map.369), channel_id=1, source_target_pairs={{0,16},{4,20},{8,24},{12,28},{16,0},{20,4},{24,8},{28,12},{1,17},{... | collective-permute-start | bytes 3981320 | tf_op jit(solution)/shard_map/ppermute | solution.py:303
  182.4 29.8 %collective-permute-start.35 = (bf16[258,1152]{1,0:T(8,128)(2,1)}, bf16[258,1152]{1,0:T(8,128)(2,1)}, u32[]{:S(2)}, u32[]{:S(2)}) collective-permute-start(bf16[258,1152]{1,0:T(8,128)(2,1)} %get-tuple-element.284.refs_0_), channel_id=1, source_target_pairs={{0,2},{1,3},{2,0},{3,1},{4,6},{5,7},{6,4},{7,5},{8,10},{9,11},{10,... | collective-permute-start | bytes 1783304 | tf_op jit(solution)/shard_map/ppermute | solution.py:307
  184.0 28.2 %collective-permute-start.36 = (bf16[258,1152]{1,0:T(8,128)(2,1)}, bf16[258,1152]{1,0:T(8,128)(2,1)}, u32[]{:S(2)}, u32[]{:S(2)}) collective-permute-start(bf16[258,1152]{1,0:T(8,128)(2,1)} %get-tuple-element.284.refs_0_), channel_id=1, source_target_pairs={{0,1},{1,0},{2,3},{3,2},{4,5},{5,4},{6,7},{7,6},{8,9},{9,8},{10,11... | collective-permute-start | bytes 1783304 | tf_op jit(solution)/shard_map/ppermute | solution.py:307
  212.3 20.2 %collective-permute-start.40 = (bf16[576,1152]{1,0:T(8,128)(2,1)S(1)}, bf16[576,1152]{1,0:T(8,128)(2,1)S(1)}, u32[]{:S(2)}, u32[]{:S(2)}) collective-permute-start(bf16[576,1152]{1,0:T(8,128)(2,1)S(1)} %collective-permute-done.33.refs_1_), channel_id=1, source_target_pairs={{0,4},{4,0},{8,12},{12,8},{16,20},{20,16},{24,28},{28,24},{1,5},{5... | collective-permute-start | bytes 3981320 | tf_op jit(solution)/shard_map/ppermute | solution.py:303
  212.8 19.7 %collective-permute-start.41 = (bf16[576,1152]{1,0:T(8,128)(2,1)S(1)}, bf16[576,1152]{1,0:T(8,128)(2,1)S(1)}, u32[]{:S(2)}, u32[]{:S(2)}) collective-permute-start(bf16[576,1152]{1,0:T(8,128)(2,1)S(1)} %collective-permute-done.34.refs_2_), channel_id=1, source_target_pairs={{0,4},{4,0},{8,12},{12,8},{16,20},{20,16},{24,28},{28,24},{1,5},{5... | collective-permute-start | bytes 3981320 | tf_op jit(solution)/shard_map/ppermute | solution.py:303
  214.0 17.5 %collective-permute-start.38 = (bf16[288,1152]{1,0:T(8,128)(2,1)}, bf16[288,1152]{1,0:T(8,128)(2,1)}, u32[]{:S(2)}, u32[]{:S(2)}) collective-permute-start(bf16[288,1152]{1,0:T(8,128)(2,1)} %slice.518), channel_id=1, source_target_pairs={{0,16},{4,20},{8,24},{12,28},{16,0},{20,4},{24,8},{28,12},{1,17},{... | collective-permute-start | bytes 1990664 | tf_op jit(solution)/shard_map/ppermute | solution.py:303
  215.4 17.1 %collective-permute-start.39 = (bf16[288,1152]{1,0:T(8,128)(2,1)S(1)}, bf16[288,1152]{1,0:T(8,128)(2,1)}, u32[]{:S(2)}, u32[]{:S(2)}) collective-permute-start(bf16[288,1152]{1,0:T(8,128)(2,1)S(1)} %slice.519), channel_id=1, source_target_pairs={{0,8},{4,12},{8,0},{12,4},{16,24},{20,28},{24,16},{28,20},{1,9},{5... | collective-permute-start | bytes 1990664 | tf_op jit(solution)/shard_map/ppermute | solution.py:303
  236.7 31.8 %collective-permute-start.43 = (bf16[2,288,1152]{2,1,0:T(8,128)(2,1)}, bf16[2,288,1152]{2,1,0:T(8,128)(2,1)S(1)}, u32[]{:S(2)}, u32[]{:S(2)}) collective-permute-start(bf16[2,288,1152]{2,1,0:T(8,128)(2,1)} %get-tuple-element.306), channel_id=1, source_target_pairs={{0,8},{4,12},{8,0},{12,4},{16,24},{20,28},{24,16},{28,20},{1,9},{5... | collective-permute-start | bytes 3981320 | tf_op jit(solution)/shard_map/ppermute | solution.py:303
  238.1 31.5 %collective-permute-start.44 = (bf16[2,288,1152]{2,1,0:T(8,128)(2,1)}, bf16[2,288,1152]{2,1,0:T(8,128)(2,1)}, u32[]{:S(2)}, u32[]{:S(2)}) collective-permute-start(bf16[2,288,1152]{2,1,0:T(8,128)(2,1)} %get-tuple-element.307), channel_id=1, source_target_pairs={{0,16},{4,20},{8,24},{12,28},{16,0},{20,4},{24,8},{28,12},{1,17},{... | collective-permute-start | bytes 3981320 | tf_op jit(solution)/shard_map/ppermute | solution.py:303
  238.6 29.6 %collective-permute-start.45 = (bf16[258,1152]{1,0:T(8,128)(2,1)S(1)}, bf16[258,1152]{1,0:T(8,128)(2,1)}, u32[]{:S(2)}, u32[]{:S(2)}) collective-permute-start(bf16[258,1152]{1,0:T(8,128)(2,1)S(1)} %copy-done.43), channel_id=1, source_target_pairs={{0,2},{1,3},{2,0},{3,1},{4,6},{5,7},{6,4},{7,5},{8,10},{9,11},{10,... | collective-permute-start | bytes 1783304 | tf_op jit(solution)/shard_map/ppermute | solution.py:307
  240.3 27.8 %collective-permute-start.46 = (bf16[258,1152]{1,0:T(8,128)(2,1)}, bf16[258,1152]{1,0:T(8,128)(2,1)S(1)}, u32[]{:S(2)}, u32[]{:S(2)}) collective-permute-start(bf16[258,1152]{1,0:T(8,128)(2,1)} %collective-permute-done.35.refs_2_), channel_id=1, source_target_pairs={{0,1},{1,0},{2,3},{3,2},{4,5},{5,4},{6,7},{7,6},{8,9},{9,8},{10,11... | collective-permute-start | bytes 1783304 | tf_op jit(solution)/shard_map/ppermute | solution.py:307
  271.4 16.9 %collective-permute-start.49 = (bf16[288,1152]{1,0:T(8,128)(2,1)S(1)}, bf16[288,1152]{1,0:T(8,128)(2,1)S(1)}, u32[]{:S(2)}, u32[]{:S(2)}) collective-permute-start(bf16[288,1152]{1,0:T(8,128)(2,1)S(1)} %fusion.2), channel_id=1, source_target_pairs={{0,8},{4,12},{8,0},{12,4},{16,24},{20,28},{24,16},{28,20},{1,9},{5... | collective-permute-start | bytes 1990664 | tf_op jit(solution)/shard_map/ppermute | solution.py:303
  272.4 16.6 %collective-permute-start.48 = (bf16[288,1152]{1,0:T(8,128)(2,1)S(1)}, bf16[288,1152]{1,0:T(8,128)(2,1)S(1)}, u32[]{:S(2)}, u32[]{:S(2)}) collective-permute-start(bf16[288,1152]{1,0:T(8,128)(2,1)S(1)} %fusion.1), channel_id=1, source_target_pairs={{0,16},{4,20},{8,24},{12,28},{16,0},{20,4},{24,8},{28,12},{1,17},{... | collective-permute-start | bytes 1990664 | tf_op jit(solution)/shard_map/ppermute | solution.py:303
  272.9 15.1 %collective-permute-start.50 = (bf16[258,1152]{1,0:T(8,128)(2,1)S(1)}, bf16[258,1152]{1,0:T(8,128)(2,1)S(1)}, u32[]{:S(2)}, u32[]{:S(2)}) collective-permute-start(bf16[258,1152]{1,0:T(8,128)(2,1)S(1)} %copy-done.43), channel_id=1, source_target_pairs={{0,1},{1,0},{2,3},{3,2},{4,5},{5,4},{6,7},{7,6},{8,9},{9,8},{10,11... | collective-permute-start | bytes 1783304 | tf_op jit(solution)/shard_map/ppermute | solution.py:307
  289.0 32.8 %collective-permute-start.53 = (bf16[2,144,2304]{2,1,0:T(8,128)(2,1)}, bf16[2,144,2304]{2,1,0:T(8,128)(2,1)S(1)}, u32[]{:S(2)}, u32[]{:S(2)}) collective-permute-start(bf16[2,144,2304]{2,1,0:T(8,128)(2,1)} %get-tuple-element.337), channel_id=1, source_target_pairs={{0,8},{4,12},{8,0},{12,4},{16,24},{20,28},{24,16},{28,20},{1,9},{5... | collective-permute-start | bytes 3981320 | tf_op jit(solution)/shard_map/ppermute | solution.py:303
  290.3 31.5 %collective-permute-start.54 = (bf16[2,144,2304]{2,1,0:T(8,128)(2,1)}, bf16[2,144,2304]{2,1,0:T(8,128)(2,1)S(1)}, u32[]{:S(2)}, u32[]{:S(2)}) collective-permute-start(bf16[2,144,2304]{2,1,0:T(8,128)(2,1)} %get-tuple-element.338), channel_id=1, source_target_pairs={{0,16},{4,20},{8,24},{12,28},{16,0},{20,4},{24,8},{28,12},{1,17},{... | collective-permute-start | bytes 3981320 | tf_op jit(solution)/shard_map/ppermute | solution.py:303
  291.7 30.1 %collective-permute-start.55 = (bf16[258,1152]{1,0:T(8,128)(2,1)}, bf16[258,1152]{1,0:T(8,128)(2,1)S(1)}, u32[]{:S(2)}, u32[]{:S(2)}) collective-permute-start(bf16[258,1152]{1,0:T(8,128)(2,1)} %collective-permute-done.45.refs_6_), channel_id=1, source_target_pairs={{0,1},{1,0},{2,3},{3,2},{4,5},{5,4},{6,7},{7,6},{8,9},{9,8},{10,11... | collective-permute-start | bytes 1783304 | tf_op jit(solution)/shard_map/ppermute | solution.py:307
  293.4 28.4 %collective-permute-start.56 = (bf16[576,384]{1,0:T(8,128)(2,1)}, bf16[576,384]{1,0:T(8,128)(2,1)S(1)}, u32[]{:S(2)}, u32[]{:S(2)}) collective-permute-start(bf16[576,384]{1,0:T(8,128)(2,1)} %get-tuple-element.345), channel_id=1, source_target_pairs={{0,4},{4,0},{8,12},{12,8},{16,20},{20,16},{24,28},{28,24},{1,5},{5... | collective-permute-start | bytes 1327112 | tf_op jit(solution)/shard_map/ppermute | solution.py:303
  322.6 24.1 %collective-permute-start.58 = (bf16[144,2304]{1,0:T(8,128)(2,1)S(1)}, bf16[144,2304]{1,0:T(8,128)(2,1)S(1)}, u32[]{:S(2)}, u32[]{:S(2)}) collective-permute-start(bf16[144,2304]{1,0:T(8,128)(2,1)S(1)} %fusion.4), channel_id=1, source_target_pairs={{0,8},{4,12},{8,0},{12,4},{16,24},{20,28},{24,16},{28,20},{1,9},{5... | collective-permute-start | bytes 1990664 | tf_op jit(solution)/shard_map/ppermute | solution.py:303
  324.2 22.4 %collective-permute-start.57 = (bf16[144,2304]{1,0:T(8,128)(2,1)S(1)}, bf16[144,2304]{1,0:T(8,128)(2,1)S(1)}, u32[]{:S(2)}, u32[]{:S(2)}) collective-permute-start(bf16[144,2304]{1,0:T(8,128)(2,1)S(1)} %fusion.3), channel_id=1, source_target_pairs={{0,16},{4,20},{8,24},{12,28},{16,0},{20,4},{24,8},{28,12},{1,17},{... | collective-permute-start | bytes 1990664 | tf_op jit(solution)/shard_map/ppermute | solution.py:303
  329.4 11.9 %collective-permute-start.59 = (bf16[144,1152]{1,0:T(8,128)(2,1)}, bf16[144,1152]{1,0:T(8,128)(2,1)S(1)}, u32[]{:S(2)}, u32[]{:S(2)}) collective-permute-start(bf16[144,1152]{1,0:T(8,128)(2,1)} %get-tuple-element.351), channel_id=1, source_target_pairs={{0,1},{1,0},{2,3},{3,2},{4,5},{5,4},{6,7},{7,6},{8,9},{9,8},{10,11... | collective-permute-start | bytes 995336 | tf_op jit(solution)/shard_map/ppermute | solution.py:307
  329.7 17.0 %collective-permute-start.60 = (bf16[144,1152]{1,0:T(8,128)(2,1)}, bf16[144,1152]{1,0:T(8,128)(2,1)S(1)}, u32[]{:S(2)}, u32[]{:S(2)}) collective-permute-start(bf16[144,1152]{1,0:T(8,128)(2,1)} %get-tuple-element.352), channel_id=1, source_target_pairs={{0,1},{1,0},{2,3},{3,2},{4,5},{5,4},{6,7},{7,6},{8,9},{9,8},{10,11... | collective-permute-start | bytes 995336 | tf_op jit(solution)/shard_map/ppermute | solution.py:307
  346.7 30.7 %collective-permute-start.62 = (bf16[2,144,2304]{2,1,0:T(8,128)(2,1)}, bf16[2,144,2304]{2,1,0:T(8,128)(2,1)S(1)}, u32[]{:S(2)}, u32[]{:S(2)}) collective-permute-start(bf16[2,144,2304]{2,1,0:T(8,128)(2,1)} %get-tuple-element.361), channel_id=1, source_target_pairs={{0,8},{4,12},{8,0},{12,4},{16,24},{20,28},{24,16},{28,20},{1,9},{5... | collective-permute-start | bytes 3981320 | tf_op jit(solution)/shard_map/ppermute | solution.py:303
  347.5 30.4 %collective-permute-start.63 = (bf16[2,144,2304]{2,1,0:T(8,128)(2,1)}, bf16[2,144,2304]{2,1,0:T(8,128)(2,1)S(1)}, u32[]{:S(2)}, u32[]{:S(2)}) collective-permute-start(bf16[2,144,2304]{2,1,0:T(8,128)(2,1)} %get-tuple-element.362), channel_id=1, source_target_pairs={{0,16},{4,20},{8,24},{12,28},{16,0},{20,4},{24,8},{28,12},{1,17},{... | collective-permute-start | bytes 3981320 | tf_op jit(solution)/shard_map/ppermute | solution.py:303
  348.9 17.8 %collective-permute-start.66 = (bf16[144,1152]{1,0:T(8,128)(2,1)S(1)}, bf16[144,1152]{1,0:T(8,128)(2,1)S(1)}, u32[]{:S(2)}, u32[]{:S(2)}) collective-permute-start(bf16[144,1152]{1,0:T(8,128)(2,1)S(1)} %add_convert_fusion.8), channel_id=1, source_target_pairs={{0,2},{1,3},{2,0},{3,1},{4,6},{5,7},{6,4},{7,5},{8,10},{9,11},{10,... | collective-permute-start | bytes 995336 | tf_op jit(solution)/shard_map/ppermute | solution.py:307
  354.0 17.7 %collective-permute-start.64 = (bf16[144,1152]{1,0:T(8,128)(2,1)}, bf16[144,1152]{1,0:T(8,128)(2,1)S(1)}, u32[]{:S(2)}, u32[]{:S(2)}) collective-permute-start(bf16[144,1152]{1,0:T(8,128)(2,1)} %get-tuple-element.365), channel_id=1, source_target_pairs={{0,1},{1,0},{2,3},{3,2},{4,5},{5,4},{6,7},{7,6},{8,9},{9,8},{10,11... | collective-permute-start | bytes 995336 | tf_op jit(solution)/shard_map/ppermute | solution.py:307
  355.2 21.4 %collective-permute-start.65 = (bf16[144,1152]{1,0:T(8,128)(2,1)}, bf16[144,1152]{1,0:T(8,128)(2,1)S(1)}, u32[]{:S(2)}, u32[]{:S(2)}) collective-permute-start(bf16[144,1152]{1,0:T(8,128)(2,1)} %get-tuple-element.366), channel_id=1, source_target_pairs={{0,1},{1,0},{2,3},{3,2},{4,5},{5,4},{6,7},{7,6},{8,9},{9,8},{10,11... | collective-permute-start | bytes 995336 | tf_op jit(solution)/shard_map/ppermute | solution.py:307
  378.0 19.6 %collective-permute-start.68 = (bf16[144,2304]{1,0:T(8,128)(2,1)S(1)}, bf16[144,2304]{1,0:T(8,128)(2,1)S(1)}, u32[]{:S(2)}, u32[]{:S(2)}) collective-permute-start(bf16[144,2304]{1,0:T(8,128)(2,1)S(1)} %fusion.6), channel_id=1, source_target_pairs={{0,8},{4,12},{8,0},{12,4},{16,24},{20,28},{24,16},{28,20},{1,9},{5... | collective-permute-start | bytes 1990664 | tf_op jit(solution)/shard_map/ppermute | solution.py:303
  379.6 18.1 %collective-permute-start.67 = (bf16[144,2304]{1,0:T(8,128)(2,1)S(1)}, bf16[144,2304]{1,0:T(8,128)(2,1)S(1)}, u32[]{:S(2)}, u32[]{:S(2)}) collective-permute-start(bf16[144,2304]{1,0:T(8,128)(2,1)S(1)} %fusion.5), channel_id=1, source_target_pairs={{0,16},{4,20},{8,24},{12,28},{16,0},{20,4},{24,8},{28,12},{1,17},{... | collective-permute-start | bytes 1990664 | tf_op jit(solution)/shard_map/ppermute | solution.py:303
  381.3 16.3 %collective-permute-start.70 = (bf16[272,288]{1,0:T(8,128)(2,1)S(1)}, bf16[272,288]{1,0:T(8,128)(2,1)S(1)}, u32[]{:S(2)}, u32[]{:S(2)}) collective-permute-start(bf16[272,288]{1,0:T(8,128)(2,1)S(1)} %copy-done.98), channel_id=1, source_target_pairs={{0,2},{1,3},{2,0},{3,1},{4,6},{5,7},{6,4},{7,5},{8,10},{9,11},{10,... | collective-permute-start | bytes 470024 | tf_op jit(solution)/shard_map/ppermute | solution.py:307
  382.9 14.8 %collective-permute-start.71 = (bf16[272,288]{1,0:T(8,128)(2,1)S(1)}, bf16[272,288]{1,0:T(8,128)(2,1)S(1)}, u32[]{:S(2)}, u32[]{:S(2)}) collective-permute-start(bf16[272,288]{1,0:T(8,128)(2,1)S(1)} %copy-done.97), channel_id=1, source_target_pairs={{0,3},{1,2},{2,1},{3,0},{4,7},{5,6},{6,5},{7,4},{8,11},{9,10},{10,... | collective-permute-start | bytes 470024 | tf_op jit(solution)/shard_map/ppermute | solution.py:307
  397.9 11.0 %collective-permute-start.74 = (bf16[4,272,288]{2,1,0:T(8,128)(2,1)S(1)}, bf16[4,272,288]{2,1,0:T(8,128)(2,1)S(1)}, u32[]{:S(2)}, u32[]{:S(2)}) collective-permute-start(bf16[4,272,288]{2,1,0:T(8,128)(2,1)S(1)} %pad_maximum_fusion.3.refs_8_), channel_id=1, source_target_pairs={{0,4},{4,0},{8,12},{12,8},{16,20},{20,16},{24,28},{28,24},{1,5},{5... | collective-permute-start | bytes 1880072 | tf_op jit(solution)/shard_map/ppermute | solution.py:303
  398.7 19.2 %collective-permute-start.75 = (bf16[144,1152]{1,0:T(8,128)(2,1)S(1)}, bf16[144,1152]{1,0:T(8,128)(2,1)S(1)}, u32[]{:S(2)}, u32[]{:S(2)}) collective-permute-start(bf16[144,1152]{1,0:T(8,128)(2,1)S(1)} %add_convert_fusion.7), channel_id=1, source_target_pairs={{0,2},{1,3},{2,0},{3,1},{4,6},{5,7},{6,4},{7,5},{8,10},{9,11},{10,... | collective-permute-start | bytes 995336 | tf_op jit(solution)/shard_map/ppermute | solution.py:307
  406.9 16.1 %collective-permute-start.72 = (bf16[144,1152]{1,0:T(8,128)(2,1)}, bf16[144,1152]{1,0:T(8,128)(2,1)S(1)}, u32[]{:S(2)}, u32[]{:S(2)}) collective-permute-start(bf16[144,1152]{1,0:T(8,128)(2,1)} %get-tuple-element.392), channel_id=1, source_target_pairs={{0,1},{1,0},{2,3},{3,2},{4,5},{5,4},{6,7},{7,6},{8,9},{9,8},{10,11... | collective-permute-start | bytes 995336 | tf_op jit(solution)/shard_map/ppermute | solution.py:307
  406.9 21.9 %collective-permute-start.73 = (bf16[144,1152]{1,0:T(8,128)(2,1)}, bf16[144,1152]{1,0:T(8,128)(2,1)S(1)}, u32[]{:S(2)}, u32[]{:S(2)}) collective-permute-start(bf16[144,1152]{1,0:T(8,128)(2,1)} %get-tuple-element.393), channel_id=1, source_target_pairs={{0,1},{1,0},{2,3},{3,2},{4,5},{5,4},{6,7},{7,6},{8,9},{9,8},{10,11... | collective-permute-start | bytes 995336 | tf_op jit(solution)/shard_map/ppermute | solution.py:307
  428.8 16.3 %collective-permute-start.79 = (bf16[144,1152]{1,0:T(8,128)(2,1)S(1)}, bf16[144,1152]{1,0:T(8,128)(2,1)S(1)}, u32[]{:S(2)}, u32[]{:S(2)}) collective-permute-start(bf16[144,1152]{1,0:T(8,128)(2,1)S(1)} %add_convert_fusion.6), channel_id=1, source_target_pairs={{0,2},{1,3},{2,0},{3,1},{4,6},{5,7},{6,4},{7,5},{8,10},{9,11},{10,... | collective-permute-start | bytes 995336 | tf_op jit(solution)/shard_map/ppermute | solution.py:307
  (116 other events, 863.8 us)
